TPU v7x, 256 devices: a whole 4x4x8 slice. The times are simulated.
256 devices in a mesh: inst: 64 (over y, z, core), head: 4 (over x).
Axes of the slice: x: 4, y: 4, z: 8, core: 2. Of those that a mesh axis runs over, the one named last changes fastest.
Arguments:
- queries: bfloat16 [64, 128, 3072], P('inst', None, 'head'), may hold values from -240 to 240
- new_keys: bfloat16 [64, 128, 3072], P('inst', None, 'head'), may hold values from -6 to 6
- new_values: bfloat16 [64, 128, 3072], P('inst', None, 'head'), may hold values from -6 to 6
- pool: bfloat16 [384, 128, 6144], P(None, 'inst', 'head'), may hold values from -6 to 6
- block_table: int32 [384], replicated, may hold values from 0 to 383, each once
- block_counts: int32 [64], replicated, may hold values from 1 to 6, 224 in all
- key_weight: bfloat16 [6144, 3072], P('inst', 'head'), may hold values from -0.078125 to 0.078125
- value_weight: bfloat16 [6144, 3072], P('inst', 'head'), may hold values from -0.078125 to 0.078125
Outputs:
- attention: bfloat16 [64, 128, 3072], P('inst', None, 'head')
Inputs may be any that keep to these rules, and one draw needn't show every extreme that they name: Every entry of block_table names a distinct pool block; conversation c uses the first block_counts[c] of its 6 entries. `block_counts`: the counts of all conversations sum to exactly 224, and some conversation has exactly 6 blocks.
All inputs are finite; a program needn't handle non-finite values.
Results may differ from a plain program's by a relative error of at most 0.0064.
Values may be sent and summed in bfloat16 or wider, within the bound.
No kernel may reach another device: no remote copies, remote signals or barrier semaphores. Data moves between devices by JAX's collectives and lax.ppermute only.
A program may use at most 128 MiB of HBM per device.

v0:
```python
import math

import jax
import jax.numpy as jnp
from jax import lax
from jax.sharding import PartitionSpec as P

HD = 64
BLOCK = 128
MAXB = 6


def project_rows(rows, key_weight, value_weight):
    keys = jnp.dot(
        rows,
        lax.all_gather(key_weight, "inst", axis=0, tiled=True),
        preferred_element_type=jnp.float32,
    )
    values = jnp.dot(
        rows,
        lax.all_gather(value_weight, "inst", axis=0, tiled=True),
        preferred_element_type=jnp.float32,
    )
    return (keys.astype(jnp.bfloat16), values.astype(jnp.bfloat16))


def attend_local(q_rows, keys, values, live_rows):
    total = keys.shape[0]
    count_new = q_rows.shape[0]
    hist_len = total - count_new
    head_count = q_rows.shape[1] // HD
    scale = 1.0 / math.sqrt(HD)
    q_heads = q_rows.reshape(count_new, head_count, HD)
    k_heads = keys.reshape(total, head_count, HD)
    v_heads = values.reshape(total, head_count, HD)
    scores = (
        jnp.einsum("qhd,khd->hqk", q_heads, k_heads, preferred_element_type=jnp.float32) * scale
    )
    column = jnp.arange(total)[None, :]
    row_pos = jnp.arange(count_new)[:, None]
    allowed = jnp.where(column < hist_len, column < live_rows, column - hist_len <= row_pos)
    scores = jnp.where(allowed[None], scores, -jnp.inf)
    top = jnp.max(scores, axis=-1, keepdims=True)
    weights = jnp.exp(scores - top)
    probs = (weights / jnp.sum(weights, axis=-1, keepdims=True)).astype(jnp.bfloat16)
    result = jnp.einsum("hqk,khd->qhd", probs, v_heads, preferred_element_type=jnp.float32)
    return result.reshape(count_new, head_count * HD).astype(jnp.bfloat16)


def per_device(
    queries, new_keys, new_values, pool, block_table, block_counts, key_weight, value_weight
):
    inst_count = lax.axis_size("inst")
    mine = lax.axis_index("inst")
    quarter = pool.shape[2]
    table = block_table.reshape(inst_count, MAXB)
    slot_order = jnp.arange(MAXB, dtype=jnp.int32)
    live_slots = slot_order[:, None] < block_counts[None, :]
    outgoing = pool[table.T] * live_slots[:, :, None, None].astype(pool.dtype)
    arrived = lax.all_to_all(outgoing, "inst", split_axis=1, concat_axis=1, tiled=True)
    fetched = arrived.reshape(MAXB * BLOCK, quarter)
    full_rows = lax.all_gather(fetched, "head", axis=1, tiled=True)
    hist_keys, hist_values = project_rows(full_rows, key_weight, value_weight)
    keys = jnp.concatenate([hist_keys, new_keys[0]], axis=0)
    values = jnp.concatenate([hist_values, new_values[0]], axis=0)
    live_rows = block_counts[mine] * BLOCK
    return attend_local(queries[0], keys, values, live_rows)[None]


def solution(mesh):
    return jax.shard_map(
        per_device,
        mesh=mesh,
        in_specs=(
            P("inst", None, "head"),
            P("inst", None, "head"),
            P("inst", None, "head"),
            P(None, "inst", "head"),
            P(),
            P(),
            P("inst", "head"),
            P("inst", "head"),
        ),
        out_specs=P("inst", None, "head"),
        check_vma=False,
    )
```

profile of v0, /device:TPU:1, one launch (start us, length us, event | category | flops | bytes accessed | tf_op | source)
XLA Modules:
  0.0 332.7 jit_solution(10696140128887699686)
XLA Ops:
  6.5 0.0 copy-start
  6.5 0.0 all-gather.8.cloned.1.call-start
  6.5 0.7 all-gather.8.cloned.1.call-update
  7.3 0.0 all-gather.4.cloned.1.call-start
  7.3 0.8 reshape.114
  8.1 0.1 copy.34
  8.2 0.1 reshape.118
  8.3 0.0 copy-done
  8.3 19.1 %gather_fusion = bf16[384,2,1536]{2,1,0:T(2,128)(2,1)} fusion(bf16[384,2,1536]{2,1,0:T(2,128)(2,1)S(1)} %copy-done, s32[1024]{0:T(1024)S(1)} %pad_clamp_fusion), kind=kCustom, calls=%fused_computation | custom fusion | bytes 4720128 | tf_op jit(solution)/shard_map/gather | solution.py:59
  27.4 0.0 copy-start.4
  27.4 1.9 copy.35
  29.3 0.0 copy-done.4
  29.3 0.2 broadcast_multiply_fusion
  29.5 2.4 copy.36
  32.0 85.7 %all_to_all.5 = bf16[6,64,2,1536]{3,2,0,1:T(2,128)(2,1)S(1)} all-to-all(bf16[6,64,2,1536]{3,2,0,1:T(2,128)(2,1)S(1)} %copy.36), channel_id=1, replica_groups=mesh['inst'=64,'head'=4] {'inst'}, dimensions={1} | all-to-all | bytes 4718592 | tf_op jit(solution)/shard_map/all_to_all | solution.py:60
  117.7 3.0 copy.37
  120.7 0.0 copy-start.1
  120.7 0.0 copy-start.2
  120.7 6.1 %reshape.115 = bf16[768,1536]{1,0:T(8,128)(2,1)} reshape(bf16[6,64,2,1536]{3,2,1,0:T(2,128)(2,1)} %copy.37) | data formatting | bytes 4718592 | tf_op jit(solution)/shard_map/reshape | solution.py:61
  126.8 0.0 copy-start.3
  126.8 0.0 all-gather.4.cloned.1.call-update
  126.8 0.0 all-gather.6.cloned.1.call-start
  126.9 0.7 all-gather.6.cloned.1.call-update
  127.6 0.6 dynamic_slice.3
  128.1 0.0 copy-done.1
  128.1 0.2 copy.39
  128.3 0.0 copy-done.2
  128.3 0.2 copy.40
  128.5 0.0 copy-done.3
  128.5 0.2 copy.38
  129.4 0.8 fusion.16
  130.2 0.0 all-gather.8.cloned.1.call-done
  130.2 89.7 %all-gather.4.cloned.1.call-done = bf16[768,6144]{1,0:T(8,128)(2,1)} async-done(((bf16[768,1536]{1,0:T(8,128)(2,1)}), bf16[768,6144]{1,0:T(8,128)(2,1)}) %all-gather.4.cloned.1.call-update) | async-done | bytes 9437200 | tf_op jit(solution)/shard_map/all_gather | solution.py:62
  219.9 12.9 %convolution_convert_fusion = bf16[768,768]{0,1:T(8,128)(2,1)S(1)} fusion(bf16[768,6144]{1,0:T(8,128)(2,1)} %all-gather.4.cloned.1.call-done, bf16[6144,768]{1,0:T(8,128)(2,1)} %all-gather.8.cloned.1.call-done), kind=kOutput, calls=%fused_computation.10 | convolution fusion | flops 7248347136 | bytes 20054016 | tf_op jit(solution)/shard_map/dot_general | solution.py:14
  232.8 1.0 fusion.9
  233.8 4.9 %fusion.22 = (f32[12,128]{1,0:T(8,128)S(1)}, f32[12,128,896]{1,2,0:T(8,128)}) fusion(f32[12,896,128]{2,1,0:T(8,128)S(1)} %fusion.9, pred[128,896]{0,1:T(8,128)(4,1)S(1)} %fusion.16), kind=kOutput, calls=%fused_computation.34 | output fusion | flops 8258431 | bytes 11130880 | tf_op jit(solution)/shard_map/sub | solution.py:44
  238.6 70.6 %all-gather.6.cloned.1.call-done = bf16[6144,768]{1,0:T(8,128)(2,1)} async-done(((bf16[96,768]{1,0:T(8,128)(2,1)}), bf16[6144,768]{1,0:T(8,128)(2,1)}) %all-gather.6.cloned.1.call-update) | async-done | bytes 9437200 | tf_op jit(solution)/shard_map/all_gather | solution.py:21
  309.2 12.9 %convolution_convert_fusion.1 = bf16[768,768]{0,1:T(8,128)(2,1)S(1)} fusion(bf16[768,6144]{1,0:T(8,128)(2,1)} %all-gather.4.cloned.1.call-done, bf16[6144,768]{1,0:T(8,128)(2,1)} %all-gather.6.cloned.1.call-done), kind=kOutput, calls=%fused_computation.11 | convolution fusion | flops 7248347136 | bytes 20054016 | tf_op jit(solution)/shard_map/dot_general | solution.py:19
  322.1 3.3 fusion.13
  325.3 0.8 copy.42
  (5 shorter events, 0.0 us)
Async XLA Ops:
  6.5 1.8 copy-start
  6.5 123.6 %all-gather.8.cloned.1.call-start = ((), (), s32[]{:S(2)}) async-start(), calls=%async_computation.3 | async-start | bytes 9584640 | tf_op jit(solution)/shard_map/all_gather | solution.py:16
  7.3 212.6 %all-gather.4.cloned.1.call-start = ((), (), s32[]{:S(2)}) async-start(), calls=%async_computation.1 | async-start | bytes 11796480 | tf_op jit(solution)/shard_map/all_gather | solution.py:62
  27.4 1.9 copy-start.4
  120.7 7.4 %copy-start.1 = (bf16[1,128,768]{2,1,0:T(8,128)(2,1)S(1)}, bf16[1,128,768]{2,1,0:T(8,128)(2,1)}, u32[]{:S(2)}) copy-start(bf16[1,128,768]{2,1,0:T(8,128)(2,1)} %param.9) | copy-start | bytes 589828
  120.7 7.6 %copy-start.2 = (bf16[1,128,768]{2,1,0:T(8,128)(2,1)S(1)}, bf16[1,128,768]{2,1,0:T(8,128)(2,1)}, u32[]{:S(2)}) copy-start(bf16[1,128,768]{2,1,0:T(8,128)(2,1)} %param.8) | copy-start | bytes 589828
  126.8 1.7 copy-start.3
  126.8 182.4 %all-gather.6.cloned.1.call-start = ((), (), s32[]{:S(2)}) async-start(), calls=%async_computation.2 | async-start | bytes 9584640 | tf_op jit(solution)/shard_map/all_gather | solution.py:21
Sparse Core Ops, SparseCore 0:
  10.1 114.9 all-gather.7
  126.9 92.9 all-gather.3
  222.7 86.4 all-gather.5
where the time goes:
time: 333 us
  waiting for transfers between devices  162 us (49%)
  blocking collectives  85.7 us (26%)
  local copies, waits for them, and re-layouts  35.3 us (11%)
  matrix products  30 us (9%)
  between operations  13.9 us (4%)
  other arithmetic  5.9 us (2%)
    all_gather x1, waiting for transfers between devices, per_device(): full_rows = lax.all_gather(fetched, 'head', axis=1, tiled=True)  89.7 us
    all_to_all x1, blocking collectives, per_device(): lax.all_to_all(outgoing, 'inst', split_axis=1, concat_axis=1, tiled=True)  85.7 us
    all_gather x1, waiting for transfers between devices, project_rows(): lax.all_gather(value_weight, 'inst', axis=0, tiled=True)  70.6 us
    gather x2, local copies, waits for them, and re-layouts, per_device(): outgoing = pool[table.T] * live_slots[:, :, None, None].astype(pool.dtype)  21 us
    dot_general x1, matrix products, project_rows(): jnp.dot(rows, lax.all_gather(key_weight, 'inst', axis=0, tiled=True), pre...  12.9 us
    dot_general x1, matrix products, project_rows(): jnp.dot(rows, lax.all_gather(value_weight, 'inst', axis=0, tiled=True), p...  12.9 us
  transfers between devices with their start and end apart: 3, of which 2 were waited for; matrix products, arithmetic and copies ran while one was open for 16% of the time, Pallas kernels for 0%

commit v1 on v0

v1 whole, which is shorter than its diff:
```python
import functools
import math

import jax
import jax.numpy as jnp
from jax import lax
from jax.experimental import pallas as pl
from jax.experimental.pallas import tpu as pltpu
from jax.sharding import Mesh, PartitionSpec as P

HD = 64
MAXB = 6
USED = 224
GRID = (4, 8, 2)
PLANE = ("y", "z", "core")
BF16 = jnp.bfloat16
F32 = jnp.float32
VMEM_LIMIT = 56 * 1024 * 1024


def dot(a, b, contract=((1,), (0,))):
    return lax.dot_general(a, b, (contract, ((), ())), preferred_element_type=F32)


def iota(shape, dim):
    return lax.broadcasted_iota(jnp.int32, shape, dim)


def live_rows_kernel(counts_ref, table_ref, pool_ref, out_ref):
    convs = counts_ref.shape[1]
    slots = table_ref.shape[1]
    parities, blocks, _ = pool_ref.shape
    used = out_ref.shape[1]
    counts = jnp.broadcast_to(counts_ref[...].astype(F32), (8, convs)).astype(BF16)
    conv_of = iota((convs, slots), 1) // MAXB
    conv_row = iota((convs, slots), 0)
    count_k = dot(counts, (conv_row == conv_of).astype(F32).astype(BF16))[0:1]
    start_k = dot(counts, (conv_row < conv_of).astype(F32).astype(BF16))[0:1]
    slot_k = iota((1, slots), 1) % MAXB
    count_k = count_k.astype(jnp.int32)
    place_k = jnp.where(slot_k < count_k, start_k.astype(jnp.int32) + slot_k, -1)
    takes = (iota((used, slots), 0) == place_k).astype(F32).astype(BF16)
    names = (iota((blocks, slots), 0) == table_ref[...]).astype(F32).astype(BF16)
    pick = dot(takes, names, ((1,), (1,))).astype(BF16)
    for r in range(parities):
        out_ref[r] = dot(pick, pool_ref[r]).astype(BF16)


def live_rows(counts, table, pool):
    blocks, parities, feats = pool.shape
    return pl.pallas_call(
        live_rows_kernel,
        out_shape=jax.ShapeDtypeStruct((parities, USED, feats), BF16),
        in_specs=[pl.BlockSpec(memory_space=pltpu.VMEM)] * 3,
        out_specs=pl.BlockSpec(memory_space=pltpu.VMEM),
        compiler_params=pltpu.CompilerParams(vmem_limit_bytes=VMEM_LIMIT),
        name="live_rows",
    )(counts[None], table[None], jnp.transpose(pool, (1, 0, 2)))


def project_kernel(dims, counts_ref, rows_ref, *rest):
    ny, nz, nh, shard = dims
    first = rest[:nz]
    second = rest[nz : nz + ny]
    out_ref, w_ref, x_ref, acc_ref, acc16_ref, w_sem, x_sem = rest[nz + ny :]
    y, z, core = (lax.axis_index(a) for a in PLANE)
    sign = 1 - 2 * core
    cols = w_ref.shape[1]
    feats = w_ref.shape[0] // nh

    copies = {}
    for s in range(ny):
        plane = lax.rem(y - s * sign + ny, ny)
        for cc in range(2):
            copies[s, "x", cc] = pltpu.make_async_copy(
                rows_ref.at[cc * nh + plane], x_ref.at[2 * s + cc], x_sem.at[2 * s + cc]
            )
        for t in range(nz):
            chip = plane * nz + lax.rem(z - t * sign + nz, nz)
            for k, (src, part, owner) in enumerate(
                ((first[t], s, core), (second[s], t, 1 - core))
            ):
                at = pl.multiple_of((chip * 2 + owner) * shard, shard)
                copies[s, t, k] = pltpu.make_async_copy(
                    src.at[pl.ds(part * shard, shard)],
                    w_ref.at[pl.ds(at, shard)],
                    w_sem.at[(s * nz + t) * 2 + k],
                )
    for c in copies.values():
        c.start()
    half = acc_ref.shape[0] // 2
    tile = 256 if cols % 256 == 0 else cols
    for s in range(ny):
        for key, c in copies.items():
            if key[0] == s:
                c.wait()
        plane = lax.rem(y - s * sign + ny, ny)
        at = pl.multiple_of(plane * feats, feats)

        @pl.loop(0, 2)
        def _(cc):
            @pl.loop(0, cols // tile)
            def _(n):
                lanes = pl.ds(pl.multiple_of(n * tile, tile), tile)
                row = pl.ds(pl.multiple_of(cc * half, half), half)
                part = dot(x_ref[2 * s + cc], w_ref[pl.ds(at, feats), lanes])
                if s == 0:
                    acc_ref[row, lanes] = part
                elif s < ny - 1:
                    acc_ref[row, lanes] += part
                else:
                    acc16_ref[row, lanes] = (acc_ref[row, lanes] + part).astype(BF16)

    convs = counts_ref.shape[1]
    each = out_ref.shape[0] // convs
    chunk = 16 * each
    used = acc_ref.shape[0] // (each // MAXB)

    @pl.loop(0, convs // 16)
    def _(g):
        i = iota((chunk, 1), 0)
        conv = g * 16 + i // each
        inside = i % each
        slot = inside % MAXB
        which = inside // MAXB
        other = iota((chunk, convs), 1)
        counts = counts_ref[...]
        start = jnp.sum(jnp.where(other < conv, counts, 0), axis=1, keepdims=True)
        count = jnp.sum(jnp.where(other == conv, counts, 0), axis=1, keepdims=True)
        source = jnp.where(slot < count, which * used + start + slot, -1)
        put = (iota((chunk, acc_ref.shape[0]), 1) == source).astype(F32).astype(BF16)
        out_ref[pl.ds(pl.multiple_of(g * chunk, chunk), chunk)] = dot(put, acc16_ref[...]).astype(BF16)


def project(counts, rows, first, second, dims):
    ny, nz, nh, shard = dims
    per, feats = rows.shape[1:]
    cols = second[0].shape[1]
    convs = counts.shape[0]
    each = 2 * (per // USED) * MAXB
    hbm = pl.BlockSpec(memory_space=pl.ANY)
    return pl.pallas_call(
        functools.partial(project_kernel, dims),
        out_shape=jax.ShapeDtypeStruct((convs * each, cols), BF16),
        in_specs=[pl.BlockSpec(memory_space=pltpu.VMEM)] + [hbm] * (1 + nz + ny),
        out_specs=pl.BlockSpec(memory_space=pltpu.VMEM),
        scratch_shapes=[
            pltpu.VMEM((nh * feats, cols), BF16),
            pltpu.VMEM((2 * nh, per, feats), BF16),
            pltpu.VMEM((2 * per, cols), F32),
            pltpu.VMEM((2 * per, cols), BF16),
            pltpu.SemaphoreType.DMA((ny * nz * 2,)),
            pltpu.SemaphoreType.DMA((2 * nh,)),
        ],
        compiler_params=pltpu.CompilerParams(vmem_limit_bytes=VMEM_LIMIT),
        cost_estimate=pl.CostEstimate(
            flops=4 * per * nh * feats * cols, bytes_accessed=2 * nh * feats * (cols + 2 * per), transcendentals=0
        ),
        name="project",
    )(counts[None], rows, *first, *second)


def attend_kernel(live_ref, q_ref, k_ref, v_ref, nk_ref, nv_ref, out_ref):
    live = live_ref[0]
    hist = k_ref.shape[0]
    new = nk_ref.shape[0]
    scale = 1.0 / math.sqrt(HD)
    hist_ok = (iota((1, hist), 1) % MAXB) < live
    new_ok = iota((new, new), 1) <= iota((new, new), 0)

    @pl.loop(0, q_ref.shape[1] // (2 * HD))
    def _(pair):
        lanes = pl.ds(pl.multiple_of(pair * 2 * HD, 2 * HD), 2 * HD)
        q, k, v = q_ref[:, lanes], k_ref[:, lanes], v_ref[:, lanes]
        nk, nv = nk_ref[:, lanes], nv_ref[:, lanes]
        low = iota(q.shape, 1) < HD
        outs = []
        for mine in (low, jnp.logical_not(low)):
            qh = jnp.where(mine, q, jnp.zeros_like(q))
            sh = jnp.where(hist_ok, dot(qh, k, ((1,), (1,))) * scale, -jnp.inf)
            sn = jnp.where(new_ok, dot(qh, nk, ((1,), (1,))) * scale, -jnp.inf)
            top = jnp.maximum(
                jnp.max(sh, axis=1, keepdims=True), jnp.max(sn, axis=1, keepdims=True)
            )
            eh, en = jnp.exp(sh - top), jnp.exp(sn - top)
            total = jnp.sum(eh, axis=1, keepdims=True) + jnp.sum(en, axis=1, keepdims=True)
            ph, pn = (eh / total).astype(BF16), (en / total).astype(BF16)
            outs.append(dot(ph, v) + dot(pn, nv))
        out_ref[:, lanes] = jnp.where(low, outs[0], outs[1]).astype(BF16)


def attend(live, q, k, v, nk, nv):
    return pl.pallas_call(
        attend_kernel,
        out_shape=jax.ShapeDtypeStruct(q.shape, BF16),
        in_specs=[pl.BlockSpec(memory_space=pltpu.SMEM)] + [pl.BlockSpec(memory_space=pltpu.VMEM)] * 5,
        out_specs=pl.BlockSpec(memory_space=pltpu.VMEM),
        compiler_params=pltpu.CompilerParams(vmem_limit_bytes=VMEM_LIMIT),
        name="attend",
    )(live, q, k, v, nk, nv)


def ring_step(x, axis):
    n = lax.axis_size(axis)
    perm = []
    for i in range(n):
        perm += [(2 * i, 2 * ((i + 1) % n)), (2 * i + 1, 2 * ((i - 1) % n) + 1)]
    return lax.ppermute(x, (axis, "core"), perm)


def ring(x, axis):
    held = [x]
    for _ in range(lax.axis_size(axis) - 1):
        held.append(ring_step(held[-1], axis))
    return held


def per_device(queries, new_keys, new_values, pool, block_table, block_counts, key_weight, value_weight):
    ny, nz, nh = lax.axis_size("y"), lax.axis_size("z"), lax.axis_size("head")
    core = lax.axis_index("core")
    own = jnp.where(core == 0, key_weight, value_weight)
    away = jnp.where(core == 0, value_weight, key_weight)
    near = lax.ppermute(away, "core", [(0, 1), (1, 0)])

    live = live_rows(block_counts, block_table, pool)
    live = live.reshape(-1, live.shape[2])
    rows = lax.all_gather(live, ("core", "head"), axis=0)

    first = ring(jnp.concatenate(ring(own, "y"), axis=0), "z")
    second = ring(jnp.concatenate(ring(near, "z"), axis=0), "y")
    dims = (ny, nz, nh, key_weight.shape[0])
    sent = project(block_counts, rows, first, second, dims)
    convs = block_counts.shape[0]
    sent = sent.reshape(convs, -1, sent.shape[1])
    got = lax.all_to_all(sent, PLANE, split_axis=0, concat_axis=0, tiled=True)
    got = got.reshape(convs // 2, 2, got.shape[1], got.shape[2])
    keys = got[:, 0].reshape(-1, got.shape[3])
    values = got[:, 1].reshape(-1, got.shape[3])
    mine = lax.axis_index(PLANE)
    count = lax.dynamic_slice(block_counts, (mine,), (1,))
    return attend(count, queries[0], keys, values, new_keys[0], new_values[0])[None]


def solution(mesh):
    grid = Mesh(mesh.devices.reshape(GRID + (mesh.devices.shape[1],)), PLANE + ("head",))
    return jax.shard_map(
        per_device,
        mesh=grid,
        in_specs=(
            P(PLANE, None, "head"),
            P(PLANE, None, "head"),
            P(PLANE, None, "head"),
            P(None, PLANE, "head"),
            P(),
            P(),
            P(PLANE, "head"),
            P(PLANE, "head"),
        ),
        out_specs=P(PLANE, None, "head"),
        check_vma=False,
    )
```

time: 333 us -> 239 us (0.72)
  blocking collectives: 85.7 us -> 0 us
  starting transfers between devices: 0.08 us -> 75.8 us
  waiting for transfers between devices: 162 us -> 101 us
  Pallas kernels: 0 us -> 37.8 us
  matrix products: 30 us -> 0 us
  local copies, waits for them, and re-layouts: 35.3 us -> 9.64 us
  other arithmetic: 5.9 us -> 0.07 us
    all_gather x3 -> x1, waiting for transfers between devices: 160 us -> 0.01 us  [per_device(): rows = lax.all_gather(live, ('core', 'head'), axis=0)]
    all_to_all x1 -> x0, blocking collectives: 85.7 us -> none  [per_device(): lax.all_to_all(outgoing, 'inst', split_axis=1, concat_axis=1, tiled=True)]
    ppermute x0 -> x21, starting transfers between devices: none -> 56.2 us  [the longest x20 52.8 us: ring_step(): return lax.ppermute(x, (axis, 'core'), perm)]
    all_to_all x0 -> x1, waiting for transfers between devices: none -> 56 us  [per_device(): got = lax.all_to_all(sent, PLANE, split_axis=0, concat_axis=0, tiled=True)]
    ppermute x0 -> x21, waiting for transfers between devices: none -> 45.4 us  [the longest x20 44.4 us: ring_step(): return lax.ppermute(x, (axis, 'core'), perm)]
    pallas_call x0 -> x3, Pallas kernels: none -> 37.8 us  [the longest x1 24.5 us: project(): pl.pallas_call(functools.partial(project_kernel, dims), out_shape=jax.Sha...]
    dot_general x4 -> x0, matrix products: 30 us -> none  [the longest x1 12.9 us: project_rows(): jnp.dot(rows, lax.all_gather(key_weight, 'inst', axis=0, tiled=True), pre...]
    gather x2 -> x0, local copies, waits for them, and re-layouts: 21 us -> none  [per_device(): outgoing = pool[table.T] * live_slots[:, :, None, None].astype(pool.dtype)]
  transfers between devices with their start and end apart: 3 -> 23, of which waited for: 2 -> 12; matrix products, arithmetic and copies ran while one was open for 16% -> 0% of each run, Pallas kernels for 0% -> 0%
where the time goes in v1:
time: 239 us; the launch traced here: 238 us
  waiting for transfers between devices  101 us (42%)
  starting transfers between devices  75.8 us (32%)
  Pallas kernels  37.8 us (16%)
  between operations  13.6 us (6%)
  local copies, waits for them, and re-layouts  9.64 us (4%)
    all_to_all x1, waiting for transfers between devices, per_device(): got = lax.all_to_all(sent, PLANE, split_axis=0, concat_axis=0, tiled=True)  56 us
    ppermute x20, starting transfers between devices, ring_step(): return lax.ppermute(x, (axis, 'core'), perm)  52.8 us
    ppermute x20, waiting for transfers between devices, ring_step(): return lax.ppermute(x, (axis, 'core'), perm)  44.4 us
    pallas_call x1, Pallas kernels, project(): pl.pallas_call(functools.partial(project_kernel, dims), out_shape=jax.Sha...  24.5 us
    all_to_all x1, starting transfers between devices, per_device(): got = lax.all_to_all(sent, PLANE, split_axis=0, concat_axis=0, tiled=True)  19.6 us
    pallas_call x1, Pallas kernels, attend(): pl.pallas_call(attend_kernel, out_shape=jax.ShapeDtypeStruct(q.shape, BF1...  9.27 us
    unnamed x36, local copies, waits for them, and re-layouts  6.23 us
  transfers between devices with their start and end apart: 23, of which 12 were waited for; matrix products, arithmetic and copies ran while one was open for 0% of the time, Pallas kernels for 0%

profile of v1, /device:TPU:1, one launch (start us, length us, event | category | flops | bytes accessed | tf_op | source)
XLA Modules:
  0.0 238.3 jit_solution(9036091623447107201)
XLA Ops:
  6.5 1.2 broadcast_in_dim.11.table_ref
  7.8 3.3 %copy.13 = bf16[384,2,1536]{2,0,1:T(8,128)(2,1)} copy(bf16[384,2,1536]{2,1,0:T(2,128)(2,1)} %param.11) | data formatting | bytes 4718592 | tf_op args[3]
  11.1 4.0 %live_rows.1 = bf16[2,224,1536]{2,1,0:T(8,128)(2,1)} custom-call(s32[1,64]{1,0:T(1,128)} %bitcast.22, s32[1,384]{1,0:T(1,128)} %broadcast_in_dim.11.table_ref, bf16[2,384,1536]{2,1,0:T(8,128)(2,1)} %bitcast.14), custom_call_target="tpu_custom_call" | custom-call | tf_op jit(solution)/shard_map/live_rows/pallas_call | solution.py:51
  15.1 0.0 all-gather.2.cloned.1.call-update
  15.2 0.9 copy-done.1
  16.0 0.1 copy-done.2
  16.1 3.3 %collective-permute-start.10 = (bf16[96,768]{1,0:T(8,128)(2,1)S(1)}, bf16[96,768]{1,0:T(8,128)(2,1)S(1)}, u32[]{:S(2)}, u32[]{:S(2)}) collective-permute-start(bf16[96,768]{1,0:T(8,128)(2,1)S(1)} %get-tuple-element.7), channel_id=1, source_target_pairs={{0,4},{4,0},{1,5},{5,1},{2,6},{6,2},{3,7},{7,3},{8,12},{12,8},{9,1... | collective-permute-start | bytes 442376 | tf_op jit(solution)/shard_map/ppermute | solution.py:223
  19.5 1.0 collective-permute-done.10
  20.5 3.8 %collective-permute-start.11 = (bf16[96,768]{1,0:T(8,128)(2,1)S(1)}, bf16[96,768]{1,0:T(8,128)(2,1)S(1)}, u32[]{:S(2)}, u32[]{:S(2)}) collective-permute-start(bf16[96,768]{1,0:T(8,128)(2,1)S(1)} %collective-permute-done.10), channel_id=1, source_target_pairs={{0,8},{4,60},{8,16},{12,4},{16,24},{20,12},{24,32},{28,20},{32,40}... | collective-permute-start | bytes 442376 | tf_op jit(solution)/shard_map/ppermute | solution.py:208
  24.3 2.7 %collective-permute-start = (bf16[96,768]{1,0:T(8,128)(2,1)S(1)}, bf16[96,768]{1,0:T(8,128)(2,1)S(1)}, u32[]{:S(2)}, u32[]{:S(2)}) collective-permute-start(bf16[96,768]{1,0:T(8,128)(2,1)S(1)} %get-tuple-element.8), channel_id=1, source_target_pairs={{0,64},{4,196},{64,128},{68,4},{128,192},{132,68},{192,0},{196,132... | collective-permute-start | bytes 442376 | tf_op jit(solution)/shard_map/ppermute | solution.py:208
  27.1 0.0 collective-permute-done.11
  27.1 2.8 %collective-permute-start.12 = (bf16[96,768]{1,0:T(8,128)(2,1)S(1)}, bf16[96,768]{1,0:T(8,128)(2,1)S(1)}, u32[]{:S(2)}, u32[]{:S(2)}) collective-permute-start(bf16[96,768]{1,0:T(8,128)(2,1)S(1)} %collective-permute-done.11), channel_id=1, source_target_pairs={{0,8},{4,60},{8,16},{12,4},{16,24},{20,12},{24,32},{28,20},{32,40}... | collective-permute-start | bytes 442376 | tf_op jit(solution)/shard_map/ppermute | solution.py:208
  29.8 2.4 %collective-permute-start.1 = (bf16[96,768]{1,0:T(8,128)(2,1)S(1)}, bf16[96,768]{1,0:T(8,128)(2,1)S(1)}, u32[]{:S(2)}, u32[]{:S(2)}) collective-permute-start(bf16[96,768]{1,0:T(8,128)(2,1)S(1)} %collective-permute-done), channel_id=1, source_target_pairs={{0,64},{4,196},{64,128},{68,4},{128,192},{132,68},{192,0},{196,132... | collective-permute-start | bytes 442376 | tf_op jit(solution)/shard_map/ppermute | solution.py:208
  32.3 2.8 %collective-permute-start.13 = (bf16[96,768]{1,0:T(8,128)(2,1)S(1)}, bf16[96,768]{1,0:T(8,128)(2,1)S(1)}, u32[]{:S(2)}, u32[]{:S(2)}) collective-permute-start(bf16[96,768]{1,0:T(8,128)(2,1)S(1)} %collective-permute-done.12), channel_id=1, source_target_pairs={{0,8},{4,60},{8,16},{12,4},{16,24},{20,12},{24,32},{28,20},{32,40}... | collective-permute-start | bytes 442376 | tf_op jit(solution)/shard_map/ppermute | solution.py:208
  35.0 2.4 %collective-permute-start.2 = (bf16[96,768]{1,0:T(8,128)(2,1)S(1)}, bf16[96,768]{1,0:T(8,128)(2,1)S(1)}, u32[]{:S(2)}, u32[]{:S(2)}) collective-permute-start(bf16[96,768]{1,0:T(8,128)(2,1)S(1)} %collective-permute-done.1), channel_id=1, source_target_pairs={{0,64},{4,196},{64,128},{68,4},{128,192},{132,68},{192,0},{196,132... | collective-permute-start | bytes 442376 | tf_op jit(solution)/shard_map/ppermute | solution.py:208
  37.5 3.2 %collective-permute-start.14 = (bf16[96,768]{1,0:T(8,128)(2,1)S(1)}, bf16[96,768]{1,0:T(8,128)(2,1)S(1)}, u32[]{:S(2)}, u32[]{:S(2)}) collective-permute-start(bf16[96,768]{1,0:T(8,128)(2,1)S(1)} %collective-permute-done.13), channel_id=1, source_target_pairs={{0,8},{4,60},{8,16},{12,4},{16,24},{20,12},{24,32},{28,20},{32,40}... | collective-permute-start | bytes 442376 | tf_op jit(solution)/shard_map/ppermute | solution.py:208
  40.7 0.1 collective-permute-start.3
  40.8 1.9 collective-permute-done.14
  42.7 3.5 %collective-permute-start.15 = (bf16[96,768]{1,0:T(8,128)(2,1)S(1)}, bf16[96,768]{1,0:T(8,128)(2,1)S(1)}, u32[]{:S(2)}, u32[]{:S(2)}) collective-permute-start(bf16[96,768]{1,0:T(8,128)(2,1)S(1)} %collective-permute-done.14), channel_id=1, source_target_pairs={{0,8},{4,60},{8,16},{12,4},{16,24},{20,12},{24,32},{28,20},{32,40}... | collective-permute-start | bytes 442376 | tf_op jit(solution)/shard_map/ppermute | solution.py:208
  46.3 5.2 %collective-permute-done.15 = bf16[96,768]{1,0:T(8,128)(2,1)S(1)} collective-permute-done((bf16[96,768]{1,0:T(8,128)(2,1)S(1)}, bf16[96,768]{1,0:T(8,128)(2,1)S(1)}, u32[]{:S(2)}, u32[]{:S(2)}) %collective-permute-start.15) | collective-permute-done | bytes 147488 | tf_op jit(solution)/shard_map/ppermute | solution.py:208
  51.5 2.6 %collective-permute-start.16 = (bf16[96,768]{1,0:T(8,128)(2,1)S(1)}, bf16[96,768]{1,0:T(8,128)(2,1)S(1)}, u32[]{:S(2)}, u32[]{:S(2)}) collective-permute-start(bf16[96,768]{1,0:T(8,128)(2,1)S(1)} %collective-permute-done.15), channel_id=1, source_target_pairs={{0,8},{4,60},{8,16},{12,4},{16,24},{20,12},{24,32},{28,20},{32,40}... | collective-permute-start | bytes 442376 | tf_op jit(solution)/shard_map/ppermute | solution.py:208
  54.2 2.1 collective-permute-done.16
  56.2 3.5 %collective-permute-start.17 = (bf16[96,768]{1,0:T(8,128)(2,1)S(1)}, bf16[96,768]{1,0:T(8,128)(2,1)S(1)}, u32[]{:S(2)}, u32[]{:S(2)}) collective-permute-start(bf16[96,768]{1,0:T(8,128)(2,1)S(1)} %collective-permute-done.16), channel_id=1, source_target_pairs={{0,8},{4,60},{8,16},{12,4},{16,24},{20,12},{24,32},{28,20},{32,40}... | collective-permute-start | bytes 442376 | tf_op jit(solution)/shard_map/ppermute | solution.py:208
  59.8 0.1 collective-permute-start.4
  59.9 2.0 collective-permute-done.17
  61.9 2.5 %collective-permute-start.18 = (bf16[768,768]{1,0:T(8,128)(2,1)S(1)}, bf16[768,768]{1,0:T(8,128)(2,1)S(1)}, u32[]{:S(2)}, u32[]{:S(2)}) collective-permute-start(bf16[768,768]{1,0:T(8,128)(2,1)S(1)} %constant_dynamic-update-slice_fusion.rest_8_), channel_id=1, source_target_pairs={{0,64},{4,196},{64,128},{68,4},{128,192},{132,68},{192,0},{196,132... | collective-permute-start | bytes 3538952 | tf_op jit(solution)/shard_map/ppermute | solution.py:208
  64.4 4.6 %collective-permute-done.4.rest_2_ = bf16[384,768]{1,0:T(8,128)(2,1)S(1)} collective-permute-done((bf16[384,768]{1,0:T(8,128)(2,1)S(1)}, bf16[384,768]{1,0:T(8,128)(2,1)S(1)}, u32[]{:S(2)}, u32[]{:S(2)}) %collective-permute-start.4) | collective-permute-done | bytes 589856 | tf_op jit(solution)/shard_map/ppermute | solution.py:208
  69.0 2.7 %collective-permute-start.5 = (bf16[384,768]{1,0:T(8,128)(2,1)S(1)}, bf16[384,768]{1,0:T(8,128)(2,1)S(1)}, u32[]{:S(2)}, u32[]{:S(2)}) collective-permute-start(bf16[384,768]{1,0:T(8,128)(2,1)S(1)} %collective-permute-done.4.rest_2_), channel_id=1, source_target_pairs={{0,8},{4,60},{8,16},{12,4},{16,24},{20,12},{24,32},{28,20},{32,40}... | collective-permute-start | bytes 1769480 | tf_op jit(solution)/shard_map/ppermute | solution.py:208
  71.7 6.8 %collective-permute-done.5.rest_3_ = bf16[384,768]{1,0:T(8,128)(2,1)S(1)} collective-permute-done((bf16[384,768]{1,0:T(8,128)(2,1)S(1)}, bf16[384,768]{1,0:T(8,128)(2,1)S(1)}, u32[]{:S(2)}, u32[]{:S(2)}) %collective-permute-start.5) | collective-permute-done | bytes 589856 | tf_op jit(solution)/shard_map/ppermute | solution.py:208
  78.5 3.5 %collective-permute-start.6 = (bf16[384,768]{1,0:T(8,128)(2,1)S(1)}, bf16[384,768]{1,0:T(8,128)(2,1)S(1)}, u32[]{:S(2)}, u32[]{:S(2)}) collective-permute-start(bf16[384,768]{1,0:T(8,128)(2,1)S(1)} %collective-permute-done.5.rest_3_), channel_id=1, source_target_pairs={{0,8},{4,60},{8,16},{12,4},{16,24},{20,12},{24,32},{28,20},{32,40}... | collective-permute-start | bytes 1769480 | tf_op jit(solution)/shard_map/ppermute | solution.py:208
  82.0 2.4 %collective-permute-start.19 = (bf16[768,768]{1,0:T(8,128)(2,1)S(1)}, bf16[768,768]{1,0:T(8,128)(2,1)S(1)}, u32[]{:S(2)}, u32[]{:S(2)}) collective-permute-start(bf16[768,768]{1,0:T(8,128)(2,1)S(1)} %collective-permute-done.18.rest_9_), channel_id=1, source_target_pairs={{0,64},{4,196},{64,128},{68,4},{128,192},{132,68},{192,0},{196,132... | collective-permute-start | bytes 3538952 | tf_op jit(solution)/shard_map/ppermute | solution.py:208
  84.5 4.4 %collective-permute-done.6.rest_4_ = bf16[384,768]{1,0:T(8,128)(2,1)S(1)} collective-permute-done((bf16[384,768]{1,0:T(8,128)(2,1)S(1)}, bf16[384,768]{1,0:T(8,128)(2,1)S(1)}, u32[]{:S(2)}, u32[]{:S(2)}) %collective-permute-start.6) | collective-permute-done | bytes 589856 | tf_op jit(solution)/shard_map/ppermute | solution.py:208
  88.8 3.1 %collective-permute-start.7 = (bf16[384,768]{1,0:T(8,128)(2,1)S(1)}, bf16[384,768]{1,0:T(8,128)(2,1)S(1)}, u32[]{:S(2)}, u32[]{:S(2)}) collective-permute-start(bf16[384,768]{1,0:T(8,128)(2,1)S(1)} %collective-permute-done.6.rest_4_), channel_id=1, source_target_pairs={{0,8},{4,60},{8,16},{12,4},{16,24},{20,12},{24,32},{28,20},{32,40}... | collective-permute-start | bytes 1769480 | tf_op jit(solution)/shard_map/ppermute | solution.py:208
  92.0 6.8 %collective-permute-done.7.rest_5_ = bf16[384,768]{1,0:T(8,128)(2,1)S(1)} collective-permute-done((bf16[384,768]{1,0:T(8,128)(2,1)S(1)}, bf16[384,768]{1,0:T(8,128)(2,1)S(1)}, u32[]{:S(2)}, u32[]{:S(2)}) %collective-permute-start.7) | collective-permute-done | bytes 589856 | tf_op jit(solution)/shard_map/ppermute | solution.py:208
  98.8 3.4 %collective-permute-start.8 = (bf16[384,768]{1,0:T(8,128)(2,1)S(1)}, bf16[384,768]{1,0:T(8,128)(2,1)S(1)}, u32[]{:S(2)}, u32[]{:S(2)}) collective-permute-start(bf16[384,768]{1,0:T(8,128)(2,1)S(1)} %collective-permute-done.7.rest_5_), channel_id=1, source_target_pairs={{0,8},{4,60},{8,16},{12,4},{16,24},{20,12},{24,32},{28,20},{32,40}... | collective-permute-start | bytes 1769480 | tf_op jit(solution)/shard_map/ppermute | solution.py:208
  102.2 1.0 copy-done.6
  103.2 2.1 collective-permute-start.20
  105.4 3.7 %collective-permute-done.8.rest_6_ = bf16[384,768]{1,0:T(8,128)(2,1)S(1)} collective-permute-done((bf16[384,768]{1,0:T(8,128)(2,1)S(1)}, bf16[384,768]{1,0:T(8,128)(2,1)S(1)}, u32[]{:S(2)}, u32[]{:S(2)}) %collective-permute-start.8) | collective-permute-done | bytes 589856 | tf_op jit(solution)/shard_map/ppermute | solution.py:208
  109.0 3.1 %collective-permute-start.9 = (bf16[384,768]{1,0:T(8,128)(2,1)S(1)}, bf16[384,768]{1,0:T(8,128)(2,1)S(1)}, u32[]{:S(2)}, u32[]{:S(2)}) collective-permute-start(bf16[384,768]{1,0:T(8,128)(2,1)S(1)} %collective-permute-done.8.rest_6_), channel_id=1, source_target_pairs={{0,8},{4,60},{8,16},{12,4},{16,24},{20,12},{24,32},{28,20},{32,40}... | collective-permute-start | bytes 1769480 | tf_op jit(solution)/shard_map/ppermute | solution.py:208
  112.2 6.8 %collective-permute-done.9.rest_7_ = bf16[384,768]{1,0:T(8,128)(2,1)S(1)} collective-permute-done((bf16[384,768]{1,0:T(8,128)(2,1)S(1)}, bf16[384,768]{1,0:T(8,128)(2,1)S(1)}, u32[]{:S(2)}, u32[]{:S(2)}) %collective-permute-start.9) | collective-permute-done | bytes 589856 | tf_op jit(solution)/shard_map/ppermute | solution.py:208
  119.0 0.8 copy-done.13
  119.9 24.5 %project.1 = bf16[1536,768]{1,0:T(8,128)(2,1)} custom-call(s32[1,64]{1,0:T(1,128)} %bitcast.23, bf16[8,448,1536]{2,1,0:T(8,128)(2,1)} %all-gather.2.cloned.1.call-done.rows_ref, bf16[384,768]{1,0:T(8,128)(2,1)} %copy-done, bf16[384,768]{1,0:T(8,128)(2,1)} %copy-done.7, bf16[384,768]{1,0:T(8,128)(2,1)} %copy-done.8, bf16[384,768]{1,0:T(8,128)(2,1)} %copy-done.9, ...), custom_call_target="tpu_custom_call" | custom-call | flops 8455716864 | bytes 20447232 | tf_op jit(solution)/shard_map/project/pallas_call | solution.py:142
  144.3 0.0 copy-start.4
  144.3 19.6 %all-to-all-start = ((bf16[64,24,768]{2,1,0:T(8,128)(2,1)}), bf16[64,24,768]{2,1,0:T(8,128)(2,1)S(1)}, u32[]{:S(2)}, u32[]{:S(2)}) async-start(bf16[64,24,768]{2,1,0:T(8,128)(2,1)} %bitcast.18), calls=%async_computation | async-start | bytes 4718592 | tf_op jit(solution)/shard_map/all_to_all | solution.py:235
  164.0 0.6 dynamic_slice.3.live_ref
  164.6 56.0 %all-to-all-done = bf16[64,24,768]{2,1,0:T(8,128)(2,1)S(1)} async-done(((bf16[64,24,768]{2,1,0:T(8,128)(2,1)}), bf16[64,24,768]{2,1,0:T(8,128)(2,1)S(1)}, u32[]{:S(2)}, u32[]{:S(2)}) %all-to-all-start) | async-done | bytes 2359328 | tf_op jit(solution)/shard_map/all_to_all | solution.py:235
  220.6 1.6 fusion
  222.2 9.3 %attend.1 = bf16[128,768]{1,0:T(8,128)(2,1)} custom-call(s32[1]{0:T(128)} %dynamic_slice.3.live_ref, bf16[128,768]{1,0:T(8,128)(2,1)} %bitcast.19, bf16[768,768]{1,0:T(8,128)(2,1)} %bitcast.17, bf16[768,768]{1,0:T(8,128)(2,1)} %bitcast.16, bf16[128,768]{1,0:T(8,128)(2,1)} %bitcast.20, bf16[128,768]{1,0:T(8,128)(2,1)} %bitcast.21), custom_call_target="tpu_custom_call" | custom-call | tf_op jit(solution)/shard_map/attend/pallas_call | solution.py:193
  (44 shorter events, 0.2 us)
Async XLA Ops:
  6.5 113.3 %all-gather.2.cloned.1.call-start = ((), (), s32[]{:S(2)}) async-start(), calls=%async_computation.1 | async-start | bytes 12386304 | tf_op jit(solution)/shard_map/all_gather | solution.py:227
  15.1 0.9 copy-start.1
  15.1 1.0 copy-start.2
  16.1 4.3 %collective-permute-start.10 = (bf16[96,768]{1,0:T(8,128)(2,1)S(1)}, bf16[96,768]{1,0:T(8,128)(2,1)S(1)}, u32[]{:S(2)}, u32[]{:S(2)}) collective-permute-start(bf16[96,768]{1,0:T(8,128)(2,1)S(1)} %get-tuple-element.7), channel_id=1, source_target_pairs={{0,4},{4,0},{1,5},{5,1},{2,6},{6,2},{3,7},{7,3},{8,12},{12,8},{9,1... | collective-permute-start | bytes 442376 | tf_op jit(solution)/shard_map/ppermute | solution.py:223
  20.5 6.6 %collective-permute-start.11 = (bf16[96,768]{1,0:T(8,128)(2,1)S(1)}, bf16[96,768]{1,0:T(8,128)(2,1)S(1)}, u32[]{:S(2)}, u32[]{:S(2)}) collective-permute-start(bf16[96,768]{1,0:T(8,128)(2,1)S(1)} %collective-permute-done.10), channel_id=1, source_target_pairs={{0,8},{4,60},{8,16},{12,4},{16,24},{20,12},{24,32},{28,20},{32,40}... | collective-permute-start | bytes 442376 | tf_op jit(solution)/shard_map/ppermute | solution.py:208
  24.3 5.5 %collective-permute-start = (bf16[96,768]{1,0:T(8,128)(2,1)S(1)}, bf16[96,768]{1,0:T(8,128)(2,1)S(1)}, u32[]{:S(2)}, u32[]{:S(2)}) collective-permute-start(bf16[96,768]{1,0:T(8,128)(2,1)S(1)} %get-tuple-element.8), channel_id=1, source_target_pairs={{0,64},{4,196},{64,128},{68,4},{128,192},{132,68},{192,0},{196,132... | collective-permute-start | bytes 442376 | tf_op jit(solution)/shard_map/ppermute | solution.py:208
  27.1 5.2 %collective-permute-start.12 = (bf16[96,768]{1,0:T(8,128)(2,1)S(1)}, bf16[96,768]{1,0:T(8,128)(2,1)S(1)}, u32[]{:S(2)}, u32[]{:S(2)}) collective-permute-start(bf16[96,768]{1,0:T(8,128)(2,1)S(1)} %collective-permute-done.11), channel_id=1, source_target_pairs={{0,8},{4,60},{8,16},{12,4},{16,24},{20,12},{24,32},{28,20},{32,40}... | collective-permute-start | bytes 442376 | tf_op jit(solution)/shard_map/ppermute | solution.py:208
  29.8 5.2 %collective-permute-start.1 = (bf16[96,768]{1,0:T(8,128)(2,1)S(1)}, bf16[96,768]{1,0:T(8,128)(2,1)S(1)}, u32[]{:S(2)}, u32[]{:S(2)}) collective-permute-start(bf16[96,768]{1,0:T(8,128)(2,1)S(1)} %collective-permute-done), channel_id=1, source_target_pairs={{0,64},{4,196},{64,128},{68,4},{128,192},{132,68},{192,0},{196,132... | collective-permute-start | bytes 442376 | tf_op jit(solution)/shard_map/ppermute | solution.py:208
  32.3 5.2 %collective-permute-start.13 = (bf16[96,768]{1,0:T(8,128)(2,1)S(1)}, bf16[96,768]{1,0:T(8,128)(2,1)S(1)}, u32[]{:S(2)}, u32[]{:S(2)}) collective-permute-start(bf16[96,768]{1,0:T(8,128)(2,1)S(1)} %collective-permute-done.12), channel_id=1, source_target_pairs={{0,8},{4,60},{8,16},{12,4},{16,24},{20,12},{24,32},{28,20},{32,40}... | collective-permute-start | bytes 442376 | tf_op jit(solution)/shard_map/ppermute | solution.py:208
  35.0 5.6 %collective-permute-start.2 = (bf16[96,768]{1,0:T(8,128)(2,1)S(1)}, bf16[96,768]{1,0:T(8,128)(2,1)S(1)}, u32[]{:S(2)}, u32[]{:S(2)}) collective-permute-start(bf16[96,768]{1,0:T(8,128)(2,1)S(1)} %collective-permute-done.1), channel_id=1, source_target_pairs={{0,64},{4,196},{64,128},{68,4},{128,192},{132,68},{192,0},{196,132... | collective-permute-start | bytes 442376 | tf_op jit(solution)/shard_map/ppermute | solution.py:208
  37.5 5.3 %collective-permute-start.14 = (bf16[96,768]{1,0:T(8,128)(2,1)S(1)}, bf16[96,768]{1,0:T(8,128)(2,1)S(1)}, u32[]{:S(2)}, u32[]{:S(2)}) collective-permute-start(bf16[96,768]{1,0:T(8,128)(2,1)S(1)} %collective-permute-done.13), channel_id=1, source_target_pairs={{0,8},{4,60},{8,16},{12,4},{16,24},{20,12},{24,32},{28,20},{32,40}... | collective-permute-start | bytes 442376 | tf_op jit(solution)/shard_map/ppermute | solution.py:208
  40.7 79.1 %copy-start = (bf16[384,768]{1,0:T(8,128)(2,1)}, bf16[384,768]{1,0:T(8,128)(2,1)S(1)}, u32[]{:S(2)}) copy-start(bf16[384,768]{1,0:T(8,128)(2,1)S(1)} %pad_maximum_fusion.rest_0_) | copy-start | bytes 1769476
  40.7 19.1 %collective-permute-start.3 = (bf16[384,768]{1,0:T(8,128)(2,1)S(1)}, bf16[384,768]{1,0:T(8,128)(2,1)S(1)}, u32[]{:S(2)}, u32[]{:S(2)}) collective-permute-start(bf16[384,768]{1,0:T(8,128)(2,1)S(1)} %pad_maximum_fusion.rest_0_), channel_id=1, source_target_pairs={{0,8},{4,60},{8,16},{12,4},{16,24},{20,12},{24,32},{28,20},{32,40}... | collective-permute-start | bytes 1769480 | tf_op jit(solution)/shard_map/ppermute | solution.py:208
  42.7 8.8 %collective-permute-start.15 = (bf16[96,768]{1,0:T(8,128)(2,1)S(1)}, bf16[96,768]{1,0:T(8,128)(2,1)S(1)}, u32[]{:S(2)}, u32[]{:S(2)}) collective-permute-start(bf16[96,768]{1,0:T(8,128)(2,1)S(1)} %collective-permute-done.14), channel_id=1, source_target_pairs={{0,8},{4,60},{8,16},{12,4},{16,24},{20,12},{24,32},{28,20},{32,40}... | collective-permute-start | bytes 442376 | tf_op jit(solution)/shard_map/ppermute | solution.py:208
  51.5 4.7 %collective-permute-start.16 = (bf16[96,768]{1,0:T(8,128)(2,1)S(1)}, bf16[96,768]{1,0:T(8,128)(2,1)S(1)}, u32[]{:S(2)}, u32[]{:S(2)}) collective-permute-start(bf16[96,768]{1,0:T(8,128)(2,1)S(1)} %collective-permute-done.15), channel_id=1, source_target_pairs={{0,8},{4,60},{8,16},{12,4},{16,24},{20,12},{24,32},{28,20},{32,40}... | collective-permute-start | bytes 442376 | tf_op jit(solution)/shard_map/ppermute | solution.py:208
  56.2 5.6 %collective-permute-start.17 = (bf16[96,768]{1,0:T(8,128)(2,1)S(1)}, bf16[96,768]{1,0:T(8,128)(2,1)S(1)}, u32[]{:S(2)}, u32[]{:S(2)}) collective-permute-start(bf16[96,768]{1,0:T(8,128)(2,1)S(1)} %collective-permute-done.16), channel_id=1, source_target_pairs={{0,8},{4,60},{8,16},{12,4},{16,24},{20,12},{24,32},{28,20},{32,40}... | collective-permute-start | bytes 442376 | tf_op jit(solution)/shard_map/ppermute | solution.py:208
  59.8 60.0 %copy-start.7 = (bf16[384,768]{1,0:T(8,128)(2,1)}, bf16[384,768]{1,0:T(8,128)(2,1)S(1)}, u32[]{:S(2)}) copy-start(bf16[384,768]{1,0:T(8,128)(2,1)S(1)} %collective-permute-done.3.rest_1_) | copy-start | bytes 1769476
  59.8 9.2 %collective-permute-start.4 = (bf16[384,768]{1,0:T(8,128)(2,1)S(1)}, bf16[384,768]{1,0:T(8,128)(2,1)S(1)}, u32[]{:S(2)}, u32[]{:S(2)}) collective-permute-start(bf16[384,768]{1,0:T(8,128)(2,1)S(1)} %collective-permute-done.3.rest_1_), channel_id=1, source_target_pairs={{0,8},{4,60},{8,16},{12,4},{16,24},{20,12},{24,32},{28,20},{32,40}... | collective-permute-start | bytes 1769480 | tf_op jit(solution)/shard_map/ppermute | solution.py:208
  61.9 58.0 %copy-start.3 = (bf16[768,768]{1,0:T(8,128)(2,1)}, bf16[768,768]{1,0:T(8,128)(2,1)S(1)}, u32[]{:S(2)}) copy-start(bf16[768,768]{1,0:T(8,128)(2,1)S(1)} %constant_dynamic-update-slice_fusion.rest_8_) | copy-start | bytes 3538948
  61.9 20.2 %collective-permute-start.18 = (bf16[768,768]{1,0:T(8,128)(2,1)S(1)}, bf16[768,768]{1,0:T(8,128)(2,1)S(1)}, u32[]{:S(2)}, u32[]{:S(2)}) collective-permute-start(bf16[768,768]{1,0:T(8,128)(2,1)S(1)} %constant_dynamic-update-slice_fusion.rest_8_), channel_id=1, source_target_pairs={{0,64},{4,196},{64,128},{68,4},{128,192},{132,68},{192,0},{196,132... | collective-permute-start | bytes 3538952 | tf_op jit(solution)/shard_map/ppermute | solution.py:208
  69.0 36.4 %copy-start.8 = (bf16[384,768]{1,0:T(8,128)(2,1)}, bf16[384,768]{1,0:T(8,128)(2,1)S(1)}, u32[]{:S(2)}) copy-start(bf16[384,768]{1,0:T(8,128)(2,1)S(1)} %collective-permute-done.4.rest_2_) | copy-start | bytes 1769476
  69.0 9.5 %collective-permute-start.5 = (bf16[384,768]{1,0:T(8,128)(2,1)S(1)}, bf16[384,768]{1,0:T(8,128)(2,1)S(1)}, u32[]{:S(2)}, u32[]{:S(2)}) collective-permute-start(bf16[384,768]{1,0:T(8,128)(2,1)S(1)} %collective-permute-done.4.rest_2_), channel_id=1, source_target_pairs={{0,8},{4,60},{8,16},{12,4},{16,24},{20,12},{24,32},{28,20},{32,40}... | collective-permute-start | bytes 1769480 | tf_op jit(solution)/shard_map/ppermute | solution.py:208
  78.5 30.5 %copy-start.9 = (bf16[384,768]{1,0:T(8,128)(2,1)}, bf16[384,768]{1,0:T(8,128)(2,1)S(1)}, u32[]{:S(2)}) copy-start(bf16[384,768]{1,0:T(8,128)(2,1)S(1)} %collective-permute-done.5.rest_3_) | copy-start | bytes 1769476
  78.5 10.3 %collective-permute-start.6 = (bf16[384,768]{1,0:T(8,128)(2,1)S(1)}, bf16[384,768]{1,0:T(8,128)(2,1)S(1)}, u32[]{:S(2)}, u32[]{:S(2)}) collective-permute-start(bf16[384,768]{1,0:T(8,128)(2,1)S(1)} %collective-permute-done.5.rest_3_), channel_id=1, source_target_pairs={{0,8},{4,60},{8,16},{12,4},{16,24},{20,12},{24,32},{28,20},{32,40}... | collective-permute-start | bytes 1769480 | tf_op jit(solution)/shard_map/ppermute | solution.py:208
  82.0 37.8 %copy-start.5 = (bf16[768,768]{1,0:T(8,128)(2,1)}, bf16[768,768]{1,0:T(8,128)(2,1)S(1)}, u32[]{:S(2)}) copy-start(bf16[768,768]{1,0:T(8,128)(2,1)S(1)} %collective-permute-done.18.rest_9_) | copy-start | bytes 3538948
  82.0 20.2 %collective-permute-start.19 = (bf16[768,768]{1,0:T(8,128)(2,1)S(1)}, bf16[768,768]{1,0:T(8,128)(2,1)S(1)}, u32[]{:S(2)}, u32[]{:S(2)}) collective-permute-start(bf16[768,768]{1,0:T(8,128)(2,1)S(1)} %collective-permute-done.18.rest_9_), channel_id=1, source_target_pairs={{0,64},{4,196},{64,128},{68,4},{128,192},{132,68},{192,0},{196,132... | collective-permute-start | bytes 3538952 | tf_op jit(solution)/shard_map/ppermute | solution.py:208
  88.8 23.3 %copy-start.10 = (bf16[384,768]{1,0:T(8,128)(2,1)}, bf16[384,768]{1,0:T(8,128)(2,1)S(1)}, u32[]{:S(2)}) copy-start(bf16[384,768]{1,0:T(8,128)(2,1)S(1)} %collective-permute-done.6.rest_4_) | copy-start | bytes 1769476
  88.8 9.9 %collective-permute-start.7 = (bf16[384,768]{1,0:T(8,128)(2,1)S(1)}, bf16[384,768]{1,0:T(8,128)(2,1)S(1)}, u32[]{:S(2)}, u32[]{:S(2)}) collective-permute-start(bf16[384,768]{1,0:T(8,128)(2,1)S(1)} %collective-permute-done.6.rest_4_), channel_id=1, source_target_pairs={{0,8},{4,60},{8,16},{12,4},{16,24},{20,12},{24,32},{28,20},{32,40}... | collective-permute-start | bytes 1769480 | tf_op jit(solution)/shard_map/ppermute | solution.py:208
  98.8 20.2 %copy-start.11 = (bf16[384,768]{1,0:T(8,128)(2,1)}, bf16[384,768]{1,0:T(8,128)(2,1)S(1)}, u32[]{:S(2)}) copy-start(bf16[384,768]{1,0:T(8,128)(2,1)S(1)} %collective-permute-done.7.rest_5_) | copy-start | bytes 1769476
  98.8 10.2 %collective-permute-start.8 = (bf16[384,768]{1,0:T(8,128)(2,1)S(1)}, bf16[384,768]{1,0:T(8,128)(2,1)S(1)}, u32[]{:S(2)}, u32[]{:S(2)}) collective-permute-start(bf16[384,768]{1,0:T(8,128)(2,1)S(1)} %collective-permute-done.7.rest_5_), channel_id=1, source_target_pairs={{0,8},{4,60},{8,16},{12,4},{16,24},{20,12},{24,32},{28,20},{32,40}... | collective-permute-start | bytes 1769480 | tf_op jit(solution)/shard_map/ppermute | solution.py:208
  102.2 1.0 copy-start.6
  103.2 16.6 %collective-permute-start.20 = (bf16[768,768]{1,0:T(8,128)(2,1)S(1)}, bf16[768,768]{1,0:T(8,128)(2,1)}, u32[]{:S(2)}, u32[]{:S(2)}) collective-permute-start(bf16[768,768]{1,0:T(8,128)(2,1)S(1)} %collective-permute-done.19.rest_10_), channel_id=1, source_target_pairs={{0,64},{4,196},{64,128},{68,4},{128,192},{132,68},{192,0},{196,132... | collective-permute-start | bytes 3538952 | tf_op jit(solution)/shard_map/ppermute | solution.py:208
  109.0 10.0 %copy-start.12 = (bf16[384,768]{1,0:T(8,128)(2,1)}, bf16[384,768]{1,0:T(8,128)(2,1)S(1)}, u32[]{:S(2)}) copy-start(bf16[384,768]{1,0:T(8,128)(2,1)S(1)} %collective-permute-done.8.rest_6_) | copy-start | bytes 1769476
  109.0 9.9 %collective-permute-start.9 = (bf16[384,768]{1,0:T(8,128)(2,1)S(1)}, bf16[384,768]{1,0:T(8,128)(2,1)S(1)}, u32[]{:S(2)}, u32[]{:S(2)}) collective-permute-start(bf16[384,768]{1,0:T(8,128)(2,1)S(1)} %collective-permute-done.8.rest_6_), channel_id=1, source_target_pairs={{0,8},{4,60},{8,16},{12,4},{16,24},{20,12},{24,32},{28,20},{32,40}... | collective-permute-start | bytes 1769480 | tf_op jit(solution)/shard_map/ppermute | solution.py:208
  119.0 0.8 copy-start.13
  144.3 19.7 %copy-start.4 = (s32[64]{0:T(128)S(1)}, s32[64]{0:T(128)}, u32[]{:S(2)}) copy-start(s32[64]{0:T(128)} %param.13) | copy-start | bytes 772
  144.3 76.3 %all-to-all-start = ((bf16[64,24,768]{2,1,0:T(8,128)(2,1)}), bf16[64,24,768]{2,1,0:T(8,128)(2,1)S(1)}, u32[]{:S(2)}, u32[]{:S(2)}) async-start(bf16[64,24,768]{2,1,0:T(8,128)(2,1)} %bitcast.18), calls=%async_computation | async-start | bytes 4718592 | tf_op jit(solution)/shard_map/all_to_all | solution.py:235
Sparse Core Ops, SparseCore 0:
  15.3 67.4 all-gather.1

commit v2 on v1

--- a/solution.py
+++ b/solution.py
@@ -58,11 +58,32 @@
     )(counts[None], table[None], jnp.transpose(pool, (1, 0, 2)))
 
 
+def piece_table(ny, nz):
+    table = []
+    dys = (0, -1, 1, -2)
+    dzs = (0, -1, -2, -3, 1, 2, 3, -4)
+    for s in range(5):
+        for j, dy in enumerate(dys):
+            table.append((s, j, dy, -s, 0))
+    for s in range(1, 4):
+        for j, dy in enumerate(dys):
+            table.append((4 + s, j, -dy, s, 0))
+    for s in range(3):
+        for j, dz in enumerate(dzs):
+            table.append((8 + s, j, -s, dz, 1))
+    for j, dz in enumerate(dzs):
+        table.append((11, j, 1, -dz, 1))
+    assert len(table) == ny * nz * 2
+    return table
+
+
+PIECES = 12
+
+
 def project_kernel(dims, counts_ref, rows_ref, *rest):
     ny, nz, nh, shard = dims
-    first = rest[:nz]
-    second = rest[nz : nz + ny]
-    out_ref, w_ref, x_ref, acc_ref, acc16_ref, w_sem, x_sem = rest[nz + ny :]
+    pieces = rest[:PIECES]
+    out_ref, w_ref, x_ref, acc_ref, acc16_ref, w_sem, x_sem = rest[PIECES:]
     y, z, core = (lax.axis_index(a) for a in PLANE)
     sign = 1 - 2 * core
     cols = w_ref.shape[1]
@@ -70,22 +91,19 @@
 
     copies = {}
     for s in range(ny):
-        plane = lax.rem(y - s * sign + ny, ny)
+        plane = lax.rem(y + s, ny)
         for cc in range(2):
             copies[s, "x", cc] = pltpu.make_async_copy(
                 rows_ref.at[cc * nh + plane], x_ref.at[2 * s + cc], x_sem.at[2 * s + cc]
             )
-        for t in range(nz):
-            chip = plane * nz + lax.rem(z - t * sign + nz, nz)
-            for k, (src, part, owner) in enumerate(
-                ((first[t], s, core), (second[s], t, 1 - core))
-            ):
-                at = pl.multiple_of((chip * 2 + owner) * shard, shard)
-                copies[s, t, k] = pltpu.make_async_copy(
-                    src.at[pl.ds(part * shard, shard)],
-                    w_ref.at[pl.ds(at, shard)],
-                    w_sem.at[(s * nz + t) * 2 + k],
-                )
+    for k, (src, part, dy, dz, owner) in enumerate(piece_table(ny, nz)):
+        chip = lax.rem(y + dy * sign + ny, ny) * nz + lax.rem(z + dz * sign + nz, nz)
+        at = pl.multiple_of((chip * 2 + owner) * shard, shard)
+        copies[0, "w", k] = pltpu.make_async_copy(
+            pieces[src].at[pl.ds(part * shard, shard)],
+            w_ref.at[pl.ds(at, shard)],
+            w_sem.at[k],
+        )
     for c in copies.values():
         c.start()
     half = acc_ref.shape[0] // 2
@@ -94,8 +112,7 @@
         for key, c in copies.items():
             if key[0] == s:
                 c.wait()
-        plane = lax.rem(y - s * sign + ny, ny)
-        at = pl.multiple_of(plane * feats, feats)
+        at = pl.multiple_of(lax.rem(y + s, ny) * feats, feats)
 
         @pl.loop(0, 2)
         def _(cc):
@@ -132,17 +149,17 @@
         out_ref[pl.ds(pl.multiple_of(g * chunk, chunk), chunk)] = dot(put, acc16_ref[...]).astype(BF16)
 
 
-def project(counts, rows, first, second, dims):
+def project(counts, rows, pieces, dims):
     ny, nz, nh, shard = dims
     per, feats = rows.shape[1:]
-    cols = second[0].shape[1]
+    cols = pieces[0].shape[1]
     convs = counts.shape[0]
     each = 2 * (per // USED) * MAXB
     hbm = pl.BlockSpec(memory_space=pl.ANY)
     return pl.pallas_call(
         functools.partial(project_kernel, dims),
         out_shape=jax.ShapeDtypeStruct((convs * each, cols), BF16),
-        in_specs=[pl.BlockSpec(memory_space=pltpu.VMEM)] + [hbm] * (1 + nz + ny),
+        in_specs=[pl.BlockSpec(memory_space=pltpu.VMEM)] + [hbm] * (1 + PIECES),
         out_specs=pl.BlockSpec(memory_space=pltpu.VMEM),
         scratch_shapes=[
             pltpu.VMEM((nh * feats, cols), BF16),
@@ -157,7 +174,7 @@
             flops=4 * per * nh * feats * cols, bytes_accessed=2 * nh * feats * (cols + 2 * per), transcendentals=0
         ),
         name="project",
-    )(counts[None], rows, *first, *second)
+    )(counts[None], rows, *pieces)
 
 
 def attend_kernel(live_ref, q_ref, k_ref, v_ref, nk_ref, nv_ref, out_ref):
@@ -208,28 +225,70 @@
     return lax.ppermute(x, (axis, "core"), perm)
 
 
-def ring(x, axis):
-    held = [x]
-    for _ in range(lax.axis_size(axis) - 1):
-        held.append(ring_step(held[-1], axis))
-    return held
+def swap_cores(x):
+    return lax.ppermute(x, "core", [(0, 1), (1, 0)])
+
+
+def kinds(x):
+    half = x.shape[0] // 2
+    return x[:half], x[half:]
+
+
+def gather_weights(key_weight, value_weight):
+    upper = lax.axis_index("core") == 0
+    mine = jnp.where(upper, key_weight, value_weight)
+    other = jnp.where(upper, value_weight, key_weight)
+    own = jnp.concatenate([mine, other])
+    near = swap_cores(jnp.concatenate([other, mine]))
+    zero = jnp.where(upper, own, near)
+    one = jnp.where(upper, near, own)
+
+    y1 = ring_step(zero, "y")
+    y2 = ring_step(kinds(y1)[0], "y")
+    got = swap_cores(jnp.concatenate([y1, y2]))
+    n = key_weight.shape[0]
+    group = jnp.concatenate(
+        [
+            kinds(zero)[0], kinds(y1)[0], got[n : 2 * n], y2,
+            kinds(zero)[1], kinds(y1)[1], got[:n], got[2 * n :],
+        ]
+    )
+    z1 = ring_step(group, "z")
+    z2 = ring_step(z1, "z")
+    z3 = ring_step(z2, "z")
+    z4 = ring_step(kinds(z3)[0], "z")
+    across = [swap_cores(kinds(t)[1]) for t in (z1, z2, z3)]
+    first = [group, z1, z2, z3, z4] + across
+
+    r1 = ring_step(one, "z")
+    r2 = ring_step(r1, "z")
+    r3 = ring_step(r2, "z")
+    r4 = ring_step(kinds(r3)[0], "z")
+    ring = [one, r1, r2, r3]
+    got = swap_cores(jnp.concatenate([r1, r2, r3, r4]))
+    line = jnp.concatenate(
+        [kinds(t)[0] for t in ring]
+        + [got[(2 * k + 1) * n : (2 * k + 2) * n] for k in range(3)]
+        + [r4]
+        + [kinds(t)[1] for t in ring]
+        + [got[2 * k * n : (2 * k + 1) * n] for k in range(3)]
+        + [got[6 * n :]]
+    )
+    l1 = ring_step(line, "y")
+    l2 = ring_step(kinds(l1)[0], "y")
+    second = [line, l1, l2, swap_cores(kinds(l1)[1])]
+    return first + second
 
 
 def per_device(queries, new_keys, new_values, pool, block_table, block_counts, key_weight, value_weight):
     ny, nz, nh = lax.axis_size("y"), lax.axis_size("z"), lax.axis_size("head")
-    core = lax.axis_index("core")
-    own = jnp.where(core == 0, key_weight, value_weight)
-    away = jnp.where(core == 0, value_weight, key_weight)
-    near = lax.ppermute(away, "core", [(0, 1), (1, 0)])
-
     live = live_rows(block_counts, block_table, pool)
     live = live.reshape(-1, live.shape[2])
     rows = lax.all_gather(live, ("core", "head"), axis=0)
 
-    first = ring(jnp.concatenate(ring(own, "y"), axis=0), "z")
-    second = ring(jnp.concatenate(ring(near, "z"), axis=0), "y")
+    pieces = gather_weights(key_weight, value_weight)
     dims = (ny, nz, nh, key_weight.shape[0])
-    sent = project(block_counts, rows, first, second, dims)
+    sent = project(block_counts, rows, pieces, dims)
     convs = block_counts.shape[0]
     sent = sent.reshape(convs, -1, sent.shape[1])
     got = lax.all_to_all(sent, PLANE, split_axis=0, concat_axis=0, tiled=True)

time: 239 us -> 228 us (0.954)
  starting transfers between devices: 75.8 us -> 55.6 us
  waiting for transfers between devices: 101 us -> 107 us
  Pallas kernels: 37.8 us -> 40.3 us
    ppermute x20 -> x12, starting transfers between devices: 52.8 us -> 28.4 us  [ring_step(): return lax.ppermute(x, (axis, 'core'), perm)]
    ppermute x1 -> x7, starting transfers between devices: 3.33 us -> 15.9 us  [swap_cores(): return lax.ppermute(x, 'core', [(0, 1), (1, 0)])]
    all_to_all x1, starting transfers between devices: 19.6 us -> 11.2 us  [per_device(): got = lax.all_to_all(sent, PLANE, split_axis=0, concat_axis=0, tiled=True)]
    ppermute x1 -> x7, waiting for transfers between devices: 1.01 us -> 5.08 us  [swap_cores(): return lax.ppermute(x, 'core', [(0, 1), (1, 0)])]
    pallas_call x1, Pallas kernels: 24.5 us -> 26.9 us  [project(): pl.pallas_call(functools.partial(project_kernel, dims), out_shape=jax.Sha...]
    ppermute x20 -> x12, waiting for transfers between devices: 44.4 us -> 46.3 us  [ring_step(): return lax.ppermute(x, (axis, 'core'), perm)]
    unnamed x36 -> x49, local copies, waits for them, and re-layouts: 6.23 us -> 6.07 us
  transfers between devices with their start and end apart: 23 -> 21, of which waited for: 12 -> 12; matrix products, arithmetic and copies ran while one was open for 0% -> 1% of each run, Pallas kernels for 0% -> 0%
where the time goes in v2:
time: 228 us; the launch traced here: 227 us
  waiting for transfers between devices  107 us (47%)
  starting transfers between devices  55.6 us (24%)
  Pallas kernels  40.3 us (18%)
  between operations  13.8 us (6%)
  local copies, waits for them, and re-layouts  9.93 us (4%)
    all_to_all x1, waiting for transfers between devices, per_device(): got = lax.all_to_all(sent, PLANE, split_axis=0, concat_axis=0, tiled=True)  56 us
    ppermute x12, waiting for transfers between devices, ring_step(): return lax.ppermute(x, (axis, 'core'), perm)  46.3 us
    ppermute x12, starting transfers between devices, ring_step(): return lax.ppermute(x, (axis, 'core'), perm)  28.4 us
    pallas_call x1, Pallas kernels, project(): pl.pallas_call(functools.partial(project_kernel, dims), out_shape=jax.Sha...  26.9 us
    ppermute x7, starting transfers between devices, swap_cores(): return lax.ppermute(x, 'core', [(0, 1), (1, 0)])  15.9 us
    all_to_all x1, starting transfers between devices, per_device(): got = lax.all_to_all(sent, PLANE, split_axis=0, concat_axis=0, tiled=True)  11.2 us
    pallas_call x1, Pallas kernels, attend(): pl.pallas_call(attend_kernel, out_shape=jax.ShapeDtypeStruct(q.shape, BF1...  9.39 us
    unnamed x49, local copies, waits for them, and re-layouts  6.07 us
  transfers between devices with their start and end apart: 21, of which 12 were waited for; matrix products, arithmetic and copies ran while one was open for 1% of the time, Pallas kernels for 0%

profile of v2, /device:TPU:1, one launch (start us, length us, event | category | flops | bytes accessed | tf_op | source)
XLA Modules:
  0.0 227.3 jit_solution(11440266421815048328)
XLA Ops:
  6.5 1.2 broadcast_in_dim.11.table_ref
  7.8 3.3 %copy.13 = bf16[384,2,1536]{2,0,1:T(8,128)(2,1)} copy(bf16[384,2,1536]{2,1,0:T(2,128)(2,1)} %param.11) | data formatting | bytes 4718592 | tf_op args[3]
  11.1 4.0 %live_rows.1 = bf16[2,224,1536]{2,1,0:T(8,128)(2,1)} custom-call(s32[1,64]{1,0:T(1,128)} %bitcast.22, s32[1,384]{1,0:T(1,128)} %broadcast_in_dim.11.table_ref, bf16[2,384,1536]{2,1,0:T(8,128)(2,1)} %bitcast.14), custom_call_target="tpu_custom_call" | custom-call | tf_op jit(solution)/shard_map/live_rows/pallas_call | solution.py:51
  15.2 0.0 all-gather.2.cloned.1.call-update
  15.3 3.3 %collective-permute-start = (bf16[192,768]{1,0:T(8,128)(2,1)S(1)}, bf16[192,768]{1,0:T(8,128)(2,1)S(1)}, u32[]{:S(2)}, u32[]{:S(2)}) collective-permute-start(bf16[192,768]{1,0:T(8,128)(2,1)S(1)} %pad_maximum_fusion.3), channel_id=1, source_target_pairs={{0,4},{4,0},{1,5},{5,1},{2,6},{6,2},{3,7},{7,3},{8,12},{12,8},{9,1... | collective-permute-start | bytes 884744 | tf_op jit(solution)/shard_map/ppermute | solution.py:229
  18.6 1.2 collective-permute-done
  19.8 0.1 broadcast_select_fusion
  19.9 3.9 %collective-permute-start.11 = (bf16[192,768]{1,0:T(8,128)(2,1)S(1)}, bf16[192,768]{1,0:T(8,128)(2,1)S(1)}, u32[]{:S(2)}, u32[]{:S(2)}) collective-permute-start(bf16[192,768]{1,0:T(8,128)(2,1)S(1)} %get-tuple-element.11), channel_id=1, source_target_pairs={{0,8},{4,60},{8,16},{12,4},{16,24},{20,12},{24,32},{28,20},{32,40}... | collective-permute-start | bytes 884744 | tf_op jit(solution)/shard_map/ppermute | solution.py:225
  23.8 2.7 %collective-permute-start.1 = (bf16[192,768]{1,0:T(8,128)(2,1)S(1)}, bf16[192,768]{1,0:T(8,128)(2,1)S(1)}, u32[]{:S(2)}, u32[]{:S(2)}) collective-permute-start(bf16[192,768]{1,0:T(8,128)(2,1)S(1)} %get-tuple-element.12), channel_id=1, source_target_pairs={{0,64},{4,196},{64,128},{68,4},{128,192},{132,68},{192,0},{196,132... | collective-permute-start | bytes 884744 | tf_op jit(solution)/shard_map/ppermute | solution.py:225
  26.6 0.9 collective-permute-done.11
  27.5 3.4 %collective-permute-start.12 = (bf16[192,768]{1,0:T(8,128)(2,1)S(1)}, bf16[192,768]{1,0:T(8,128)(2,1)S(1)}, u32[]{:S(2)}, u32[]{:S(2)}) collective-permute-start(bf16[192,768]{1,0:T(8,128)(2,1)S(1)} %collective-permute-done.11), channel_id=1, source_target_pairs={{0,8},{4,60},{8,16},{12,4},{16,24},{20,12},{24,32},{28,20},{32,40}... | collective-permute-start | bytes 884744 | tf_op jit(solution)/shard_map/ppermute | solution.py:225
  30.9 2.5 %collective-permute-start.2 = (bf16[96,768]{1,0:T(8,128)(2,1)S(1)}, bf16[96,768]{1,0:T(8,128)(2,1)S(1)}, u32[]{:S(2)}, u32[]{:S(2)}) collective-permute-start(bf16[96,768]{1,0:T(8,128)(2,1)S(1)} %get-tuple-element.15), channel_id=1, source_target_pairs={{0,64},{4,196},{64,128},{68,4},{128,192},{132,68},{192,0},{196,132... | collective-permute-start | bytes 442376 | tf_op jit(solution)/shard_map/ppermute | solution.py:225
  33.5 1.1 collective-permute-done.12
  34.6 3.4 %collective-permute-start.13 = (bf16[192,768]{1,0:T(8,128)(2,1)S(1)}, bf16[192,768]{1,0:T(8,128)(2,1)S(1)}, u32[]{:S(2)}, u32[]{:S(2)}) collective-permute-start(bf16[192,768]{1,0:T(8,128)(2,1)S(1)} %collective-permute-done.12), channel_id=1, source_target_pairs={{0,8},{4,60},{8,16},{12,4},{16,24},{20,12},{24,32},{28,20},{32,40}... | collective-permute-start | bytes 884744 | tf_op jit(solution)/shard_map/ppermute | solution.py:225
  38.0 0.1 collective-permute-start.3
  38.1 3.5 %collective-permute-done.13 = bf16[192,768]{1,0:T(8,128)(2,1)S(1)} collective-permute-done((bf16[192,768]{1,0:T(8,128)(2,1)S(1)}, bf16[192,768]{1,0:T(8,128)(2,1)S(1)}, u32[]{:S(2)}, u32[]{:S(2)}) %collective-permute-start.13) | collective-permute-done | bytes 294944 | tf_op jit(solution)/shard_map/ppermute | solution.py:225
  41.7 3.6 %collective-permute-start.14 = (bf16[96,768]{1,0:T(8,128)(2,1)S(1)}, bf16[96,768]{1,0:T(8,128)(2,1)S(1)}, u32[]{:S(2)}, u32[]{:S(2)}) collective-permute-start(bf16[96,768]{1,0:T(8,128)(2,1)S(1)} %get-tuple-element.13), channel_id=1, source_target_pairs={{0,8},{4,60},{8,16},{12,4},{16,24},{20,12},{24,32},{28,20},{32,40}... | collective-permute-start | bytes 442376 | tf_op jit(solution)/shard_map/ppermute | solution.py:225
  45.3 2.1 collective-permute-done.14
  47.4 0.1 pad_maximum_fusion
  47.4 4.2 %collective-permute-start.15 = (bf16[672,768]{1,0:T(8,128)(2,1)S(1)}, bf16[672,768]{1,0:T(8,128)(2,1)S(1)}, u32[]{:S(2)}, u32[]{:S(2)}) collective-permute-start(bf16[672,768]{1,0:T(8,128)(2,1)S(1)} %pad_maximum_fusion), channel_id=1, source_target_pairs={{0,4},{4,0},{1,5},{5,1},{2,6},{6,2},{3,7},{7,3},{8,12},{12,8},{9,1... | collective-permute-start | bytes 3096584 | tf_op jit(solution)/shard_map/ppermute | solution.py:229
  51.8 0.1 collective-permute-start.4
  51.9 2.3 collective-permute-done.15
  54.4 2.6 %collective-permute-start.16 = (bf16[1536,768]{1,0:T(8,128)(2,1)S(1)}, bf16[1536,768]{1,0:T(8,128)(2,1)S(1)}, u32[]{:S(2)}, u32[]{:S(2)}) collective-permute-start(bf16[1536,768]{1,0:T(8,128)(2,1)S(1)} %slice_dynamic-update-slice_fusion.rest_8_), channel_id=1, source_target_pairs={{0,64},{4,196},{64,128},{68,4},{128,192},{132,68},{192,0},{196,132... | collective-permute-start | bytes 7077896 | tf_op jit(solution)/shard_map/ppermute | solution.py:225
  57.0 10.3 %collective-permute-done.4.rest_1_ = bf16[768,768]{1,0:T(8,128)(2,1)S(1)} collective-permute-done((bf16[768,768]{1,0:T(8,128)(2,1)S(1)}, bf16[768,768]{1,0:T(8,128)(2,1)S(1)}, u32[]{:S(2)}, u32[]{:S(2)}) %collective-permute-start.4) | collective-permute-done | bytes 1179680 | tf_op jit(solution)/shard_map/ppermute | solution.py:225
  67.3 1.2 collective-permute-start.5
  68.5 14.1 %collective-permute-done.5.rest_2_ = bf16[768,768]{1,0:T(8,128)(2,1)S(1)} collective-permute-done((bf16[768,768]{1,0:T(8,128)(2,1)S(1)}, bf16[768,768]{1,0:T(8,128)(2,1)S(1)}, u32[]{:S(2)}, u32[]{:S(2)}) %collective-permute-start.5) | collective-permute-done | bytes 1179680 | tf_op jit(solution)/shard_map/ppermute | solution.py:225
  82.7 2.2 collective-permute-start.6
  84.9 2.0 collective-permute-start.8
  86.9 0.2 fusion.1
  87.0 1.2 copy-done
  88.3 0.1 collective-permute-start.18
  88.4 2.7 %collective-permute-start.17 = (bf16[768,768]{1,0:T(8,128)(2,1)S(1)}, bf16[768,768]{1,0:T(8,128)(2,1)}, u32[]{:S(2)}, u32[]{:S(2)}) collective-permute-start(bf16[768,768]{1,0:T(8,128)(2,1)S(1)} %get-tuple-element.8), channel_id=1, source_target_pairs={{0,64},{4,196},{64,128},{68,4},{128,192},{132,68},{192,0},{196,132... | collective-permute-start | bytes 3538952 | tf_op jit(solution)/shard_map/ppermute | solution.py:225
  91.2 0.1 collective-permute-start.9
  91.3 6.8 %collective-permute-done.6.rest_3_ = bf16[768,768]{1,0:T(8,128)(2,1)S(1)} collective-permute-done((bf16[768,768]{1,0:T(8,128)(2,1)S(1)}, bf16[768,768]{1,0:T(8,128)(2,1)S(1)}, u32[]{:S(2)}, u32[]{:S(2)}) %collective-permute-start.6) | collective-permute-done | bytes 1179680 | tf_op jit(solution)/shard_map/ppermute | solution.py:225
  98.1 0.1 fusion.2
  98.2 6.1 %collective-permute-start.10 = (bf16[384,768]{1,0:T(8,128)(2,1)S(1)}, bf16[384,768]{1,0:T(8,128)(2,1)S(1)}, u32[]{:S(2)}, u32[]{:S(2)}) collective-permute-start(bf16[384,768]{1,0:T(8,128)(2,1)S(1)} %get-tuple-element.9), channel_id=1, source_target_pairs={{0,4},{4,0},{1,5},{5,1},{2,6},{6,2},{3,7},{7,3},{8,12},{12,8},{9,1... | collective-permute-start | bytes 1769480 | tf_op jit(solution)/shard_map/ppermute | solution.py:229
  104.3 1.6 collective-permute-done.10.rest_7_
  105.9 7.4 %collective-permute-done.7.rest_4_ = bf16[384,768]{1,0:T(8,128)(2,1)S(1)} collective-permute-done((bf16[384,768]{1,0:T(8,128)(2,1)S(1)}, bf16[384,768]{1,0:T(8,128)(2,1)S(1)}, u32[]{:S(2)}, u32[]{:S(2)}) %collective-permute-start.7) | collective-permute-done | bytes 589856 | tf_op jit(solution)/shard_map/ppermute | solution.py:225
  113.4 0.0 all-gather.2.cloned.1.call-done.rows_ref
  113.4 0.7 copy-done.13
  114.2 0.5 copy-done.9
  114.6 26.9 %project.1 = bf16[1536,768]{1,0:T(8,128)(2,1)} custom-call(s32[1,64]{1,0:T(1,128)} %bitcast.23, bf16[8,448,1536]{2,1,0:T(8,128)(2,1)} %all-gather.2.cloned.1.call-done.rows_ref, bf16[768,768]{1,0:T(8,128)(2,1)} %copy-done.6, bf16[768,768]{1,0:T(8,128)(2,1)} %copy-done.2, bf16[768,768]{1,0:T(8,128)(2,1)} %copy-done.3, bf16[768,768]{1,0:T(8,128)(2,1)} %copy-done.1, ...), custom_call_target="tpu_custom_call" | custom-call | flops 8455716864 | bytes 20447232 | tf_op jit(solution)/shard_map/project/pallas_call | solution.py:159
  141.6 0.0 copy-start.8
  141.6 11.2 %all-to-all-start = ((bf16[64,24,768]{2,1,0:T(8,128)(2,1)}), bf16[64,24,768]{2,1,0:T(8,128)(2,1)S(1)}, u32[]{:S(2)}, u32[]{:S(2)}) async-start(bf16[64,24,768]{2,1,0:T(8,128)(2,1)} %bitcast.18), calls=%async_computation | async-start | bytes 4718592 | tf_op jit(solution)/shard_map/all_to_all | solution.py:294
  152.8 0.7 dynamic_slice.3.live_ref
  153.5 56.0 %all-to-all-done = bf16[64,24,768]{2,1,0:T(8,128)(2,1)S(1)} async-done(((bf16[64,24,768]{2,1,0:T(8,128)(2,1)}), bf16[64,24,768]{2,1,0:T(8,128)(2,1)S(1)}, u32[]{:S(2)}, u32[]{:S(2)}) %all-to-all-start) | async-done | bytes 2359328 | tf_op jit(solution)/shard_map/all_to_all | solution.py:294
  209.4 1.6 fusion
  211.0 9.4 %attend.1 = bf16[128,768]{1,0:T(8,128)(2,1)} custom-call(s32[1]{0:T(128)} %dynamic_slice.3.live_ref, bf16[128,768]{1,0:T(8,128)(2,1)} %bitcast.19, bf16[768,768]{1,0:T(8,128)(2,1)} %bitcast.17, bf16[768,768]{1,0:T(8,128)(2,1)} %bitcast.16, bf16[128,768]{1,0:T(8,128)(2,1)} %bitcast.20, bf16[128,768]{1,0:T(8,128)(2,1)} %bitcast.21), custom_call_target="tpu_custom_call" | custom-call | tf_op jit(solution)/shard_map/attend/pallas_call | solution.py:210
  (63 shorter events, 0.5 us)
Async XLA Ops:
  6.5 106.9 %all-gather.2.cloned.1.call-start = ((), (), s32[]{:S(2)}) async-start(), calls=%async_computation.1 | async-start | bytes 12386304 | tf_op jit(solution)/shard_map/all_gather | solution.py:287
  11.1 4.1 %copy-start.4 = (bf16[96,768]{1,0:T(8,128)(2,1)S(1)}, bf16[96,768]{1,0:T(8,128)(2,1)}, u32[]{:S(2)}) copy-start(bf16[96,768]{1,0:T(8,128)(2,1)} %param.15) | copy-start | bytes 442372
  11.1 4.1 %copy-start.5 = (bf16[96,768]{1,0:T(8,128)(2,1)S(1)}, bf16[96,768]{1,0:T(8,128)(2,1)}, u32[]{:S(2)}) copy-start(bf16[96,768]{1,0:T(8,128)(2,1)} %param.14) | copy-start | bytes 442372
  15.3 4.5 %collective-permute-start = (bf16[192,768]{1,0:T(8,128)(2,1)S(1)}, bf16[192,768]{1,0:T(8,128)(2,1)S(1)}, u32[]{:S(2)}, u32[]{:S(2)}) collective-permute-start(bf16[192,768]{1,0:T(8,128)(2,1)S(1)} %pad_maximum_fusion.3), channel_id=1, source_target_pairs={{0,4},{4,0},{1,5},{5,1},{2,6},{6,2},{3,7},{7,3},{8,12},{12,8},{9,1... | collective-permute-start | bytes 884744 | tf_op jit(solution)/shard_map/ppermute | solution.py:229
  19.9 7.6 %collective-permute-start.11 = (bf16[192,768]{1,0:T(8,128)(2,1)S(1)}, bf16[192,768]{1,0:T(8,128)(2,1)S(1)}, u32[]{:S(2)}, u32[]{:S(2)}) collective-permute-start(bf16[192,768]{1,0:T(8,128)(2,1)S(1)} %get-tuple-element.11), channel_id=1, source_target_pairs={{0,8},{4,60},{8,16},{12,4},{16,24},{20,12},{24,32},{28,20},{32,40}... | collective-permute-start | bytes 884744 | tf_op jit(solution)/shard_map/ppermute | solution.py:225
  23.8 7.1 %collective-permute-start.1 = (bf16[192,768]{1,0:T(8,128)(2,1)S(1)}, bf16[192,768]{1,0:T(8,128)(2,1)S(1)}, u32[]{:S(2)}, u32[]{:S(2)}) collective-permute-start(bf16[192,768]{1,0:T(8,128)(2,1)S(1)} %get-tuple-element.12), channel_id=1, source_target_pairs={{0,64},{4,196},{64,128},{68,4},{128,192},{132,68},{192,0},{196,132... | collective-permute-start | bytes 884744 | tf_op jit(solution)/shard_map/ppermute | solution.py:225
  27.5 7.1 %collective-permute-start.12 = (bf16[192,768]{1,0:T(8,128)(2,1)S(1)}, bf16[192,768]{1,0:T(8,128)(2,1)S(1)}, u32[]{:S(2)}, u32[]{:S(2)}) collective-permute-start(bf16[192,768]{1,0:T(8,128)(2,1)S(1)} %collective-permute-done.11), channel_id=1, source_target_pairs={{0,8},{4,60},{8,16},{12,4},{16,24},{20,12},{24,32},{28,20},{32,40}... | collective-permute-start | bytes 884744 | tf_op jit(solution)/shard_map/ppermute | solution.py:225
  30.9 7.1 %collective-permute-start.2 = (bf16[96,768]{1,0:T(8,128)(2,1)S(1)}, bf16[96,768]{1,0:T(8,128)(2,1)S(1)}, u32[]{:S(2)}, u32[]{:S(2)}) collective-permute-start(bf16[96,768]{1,0:T(8,128)(2,1)S(1)} %get-tuple-element.15), channel_id=1, source_target_pairs={{0,64},{4,196},{64,128},{68,4},{128,192},{132,68},{192,0},{196,132... | collective-permute-start | bytes 442376 | tf_op jit(solution)/shard_map/ppermute | solution.py:225
  34.6 7.1 %collective-permute-start.13 = (bf16[192,768]{1,0:T(8,128)(2,1)S(1)}, bf16[192,768]{1,0:T(8,128)(2,1)S(1)}, u32[]{:S(2)}, u32[]{:S(2)}) collective-permute-start(bf16[192,768]{1,0:T(8,128)(2,1)S(1)} %collective-permute-done.12), channel_id=1, source_target_pairs={{0,8},{4,60},{8,16},{12,4},{16,24},{20,12},{24,32},{28,20},{32,40}... | collective-permute-start | bytes 884744 | tf_op jit(solution)/shard_map/ppermute | solution.py:225
  38.0 7.3 %collective-permute-start.3 = (bf16[288,768]{1,0:T(8,128)(2,1)S(1)}, bf16[288,768]{1,0:T(8,128)(2,1)S(1)}, u32[]{:S(2)}, u32[]{:S(2)}) collective-permute-start(bf16[288,768]{1,0:T(8,128)(2,1)S(1)} %pad_maximum_fusion.1), channel_id=1, source_target_pairs={{0,4},{4,0},{1,5},{5,1},{2,6},{6,2},{3,7},{7,3},{8,12},{12,8},{9,1... | collective-permute-start | bytes 1327112 | tf_op jit(solution)/shard_map/ppermute | solution.py:229
  41.7 5.7 %collective-permute-start.14 = (bf16[96,768]{1,0:T(8,128)(2,1)S(1)}, bf16[96,768]{1,0:T(8,128)(2,1)S(1)}, u32[]{:S(2)}, u32[]{:S(2)}) collective-permute-start(bf16[96,768]{1,0:T(8,128)(2,1)S(1)} %get-tuple-element.13), channel_id=1, source_target_pairs={{0,8},{4,60},{8,16},{12,4},{16,24},{20,12},{24,32},{28,20},{32,40}... | collective-permute-start | bytes 442376 | tf_op jit(solution)/shard_map/ppermute | solution.py:225
  47.4 6.7 %collective-permute-start.15 = (bf16[672,768]{1,0:T(8,128)(2,1)S(1)}, bf16[672,768]{1,0:T(8,128)(2,1)S(1)}, u32[]{:S(2)}, u32[]{:S(2)}) collective-permute-start(bf16[672,768]{1,0:T(8,128)(2,1)S(1)} %pad_maximum_fusion), channel_id=1, source_target_pairs={{0,4},{4,0},{1,5},{5,1},{2,6},{6,2},{3,7},{7,3},{8,12},{12,8},{9,1... | collective-permute-start | bytes 3096584 | tf_op jit(solution)/shard_map/ppermute | solution.py:229
  51.8 33.1 %copy-start.6 = (bf16[768,768]{1,0:T(8,128)(2,1)}, bf16[768,768]{1,0:T(8,128)(2,1)S(1)}, u32[]{:S(2)}) copy-start(bf16[768,768]{1,0:T(8,128)(2,1)S(1)} %slice_dynamic-update-slice_fusion.14.rest_0_) | copy-start | bytes 3538948
  51.8 15.5 %collective-permute-start.4 = (bf16[768,768]{1,0:T(8,128)(2,1)S(1)}, bf16[768,768]{1,0:T(8,128)(2,1)S(1)}, u32[]{:S(2)}, u32[]{:S(2)}) collective-permute-start(bf16[768,768]{1,0:T(8,128)(2,1)S(1)} %slice_dynamic-update-slice_fusion.14.rest_0_), channel_id=1, source_target_pairs={{0,8},{4,60},{8,16},{12,4},{16,24},{20,12},{24,32},{28,20},{32,40}... | collective-permute-start | bytes 3538952 | tf_op jit(solution)/shard_map/ppermute | solution.py:225
  54.4 59.0 %copy-start.7 = (bf16[1536,768]{1,0:T(8,128)(2,1)}, bf16[1536,768]{1,0:T(8,128)(2,1)S(1)}, u32[]{:S(2)}) copy-start(bf16[1536,768]{1,0:T(8,128)(2,1)S(1)} %slice_dynamic-update-slice_fusion.rest_8_) | copy-start | bytes 7077892
  54.4 32.5 %collective-permute-start.16 = (bf16[1536,768]{1,0:T(8,128)(2,1)S(1)}, bf16[1536,768]{1,0:T(8,128)(2,1)S(1)}, u32[]{:S(2)}, u32[]{:S(2)}) collective-permute-start(bf16[1536,768]{1,0:T(8,128)(2,1)S(1)} %slice_dynamic-update-slice_fusion.rest_8_), channel_id=1, source_target_pairs={{0,64},{4,196},{64,128},{68,4},{128,192},{132,68},{192,0},{196,132... | collective-permute-start | bytes 7077896 | tf_op jit(solution)/shard_map/ppermute | solution.py:225
  67.3 19.7 %copy-start.2 = (bf16[768,768]{1,0:T(8,128)(2,1)}, bf16[768,768]{1,0:T(8,128)(2,1)S(1)}, u32[]{:S(2)}) copy-start(bf16[768,768]{1,0:T(8,128)(2,1)S(1)} %collective-permute-done.4.rest_1_) | copy-start | bytes 3538948
  67.3 15.3 %collective-permute-start.5 = (bf16[768,768]{1,0:T(8,128)(2,1)S(1)}, bf16[768,768]{1,0:T(8,128)(2,1)S(1)}, u32[]{:S(2)}, u32[]{:S(2)}) collective-permute-start(bf16[768,768]{1,0:T(8,128)(2,1)S(1)} %collective-permute-done.4.rest_1_), channel_id=1, source_target_pairs={{0,8},{4,60},{8,16},{12,4},{16,24},{20,12},{24,32},{28,20},{32,40}... | collective-permute-start | bytes 3538952 | tf_op jit(solution)/shard_map/ppermute | solution.py:225
  82.7 8.5 %copy-start.3 = (bf16[768,768]{1,0:T(8,128)(2,1)}, bf16[768,768]{1,0:T(8,128)(2,1)S(1)}, u32[]{:S(2)}) copy-start(bf16[768,768]{1,0:T(8,128)(2,1)S(1)} %collective-permute-done.5.rest_2_) | copy-start | bytes 3538948
  82.7 15.5 %collective-permute-start.6 = (bf16[768,768]{1,0:T(8,128)(2,1)S(1)}, bf16[768,768]{1,0:T(8,128)(2,1)S(1)}, u32[]{:S(2)}, u32[]{:S(2)}) collective-permute-start(bf16[768,768]{1,0:T(8,128)(2,1)S(1)} %collective-permute-done.5.rest_2_), channel_id=1, source_target_pairs={{0,8},{4,60},{8,16},{12,4},{16,24},{20,12},{24,32},{28,20},{32,40}... | collective-permute-start | bytes 3538952 | tf_op jit(solution)/shard_map/ppermute | solution.py:225
  84.9 19.4 %collective-permute-start.8 = (bf16[384,768]{1,0:T(8,128)(2,1)S(1)}, bf16[384,768]{1,0:T(8,128)(2,1)S(1)}, u32[]{:S(2)}, u32[]{:S(2)}) collective-permute-start(bf16[384,768]{1,0:T(8,128)(2,1)S(1)} %slice.130), channel_id=1, source_target_pairs={{0,4},{4,0},{1,5},{5,1},{2,6},{6,2},{3,7},{7,3},{8,12},{12,8},{9,1... | collective-permute-start | bytes 1769480 | tf_op jit(solution)/shard_map/ppermute | solution.py:229
  86.8 1.4 copy-start
  88.3 25.1 %collective-permute-start.18 = (bf16[768,768]{1,0:T(8,128)(2,1)S(1)}, bf16[768,768]{1,0:T(8,128)(2,1)S(1)}, u32[]{:S(2)}, u32[]{:S(2)}) collective-permute-start(bf16[768,768]{1,0:T(8,128)(2,1)S(1)} %get-tuple-element.7), channel_id=1, source_target_pairs={{0,4},{4,0},{1,5},{5,1},{2,6},{6,2},{3,7},{7,3},{8,12},{12,8},{9,1... | collective-permute-start | bytes 3538952 | tf_op jit(solution)/shard_map/ppermute | solution.py:229
  88.4 25.0 %collective-permute-start.17 = (bf16[768,768]{1,0:T(8,128)(2,1)S(1)}, bf16[768,768]{1,0:T(8,128)(2,1)}, u32[]{:S(2)}, u32[]{:S(2)}) collective-permute-start(bf16[768,768]{1,0:T(8,128)(2,1)S(1)} %get-tuple-element.8), channel_id=1, source_target_pairs={{0,64},{4,196},{64,128},{68,4},{128,192},{132,68},{192,0},{196,132... | collective-permute-start | bytes 3538952 | tf_op jit(solution)/shard_map/ppermute | solution.py:225
  91.2 13.1 %collective-permute-start.9 = (bf16[384,768]{1,0:T(8,128)(2,1)S(1)}, bf16[384,768]{1,0:T(8,128)(2,1)S(1)}, u32[]{:S(2)}, u32[]{:S(2)}) collective-permute-start(bf16[384,768]{1,0:T(8,128)(2,1)S(1)} %slice.131), channel_id=1, source_target_pairs={{0,4},{4,0},{1,5},{5,1},{2,6},{6,2},{3,7},{7,3},{8,12},{12,8},{9,1... | collective-permute-start | bytes 1769480 | tf_op jit(solution)/shard_map/ppermute | solution.py:229
  98.1 15.3 %copy-start.1 = (bf16[768,768]{1,0:T(8,128)(2,1)}, bf16[768,768]{1,0:T(8,128)(2,1)S(1)}, u32[]{:S(2)}) copy-start(bf16[768,768]{1,0:T(8,128)(2,1)S(1)} %collective-permute-done.6.rest_3_) | copy-start | bytes 3538948
  98.2 7.7 %collective-permute-start.10 = (bf16[384,768]{1,0:T(8,128)(2,1)S(1)}, bf16[384,768]{1,0:T(8,128)(2,1)S(1)}, u32[]{:S(2)}, u32[]{:S(2)}) collective-permute-start(bf16[384,768]{1,0:T(8,128)(2,1)S(1)} %get-tuple-element.9), channel_id=1, source_target_pairs={{0,4},{4,0},{1,5},{5,1},{2,6},{6,2},{3,7},{7,3},{8,12},{12,8},{9,1... | collective-permute-start | bytes 1769480 | tf_op jit(solution)/shard_map/ppermute | solution.py:229
  104.3 9.0 %copy-start.10 = (bf16[384,768]{1,0:T(8,128)(2,1)}, bf16[384,768]{1,0:T(8,128)(2,1)S(1)}, u32[]{:S(2)}) copy-start(bf16[384,768]{1,0:T(8,128)(2,1)S(1)} %collective-permute-done.8.rest_5_) | copy-start | bytes 1769476
  104.3 9.0 %collective-permute-start.7 = (bf16[384,768]{1,0:T(8,128)(2,1)S(1)}, bf16[384,768]{1,0:T(8,128)(2,1)S(1)}, u32[]{:S(2)}, u32[]{:S(2)}) collective-permute-start(bf16[384,768]{1,0:T(8,128)(2,1)S(1)} %get-tuple-element.10), channel_id=1, source_target_pairs={{0,8},{4,60},{8,16},{12,4},{16,24},{20,12},{24,32},{28,20},{32,40}... | collective-permute-start | bytes 1769480 | tf_op jit(solution)/shard_map/ppermute | solution.py:225
  104.3 9.0 %copy-start.11 = (bf16[384,768]{1,0:T(8,128)(2,1)}, bf16[384,768]{1,0:T(8,128)(2,1)S(1)}, u32[]{:S(2)}) copy-start(bf16[384,768]{1,0:T(8,128)(2,1)S(1)} %collective-permute-done.9.rest_6_) | copy-start | bytes 1769476
  105.9 7.5 %copy-start.12 = (bf16[384,768]{1,0:T(8,128)(2,1)}, bf16[384,768]{1,0:T(8,128)(2,1)S(1)}, u32[]{:S(2)}) copy-start(bf16[384,768]{1,0:T(8,128)(2,1)S(1)} %collective-permute-done.10.rest_7_) | copy-start | bytes 1769476
  113.3 0.8 copy-start.13
  113.4 1.3 copy-start.9
  141.6 11.2 %copy-start.8 = (s32[64]{0:T(128)S(1)}, s32[64]{0:T(128)}, u32[]{:S(2)}) copy-start(s32[64]{0:T(128)} %param.13) | copy-start | bytes 772
  141.6 67.9 %all-to-all-start = ((bf16[64,24,768]{2,1,0:T(8,128)(2,1)}), bf16[64,24,768]{2,1,0:T(8,128)(2,1)S(1)}, u32[]{:S(2)}, u32[]{:S(2)}) async-start(bf16[64,24,768]{2,1,0:T(8,128)(2,1)} %bitcast.18), calls=%async_computation | async-start | bytes 4718592 | tf_op jit(solution)/shard_map/all_to_all | solution.py:294
Sparse Core Ops, SparseCore 0:
  15.3 67.4 all-gather.1

commit v3 on v2

--- a/solution.py
+++ b/solution.py
@@ -80,78 +80,91 @@
 PIECES = 12
 
 
-def project_kernel(dims, counts_ref, rows_ref, *rest):
+def project_kernel(dims, counts_ref, *rest):
     ny, nz, nh, shard = dims
-    pieces = rest[:PIECES]
-    out_ref, w_ref, x_ref, acc_ref, acc16_ref, w_sem, x_sem = rest[PIECES:]
+    rows = rest[: 2 * nh]
+    pieces = rest[2 * nh : 2 * nh + PIECES]
+    out_ref, w_ref, x_ref, put_ref, acc_ref, acc16_ref, w_sem, x_sem = rest[2 * nh + PIECES :]
     y, z, core = (lax.axis_index(a) for a in PLANE)
+    head = lax.axis_index("head")
     sign = 1 - 2 * core
     cols = w_ref.shape[1]
     feats = w_ref.shape[0] // nh
 
-    copies = {}
-    for s in range(ny):
-        plane = lax.rem(y + s, ny)
-        for cc in range(2):
-            copies[s, "x", cc] = pltpu.make_async_copy(
-                rows_ref.at[cc * nh + plane], x_ref.at[2 * s + cc], x_sem.at[2 * s + cc]
-            )
+    w_copies, x_copies = [], []
     for k, (src, part, dy, dz, owner) in enumerate(piece_table(ny, nz)):
         chip = lax.rem(y + dy * sign + ny, ny) * nz + lax.rem(z + dz * sign + nz, nz)
         at = pl.multiple_of((chip * 2 + owner) * shard, shard)
-        copies[0, "w", k] = pltpu.make_async_copy(
-            pieces[src].at[pl.ds(part * shard, shard)],
-            w_ref.at[pl.ds(at, shard)],
-            w_sem.at[k],
+        w_copies.append(
+            pltpu.make_async_copy(
+                pieces[src].at[pl.ds(part * shard, shard)],
+                w_ref.at[pl.ds(at, shard)],
+                w_sem.at[k],
+            )
         )
-    for c in copies.values():
+    for k in range(2 * nh):
+        who = core if k % 2 == 0 else 1 - core
+        x_copies.append(
+            pltpu.make_async_copy(rows[k], x_ref.at[2 * (k // 2) + who], x_sem.at[k])
+        )
+    for c in w_copies + x_copies:
         c.start()
-    half = acc_ref.shape[0] // 2
-    tile = 256 if cols % 256 == 0 else cols
-    for s in range(ny):
-        for key, c in copies.items():
-            if key[0] == s:
-                c.wait()
-        at = pl.multiple_of(lax.rem(y + s, ny) * feats, feats)
-
-        @pl.loop(0, 2)
-        def _(cc):
-            @pl.loop(0, cols // tile)
-            def _(n):
-                lanes = pl.ds(pl.multiple_of(n * tile, tile), tile)
-                row = pl.ds(pl.multiple_of(cc * half, half), half)
-                part = dot(x_ref[2 * s + cc], w_ref[pl.ds(at, feats), lanes])
-                if s == 0:
-                    acc_ref[row, lanes] = part
-                elif s < ny - 1:
-                    acc_ref[row, lanes] += part
-                else:
-                    acc16_ref[row, lanes] = (acc_ref[row, lanes] + part).astype(BF16)
 
     convs = counts_ref.shape[1]
     each = out_ref.shape[0] // convs
     chunk = 16 * each
-    used = acc_ref.shape[0] // (each // MAXB)
+    total = acc_ref.shape[0]
+    used = total // (each // MAXB)
 
     @pl.loop(0, convs // 16)
     def _(g):
-        i = iota((chunk, 1), 0)
-        conv = g * 16 + i // each
-        inside = i % each
-        slot = inside % MAXB
-        which = inside // MAXB
+        i = iota((chunk, 1), 0) + g * chunk
+        conv = lax.shift_right_logical(i * (65536 // each + 1), 16)
+        inside = i - conv * each
+        which = lax.shift_right_logical(inside * (65536 // MAXB + 1), 16)
+        slot = inside - which * MAXB
         other = iota((chunk, convs), 1)
         counts = counts_ref[...]
-        start = jnp.sum(jnp.where(other < conv, counts, 0), axis=1, keepdims=True)
-        count = jnp.sum(jnp.where(other == conv, counts, 0), axis=1, keepdims=True)
+        both = jnp.sum(
+            jnp.where(other < conv, counts * 8, jnp.where(other == conv, counts, 0)),
+            axis=1,
+            keepdims=True,
+        )
+        start, count = lax.shift_right_logical(both, 3), lax.bitwise_and(both, 7)
         source = jnp.where(slot < count, which * used + start + slot, -1)
-        put = (iota((chunk, acc_ref.shape[0]), 1) == source).astype(F32).astype(BF16)
-        out_ref[pl.ds(pl.multiple_of(g * chunk, chunk), chunk)] = dot(put, acc16_ref[...]).astype(BF16)
+        rows_of = pl.ds(pl.multiple_of(g * chunk, chunk), chunk)
+        put_ref[rows_of] = (iota((chunk, total), 1) == source).astype(F32).astype(BF16)
+
+    for c in w_copies:
+        c.wait()
+    half = total // 2
+    quarters = (0, -1, 1, -2)
+    for s in range(nh):
+        for c in x_copies[2 * s : 2 * s + 2]:
+            c.wait()
+        quarter = lax.rem(head + quarters[s] * sign + nh, nh)
+        at = pl.multiple_of(quarter * feats, feats)
+
+        @pl.loop(0, 2)
+        def _(cc):
+            row = pl.ds(pl.multiple_of(cc * half, half), half)
+            part = dot(x_ref[2 * s + cc], w_ref[pl.ds(at, feats)])
+            if s == 0:
+                acc_ref[row] = part
+            elif s < nh - 1:
+                acc_ref[row] += part
+            else:
+                acc16_ref[row] = (acc_ref[row] + part).astype(BF16)
+
+    @pl.loop(0, convs // 16)
+    def _(g):
+        rows_of = pl.ds(pl.multiple_of(g * chunk, chunk), chunk)
+        out_ref[rows_of] = dot(put_ref[rows_of], acc16_ref[...]).astype(BF16)
 
 
 def project(counts, rows, pieces, dims):
     ny, nz, nh, shard = dims
-    per, feats = rows.shape[1:]
+    per, feats = rows[0].shape
     cols = pieces[0].shape[1]
     convs = counts.shape[0]
     each = 2 * (per // USED) * MAXB
@@ -159,11 +172,12 @@
     return pl.pallas_call(
         functools.partial(project_kernel, dims),
         out_shape=jax.ShapeDtypeStruct((convs * each, cols), BF16),
-        in_specs=[pl.BlockSpec(memory_space=pltpu.VMEM)] + [hbm] * (1 + PIECES),
+        in_specs=[pl.BlockSpec(memory_space=pltpu.VMEM)] + [hbm] * (2 * nh + PIECES),
         out_specs=pl.BlockSpec(memory_space=pltpu.VMEM),
         scratch_shapes=[
             pltpu.VMEM((nh * feats, cols), BF16),
             pltpu.VMEM((2 * nh, per, feats), BF16),
+            pltpu.VMEM((convs * each, 2 * per), BF16),
             pltpu.VMEM((2 * per, cols), F32),
             pltpu.VMEM((2 * per, cols), BF16),
             pltpu.SemaphoreType.DMA((ny * nz * 2,)),
@@ -174,7 +188,7 @@
             flops=4 * per * nh * feats * cols, bytes_accessed=2 * nh * feats * (cols + 2 * per), transcendentals=0
         ),
         name="project",
-    )(counts[None], rows, *pieces)
+    )(counts[None], *rows, *pieces)
 
 
 def attend_kernel(live_ref, q_ref, k_ref, v_ref, nk_ref, nv_ref, out_ref):
@@ -188,20 +202,22 @@
     @pl.loop(0, q_ref.shape[1] // (2 * HD))
     def _(pair):
         lanes = pl.ds(pl.multiple_of(pair * 2 * HD, 2 * HD), 2 * HD)
-        q, k, v = q_ref[:, lanes], k_ref[:, lanes], v_ref[:, lanes]
+        q = q_ref[:, lanes] * jnp.asarray(scale, BF16)
+        k, v = k_ref[:, lanes], v_ref[:, lanes]
         nk, nv = nk_ref[:, lanes], nv_ref[:, lanes]
         low = iota(q.shape, 1) < HD
         outs = []
         for mine in (low, jnp.logical_not(low)):
             qh = jnp.where(mine, q, jnp.zeros_like(q))
-            sh = jnp.where(hist_ok, dot(qh, k, ((1,), (1,))) * scale, -jnp.inf)
-            sn = jnp.where(new_ok, dot(qh, nk, ((1,), (1,))) * scale, -jnp.inf)
+            sh = jnp.where(hist_ok, dot(qh, k, ((1,), (1,))), -jnp.inf)
+            sn = jnp.where(new_ok, dot(qh, nk, ((1,), (1,))), -jnp.inf)
             top = jnp.maximum(
                 jnp.max(sh, axis=1, keepdims=True), jnp.max(sn, axis=1, keepdims=True)
             )
             eh, en = jnp.exp(sh - top), jnp.exp(sn - top)
             total = jnp.sum(eh, axis=1, keepdims=True) + jnp.sum(en, axis=1, keepdims=True)
-            ph, pn = (eh / total).astype(BF16), (en / total).astype(BF16)
+            share = 1.0 / total
+            ph, pn = (eh * share).astype(BF16), (en * share).astype(BF16)
             outs.append(dot(ph, v) + dot(pn, nv))
         out_ref[:, lanes] = jnp.where(low, outs[0], outs[1]).astype(BF16)
 
@@ -217,12 +233,26 @@
     )(live, q, k, v, nk, nv)
 
 
-def ring_step(x, axis):
+def ring_step(x, axis, way=1):
     n = lax.axis_size(axis)
+    order = (axis, "core") if axis != "head" else ("core", axis)
+    place = (lambda i, c: 2 * i + c) if axis != "head" else (lambda i, c: c * n + i)
     perm = []
     for i in range(n):
-        perm += [(2 * i, 2 * ((i + 1) % n)), (2 * i + 1, 2 * ((i - 1) % n) + 1)]
-    return lax.ppermute(x, (axis, "core"), perm)
+        perm += [(place(i, 0), place((i + way) % n, 0)), (place(i, 1), place((i - way) % n, 1))]
+    return lax.ppermute(x, order, perm)
+
+
+def gather_rows(own):
+    behind = ring_step(own, "head")
+    ahead = ring_step(own, "head", -1)
+    opposite = ring_step(behind, "head")
+    return [
+        own, swap_cores(own),
+        behind, swap_cores(ahead),
+        ahead, swap_cores(behind),
+        opposite, swap_cores(opposite),
+    ]
 
 
 def swap_cores(x):
@@ -284,7 +314,7 @@
     ny, nz, nh = lax.axis_size("y"), lax.axis_size("z"), lax.axis_size("head")
     live = live_rows(block_counts, block_table, pool)
     live = live.reshape(-1, live.shape[2])
-    rows = lax.all_gather(live, ("core", "head"), axis=0)
+    rows = gather_rows(live)
 
     pieces = gather_weights(key_weight, value_weight)
     dims = (ny, nz, nh, key_weight.shape[0])

time: 228 us -> 216 us (0.947)
  between operations: 13.8 us -> 0.53 us
  starting transfers between devices: 55.6 us -> 65.9 us
  Pallas kernels: 40.3 us -> 36 us
  waiting for transfers between devices: 107 us -> 103 us
    ppermute x12 -> x15, starting transfers between devices: 28.4 us -> 34.5 us  [ring_step(): return lax.ppermute(x, order, perm)]
    pallas_call x1, Pallas kernels: 26.9 us -> 22.6 us  [project(): pl.pallas_call(functools.partial(project_kernel, dims), out_shape=jax.Sha...]
    ppermute x7 -> x11, waiting for transfers between devices: 5.08 us -> 1.63 us  [swap_cores(): return lax.ppermute(x, 'core', [(0, 1), (1, 0)])]
    ppermute x7 -> x11, starting transfers between devices: 15.9 us -> 18.2 us  [swap_cores(): return lax.ppermute(x, 'core', [(0, 1), (1, 0)])]
    ppermute x12 -> x15, waiting for transfers between devices: 46.3 us -> 45.3 us  [ring_step(): return lax.ppermute(x, order, perm)]
    unnamed x49 -> x63, local copies, waits for them, and re-layouts: 6.07 us -> 5.81 us
  transfers between devices with their start and end apart: 21 -> 27, of which waited for: 12 -> 11; matrix products, arithmetic and copies ran while one was open for 1% -> 3% of each run, Pallas kernels for 0% -> 2%
where the time goes in v3:
time: 216 us
  waiting for transfers between devices  103 us (48%)
  starting transfers between devices  65.9 us (31%)
  Pallas kernels  36 us (17%)
  local copies, waits for them, and re-layouts  9.58 us (4%)
    all_to_all x1, waiting for transfers between devices, per_device(): got = lax.all_to_all(sent, PLANE, split_axis=0, concat_axis=0, tiled=True)  56 us
    ppermute x15, waiting for transfers between devices, ring_step(): return lax.ppermute(x, order, perm)  45.3 us
    ppermute x15, starting transfers between devices, ring_step(): return lax.ppermute(x, order, perm)  34.5 us
    pallas_call x1, Pallas kernels, project(): pl.pallas_call(functools.partial(project_kernel, dims), out_shape=jax.Sha...  22.6 us
    ppermute x11, starting transfers between devices, swap_cores(): return lax.ppermute(x, 'core', [(0, 1), (1, 0)])  18.2 us
    all_to_all x1, starting transfers between devices, per_device(): got = lax.all_to_all(sent, PLANE, split_axis=0, concat_axis=0, tiled=True)  13.2 us
    pallas_call x1, Pallas kernels, attend(): pl.pallas_call(attend_kernel, out_shape=jax.ShapeDtypeStruct(q.shape, BF1...  9.28 us
    unnamed x63, local copies, waits for them, and re-layouts  5.81 us
  transfers between devices with their start and end apart: 27, of which 11 were waited for; matrix products, arithmetic and copies ran while one was open for 3% of the time, Pallas kernels for 2%

profile of v3, /device:TPU:1, one launch (start us, length us, event | category | flops | bytes accessed | tf_op | source)
XLA Modules:
  0.0 216.2 jit_solution(11205967390848842702)
XLA Ops:
  0.0 1.0 broadcast_select_fusion.2
  1.0 3.3 %collective-permute-start.7 = (bf16[192,768]{1,0:T(8,128)(2,1)S(1)}, bf16[192,768]{1,0:T(8,128)(2,1)S(1)}, u32[]{:S(2)}, u32[]{:S(2)}) collective-permute-start(bf16[192,768]{1,0:T(8,128)(2,1)S(1)} %pad_maximum_fusion.3), channel_id=1, source_target_pairs={{0,4},{4,0},{1,5},{5,1},{2,6},{6,2},{3,7},{7,3},{8,12},{12,8},{9,1... | collective-permute-start | bytes 884744 | tf_op jit(solution)/shard_map/ppermute | solution.py:259
  4.4 1.2 broadcast_in_dim.11.table_ref
  5.6 3.3 %copy.12 = bf16[384,2,1536]{2,0,1:T(8,128)(2,1)} copy(bf16[384,2,1536]{2,1,0:T(2,128)(2,1)} %param.11) | data formatting | bytes 4718592 | tf_op args[3]
  8.9 4.1 %live_rows.1 = bf16[2,224,1536]{2,1,0:T(8,128)(2,1)} custom-call(s32[1,64]{1,0:T(1,128)} %bitcast.25, s32[1,384]{1,0:T(1,128)} %broadcast_in_dim.11.table_ref, bf16[2,384,1536]{2,1,0:T(8,128)(2,1)} %bitcast.14), custom_call_target="tpu_custom_call" | custom-call | tf_op jit(solution)/shard_map/live_rows/pallas_call | solution.py:51
  13.0 2.7 %collective-permute-start.1 = (bf16[448,1536]{1,0:T(8,128)(2,1)}, bf16[448,1536]{1,0:T(8,128)(2,1)S(1)}, u32[]{:S(2)}, u32[]{:S(2)}) collective-permute-start(bf16[448,1536]{1,0:T(8,128)(2,1)} %bitcast.19), channel_id=1, source_target_pairs={{0,1},{4,7},{1,2},{5,4},{2,3},{6,5},{3,0},{7,6},{8,9},{12,15},{9,1... | collective-permute-start | bytes 4128776 | tf_op jit(solution)/shard_map/ppermute | solution.py:243
  15.7 0.1 broadcast_select_fusion
  15.8 3.9 %collective-permute-start.18 = (bf16[192,768]{1,0:T(8,128)(2,1)S(1)}, bf16[192,768]{1,0:T(8,128)(2,1)S(1)}, u32[]{:S(2)}, u32[]{:S(2)}) collective-permute-start(bf16[192,768]{1,0:T(8,128)(2,1)S(1)} %get-tuple-element.11), channel_id=1, source_target_pairs={{0,8},{4,60},{8,16},{12,4},{16,24},{20,12},{24,32},{28,20},{32,40}... | collective-permute-start | bytes 884744 | tf_op jit(solution)/shard_map/ppermute | solution.py:243
  19.7 2.7 %collective-permute-start.8 = (bf16[192,768]{1,0:T(8,128)(2,1)S(1)}, bf16[192,768]{1,0:T(8,128)(2,1)S(1)}, u32[]{:S(2)}, u32[]{:S(2)}) collective-permute-start(bf16[192,768]{1,0:T(8,128)(2,1)S(1)} %get-tuple-element.12), channel_id=1, source_target_pairs={{0,64},{4,196},{64,128},{68,4},{128,192},{132,68},{192,0},{196,132... | collective-permute-start | bytes 884744 | tf_op jit(solution)/shard_map/ppermute | solution.py:243
  22.4 0.9 collective-permute-done.18
  23.4 3.4 %collective-permute-start.19 = (bf16[192,768]{1,0:T(8,128)(2,1)S(1)}, bf16[192,768]{1,0:T(8,128)(2,1)S(1)}, u32[]{:S(2)}, u32[]{:S(2)}) collective-permute-start(bf16[192,768]{1,0:T(8,128)(2,1)S(1)} %collective-permute-done.18), channel_id=1, source_target_pairs={{0,8},{4,60},{8,16},{12,4},{16,24},{20,12},{24,32},{28,20},{32,40}... | collective-permute-start | bytes 884744 | tf_op jit(solution)/shard_map/ppermute | solution.py:243
  26.8 2.8 %collective-permute-start.9 = (bf16[96,768]{1,0:T(8,128)(2,1)S(1)}, bf16[96,768]{1,0:T(8,128)(2,1)S(1)}, u32[]{:S(2)}, u32[]{:S(2)}) collective-permute-start(bf16[96,768]{1,0:T(8,128)(2,1)S(1)} %get-tuple-element.15), channel_id=1, source_target_pairs={{0,64},{4,196},{64,128},{68,4},{128,192},{132,68},{192,0},{196,132... | collective-permute-start | bytes 442376 | tf_op jit(solution)/shard_map/ppermute | solution.py:243
  29.6 0.8 collective-permute-done.19
  30.4 3.4 %collective-permute-start.20 = (bf16[192,768]{1,0:T(8,128)(2,1)S(1)}, bf16[192,768]{1,0:T(8,128)(2,1)S(1)}, u32[]{:S(2)}, u32[]{:S(2)}) collective-permute-start(bf16[192,768]{1,0:T(8,128)(2,1)S(1)} %collective-permute-done.19), channel_id=1, source_target_pairs={{0,8},{4,60},{8,16},{12,4},{16,24},{20,12},{24,32},{28,20},{32,40}... | collective-permute-start | bytes 884744 | tf_op jit(solution)/shard_map/ppermute | solution.py:243
  33.9 0.1 collective-permute-start.10
  34.0 3.5 %collective-permute-done.20 = bf16[192,768]{1,0:T(8,128)(2,1)S(1)} collective-permute-done((bf16[192,768]{1,0:T(8,128)(2,1)S(1)}, bf16[192,768]{1,0:T(8,128)(2,1)S(1)}, u32[]{:S(2)}, u32[]{:S(2)}) %collective-permute-start.20) | collective-permute-done | bytes 294944 | tf_op jit(solution)/shard_map/ppermute | solution.py:243
  37.5 3.5 %collective-permute-start.21 = (bf16[96,768]{1,0:T(8,128)(2,1)S(1)}, bf16[96,768]{1,0:T(8,128)(2,1)S(1)}, u32[]{:S(2)}, u32[]{:S(2)}) collective-permute-start(bf16[96,768]{1,0:T(8,128)(2,1)S(1)} %get-tuple-element.13), channel_id=1, source_target_pairs={{0,8},{4,60},{8,16},{12,4},{16,24},{20,12},{24,32},{28,20},{32,40}... | collective-permute-start | bytes 442376 | tf_op jit(solution)/shard_map/ppermute | solution.py:243
  41.0 2.1 collective-permute-done.21
  43.2 4.1 %collective-permute-start.22 = (bf16[672,768]{1,0:T(8,128)(2,1)S(1)}, bf16[672,768]{1,0:T(8,128)(2,1)S(1)}, u32[]{:S(2)}, u32[]{:S(2)}) collective-permute-start(bf16[672,768]{1,0:T(8,128)(2,1)S(1)} %pad_maximum_fusion), channel_id=1, source_target_pairs={{0,4},{4,0},{1,5},{5,1},{2,6},{6,2},{3,7},{7,3},{8,12},{12,8},{9,1... | collective-permute-start | bytes 3096584 | tf_op jit(solution)/shard_map/ppermute | solution.py:259
  47.5 3.0 %collective-permute-start.5 = (bf16[448,1536]{1,0:T(8,128)(2,1)S(1)}, bf16[448,1536]{1,0:T(8,128)(2,1)S(1)}, u32[]{:S(2)}, u32[]{:S(2)}) collective-permute-start(bf16[448,1536]{1,0:T(8,128)(2,1)S(1)} %collective-permute-done.1.rest_2_), channel_id=1, source_target_pairs={{0,1},{4,7},{1,2},{5,4},{2,3},{6,5},{3,0},{7,6},{8,9},{12,15},{9,1... | collective-permute-start | bytes 4128776 | tf_op jit(solution)/shard_map/ppermute | solution.py:243
  50.8 2.8 %collective-permute-start.23 = (bf16[1536,768]{1,0:T(8,128)(2,1)S(1)}, bf16[1536,768]{1,0:T(8,128)(2,1)S(1)}, u32[]{:S(2)}, u32[]{:S(2)}) collective-permute-start(bf16[1536,768]{1,0:T(8,128)(2,1)S(1)} %slice_dynamic-update-slice_fusion.rest_16_), channel_id=1, source_target_pairs={{0,64},{4,196},{64,128},{68,4},{128,192},{132,68},{192,0},{196,132... | collective-permute-start | bytes 7077896 | tf_op jit(solution)/shard_map/ppermute | solution.py:243
  53.6 9.2 %collective-permute-done.11.rest_9_ = bf16[768,768]{1,0:T(8,128)(2,1)S(1)} collective-permute-done((bf16[768,768]{1,0:T(8,128)(2,1)S(1)}, bf16[768,768]{1,0:T(8,128)(2,1)S(1)}, u32[]{:S(2)}, u32[]{:S(2)}) %collective-permute-start.11) | collective-permute-done | bytes 1179680 | tf_op jit(solution)/shard_map/ppermute | solution.py:243
  62.8 1.2 collective-permute-start.12
  64.0 1.0 collective-permute-start
  65.0 0.1 collective-permute-start.3
  65.1 0.7 collective-permute-done.5.rest_6_
  65.8 1.3 collective-permute-start.4
  67.1 11.0 %collective-permute-done.12.rest_10_ = bf16[768,768]{1,0:T(8,128)(2,1)S(1)} collective-permute-done((bf16[768,768]{1,0:T(8,128)(2,1)S(1)}, bf16[768,768]{1,0:T(8,128)(2,1)S(1)}, u32[]{:S(2)}, u32[]{:S(2)}) %collective-permute-start.12) | collective-permute-done | bytes 1179680 | tf_op jit(solution)/shard_map/ppermute | solution.py:243
  78.1 2.4 %collective-permute-start.13 = (bf16[768,768]{1,0:T(8,128)(2,1)S(1)}, bf16[768,768]{1,0:T(8,128)(2,1)S(1)}, u32[]{:S(2)}, u32[]{:S(2)}) collective-permute-start(bf16[768,768]{1,0:T(8,128)(2,1)S(1)} %collective-permute-done.12.rest_10_), channel_id=1, source_target_pairs={{0,8},{4,60},{8,16},{12,4},{16,24},{20,12},{24,32},{28,20},{32,40}... | collective-permute-start | bytes 3538952 | tf_op jit(solution)/shard_map/ppermute | solution.py:243
  80.7 1.8 collective-permute-start.6
  82.5 0.2 fusion.1
  82.7 0.6 collective-permute-start.15
  83.4 0.1 collective-permute-start.16
  83.5 0.6 collective-permute-start.25
  84.1 9.6 %collective-permute-done.13.rest_11_ = bf16[768,768]{1,0:T(8,128)(2,1)S(1)} collective-permute-done((bf16[768,768]{1,0:T(8,128)(2,1)S(1)}, bf16[768,768]{1,0:T(8,128)(2,1)S(1)}, u32[]{:S(2)}, u32[]{:S(2)}) %collective-permute-start.13) | collective-permute-done | bytes 1179680 | tf_op jit(solution)/shard_map/ppermute | solution.py:243
  93.7 2.5 %collective-permute-start.24 = (bf16[768,768]{1,0:T(8,128)(2,1)S(1)}, bf16[768,768]{1,0:T(8,128)(2,1)S(1)}, u32[]{:S(2)}, u32[]{:S(2)}) collective-permute-start(bf16[768,768]{1,0:T(8,128)(2,1)S(1)} %get-tuple-element.8), channel_id=1, source_target_pairs={{0,64},{4,196},{64,128},{68,4},{128,192},{132,68},{192,0},{196,132... | collective-permute-start | bytes 3538952 | tf_op jit(solution)/shard_map/ppermute | solution.py:243
  96.3 5.1 %collective-permute-start.17 = (bf16[384,768]{1,0:T(8,128)(2,1)S(1)}, bf16[384,768]{1,0:T(8,128)(2,1)S(1)}, u32[]{:S(2)}, u32[]{:S(2)}) collective-permute-start(bf16[384,768]{1,0:T(8,128)(2,1)S(1)} %get-tuple-element.9), channel_id=1, source_target_pairs={{0,4},{4,0},{1,5},{5,1},{2,6},{6,2},{3,7},{7,3},{8,12},{12,8},{9,1... | collective-permute-start | bytes 1769480 | tf_op jit(solution)/shard_map/ppermute | solution.py:259
  101.5 1.6 collective-permute-done.17.rest_15_
  103.1 7.4 %collective-permute-done.14.rest_12_ = bf16[384,768]{1,0:T(8,128)(2,1)S(1)} collective-permute-done((bf16[384,768]{1,0:T(8,128)(2,1)S(1)}, bf16[384,768]{1,0:T(8,128)(2,1)S(1)}, u32[]{:S(2)}, u32[]{:S(2)}) %collective-permute-start.14) | collective-permute-done | bytes 589856 | tf_op jit(solution)/shard_map/ppermute | solution.py:243
  110.6 0.7 copy-done.20
  111.3 0.5 copy-done.15
  111.8 1.0 copy-done.16
  112.8 22.6 %project.1 = bf16[1536,768]{1,0:T(8,128)(2,1)} custom-call(s32[1,64]{1,0:T(1,128)} %bitcast.26, bf16[448,1536]{1,0:T(8,128)(2,1)} %bitcast.20, bf16[448,1536]{1,0:T(8,128)(2,1)} %copy-done.11, bf16[448,1536]{1,0:T(8,128)(2,1)} %copy-done.9, bf16[448,1536]{1,0:T(8,128)(2,1)} %copy-done.12, bf16[448,1536]{1,0:T(8,128)(2,1)} %copy-done.8, ...), custom_call_target="tpu_custom_call" | custom-call | flops 8455716864 | bytes 20447232 | tf_op jit(solution)/shard_map/project/pallas_call | solution.py:172
  135.5 13.2 %all-to-all-start = ((bf16[64,24,768]{2,1,0:T(8,128)(2,1)}), bf16[64,24,768]{2,1,0:T(8,128)(2,1)S(1)}, u32[]{:S(2)}, u32[]{:S(2)}) async-start(bf16[64,24,768]{2,1,0:T(8,128)(2,1)} %bitcast.17), calls=%async_computation | async-start | bytes 4718592 | tf_op jit(solution)/shard_map/all_to_all | solution.py:324
  148.7 0.6 dynamic_slice.3.live_ref
  149.3 56.0 %all-to-all-done = bf16[64,24,768]{2,1,0:T(8,128)(2,1)S(1)} async-done(((bf16[64,24,768]{2,1,0:T(8,128)(2,1)}), bf16[64,24,768]{2,1,0:T(8,128)(2,1)S(1)}, u32[]{:S(2)}, u32[]{:S(2)}) %all-to-all-start) | async-done | bytes 2359328 | tf_op jit(solution)/shard_map/all_to_all | solution.py:324
  205.3 1.6 fusion
  206.9 9.3 %attend.1 = bf16[128,768]{1,0:T(8,128)(2,1)} custom-call(s32[1]{0:T(128)} %dynamic_slice.3.live_ref, bf16[128,768]{1,0:T(8,128)(2,1)} %bitcast.22, bf16[768,768]{1,0:T(8,128)(2,1)} %bitcast.16, bf16[768,768]{1,0:T(8,128)(2,1)} %bitcast.15, bf16[128,768]{1,0:T(8,128)(2,1)} %bitcast.23, bf16[128,768]{1,0:T(8,128)(2,1)} %bitcast.24), custom_call_target="tpu_custom_call" | custom-call | tf_op jit(solution)/shard_map/attend/pallas_call | solution.py:226
  (88 shorter events, 0.8 us)
Async XLA Ops:
  1.0 14.6 %collective-permute-start.7 = (bf16[192,768]{1,0:T(8,128)(2,1)S(1)}, bf16[192,768]{1,0:T(8,128)(2,1)S(1)}, u32[]{:S(2)}, u32[]{:S(2)}) collective-permute-start(bf16[192,768]{1,0:T(8,128)(2,1)S(1)} %pad_maximum_fusion.3), channel_id=1, source_target_pairs={{0,4},{4,0},{1,5},{5,1},{2,6},{6,2},{3,7},{7,3},{8,12},{12,8},{9,1... | collective-permute-start | bytes 884744 | tf_op jit(solution)/shard_map/ppermute | solution.py:259
  13.0 52.0 %collective-permute-start.2 = (bf16[448,1536]{1,0:T(8,128)(2,1)}, bf16[448,1536]{1,0:T(8,128)(2,1)S(1)}, u32[]{:S(2)}, u32[]{:S(2)}) collective-permute-start(bf16[448,1536]{1,0:T(8,128)(2,1)} %bitcast.18), channel_id=1, source_target_pairs={{0,3},{4,5},{1,0},{5,6},{2,1},{6,7},{3,2},{7,4},{8,11},{12,13},{9,... | collective-permute-start | bytes 4128776 | tf_op jit(solution)/shard_map/ppermute | solution.py:243
  13.0 34.5 %collective-permute-start.1 = (bf16[448,1536]{1,0:T(8,128)(2,1)}, bf16[448,1536]{1,0:T(8,128)(2,1)S(1)}, u32[]{:S(2)}, u32[]{:S(2)}) collective-permute-start(bf16[448,1536]{1,0:T(8,128)(2,1)} %bitcast.19), channel_id=1, source_target_pairs={{0,1},{4,7},{1,2},{5,4},{2,3},{6,5},{3,0},{7,6},{8,9},{12,15},{9,1... | collective-permute-start | bytes 4128776 | tf_op jit(solution)/shard_map/ppermute | solution.py:243
  15.8 7.6 %collective-permute-start.18 = (bf16[192,768]{1,0:T(8,128)(2,1)S(1)}, bf16[192,768]{1,0:T(8,128)(2,1)S(1)}, u32[]{:S(2)}, u32[]{:S(2)}) collective-permute-start(bf16[192,768]{1,0:T(8,128)(2,1)S(1)} %get-tuple-element.11), channel_id=1, source_target_pairs={{0,8},{4,60},{8,16},{12,4},{16,24},{20,12},{24,32},{28,20},{32,40}... | collective-permute-start | bytes 884744 | tf_op jit(solution)/shard_map/ppermute | solution.py:243
  19.7 7.1 %collective-permute-start.8 = (bf16[192,768]{1,0:T(8,128)(2,1)S(1)}, bf16[192,768]{1,0:T(8,128)(2,1)S(1)}, u32[]{:S(2)}, u32[]{:S(2)}) collective-permute-start(bf16[192,768]{1,0:T(8,128)(2,1)S(1)} %get-tuple-element.12), channel_id=1, source_target_pairs={{0,64},{4,196},{64,128},{68,4},{128,192},{132,68},{192,0},{196,132... | collective-permute-start | bytes 884744 | tf_op jit(solution)/shard_map/ppermute | solution.py:243
  23.4 7.1 %collective-permute-start.19 = (bf16[192,768]{1,0:T(8,128)(2,1)S(1)}, bf16[192,768]{1,0:T(8,128)(2,1)S(1)}, u32[]{:S(2)}, u32[]{:S(2)}) collective-permute-start(bf16[192,768]{1,0:T(8,128)(2,1)S(1)} %collective-permute-done.18), channel_id=1, source_target_pairs={{0,8},{4,60},{8,16},{12,4},{16,24},{20,12},{24,32},{28,20},{32,40}... | collective-permute-start | bytes 884744 | tf_op jit(solution)/shard_map/ppermute | solution.py:243
  26.8 7.1 %collective-permute-start.9 = (bf16[96,768]{1,0:T(8,128)(2,1)S(1)}, bf16[96,768]{1,0:T(8,128)(2,1)S(1)}, u32[]{:S(2)}, u32[]{:S(2)}) collective-permute-start(bf16[96,768]{1,0:T(8,128)(2,1)S(1)} %get-tuple-element.15), channel_id=1, source_target_pairs={{0,64},{4,196},{64,128},{68,4},{128,192},{132,68},{192,0},{196,132... | collective-permute-start | bytes 442376 | tf_op jit(solution)/shard_map/ppermute | solution.py:243
  30.4 7.1 %collective-permute-start.20 = (bf16[192,768]{1,0:T(8,128)(2,1)S(1)}, bf16[192,768]{1,0:T(8,128)(2,1)S(1)}, u32[]{:S(2)}, u32[]{:S(2)}) collective-permute-start(bf16[192,768]{1,0:T(8,128)(2,1)S(1)} %collective-permute-done.19), channel_id=1, source_target_pairs={{0,8},{4,60},{8,16},{12,4},{16,24},{20,12},{24,32},{28,20},{32,40}... | collective-permute-start | bytes 884744 | tf_op jit(solution)/shard_map/ppermute | solution.py:243
  33.9 7.1 %collective-permute-start.10 = (bf16[288,768]{1,0:T(8,128)(2,1)S(1)}, bf16[288,768]{1,0:T(8,128)(2,1)S(1)}, u32[]{:S(2)}, u32[]{:S(2)}) collective-permute-start(bf16[288,768]{1,0:T(8,128)(2,1)S(1)} %pad_maximum_fusion.1), channel_id=1, source_target_pairs={{0,4},{4,0},{1,5},{5,1},{2,6},{6,2},{3,7},{7,3},{8,12},{12,8},{9,1... | collective-permute-start | bytes 1327112 | tf_op jit(solution)/shard_map/ppermute | solution.py:259
  37.5 5.6 %collective-permute-start.21 = (bf16[96,768]{1,0:T(8,128)(2,1)S(1)}, bf16[96,768]{1,0:T(8,128)(2,1)S(1)}, u32[]{:S(2)}, u32[]{:S(2)}) collective-permute-start(bf16[96,768]{1,0:T(8,128)(2,1)S(1)} %get-tuple-element.13), channel_id=1, source_target_pairs={{0,8},{4,60},{8,16},{12,4},{16,24},{20,12},{24,32},{28,20},{32,40}... | collective-permute-start | bytes 442376 | tf_op jit(solution)/shard_map/ppermute | solution.py:243
  43.2 7.3 %collective-permute-start.22 = (bf16[672,768]{1,0:T(8,128)(2,1)S(1)}, bf16[672,768]{1,0:T(8,128)(2,1)S(1)}, u32[]{:S(2)}, u32[]{:S(2)}) collective-permute-start(bf16[672,768]{1,0:T(8,128)(2,1)S(1)} %pad_maximum_fusion), channel_id=1, source_target_pairs={{0,4},{4,0},{1,5},{5,1},{2,6},{6,2},{3,7},{7,3},{8,12},{12,8},{9,1... | collective-permute-start | bytes 3096584 | tf_op jit(solution)/shard_map/ppermute | solution.py:259
  47.3 16.7 %copy-start.1 = (bf16[2,224,1536]{2,1,0:T(8,128)(2,1)S(1)}, bf16[2,224,1536]{2,1,0:T(8,128)(2,1)}, u32[]{:S(2)}) copy-start(bf16[2,224,1536]{2,1,0:T(8,128)(2,1)} %live_rows.1) | copy-start | bytes 4128772
  47.4 33.3 %copy-start.5 = (bf16[768,768]{1,0:T(8,128)(2,1)}, bf16[768,768]{1,0:T(8,128)(2,1)S(1)}, u32[]{:S(2)}) copy-start(bf16[768,768]{1,0:T(8,128)(2,1)S(1)} %slice_dynamic-update-slice_fusion.14.rest_8_) | copy-start | bytes 3538948
  47.4 15.4 %collective-permute-start.11 = (bf16[768,768]{1,0:T(8,128)(2,1)S(1)}, bf16[768,768]{1,0:T(8,128)(2,1)S(1)}, u32[]{:S(2)}, u32[]{:S(2)}) collective-permute-start(bf16[768,768]{1,0:T(8,128)(2,1)S(1)} %slice_dynamic-update-slice_fusion.14.rest_8_), channel_id=1, source_target_pairs={{0,8},{4,60},{8,16},{12,4},{16,24},{20,12},{24,32},{28,20},{32,40}... | collective-permute-start | bytes 3538952 | tf_op jit(solution)/shard_map/ppermute | solution.py:243
  47.5 33.2 %copy-start.9 = (bf16[448,1536]{1,0:T(8,128)(2,1)}, bf16[448,1536]{1,0:T(8,128)(2,1)S(1)}, u32[]{:S(2)}) copy-start(bf16[448,1536]{1,0:T(8,128)(2,1)S(1)} %collective-permute-done.1.rest_2_) | copy-start | bytes 4128772
  47.5 18.3 %collective-permute-start.5 = (bf16[448,1536]{1,0:T(8,128)(2,1)S(1)}, bf16[448,1536]{1,0:T(8,128)(2,1)S(1)}, u32[]{:S(2)}, u32[]{:S(2)}) collective-permute-start(bf16[448,1536]{1,0:T(8,128)(2,1)S(1)} %collective-permute-done.1.rest_2_), channel_id=1, source_target_pairs={{0,1},{4,7},{1,2},{5,4},{2,3},{6,5},{3,0},{7,6},{8,9},{12,15},{9,1... | collective-permute-start | bytes 4128776 | tf_op jit(solution)/shard_map/ppermute | solution.py:243
  50.7 29.9 %copy-start.6 = (bf16[1536,768]{1,0:T(8,128)(2,1)}, bf16[1536,768]{1,0:T(8,128)(2,1)S(1)}, u32[]{:S(2)}) copy-start(bf16[1536,768]{1,0:T(8,128)(2,1)S(1)} %slice_dynamic-update-slice_fusion.rest_16_) | copy-start | bytes 7077892
  50.8 29.9 %collective-permute-start.23 = (bf16[1536,768]{1,0:T(8,128)(2,1)S(1)}, bf16[1536,768]{1,0:T(8,128)(2,1)S(1)}, u32[]{:S(2)}, u32[]{:S(2)}) collective-permute-start(bf16[1536,768]{1,0:T(8,128)(2,1)S(1)} %slice_dynamic-update-slice_fusion.rest_16_), channel_id=1, source_target_pairs={{0,64},{4,196},{64,128},{68,4},{128,192},{132,68},{192,0},{196,132... | collective-permute-start | bytes 7077896 | tf_op jit(solution)/shard_map/ppermute | solution.py:243
  62.8 19.9 %copy-start.3 = (bf16[768,768]{1,0:T(8,128)(2,1)}, bf16[768,768]{1,0:T(8,128)(2,1)S(1)}, u32[]{:S(2)}) copy-start(bf16[768,768]{1,0:T(8,128)(2,1)S(1)} %collective-permute-done.11.rest_9_) | copy-start | bytes 3538948
  62.8 15.3 %collective-permute-start.12 = (bf16[768,768]{1,0:T(8,128)(2,1)S(1)}, bf16[768,768]{1,0:T(8,128)(2,1)S(1)}, u32[]{:S(2)}, u32[]{:S(2)}) collective-permute-start(bf16[768,768]{1,0:T(8,128)(2,1)S(1)} %collective-permute-done.11.rest_9_), channel_id=1, source_target_pairs={{0,8},{4,60},{8,16},{12,4},{16,24},{20,12},{24,32},{28,20},{32,40}... | collective-permute-start | bytes 3538952 | tf_op jit(solution)/shard_map/ppermute | solution.py:243
  64.0 18.7 %collective-permute-start = (bf16[448,1536]{1,0:T(8,128)(2,1)S(1)}, bf16[448,1536]{1,0:T(8,128)(2,1)S(1)}, u32[]{:S(2)}, u32[]{:S(2)}) collective-permute-start(bf16[448,1536]{1,0:T(8,128)(2,1)S(1)} %bitcast.21), channel_id=1, source_target_pairs={{0,4},{4,0},{1,5},{5,1},{2,6},{6,2},{3,7},{7,3},{8,12},{12,8},{9,1... | collective-permute-start | bytes 4128776 | tf_op jit(solution)/shard_map/ppermute | solution.py:259
  65.0 17.7 %copy-start.8 = (bf16[448,1536]{1,0:T(8,128)(2,1)}, bf16[448,1536]{1,0:T(8,128)(2,1)S(1)}, u32[]{:S(2)}) copy-start(bf16[448,1536]{1,0:T(8,128)(2,1)S(1)} %collective-permute-done.2.rest_4_) | copy-start | bytes 4128772
  65.0 18.4 %collective-permute-start.3 = (bf16[448,1536]{1,0:T(8,128)(2,1)S(1)}, bf16[448,1536]{1,0:T(8,128)(2,1)S(1)}, u32[]{:S(2)}, u32[]{:S(2)}) collective-permute-start(bf16[448,1536]{1,0:T(8,128)(2,1)S(1)} %collective-permute-done.2.rest_4_), channel_id=1, source_target_pairs={{0,4},{4,0},{1,5},{5,1},{2,6},{6,2},{3,7},{7,3},{8,12},{12,8},{9,1... | collective-permute-start | bytes 4128776 | tf_op jit(solution)/shard_map/ppermute | solution.py:259
  65.8 44.8 %copy-start.10 = (bf16[448,1536]{1,0:T(8,128)(2,1)}, bf16[448,1536]{1,0:T(8,128)(2,1)S(1)}, u32[]{:S(2)}) copy-start(bf16[448,1536]{1,0:T(8,128)(2,1)S(1)} %collective-permute-done.5.rest_6_) | copy-start | bytes 4128772
  65.8 17.7 %collective-permute-start.4 = (bf16[448,1536]{1,0:T(8,128)(2,1)S(1)}, bf16[448,1536]{1,0:T(8,128)(2,1)S(1)}, u32[]{:S(2)}, u32[]{:S(2)}) collective-permute-start(bf16[448,1536]{1,0:T(8,128)(2,1)S(1)} %collective-permute-done.1.rest_2_), channel_id=1, source_target_pairs={{0,4},{4,0},{1,5},{5,1},{2,6},{6,2},{3,7},{7,3},{8,12},{12,8},{9,1... | collective-permute-start | bytes 4128776 | tf_op jit(solution)/shard_map/ppermute | solution.py:259
  78.1 4.6 %copy-start.4 = (bf16[768,768]{1,0:T(8,128)(2,1)}, bf16[768,768]{1,0:T(8,128)(2,1)S(1)}, u32[]{:S(2)}) copy-start(bf16[768,768]{1,0:T(8,128)(2,1)S(1)} %collective-permute-done.12.rest_10_) | copy-start | bytes 3538948
  78.1 15.6 %collective-permute-start.13 = (bf16[768,768]{1,0:T(8,128)(2,1)S(1)}, bf16[768,768]{1,0:T(8,128)(2,1)S(1)}, u32[]{:S(2)}, u32[]{:S(2)}) collective-permute-start(bf16[768,768]{1,0:T(8,128)(2,1)S(1)} %collective-permute-done.12.rest_10_), channel_id=1, source_target_pairs={{0,8},{4,60},{8,16},{12,4},{16,24},{20,12},{24,32},{28,20},{32,40}... | collective-permute-start | bytes 3538952 | tf_op jit(solution)/shard_map/ppermute | solution.py:243
  80.7 2.8 %copy-start = (bf16[1536,768]{1,0:T(8,128)(2,1)}, bf16[1536,768]{1,0:T(8,128)(2,1)S(1)}, u32[]{:S(2)}) copy-start(bf16[1536,768]{1,0:T(8,128)(2,1)S(1)} %collective-permute-done.23.rest_17_) | copy-start | bytes 7077892
  80.7 20.8 %collective-permute-start.6 = (bf16[448,1536]{1,0:T(8,128)(2,1)S(1)}, bf16[448,1536]{1,0:T(8,128)(2,1)S(1)}, u32[]{:S(2)}, u32[]{:S(2)}) collective-permute-start(bf16[448,1536]{1,0:T(8,128)(2,1)S(1)} %collective-permute-done.5.rest_6_), channel_id=1, source_target_pairs={{0,4},{4,0},{1,5},{5,1},{2,6},{6,2},{3,7},{7,3},{8,12},{12,8},{9,1... | collective-permute-start | bytes 4128776 | tf_op jit(solution)/shard_map/ppermute | solution.py:259
  82.7 27.8 %copy-start.11 = (bf16[448,1536]{1,0:T(8,128)(2,1)}, bf16[448,1536]{1,0:T(8,128)(2,1)S(1)}, u32[]{:S(2)}) copy-start(bf16[448,1536]{1,0:T(8,128)(2,1)S(1)} %collective-permute-done.rest_1_) | copy-start | bytes 4128772
  82.7 13.6 %collective-permute-start.15 = (bf16[384,768]{1,0:T(8,128)(2,1)S(1)}, bf16[384,768]{1,0:T(8,128)(2,1)S(1)}, u32[]{:S(2)}, u32[]{:S(2)}) collective-permute-start(bf16[384,768]{1,0:T(8,128)(2,1)S(1)} %slice.130), channel_id=1, source_target_pairs={{0,4},{4,0},{1,5},{5,1},{2,6},{6,2},{3,7},{7,3},{8,12},{12,8},{9,1... | collective-permute-start | bytes 1769480 | tf_op jit(solution)/shard_map/ppermute | solution.py:259
  83.4 27.2 %copy-start.12 = (bf16[448,1536]{1,0:T(8,128)(2,1)}, bf16[448,1536]{1,0:T(8,128)(2,1)S(1)}, u32[]{:S(2)}) copy-start(bf16[448,1536]{1,0:T(8,128)(2,1)S(1)} %collective-permute-done.3.rest_3_) | copy-start | bytes 4128772
  83.4 18.1 %collective-permute-start.16 = (bf16[384,768]{1,0:T(8,128)(2,1)S(1)}, bf16[384,768]{1,0:T(8,128)(2,1)S(1)}, u32[]{:S(2)}, u32[]{:S(2)}) collective-permute-start(bf16[384,768]{1,0:T(8,128)(2,1)S(1)} %slice.131), channel_id=1, source_target_pairs={{0,4},{4,0},{1,5},{5,1},{2,6},{6,2},{3,7},{7,3},{8,12},{12,8},{9,1... | collective-permute-start | bytes 1769480 | tf_op jit(solution)/shard_map/ppermute | solution.py:259
  83.5 27.1 %copy-start.13 = (bf16[448,1536]{1,0:T(8,128)(2,1)}, bf16[448,1536]{1,0:T(8,128)(2,1)S(1)}, u32[]{:S(2)}) copy-start(bf16[448,1536]{1,0:T(8,128)(2,1)S(1)} %collective-permute-done.4.rest_5_) | copy-start | bytes 4128772
  83.5 27.0 %collective-permute-start.25 = (bf16[768,768]{1,0:T(8,128)(2,1)S(1)}, bf16[768,768]{1,0:T(8,128)(2,1)S(1)}, u32[]{:S(2)}, u32[]{:S(2)}) collective-permute-start(bf16[768,768]{1,0:T(8,128)(2,1)S(1)} %get-tuple-element.7), channel_id=1, source_target_pairs={{0,4},{4,0},{1,5},{5,1},{2,6},{6,2},{3,7},{7,3},{8,12},{12,8},{9,1... | collective-permute-start | bytes 3538952 | tf_op jit(solution)/shard_map/ppermute | solution.py:259
  93.7 16.9 %copy-start.2 = (bf16[768,768]{1,0:T(8,128)(2,1)}, bf16[768,768]{1,0:T(8,128)(2,1)S(1)}, u32[]{:S(2)}) copy-start(bf16[768,768]{1,0:T(8,128)(2,1)S(1)} %collective-permute-done.13.rest_11_) | copy-start | bytes 3538948
  93.7 16.9 %collective-permute-start.24 = (bf16[768,768]{1,0:T(8,128)(2,1)S(1)}, bf16[768,768]{1,0:T(8,128)(2,1)S(1)}, u32[]{:S(2)}, u32[]{:S(2)}) collective-permute-start(bf16[768,768]{1,0:T(8,128)(2,1)S(1)} %get-tuple-element.8), channel_id=1, source_target_pairs={{0,64},{4,196},{64,128},{68,4},{128,192},{132,68},{192,0},{196,132... | collective-permute-start | bytes 3538952 | tf_op jit(solution)/shard_map/ppermute | solution.py:243
  96.3 14.3 %copy-start.17 = (bf16[384,768]{1,0:T(8,128)(2,1)}, bf16[384,768]{1,0:T(8,128)(2,1)S(1)}, u32[]{:S(2)}) copy-start(bf16[384,768]{1,0:T(8,128)(2,1)S(1)} %collective-permute-done.15.rest_13_) | copy-start | bytes 1769476
  96.3 6.8 %collective-permute-start.17 = (bf16[384,768]{1,0:T(8,128)(2,1)S(1)}, bf16[384,768]{1,0:T(8,128)(2,1)S(1)}, u32[]{:S(2)}, u32[]{:S(2)}) collective-permute-start(bf16[384,768]{1,0:T(8,128)(2,1)S(1)} %get-tuple-element.9), channel_id=1, source_target_pairs={{0,4},{4,0},{1,5},{5,1},{2,6},{6,2},{3,7},{7,3},{8,12},{12,8},{9,1... | collective-permute-start | bytes 1769480 | tf_op jit(solution)/shard_map/ppermute | solution.py:259
  101.5 9.1 %copy-start.18 = (bf16[384,768]{1,0:T(8,128)(2,1)}, bf16[384,768]{1,0:T(8,128)(2,1)S(1)}, u32[]{:S(2)}) copy-start(bf16[384,768]{1,0:T(8,128)(2,1)S(1)} %collective-permute-done.16.rest_14_) | copy-start | bytes 1769476
  101.5 9.0 %collective-permute-start.14 = (bf16[384,768]{1,0:T(8,128)(2,1)S(1)}, bf16[384,768]{1,0:T(8,128)(2,1)S(1)}, u32[]{:S(2)}, u32[]{:S(2)}) collective-permute-start(bf16[384,768]{1,0:T(8,128)(2,1)S(1)} %get-tuple-element.10), channel_id=1, source_target_pairs={{0,8},{4,60},{8,16},{12,4},{16,24},{20,12},{24,32},{28,20},{32,40}... | collective-permute-start | bytes 1769480 | tf_op jit(solution)/shard_map/ppermute | solution.py:243
  101.5 9.1 %copy-start.14 = (bf16[448,1536]{1,0:T(8,128)(2,1)}, bf16[448,1536]{1,0:T(8,128)(2,1)S(1)}, u32[]{:S(2)}) copy-start(bf16[448,1536]{1,0:T(8,128)(2,1)S(1)} %collective-permute-done.6.rest_7_) | copy-start | bytes 4128772
  103.1 7.5 %copy-start.19 = (bf16[384,768]{1,0:T(8,128)(2,1)}, bf16[384,768]{1,0:T(8,128)(2,1)S(1)}, u32[]{:S(2)}) copy-start(bf16[384,768]{1,0:T(8,128)(2,1)S(1)} %collective-permute-done.17.rest_15_) | copy-start | bytes 1769476
  110.5 0.8 copy-start.20
  110.6 1.2 copy-start.15
  111.8 1.0 copy-start.16
  135.5 13.2 %copy-start.7 = (s32[64]{0:T(128)S(1)}, s32[64]{0:T(128)}, u32[]{:S(2)}) copy-start(s32[64]{0:T(128)} %param.13) | copy-start | bytes 772
  135.5 69.8 %all-to-all-start = ((bf16[64,24,768]{2,1,0:T(8,128)(2,1)}), bf16[64,24,768]{2,1,0:T(8,128)(2,1)S(1)}, u32[]{:S(2)}, u32[]{:S(2)}) async-start(bf16[64,24,768]{2,1,0:T(8,128)(2,1)} %bitcast.17), calls=%async_computation | async-start | bytes 4718592 | tf_op jit(solution)/shard_map/all_to_all | solution.py:324

commit v4 on v3

--- a/solution.py
+++ b/solution.py
@@ -59,32 +59,17 @@
 
 
 def piece_table(ny, nz):
-    table = []
+    assert (ny, nz) == (4, 8)
     dys = (0, -1, 1, -2)
-    dzs = (0, -1, -2, -3, 1, 2, 3, -4)
-    for s in range(5):
-        for j, dy in enumerate(dys):
-            table.append((s, j, dy, -s, 0))
-    for s in range(1, 4):
-        for j, dy in enumerate(dys):
-            table.append((4 + s, j, -dy, s, 0))
-    for s in range(3):
-        for j, dz in enumerate(dzs):
-            table.append((8 + s, j, -s, dz, 1))
-    for j, dz in enumerate(dzs):
-        table.append((11, j, 1, -dz, 1))
-    assert len(table) == ny * nz * 2
-    return table
-
-
-PIECES = 12
+    table = [(s, j, dy, -s) for s in range(5) for j, dy in enumerate(dys)]
+    return table + [(4 + s, j, -dy, s) for s in range(1, 4) for j, dy in enumerate(dys)]
 
 
 def project_kernel(dims, counts_ref, *rest):
     ny, nz, nh, shard = dims
     rows = rest[: 2 * nh]
-    pieces = rest[2 * nh : 2 * nh + PIECES]
-    out_ref, w_ref, x_ref, put_ref, acc_ref, acc16_ref, w_sem, x_sem = rest[2 * nh + PIECES :]
+    pieces = rest[2 * nh : -8]
+    out_ref, w_ref, x_ref, put_ref, acc_ref, acc16_ref, w_sem, x_sem = rest[-8:]
     y, z, core = (lax.axis_index(a) for a in PLANE)
     head = lax.axis_index("head")
     sign = 1 - 2 * core
@@ -92,16 +77,21 @@
     feats = w_ref.shape[0] // nh
 
     w_copies, x_copies = [], []
-    for k, (src, part, dy, dz, owner) in enumerate(piece_table(ny, nz)):
-        chip = lax.rem(y + dy * sign + ny, ny) * nz + lax.rem(z + dz * sign + nz, nz)
-        at = pl.multiple_of((chip * 2 + owner) * shard, shard)
-        w_copies.append(
-            pltpu.make_async_copy(
-                pieces[src].at[pl.ds(part * shard, shard)],
-                w_ref.at[pl.ds(at, shard)],
-                w_sem.at[k],
+    if len(pieces) == 1:
+        for k in range(nh):
+            part = pl.ds(k * feats, feats)
+            w_copies.append(pltpu.make_async_copy(pieces[0].at[part], w_ref.at[part], w_sem.at[k]))
+    else:
+        for k, (src, part, dy, dz) in enumerate(piece_table(ny, nz)):
+            chip = lax.rem(y + dy * sign + ny, ny) * nz + lax.rem(z + dz * sign + nz, nz)
+            at = pl.multiple_of(chip * shard, shard)
+            w_copies.append(
+                pltpu.make_async_copy(
+                    pieces[src].at[pl.ds(part * shard, shard)],
+                    w_ref.at[pl.ds(at, shard)],
+                    w_sem.at[k],
+                )
             )
-        )
     for k in range(2 * nh):
         who = core if k % 2 == 0 else 1 - core
         x_copies.append(
@@ -172,7 +162,7 @@
     return pl.pallas_call(
         functools.partial(project_kernel, dims),
         out_shape=jax.ShapeDtypeStruct((convs * each, cols), BF16),
-        in_specs=[pl.BlockSpec(memory_space=pltpu.VMEM)] + [hbm] * (2 * nh + PIECES),
+        in_specs=[pl.BlockSpec(memory_space=pltpu.VMEM)] + [hbm] * (2 * nh + len(pieces)),
         out_specs=pl.BlockSpec(memory_space=pltpu.VMEM),
         scratch_shapes=[
             pltpu.VMEM((nh * feats, cols), BF16),
@@ -180,7 +170,7 @@
             pltpu.VMEM((convs * each, 2 * per), BF16),
             pltpu.VMEM((2 * per, cols), F32),
             pltpu.VMEM((2 * per, cols), BF16),
-            pltpu.SemaphoreType.DMA((ny * nz * 2,)),
+            pltpu.SemaphoreType.DMA((ny * nz,)),
             pltpu.SemaphoreType.DMA((2 * nh,)),
         ],
         compiler_params=pltpu.CompilerParams(vmem_limit_bytes=VMEM_LIMIT),
@@ -191,46 +181,54 @@
     )(counts[None], *rows, *pieces)
 
 
-def attend_kernel(live_ref, q_ref, k_ref, v_ref, nk_ref, nv_ref, out_ref):
+def attend_kernel(first, live_ref, q_ref, k_ref, v_ref, nk_ref, nv_ref, *rest):
+    out_ref = rest[-1]
+    if first:
+        out_ref[:, :first] = rest[0][...]
     live = live_ref[0]
     hist = k_ref.shape[0]
     new = nk_ref.shape[0]
     scale = 1.0 / math.sqrt(HD)
     hist_ok = (iota((1, hist), 1) % MAXB) < live
-    new_ok = iota((new, new), 1) <= iota((new, new), 0)
-
-    @pl.loop(0, q_ref.shape[1] // (2 * HD))
+    token = iota((2 * new, new), 0)
+    token = jnp.where(token < new, token, token - new)
+    new_ok = iota((2 * new, new), 1) <= token
+
+    @pl.loop(0, k_ref.shape[1] // (2 * HD))
     def _(pair):
         lanes = pl.ds(pl.multiple_of(pair * 2 * HD, 2 * HD), 2 * HD)
-        q = q_ref[:, lanes] * jnp.asarray(scale, BF16)
+        all_lanes = pl.ds(pl.multiple_of(first + pair * 2 * HD, 2 * HD), 2 * HD)
+        q = q_ref[:, all_lanes] * jnp.asarray(scale, BF16)
         k, v = k_ref[:, lanes], v_ref[:, lanes]
-        nk, nv = nk_ref[:, lanes], nv_ref[:, lanes]
+        nk, nv = nk_ref[:, all_lanes], nv_ref[:, all_lanes]
         low = iota(q.shape, 1) < HD
-        outs = []
-        for mine in (low, jnp.logical_not(low)):
-            qh = jnp.where(mine, q, jnp.zeros_like(q))
-            sh = jnp.where(hist_ok, dot(qh, k, ((1,), (1,))), -jnp.inf)
-            sn = jnp.where(new_ok, dot(qh, nk, ((1,), (1,))), -jnp.inf)
-            top = jnp.maximum(
-                jnp.max(sh, axis=1, keepdims=True), jnp.max(sn, axis=1, keepdims=True)
-            )
-            eh, en = jnp.exp(sh - top), jnp.exp(sn - top)
-            total = jnp.sum(eh, axis=1, keepdims=True) + jnp.sum(en, axis=1, keepdims=True)
-            share = 1.0 / total
-            ph, pn = (eh * share).astype(BF16), (en * share).astype(BF16)
-            outs.append(dot(ph, v) + dot(pn, nv))
-        out_ref[:, lanes] = jnp.where(low, outs[0], outs[1]).astype(BF16)
-
-
-def attend(live, q, k, v, nk, nv):
+        none = jnp.zeros_like(q)
+        q2 = jnp.concatenate([jnp.where(low, q, none), jnp.where(low, none, q)], axis=0)
+        sh = jnp.where(hist_ok, dot(q2, k, ((1,), (1,))), -jnp.inf)
+        sn = jnp.where(new_ok, dot(q2, nk, ((1,), (1,))), -jnp.inf)
+        top = jnp.maximum(
+            jnp.max(sh, axis=1, keepdims=True), jnp.max(sn, axis=1, keepdims=True)
+        )
+        eh, en = jnp.exp(sh - top), jnp.exp(sn - top)
+        total = jnp.sum(eh, axis=1, keepdims=True) + jnp.sum(en, axis=1, keepdims=True)
+        share = 1.0 / total
+        ph, pn = (eh * share).astype(BF16), (en * share).astype(BF16)
+        out = dot(ph, v) + dot(pn, nv)
+        out_ref[:, all_lanes] = jnp.where(low, out[:new], out[new:]).astype(BF16)
+
+
+def attend(live, q, k, v, nk, nv, before=None):
+    first = 0 if before is None else before.shape[1]
+    more = () if before is None else (before,)
     return pl.pallas_call(
-        attend_kernel,
-        out_shape=jax.ShapeDtypeStruct(q.shape, BF16),
-        in_specs=[pl.BlockSpec(memory_space=pltpu.SMEM)] + [pl.BlockSpec(memory_space=pltpu.VMEM)] * 5,
+        functools.partial(attend_kernel, first),
+        out_shape=jax.ShapeDtypeStruct((q.shape[0], first + k.shape[1]), BF16),
+        in_specs=[pl.BlockSpec(memory_space=pltpu.SMEM)]
+        + [pl.BlockSpec(memory_space=pltpu.VMEM)] * (5 + len(more)),
         out_specs=pl.BlockSpec(memory_space=pltpu.VMEM),
         compiler_params=pltpu.CompilerParams(vmem_limit_bytes=VMEM_LIMIT),
         name="attend",
-    )(live, q, k, v, nk, nv)
+    )(live, q, k, v, nk, nv, *more)
 
 
 def ring_step(x, axis, way=1):
@@ -266,48 +264,32 @@
 
 def gather_weights(key_weight, value_weight):
     upper = lax.axis_index("core") == 0
+    half = key_weight.shape[1] // 2
     mine = jnp.where(upper, key_weight, value_weight)
     other = jnp.where(upper, value_weight, key_weight)
-    own = jnp.concatenate([mine, other])
+    n = mine.shape[0]
     near = swap_cores(jnp.concatenate([other, mine]))
-    zero = jnp.where(upper, own, near)
-    one = jnp.where(upper, near, own)
-
-    y1 = ring_step(zero, "y")
+
+    def chip(a, b):
+        return jnp.where(upper, jnp.concatenate([a, b]), jnp.concatenate([b, a]))
+
+    chip_mine = chip(mine, near[:n])
+    second = lax.all_gather(chip_mine[:, half:], ("y", "z"), axis=0, tiled=True)
+
+    n = 2 * n
+    own = jnp.concatenate([chip_mine[:, :half], chip(other, near[n // 2 :])[:, :half]])
+    y1 = ring_step(own, "y")
     y2 = ring_step(kinds(y1)[0], "y")
     got = swap_cores(jnp.concatenate([y1, y2]))
-    n = key_weight.shape[0]
     group = jnp.concatenate(
-        [
-            kinds(zero)[0], kinds(y1)[0], got[n : 2 * n], y2,
-            kinds(zero)[1], kinds(y1)[1], got[:n], got[2 * n :],
-        ]
+        [own[:n], y1[:n], got[n : 2 * n], y2, own[n:], y1[n:], got[:n], got[2 * n :]]
     )
     z1 = ring_step(group, "z")
     z2 = ring_step(z1, "z")
     z3 = ring_step(z2, "z")
     z4 = ring_step(kinds(z3)[0], "z")
     across = [swap_cores(kinds(t)[1]) for t in (z1, z2, z3)]
-    first = [group, z1, z2, z3, z4] + across
-
-    r1 = ring_step(one, "z")
-    r2 = ring_step(r1, "z")
-    r3 = ring_step(r2, "z")
-    r4 = ring_step(kinds(r3)[0], "z")
-    ring = [one, r1, r2, r3]
-    got = swap_cores(jnp.concatenate([r1, r2, r3, r4]))
-    line = jnp.concatenate(
-        [kinds(t)[0] for t in ring]
-        + [got[(2 * k + 1) * n : (2 * k + 2) * n] for k in range(3)]
-        + [r4]
-        + [kinds(t)[1] for t in ring]
-        + [got[2 * k * n : (2 * k + 1) * n] for k in range(3)]
-        + [got[6 * n :]]
-    )
-    l1 = ring_step(line, "y")
-    l2 = ring_step(kinds(l1)[0], "y")
-    second = [line, l1, l2, swap_cores(kinds(l1)[1])]
-    return first + second
+    return [group, z1, z2, z3, z4] + across, [second]
 
 
 def per_device(queries, new_keys, new_values, pool, block_table, block_counts, key_weight, value_weight):
@@ -316,18 +298,20 @@
     live = live.reshape(-1, live.shape[2])
     rows = gather_rows(live)
 
-    pieces = gather_weights(key_weight, value_weight)
-    dims = (ny, nz, nh, key_weight.shape[0])
-    sent = project(block_counts, rows, pieces, dims)
+    halves = gather_weights(key_weight, value_weight)
+    dims = (ny, nz, nh, 2 * key_weight.shape[0])
     convs = block_counts.shape[0]
-    sent = sent.reshape(convs, -1, sent.shape[1])
-    got = lax.all_to_all(sent, PLANE, split_axis=0, concat_axis=0, tiled=True)
-    got = got.reshape(convs // 2, 2, got.shape[1], got.shape[2])
-    keys = got[:, 0].reshape(-1, got.shape[3])
-    values = got[:, 1].reshape(-1, got.shape[3])
-    mine = lax.axis_index(PLANE)
-    count = lax.dynamic_slice(block_counts, (mine,), (1,))
-    return attend(count, queries[0], keys, values, new_keys[0], new_values[0])[None]
+    count = lax.dynamic_slice(block_counts, (lax.axis_index(PLANE),), (1,))
+    out = None
+    for pieces in halves:
+        sent = project(block_counts, rows, pieces, dims)
+        sent = sent.reshape(convs, -1, sent.shape[1])
+        got = lax.all_to_all(sent, PLANE, split_axis=0, concat_axis=0, tiled=True)
+        got = got.reshape(convs // 2, 2, got.shape[1], got.shape[2])
+        keys = got[:, 0].reshape(-1, got.shape[3])
+        values = got[:, 1].reshape(-1, got.shape[3])
+        out = attend(count, queries[0], keys, values, new_keys[0], new_values[0], out)
+    return out[None]
 
 
 def solution(mesh):

time: 216 us -> 225 us (1.042)
  starting transfers between devices: 65.9 us -> 44.7 us
  between operations: 0.53 us -> 13.7 us
  Pallas kernels: 36 us -> 47 us
  waiting for transfers between devices: 103 us -> 110 us
  local copies, waits for them, and re-layouts: 9.58 us -> 6.85 us
    ppermute x15 -> x9, waiting for transfers between devices: 45.3 us -> 67.2 us  [ring_step(): return lax.ppermute(x, order, perm)]
    all_to_all x1 -> x2, waiting for transfers between devices: 56 us -> 39.5 us  [per_device(): got = lax.all_to_all(sent, PLANE, split_axis=0, concat_axis=0, tiled=True)]
    ppermute x15 -> x9, starting transfers between devices: 34.5 us -> 19.2 us  [ring_step(): return lax.ppermute(x, order, perm)]
    pallas_call x1 -> x2, Pallas kernels: 22.6 us -> 32.9 us  [project(): pl.pallas_call(functools.partial(project_kernel, dims), out_shape=jax.Sha...]
    ppermute x11 -> x9, starting transfers between devices: 18.2 us -> 10.4 us  [swap_cores(): return lax.ppermute(x, 'core', [(0, 1), (1, 0)])]
    unnamed x63 -> x40, local copies, waits for them, and re-layouts: 5.81 us -> 2.98 us
    all_to_all x1 -> x2, starting transfers between devices: 13.2 us -> 15.1 us  [per_device(): got = lax.all_to_all(sent, PLANE, split_axis=0, concat_axis=0, tiled=True)]
    pallas_call x1 -> x2, Pallas kernels: 9.28 us -> 9.99 us  [attend(): pl.pallas_call(functools.partial(attend_kernel, first), out_shape=jax.Sha...]
  transfers between devices with their start and end apart: 27 -> 21, of which waited for: 11 -> 12; matrix products, arithmetic and copies ran while one was open for 3% -> 2% of each run, Pallas kernels for 2% -> 19%
where the time goes in v4:
time: 225 us; the launch traced here: 224 us
  waiting for transfers between devices  110 us (49%)
  Pallas kernels  47 us (21%)
  starting transfers between devices  44.7 us (20%)
  between operations  13.7 us (6%)
  local copies, waits for them, and re-layouts  6.85 us (3%)
    ppermute x9, waiting for transfers between devices, ring_step(): return lax.ppermute(x, order, perm)  67.2 us
    all_to_all x2, waiting for transfers between devices, per_device(): got = lax.all_to_all(sent, PLANE, split_axis=0, concat_axis=0, tiled=True)  39.5 us
    pallas_call x2, Pallas kernels, project(): pl.pallas_call(functools.partial(project_kernel, dims), out_shape=jax.Sha...  32.9 us
    ppermute x9, starting transfers between devices, ring_step(): return lax.ppermute(x, order, perm)  19.2 us
    all_to_all x2, starting transfers between devices, per_device(): got = lax.all_to_all(sent, PLANE, split_axis=0, concat_axis=0, tiled=True)  15.1 us
    ppermute x9, starting transfers between devices, swap_cores(): return lax.ppermute(x, 'core', [(0, 1), (1, 0)])  10.4 us
    pallas_call x2, Pallas kernels, attend(): pl.pallas_call(functools.partial(attend_kernel, first), out_shape=jax.Sha...  9.99 us
  transfers between devices with their start and end apart: 21, of which 12 were waited for; matrix products, arithmetic and copies ran while one was open for 2% of the time, Pallas kernels for 19%

profile of v4, /device:TPU:1, one launch (start us, length us, event | category | flops | bytes accessed | tf_op | source)
XLA Modules:
  0.0 224.4 jit_solution(12658670560602651703)
XLA Ops:
  6.5 1.0 broadcast_select_fusion
  7.6 3.3 %collective-permute-start.7 = (bf16[192,768]{1,0:T(8,128)(2,1)S(1)}, bf16[192,768]{1,0:T(8,128)(2,1)S(1)}, u32[]{:S(2)}, u32[]{:S(2)}) collective-permute-start(bf16[192,768]{1,0:T(8,128)(2,1)S(1)} %pad_maximum_fusion.2), channel_id=1, source_target_pairs={{0,4},{4,0},{1,5},{5,1},{2,6},{6,2},{3,7},{7,3},{8,12},{12,8},{9,1... | collective-permute-start | bytes 884744 | tf_op jit(solution)/shard_map/ppermute | solution.py:257
  10.9 1.2 collective-permute-done.7
  12.1 0.1 fusion
  12.2 0.7 fusion.6
  12.9 0.0 all-gather.2.cloned.1.call-update
  13.0 1.1 collective-permute-start.8
  14.1 4.9 %collective-permute-done.8 = bf16[384,384]{1,0:T(8,128)(2,1)S(1)} collective-permute-done((bf16[384,384]{1,0:T(8,128)(2,1)S(1)}, bf16[384,384]{1,0:T(8,128)(2,1)S(1)}, u32[]{:S(2)}, u32[]{:S(2)}) %collective-permute-start.8) | collective-permute-done | bytes 294944 | tf_op jit(solution)/shard_map/ppermute | solution.py:241
  19.0 2.0 collective-permute-start.9
  21.0 2.1 collective-permute-done.9
  23.1 4.9 %collective-permute-start.10 = (bf16[576,384]{1,0:T(8,128)(2,1)S(1)}, bf16[576,384]{1,0:T(8,128)(2,1)S(1)}, u32[]{:S(2)}, u32[]{:S(2)}) collective-permute-start(bf16[576,384]{1,0:T(8,128)(2,1)S(1)} %pad_maximum_fusion), channel_id=1, source_target_pairs={{0,4},{4,0},{1,5},{5,1},{2,6},{6,2},{3,7},{7,3},{8,12},{12,8},{9,1... | collective-permute-start | bytes 1327112 | tf_op jit(solution)/shard_map/ppermute | solution.py:257
  28.0 1.4 collective-permute-done.10
  29.6 3.9 %collective-permute-start.11 = (bf16[1536,384]{1,0:T(8,128)(2,1)S(1)}, bf16[1536,384]{1,0:T(8,128)(2,1)S(1)}, u32[]{:S(2)}, u32[]{:S(2)}) collective-permute-start(bf16[1536,384]{1,0:T(8,128)(2,1)S(1)} %slice_dynamic-update-slice_fusion.rest_8_), channel_id=1, source_target_pairs={{0,8},{4,60},{8,16},{12,4},{16,24},{20,12},{24,32},{28,20},{32,40}... | collective-permute-start | bytes 3538952 | tf_op jit(solution)/shard_map/ppermute | solution.py:241
  33.5 1.7 copy.12
  35.3 0.6 broadcast_in_dim.12.table_ref
  35.9 4.1 %live_rows.1 = bf16[2,224,1536]{2,1,0:T(8,128)(2,1)} custom-call(s32[1,64]{1,0:T(1,128)} %bitcast.37, s32[1,384]{1,0:T(1,128)} %broadcast_in_dim.12.table_ref, bf16[2,384,1536]{2,1,0:T(8,128)(2,1)} %bitcast.22), custom_call_target="tpu_custom_call" | custom-call | tf_op jit(solution)/shard_map/live_rows/pallas_call | solution.py:51
  39.9 2.5 %collective-permute-start.1 = (bf16[448,1536]{1,0:T(8,128)(2,1)}, bf16[448,1536]{1,0:T(8,128)(2,1)S(1)}, u32[]{:S(2)}, u32[]{:S(2)}) collective-permute-start(bf16[448,1536]{1,0:T(8,128)(2,1)} %bitcast.17), channel_id=1, source_target_pairs={{0,1},{4,7},{1,2},{5,4},{2,3},{6,5},{3,0},{7,6},{8,9},{12,15},{9,1... | collective-permute-start | bytes 4128776 | tf_op jit(solution)/shard_map/ppermute | solution.py:241
  42.4 7.8 %collective-permute-done.11.rest_9_ = bf16[1536,384]{1,0:T(8,128)(2,1)S(1)} collective-permute-done((bf16[1536,384]{1,0:T(8,128)(2,1)S(1)}, bf16[1536,384]{1,0:T(8,128)(2,1)S(1)}, u32[]{:S(2)}, u32[]{:S(2)}) %collective-permute-start.11) | collective-permute-done | bytes 1179680 | tf_op jit(solution)/shard_map/ppermute | solution.py:241
  50.2 3.4 %collective-permute-start.12 = (bf16[1536,384]{1,0:T(8,128)(2,1)S(1)}, bf16[1536,384]{1,0:T(8,128)(2,1)S(1)}, u32[]{:S(2)}, u32[]{:S(2)}) collective-permute-start(bf16[1536,384]{1,0:T(8,128)(2,1)S(1)} %collective-permute-done.11.rest_9_), channel_id=1, source_target_pairs={{0,8},{4,60},{8,16},{12,4},{16,24},{20,12},{24,32},{28,20},{32,40}... | collective-permute-start | bytes 3538952 | tf_op jit(solution)/shard_map/ppermute | solution.py:241
  53.7 17.5 %collective-permute-done.1.rest_2_ = bf16[448,1536]{1,0:T(8,128)(2,1)S(1)} collective-permute-done((bf16[448,1536]{1,0:T(8,128)(2,1)}, bf16[448,1536]{1,0:T(8,128)(2,1)S(1)}, u32[]{:S(2)}, u32[]{:S(2)}) %collective-permute-start.1) | collective-permute-done | bytes 1376288 | tf_op jit(solution)/shard_map/ppermute | solution.py:241
  71.1 2.7 %collective-permute-start.5 = (bf16[448,1536]{1,0:T(8,128)(2,1)S(1)}, bf16[448,1536]{1,0:T(8,128)(2,1)S(1)}, u32[]{:S(2)}, u32[]{:S(2)}) collective-permute-start(bf16[448,1536]{1,0:T(8,128)(2,1)S(1)} %collective-permute-done.1.rest_2_), channel_id=1, source_target_pairs={{0,1},{4,7},{1,2},{5,4},{2,3},{6,5},{3,0},{7,6},{8,9},{12,15},{9,1... | collective-permute-start | bytes 4128776 | tf_op jit(solution)/shard_map/ppermute | solution.py:241
  73.8 2.5 %collective-permute-start.13 = (bf16[1536,384]{1,0:T(8,128)(2,1)S(1)}, bf16[1536,384]{1,0:T(8,128)(2,1)S(1)}, u32[]{:S(2)}, u32[]{:S(2)}) collective-permute-start(bf16[1536,384]{1,0:T(8,128)(2,1)S(1)} %collective-permute-done.12.rest_10_), channel_id=1, source_target_pairs={{0,8},{4,60},{8,16},{12,4},{16,24},{20,12},{24,32},{28,20},{32,40}... | collective-permute-start | bytes 3538952 | tf_op jit(solution)/shard_map/ppermute | solution.py:241
  76.3 0.5 collective-permute-start.4
  76.8 0.1 collective-permute-start.3
  76.9 12.1 %collective-permute-done.5.rest_6_ = bf16[448,1536]{1,0:T(8,128)(2,1)S(1)} collective-permute-done((bf16[448,1536]{1,0:T(8,128)(2,1)S(1)}, bf16[448,1536]{1,0:T(8,128)(2,1)S(1)}, u32[]{:S(2)}, u32[]{:S(2)}) %collective-permute-start.5) | collective-permute-done | bytes 1376288 | tf_op jit(solution)/shard_map/ppermute | solution.py:241
  89.1 0.1 slice.85
  89.1 0.1 slice.86
  89.2 16.0 %collective-permute-done.13.rest_11_ = bf16[1536,384]{1,0:T(8,128)(2,1)S(1)} collective-permute-done((bf16[1536,384]{1,0:T(8,128)(2,1)S(1)}, bf16[1536,384]{1,0:T(8,128)(2,1)S(1)}, u32[]{:S(2)}, u32[]{:S(2)}) %collective-permute-start.13) | collective-permute-done | bytes 1179680 | tf_op jit(solution)/shard_map/ppermute | solution.py:241
  105.2 1.3 collective-permute-start.15
  106.5 0.1 fusion.3
  106.7 0.3 collective-permute-start.16
  107.0 1.2 collective-permute-start.14
  108.2 0.8 collective-permute-done.16.rest_14_
  109.0 0.3 copy-done.5
  109.3 6.8 %collective-permute-done.14.rest_12_ = bf16[768,384]{1,0:T(8,128)(2,1)S(1)} collective-permute-done((bf16[768,384]{1,0:T(8,128)(2,1)S(1)}, bf16[768,384]{1,0:T(8,128)(2,1)S(1)}, u32[]{:S(2)}, u32[]{:S(2)}) %collective-permute-start.14) | collective-permute-done | bytes 589856 | tf_op jit(solution)/shard_map/ppermute | solution.py:241
  116.1 0.8 copy-done.14
  117.0 16.5 %project.3 = bf16[1536,384]{1,0:T(8,128)(2,1)} custom-call(s32[1,64]{1,0:T(1,128)} %bitcast.38, bf16[448,1536]{1,0:T(8,128)(2,1)} %bitcast.20, bf16[448,1536]{1,0:T(8,128)(2,1)} %copy-done.3, bf16[448,1536]{1,0:T(8,128)(2,1)} %copy-done, bf16[448,1536]{1,0:T(8,128)(2,1)} %copy-done.5, bf16[448,1536]{1,0:T(8,128)(2,1)} %copy-done.1, ...), custom_call_target="tpu_custom_call" | custom-call | flops 4227858432 | bytes 15728640 | tf_op jit(solution)/shard_map/project/pallas_call | solution.py:162
  133.5 8.8 %all-to-all-start.1 = ((bf16[64,24,384]{2,1,0:T(8,128)(2,1)}), bf16[64,24,384]{2,1,0:T(8,128)(2,1)S(1)}, u32[]{:S(2)}, u32[]{:S(2)}) async-start(bf16[64,24,384]{2,1,0:T(8,128)(2,1)} %bitcast.24), calls=%async_computation.1 | async-start | bytes 2359296 | tf_op jit(solution)/shard_map/all_to_all | solution.py:309
  142.3 0.0 all-gather.2.cloned.1.call-done.rest_8_
  142.3 16.4 %project.2 = bf16[1536,384]{1,0:T(8,128)(2,1)} custom-call(s32[1,64]{1,0:T(1,128)} %bitcast.39, bf16[448,1536]{1,0:T(8,128)(2,1)} %bitcast.21, bf16[448,1536]{1,0:T(8,128)(2,1)} %copy-done.3, bf16[448,1536]{1,0:T(8,128)(2,1)} %copy-done, bf16[448,1536]{1,0:T(8,128)(2,1)} %copy-done.5, bf16[448,1536]{1,0:T(8,128)(2,1)} %copy-done.1, ...), custom_call_target="tpu_custom_call" | custom-call | flops 4227858432 | bytes 15728640 | tf_op jit(solution)/shard_map/project/pallas_call | solution.py:162
  158.7 14.9 %all-to-all-done.1 = bf16[64,24,384]{2,1,0:T(8,128)(2,1)S(1)} async-done(((bf16[64,24,384]{2,1,0:T(8,128)(2,1)}), bf16[64,24,384]{2,1,0:T(8,128)(2,1)S(1)}, u32[]{:S(2)}, u32[]{:S(2)}) %all-to-all-start.1) | async-done | bytes 1179680 | tf_op jit(solution)/shard_map/all_to_all | solution.py:309
  173.6 6.3 %all-to-all-start = ((bf16[64,24,384]{2,1,0:T(8,128)(2,1)}), bf16[64,24,384]{2,1,0:T(8,128)(2,1)S(1)}, u32[]{:S(2)}, u32[]{:S(2)}) async-start(bf16[64,24,384]{2,1,0:T(8,128)(2,1)} %bitcast.23), calls=%async_computation | async-start | bytes 2359296 | tf_op jit(solution)/shard_map/all_to_all | solution.py:309
  180.0 0.6 dynamic_slice.3.live_ref
  180.5 1.2 fusion.2
  181.7 5.0 %attend.2.rest_0_ = bf16[128,384]{1,0:T(8,128)(2,1)} custom-call(s32[1]{0:T(128)} %dynamic_slice.3.live_ref, bf16[128,768]{1,0:T(8,128)(2,1)} %bitcast.31, bf16[768,384]{1,0:T(8,128)(2,1)} %bitcast.30, bf16[768,384]{1,0:T(8,128)(2,1)} %bitcast.29, bf16[128,768]{1,0:T(8,128)(2,1)} %bitcast.33, bf16[128,768]{1,0:T(8,128)(2,1)} %bitcast.35), custom_call_target="tpu_custom_call" | custom-call | tf_op jit(solution)/shard_map/attend/pallas_call | solution.py:223
  186.7 24.6 %all-to-all-done = bf16[64,24,384]{2,1,0:T(8,128)(2,1)S(1)} async-done(((bf16[64,24,384]{2,1,0:T(8,128)(2,1)}), bf16[64,24,384]{2,1,0:T(8,128)(2,1)S(1)}, u32[]{:S(2)}, u32[]{:S(2)}) %all-to-all-start) | async-done | bytes 1179680 | tf_op jit(solution)/shard_map/all_to_all | solution.py:309
  211.3 1.2 fusion.4
  212.5 5.0 %attend.3 = bf16[128,768]{1,0:T(8,128)(2,1)} custom-call(s32[1]{0:T(128)} %dynamic_slice.3.live_ref, bf16[128,768]{1,0:T(8,128)(2,1)} %bitcast.32, bf16[768,384]{1,0:T(8,128)(2,1)} %bitcast.28, bf16[768,384]{1,0:T(8,128)(2,1)} %bitcast.27, bf16[128,768]{1,0:T(8,128)(2,1)} %bitcast.34, bf16[128,768]{1,0:T(8,128)(2,1)} %bitcast.36, bf16[128,384]{1,0:T(8,128)(2,1)} %attend.2.rest_0_), custom_call_target="tpu_custom_call" | custom-call | tf_op jit(solution)/shard_map/attend/pallas_call | solution.py:223
  (56 shorter events, 0.4 us)
Async XLA Ops:
  6.5 135.8 %all-gather.2.cloned.1.call-start = ((), (), s32[]{:S(2)}) async-start(), calls=%async_computation.2 | async-start | bytes 4866048 | tf_op jit(solution)/shard_map/all_gather | solution.py:277
  7.6 4.5 %collective-permute-start.7 = (bf16[192,768]{1,0:T(8,128)(2,1)S(1)}, bf16[192,768]{1,0:T(8,128)(2,1)S(1)}, u32[]{:S(2)}, u32[]{:S(2)}) collective-permute-start(bf16[192,768]{1,0:T(8,128)(2,1)S(1)} %pad_maximum_fusion.2), channel_id=1, source_target_pairs={{0,4},{4,0},{1,5},{5,1},{2,6},{6,2},{3,7},{7,3},{8,12},{12,8},{9,1... | collective-permute-start | bytes 884744 | tf_op jit(solution)/shard_map/ppermute | solution.py:257
  13.0 5.9 %collective-permute-start.8 = (bf16[384,384]{1,0:T(8,128)(2,1)S(1)}, bf16[384,384]{1,0:T(8,128)(2,1)S(1)}, u32[]{:S(2)}, u32[]{:S(2)}) collective-permute-start(bf16[384,384]{1,0:T(8,128)(2,1)S(1)} %pad_maximum_fusion.3), channel_id=1, source_target_pairs={{0,64},{4,196},{64,128},{68,4},{128,192},{132,68},{192,0},{196,132... | collective-permute-start | bytes 884744 | tf_op jit(solution)/shard_map/ppermute | solution.py:241
  19.0 14.6 %copy-start.10 = (bf16[384,2,1536]{2,1,0:T(2,128)(2,1)S(1)}, bf16[384,2,1536]{2,1,0:T(2,128)(2,1)}, u32[]{:S(2)}) copy-start(bf16[384,2,1536]{2,1,0:T(2,128)(2,1)} %param.11) | copy-start | bytes 7077892
  19.0 4.1 %collective-permute-start.9 = (bf16[192,384]{1,0:T(8,128)(2,1)S(1)}, bf16[192,384]{1,0:T(8,128)(2,1)S(1)}, u32[]{:S(2)}, u32[]{:S(2)}) collective-permute-start(bf16[192,384]{1,0:T(8,128)(2,1)S(1)} %get-tuple-element.11), channel_id=1, source_target_pairs={{0,64},{4,196},{64,128},{68,4},{128,192},{132,68},{192,0},{196,132... | collective-permute-start | bytes 442376 | tf_op jit(solution)/shard_map/ppermute | solution.py:241
  23.1 6.3 %collective-permute-start.10 = (bf16[576,384]{1,0:T(8,128)(2,1)S(1)}, bf16[576,384]{1,0:T(8,128)(2,1)S(1)}, u32[]{:S(2)}, u32[]{:S(2)}) collective-permute-start(bf16[576,384]{1,0:T(8,128)(2,1)S(1)} %pad_maximum_fusion), channel_id=1, source_target_pairs={{0,4},{4,0},{1,5},{5,1},{2,6},{6,2},{3,7},{7,3},{8,12},{12,8},{9,1... | collective-permute-start | bytes 1327112 | tf_op jit(solution)/shard_map/ppermute | solution.py:257
  29.6 5.6 %copy-start.11 = (bf16[1536,384]{1,0:T(8,128)(2,1)}, bf16[1536,384]{1,0:T(8,128)(2,1)S(1)}, u32[]{:S(2)}) copy-start(bf16[1536,384]{1,0:T(8,128)(2,1)S(1)} %slice_dynamic-update-slice_fusion.rest_8_) | copy-start | bytes 3538948
  29.6 5.6 %copy-start.16 = (s32[384]{0:T(512)S(1)}, s32[384]{0:T(512)}, u32[]{:S(2)}) copy-start(s32[384]{0:T(512)} %param.12) | copy-start | bytes 4612
  29.6 20.6 %collective-permute-start.11 = (bf16[1536,384]{1,0:T(8,128)(2,1)S(1)}, bf16[1536,384]{1,0:T(8,128)(2,1)S(1)}, u32[]{:S(2)}, u32[]{:S(2)}) collective-permute-start(bf16[1536,384]{1,0:T(8,128)(2,1)S(1)} %slice_dynamic-update-slice_fusion.rest_8_), channel_id=1, source_target_pairs={{0,8},{4,60},{8,16},{12,4},{16,24},{20,12},{24,32},{28,20},{32,40}... | collective-permute-start | bytes 3538952 | tf_op jit(solution)/shard_map/ppermute | solution.py:241
  39.9 31.2 %collective-permute-start.1 = (bf16[448,1536]{1,0:T(8,128)(2,1)}, bf16[448,1536]{1,0:T(8,128)(2,1)S(1)}, u32[]{:S(2)}, u32[]{:S(2)}) collective-permute-start(bf16[448,1536]{1,0:T(8,128)(2,1)} %bitcast.17), channel_id=1, source_target_pairs={{0,1},{4,7},{1,2},{5,4},{2,3},{6,5},{3,0},{7,6},{8,9},{12,15},{9,1... | collective-permute-start | bytes 4128776 | tf_op jit(solution)/shard_map/ppermute | solution.py:241
  42.4 34.4 %collective-permute-start.2 = (bf16[448,1536]{1,0:T(8,128)(2,1)}, bf16[448,1536]{1,0:T(8,128)(2,1)S(1)}, u32[]{:S(2)}, u32[]{:S(2)}) collective-permute-start(bf16[448,1536]{1,0:T(8,128)(2,1)} %bitcast.18), channel_id=1, source_target_pairs={{0,3},{4,5},{1,0},{5,6},{2,1},{6,7},{3,2},{7,4},{8,11},{12,13},{9,... | collective-permute-start | bytes 4128776 | tf_op jit(solution)/shard_map/ppermute | solution.py:241
  50.2 66.7 %copy-start.8 = (bf16[1536,384]{1,0:T(8,128)(2,1)}, bf16[1536,384]{1,0:T(8,128)(2,1)S(1)}, u32[]{:S(2)}) copy-start(bf16[1536,384]{1,0:T(8,128)(2,1)S(1)} %collective-permute-done.11.rest_9_) | copy-start | bytes 3538948
  50.2 23.6 %collective-permute-start.12 = (bf16[1536,384]{1,0:T(8,128)(2,1)S(1)}, bf16[1536,384]{1,0:T(8,128)(2,1)S(1)}, u32[]{:S(2)}, u32[]{:S(2)}) collective-permute-start(bf16[1536,384]{1,0:T(8,128)(2,1)S(1)} %collective-permute-done.11.rest_9_), channel_id=1, source_target_pairs={{0,8},{4,60},{8,16},{12,4},{16,24},{20,12},{24,32},{28,20},{32,40}... | collective-permute-start | bytes 3538952 | tf_op jit(solution)/shard_map/ppermute | solution.py:241
  71.1 18.1 %copy-start = (bf16[448,1536]{1,0:T(8,128)(2,1)}, bf16[448,1536]{1,0:T(8,128)(2,1)S(1)}, u32[]{:S(2)}) copy-start(bf16[448,1536]{1,0:T(8,128)(2,1)S(1)} %collective-permute-done.1.rest_2_) | copy-start | bytes 4128772
  71.1 17.9 %collective-permute-start.5 = (bf16[448,1536]{1,0:T(8,128)(2,1)S(1)}, bf16[448,1536]{1,0:T(8,128)(2,1)S(1)}, u32[]{:S(2)}, u32[]{:S(2)}) collective-permute-start(bf16[448,1536]{1,0:T(8,128)(2,1)S(1)} %collective-permute-done.1.rest_2_), channel_id=1, source_target_pairs={{0,1},{4,7},{1,2},{5,4},{2,3},{6,5},{3,0},{7,6},{8,9},{12,15},{9,1... | collective-permute-start | bytes 4128776 | tf_op jit(solution)/shard_map/ppermute | solution.py:241
  73.8 43.1 %copy-start.9 = (bf16[1536,384]{1,0:T(8,128)(2,1)}, bf16[1536,384]{1,0:T(8,128)(2,1)S(1)}, u32[]{:S(2)}) copy-start(bf16[1536,384]{1,0:T(8,128)(2,1)S(1)} %collective-permute-done.12.rest_10_) | copy-start | bytes 3538948
  73.8 31.4 %collective-permute-start.13 = (bf16[1536,384]{1,0:T(8,128)(2,1)S(1)}, bf16[1536,384]{1,0:T(8,128)(2,1)S(1)}, u32[]{:S(2)}, u32[]{:S(2)}) collective-permute-start(bf16[1536,384]{1,0:T(8,128)(2,1)S(1)} %collective-permute-done.12.rest_10_), channel_id=1, source_target_pairs={{0,8},{4,60},{8,16},{12,4},{16,24},{20,12},{24,32},{28,20},{32,40}... | collective-permute-start | bytes 3538952 | tf_op jit(solution)/shard_map/ppermute | solution.py:241
  76.3 30.4 %collective-permute-start = (bf16[448,1536]{1,0:T(8,128)(2,1)}, bf16[448,1536]{1,0:T(8,128)(2,1)S(1)}, u32[]{:S(2)}, u32[]{:S(2)}) collective-permute-start(bf16[448,1536]{1,0:T(8,128)(2,1)} %bitcast.19), channel_id=1, source_target_pairs={{0,4},{4,0},{1,5},{5,1},{2,6},{6,2},{3,7},{7,3},{8,12},{12,8},{9,1... | collective-permute-start | bytes 4128776 | tf_op jit(solution)/shard_map/ppermute | solution.py:257
  76.3 30.7 %collective-permute-start.4 = (bf16[448,1536]{1,0:T(8,128)(2,1)S(1)}, bf16[448,1536]{1,0:T(8,128)(2,1)S(1)}, u32[]{:S(2)}, u32[]{:S(2)}) collective-permute-start(bf16[448,1536]{1,0:T(8,128)(2,1)S(1)} %collective-permute-done.1.rest_2_), channel_id=1, source_target_pairs={{0,4},{4,0},{1,5},{5,1},{2,6},{6,2},{3,7},{7,3},{8,12},{12,8},{9,1... | collective-permute-start | bytes 4128776 | tf_op jit(solution)/shard_map/ppermute | solution.py:257
  76.8 40.1 %copy-start.1 = (bf16[448,1536]{1,0:T(8,128)(2,1)}, bf16[448,1536]{1,0:T(8,128)(2,1)S(1)}, u32[]{:S(2)}) copy-start(bf16[448,1536]{1,0:T(8,128)(2,1)S(1)} %collective-permute-done.2.rest_4_) | copy-start | bytes 4128772
  76.8 31.3 %collective-permute-start.3 = (bf16[448,1536]{1,0:T(8,128)(2,1)S(1)}, bf16[448,1536]{1,0:T(8,128)(2,1)S(1)}, u32[]{:S(2)}, u32[]{:S(2)}) collective-permute-start(bf16[448,1536]{1,0:T(8,128)(2,1)S(1)} %collective-permute-done.2.rest_4_), channel_id=1, source_target_pairs={{0,4},{4,0},{1,5},{5,1},{2,6},{6,2},{3,7},{7,3},{8,12},{12,8},{9,1... | collective-permute-start | bytes 4128776 | tf_op jit(solution)/shard_map/ppermute | solution.py:257
  89.1 27.9 %copy-start.2 = (bf16[448,1536]{1,0:T(8,128)(2,1)}, bf16[448,1536]{1,0:T(8,128)(2,1)S(1)}, u32[]{:S(2)}) copy-start(bf16[448,1536]{1,0:T(8,128)(2,1)S(1)} %collective-permute-done.5.rest_6_) | copy-start | bytes 4128772
  89.1 20.0 %collective-permute-start.6 = (bf16[448,1536]{1,0:T(8,128)(2,1)S(1)}, bf16[448,1536]{1,0:T(8,128)(2,1)S(1)}, u32[]{:S(2)}, u32[]{:S(2)}) collective-permute-start(bf16[448,1536]{1,0:T(8,128)(2,1)S(1)} %collective-permute-done.5.rest_6_), channel_id=1, source_target_pairs={{0,4},{4,0},{1,5},{5,1},{2,6},{6,2},{3,7},{7,3},{8,12},{12,8},{9,1... | collective-permute-start | bytes 4128776 | tf_op jit(solution)/shard_map/ppermute | solution.py:257
  105.2 10.9 %copy-start.7 = (bf16[1536,384]{1,0:T(8,128)(2,1)}, bf16[1536,384]{1,0:T(8,128)(2,1)S(1)}, u32[]{:S(2)}) copy-start(bf16[1536,384]{1,0:T(8,128)(2,1)S(1)} %collective-permute-done.13.rest_11_) | copy-start | bytes 3538948
  105.2 3.0 %collective-permute-start.15 = (bf16[768,384]{1,0:T(8,128)(2,1)S(1)}, bf16[768,384]{1,0:T(8,128)(2,1)S(1)}, u32[]{:S(2)}, u32[]{:S(2)}) collective-permute-start(bf16[768,384]{1,0:T(8,128)(2,1)S(1)} %slice.85), channel_id=1, source_target_pairs={{0,4},{4,0},{1,5},{5,1},{2,6},{6,2},{3,7},{7,3},{8,12},{12,8},{9,1... | collective-permute-start | bytes 1769480 | tf_op jit(solution)/shard_map/ppermute | solution.py:257
  106.7 10.3 %copy-start.3 = (bf16[448,1536]{1,0:T(8,128)(2,1)}, bf16[448,1536]{1,0:T(8,128)(2,1)S(1)}, u32[]{:S(2)}) copy-start(bf16[448,1536]{1,0:T(8,128)(2,1)S(1)} %collective-permute-done.rest_1_) | copy-start | bytes 4128772
  106.7 2.3 %collective-permute-start.16 = (bf16[768,384]{1,0:T(8,128)(2,1)S(1)}, bf16[768,384]{1,0:T(8,128)(2,1)S(1)}, u32[]{:S(2)}, u32[]{:S(2)}) collective-permute-start(bf16[768,384]{1,0:T(8,128)(2,1)S(1)} %slice.86), channel_id=1, source_target_pairs={{0,4},{4,0},{1,5},{5,1},{2,6},{6,2},{3,7},{7,3},{8,12},{12,8},{9,1... | collective-permute-start | bytes 1769480 | tf_op jit(solution)/shard_map/ppermute | solution.py:257
  107.0 10.0 %copy-start.4 = (bf16[448,1536]{1,0:T(8,128)(2,1)}, bf16[448,1536]{1,0:T(8,128)(2,1)S(1)}, u32[]{:S(2)}) copy-start(bf16[448,1536]{1,0:T(8,128)(2,1)S(1)} %collective-permute-done.4.rest_5_) | copy-start | bytes 4128772
  107.0 9.1 %collective-permute-start.14 = (bf16[768,384]{1,0:T(8,128)(2,1)S(1)}, bf16[768,384]{1,0:T(8,128)(2,1)S(1)}, u32[]{:S(2)}, u32[]{:S(2)}) collective-permute-start(bf16[768,384]{1,0:T(8,128)(2,1)S(1)} %get-tuple-element.8), channel_id=1, source_target_pairs={{0,8},{4,60},{8,16},{12,4},{16,24},{20,12},{24,32},{28,20},{32,40}... | collective-permute-start | bytes 1769480 | tf_op jit(solution)/shard_map/ppermute | solution.py:241
  108.2 1.1 copy-start.5
  108.2 8.8 %collective-permute-start.17 = (bf16[768,384]{1,0:T(8,128)(2,1)S(1)}, bf16[768,384]{1,0:T(8,128)(2,1)}, u32[]{:S(2)}, u32[]{:S(2)}) collective-permute-start(bf16[768,384]{1,0:T(8,128)(2,1)S(1)} %get-tuple-element.7), channel_id=1, source_target_pairs={{0,4},{4,0},{1,5},{5,1},{2,6},{6,2},{3,7},{7,3},{8,12},{12,8},{9,1... | collective-permute-start | bytes 1769480 | tf_op jit(solution)/shard_map/ppermute | solution.py:257
  108.2 7.9 %copy-start.12 = (bf16[768,384]{1,0:T(8,128)(2,1)}, bf16[768,384]{1,0:T(8,128)(2,1)S(1)}, u32[]{:S(2)}) copy-start(bf16[768,384]{1,0:T(8,128)(2,1)S(1)} %collective-permute-done.15.rest_13_) | copy-start | bytes 1769476
  109.0 7.1 %copy-start.13 = (bf16[768,384]{1,0:T(8,128)(2,1)}, bf16[768,384]{1,0:T(8,128)(2,1)S(1)}, u32[]{:S(2)}) copy-start(bf16[768,384]{1,0:T(8,128)(2,1)S(1)} %collective-permute-done.16.rest_14_) | copy-start | bytes 1769476
  109.3 6.8 %copy-start.6 = (bf16[448,1536]{1,0:T(8,128)(2,1)}, bf16[448,1536]{1,0:T(8,128)(2,1)S(1)}, u32[]{:S(2)}) copy-start(bf16[448,1536]{1,0:T(8,128)(2,1)S(1)} %collective-permute-done.6.rest_7_) | copy-start | bytes 4128772
  116.1 0.8 copy-start.14
  133.5 40.2 %all-to-all-start.1 = ((bf16[64,24,384]{2,1,0:T(8,128)(2,1)}), bf16[64,24,384]{2,1,0:T(8,128)(2,1)S(1)}, u32[]{:S(2)}, u32[]{:S(2)}) async-start(bf16[64,24,384]{2,1,0:T(8,128)(2,1)} %bitcast.24), calls=%async_computation.1 | async-start | bytes 2359296 | tf_op jit(solution)/shard_map/all_to_all | solution.py:309
  173.6 6.3 %copy-start.15 = (s32[64]{0:T(128)S(1)}, s32[64]{0:T(128)}, u32[]{:S(2)}) copy-start(s32[64]{0:T(128)} %param.13) | copy-start | bytes 772
  173.6 37.7 %all-to-all-start = ((bf16[64,24,384]{2,1,0:T(8,128)(2,1)}), bf16[64,24,384]{2,1,0:T(8,128)(2,1)S(1)}, u32[]{:S(2)}, u32[]{:S(2)}) async-start(bf16[64,24,384]{2,1,0:T(8,128)(2,1)} %bitcast.23), calls=%async_computation | async-start | bytes 2359296 | tf_op jit(solution)/shard_map/all_to_all | solution.py:309
Sparse Core Ops, SparseCore 0:
  13.1 89.6 all-gather.1

commit v5 on v4

--- a/solution.py
+++ b/solution.py
@@ -11,6 +11,7 @@
 HD = 64
 MAXB = 6
 USED = 224
+FIRST = 256
 GRID = (4, 8, 2)
 PLANE = ("y", "z", "core")
 BF16 = jnp.bfloat16
@@ -97,7 +98,7 @@
         x_copies.append(
             pltpu.make_async_copy(rows[k], x_ref.at[2 * (k // 2) + who], x_sem.at[k])
         )
-    for c in w_copies + x_copies:
+    for c in w_copies + x_copies[:2]:
         c.start()
 
     convs = counts_ref.shape[1]
@@ -132,6 +133,8 @@
     for s in range(nh):
         for c in x_copies[2 * s : 2 * s + 2]:
             c.wait()
+        for c in x_copies[2 * s + 2 : 2 * s + 4]:
+            c.start()
         quarter = lax.rem(head + quarters[s] * sign + nh, nh)
         at = pl.multiple_of(quarter * feats, feats)
 
@@ -241,18 +244,6 @@
     return lax.ppermute(x, order, perm)
 
 
-def gather_rows(own):
-    behind = ring_step(own, "head")
-    ahead = ring_step(own, "head", -1)
-    opposite = ring_step(behind, "head")
-    return [
-        own, swap_cores(own),
-        behind, swap_cores(ahead),
-        ahead, swap_cores(behind),
-        opposite, swap_cores(opposite),
-    ]
-
-
 def swap_cores(x):
     return lax.ppermute(x, "core", [(0, 1), (1, 0)])
 
@@ -262,22 +253,25 @@
     return x[:half], x[half:]
 
 
-def gather_weights(key_weight, value_weight):
+def gather(key_weight, value_weight, rows_of):
+    hold = lax.optimization_barrier
     upper = lax.axis_index("core") == 0
-    half = key_weight.shape[1] // 2
     mine = jnp.where(upper, key_weight, value_weight)
     other = jnp.where(upper, value_weight, key_weight)
     n = mine.shape[0]
-    near = swap_cores(jnp.concatenate([other, mine]))
+    both, rows = hold((jnp.concatenate([other, mine]), rows_of()))
+    near = swap_cores(both)
 
     def chip(a, b):
         return jnp.where(upper, jnp.concatenate([a, b]), jnp.concatenate([b, a]))
 
     chip_mine = chip(mine, near[:n])
-    second = lax.all_gather(chip_mine[:, half:], ("y", "z"), axis=0, tiled=True)
+    second = lax.all_gather(chip_mine[:, FIRST:], ("y", "z"), axis=0, tiled=True)
 
     n = 2 * n
-    own = jnp.concatenate([chip_mine[:, :half], chip(other, near[n // 2 :])[:, :half]])
+    own = jnp.concatenate([chip_mine[:, :FIRST], chip(other, near[n // 2 :])[:, :FIRST]])
+    behind = ring_step(rows, "head")
+    ahead = ring_step(rows, "head", -1)
     y1 = ring_step(own, "y")
     y2 = ring_step(kinds(y1)[0], "y")
     got = swap_cores(jnp.concatenate([y1, y2]))
@@ -286,24 +280,31 @@
     )
     z1 = ring_step(group, "z")
     z2 = ring_step(z1, "z")
+    z2, z1 = hold((z2, z1))
     z3 = ring_step(z2, "z")
+    opposite = ring_step(behind, "head")
+    across = [swap_cores(kinds(z1)[1])]
+    near_rows = [swap_cores(rows), swap_cores(ahead), swap_cores(behind)]
+    z3, z2, opposite = hold((z3, z2, opposite))
     z4 = ring_step(kinds(z3)[0], "z")
-    across = [swap_cores(kinds(t)[1]) for t in (z1, z2, z3)]
-    return [group, z1, z2, z3, z4] + across, [second]
+    across += [swap_cores(kinds(z2)[1]), swap_cores(kinds(z3)[1])]
+    near_rows.append(swap_cores(opposite))
+    rows = [r for pair in zip((rows, behind, ahead, opposite), near_rows) for r in pair]
+    return rows, ([group, z1, z2, z3, z4] + across, [second])
 
 
 def per_device(queries, new_keys, new_values, pool, block_table, block_counts, key_weight, value_weight):
     ny, nz, nh = lax.axis_size("y"), lax.axis_size("z"), lax.axis_size("head")
-    live = live_rows(block_counts, block_table, pool)
-    live = live.reshape(-1, live.shape[2])
-    rows = gather_rows(live)
-
-    halves = gather_weights(key_weight, value_weight)
+    def rows_of():
+        live = live_rows(block_counts, block_table, pool)
+        return live.reshape(-1, live.shape[2])
+
+    rows, parts = gather(key_weight, value_weight, rows_of)
     dims = (ny, nz, nh, 2 * key_weight.shape[0])
     convs = block_counts.shape[0]
     count = lax.dynamic_slice(block_counts, (lax.axis_index(PLANE),), (1,))
     out = None
-    for pieces in halves:
+    for pieces in parts:
         sent = project(block_counts, rows, pieces, dims)
         sent = sent.reshape(convs, -1, sent.shape[1])
         got = lax.all_to_all(sent, PLANE, split_axis=0, concat_axis=0, tiled=True)

time: 225 us -> 216 us (0.960)
  Pallas kernels: 47 us -> 41.9 us
  local copies, waits for them, and re-layouts: 6.85 us -> 11 us
  waiting for transfers between devices: 110 us -> 106 us
    ppermute x9, waiting for transfers between devices: 67.2 us -> 61.9 us  [ring_step(): return lax.ppermute(x, order, perm)]
    pallas_call x2, Pallas kernels: 32.9 us -> 27.7 us  [project(): pl.pallas_call(functools.partial(project_kernel, dims), out_shape=jax.Sha...]
    unnamed x40 -> x44, local copies, waits for them, and re-layouts: 2.98 us -> 6.76 us
    all_to_all x2, starting transfers between devices: 15.1 us -> 12.5 us  [per_device(): got = lax.all_to_all(sent, PLANE, split_axis=0, concat_axis=0, tiled=True)]
    all_to_all x2, waiting for transfers between devices: 39.5 us -> 41.9 us  [per_device(): got = lax.all_to_all(sent, PLANE, split_axis=0, concat_axis=0, tiled=True)]
  transfers between devices with their start and end apart: 21 -> 21, of which waited for: 12 -> 12; matrix products, arithmetic and copies ran while one was open for 2% -> 1% of each run, Pallas kernels for 19% -> 15%
where the time goes in v5:
time: 216 us; the launch traced here: 215 us
  waiting for transfers between devices  106 us (49%)
  starting transfers between devices  43.1 us (20%)
  Pallas kernels  41.9 us (19%)
  between operations  13.7 us (6%)
  local copies, waits for them, and re-layouts  11 us (5%)
    ppermute x9, waiting for transfers between devices, ring_step(): return lax.ppermute(x, order, perm)  61.9 us
    all_to_all x2, waiting for transfers between devices, per_device(): got = lax.all_to_all(sent, PLANE, split_axis=0, concat_axis=0, tiled=True)  41.9 us
    pallas_call x2, Pallas kernels, project(): pl.pallas_call(functools.partial(project_kernel, dims), out_shape=jax.Sha...  27.7 us
    ppermute x9, starting transfers between devices, ring_step(): return lax.ppermute(x, order, perm)  21.3 us
    all_to_all x2, starting transfers between devices, per_device(): got = lax.all_to_all(sent, PLANE, split_axis=0, concat_axis=0, tiled=True)  12.5 us
    pallas_call x2, Pallas kernels, attend(): pl.pallas_call(functools.partial(attend_kernel, first), out_shape=jax.Sha...  10.2 us
    ppermute x9, starting transfers between devices, swap_cores(): return lax.ppermute(x, 'core', [(0, 1), (1, 0)])  9.23 us
    unnamed x44, local copies, waits for them, and re-layouts  6.76 us
  transfers between devices with their start and end apart: 21, of which 12 were waited for; matrix products, arithmetic and copies ran while one was open for 1% of the time, Pallas kernels for 15%

profile of v5, /device:TPU:1, one launch (start us, length us, event | category | flops | bytes accessed | tf_op | source)
XLA Modules:
  0.0 215.4 jit_solution(13755610708572753302)
XLA Ops:
  6.5 3.4 %copy.12 = bf16[384,2,1536]{2,0,1:T(8,128)(2,1)} copy(bf16[384,2,1536]{2,1,0:T(2,128)(2,1)} %param.11) | data formatting | bytes 4718592 | tf_op args[3]
  9.9 0.6 broadcast_in_dim.12.table_ref
  10.5 4.1 %live_rows.1 = bf16[2,224,1536]{2,1,0:T(8,128)(2,1)} custom-call(s32[1,64]{1,0:T(1,128)} %bitcast.37, s32[1,384]{1,0:T(1,128)} %broadcast_in_dim.12.table_ref, bf16[2,384,1536]{2,1,0:T(8,128)(2,1)} %bitcast.17), custom_call_target="tpu_custom_call" | custom-call | tf_op jit(solution)/shard_map/live_rows/pallas_call | solution.py:52
  14.6 3.2 %collective-permute-start.5 = (bf16[192,768]{1,0:T(8,128)(2,1)S(1)}, bf16[192,768]{1,0:T(8,128)(2,1)S(1)}, u32[]{:S(2)}, u32[]{:S(2)}) collective-permute-start(bf16[192,768]{1,0:T(8,128)(2,1)S(1)} %pad_maximum_fusion.1), channel_id=1, source_target_pairs={{0,4},{4,0},{1,5},{5,1},{2,6},{6,2},{3,7},{7,3},{8,12},{12,8},{9,1... | collective-permute-start | bytes 884744 | tf_op jit(solution)/shard_map/ppermute | solution.py:248
  17.8 1.2 collective-permute-done.5
  19.1 0.1 fusion
  19.1 0.7 slice.81
  19.8 0.0 all-gather.2.cloned.1.call-update
  19.9 1.1 collective-permute-start.6
  21.0 3.8 %collective-permute-done.6 = bf16[384,256]{1,0:T(8,128)(2,1)S(1)} collective-permute-done((bf16[384,256]{1,0:T(8,128)(2,1)S(1)}, bf16[384,256]{1,0:T(8,128)(2,1)S(1)}, u32[]{:S(2)}, u32[]{:S(2)}) %collective-permute-start.6) | collective-permute-done | bytes 196640 | tf_op jit(solution)/shard_map/ppermute | solution.py:244
  24.8 2.0 collective-permute-start.7
  26.8 1.6 collective-permute-done.7
  28.5 4.8 %collective-permute-start.8 = (bf16[576,256]{1,0:T(8,128)(2,1)S(1)}, bf16[576,256]{1,0:T(8,128)(2,1)S(1)}, u32[]{:S(2)}, u32[]{:S(2)}) collective-permute-start(bf16[576,256]{1,0:T(8,128)(2,1)S(1)} %pad_maximum_fusion.2), channel_id=1, source_target_pairs={{0,4},{4,0},{1,5},{5,1},{2,6},{6,2},{3,7},{7,3},{8,12},{12,8},{9,1... | collective-permute-start | bytes 884744 | tf_op jit(solution)/shard_map/ppermute | solution.py:248
  33.3 0.7 collective-permute-start.1
  34.0 0.5 collective-permute-done.8
  34.6 5.2 %collective-permute-start.9 = (bf16[1536,256]{1,0:T(8,128)(2,1)S(1)}, bf16[1536,256]{1,0:T(8,128)(2,1)S(1)}, u32[]{:S(2)}, u32[]{:S(2)}) collective-permute-start(bf16[1536,256]{1,0:T(8,128)(2,1)S(1)} %slice_dynamic-update-slice_fusion.rest_8_), channel_id=1, source_target_pairs={{0,8},{4,60},{8,16},{12,4},{16,24},{20,12},{24,32},{28,20},{32,40}... | collective-permute-start | bytes 2359304 | tf_op jit(solution)/shard_map/ppermute | solution.py:244
  39.8 12.1 %collective-permute-done.9.rest_9_ = bf16[1536,256]{1,0:T(8,128)(2,1)S(1)} collective-permute-done((bf16[1536,256]{1,0:T(8,128)(2,1)S(1)}, bf16[1536,256]{1,0:T(8,128)(2,1)S(1)}, u32[]{:S(2)}, u32[]{:S(2)}) %collective-permute-start.9) | collective-permute-done | bytes 786464 | tf_op jit(solution)/shard_map/ppermute | solution.py:244
  51.9 3.4 %collective-permute-start.10 = (bf16[1536,256]{1,0:T(8,128)(2,1)S(1)}, bf16[1536,256]{1,0:T(8,128)(2,1)S(1)}, u32[]{:S(2)}, u32[]{:S(2)}) collective-permute-start(bf16[1536,256]{1,0:T(8,128)(2,1)S(1)} %collective-permute-done.9.rest_9_), channel_id=1, source_target_pairs={{0,8},{4,60},{8,16},{12,4},{16,24},{20,12},{24,32},{28,20},{32,40}... | collective-permute-start | bytes 2359304 | tf_op jit(solution)/shard_map/ppermute | solution.py:244
  55.3 7.8 %collective-permute-done.1.rest_2_ = bf16[448,1536]{1,0:T(8,128)(2,1)S(1)} collective-permute-done((bf16[448,1536]{1,0:T(8,128)(2,1)S(1)}, bf16[448,1536]{1,0:T(8,128)(2,1)S(1)}, u32[]{:S(2)}, u32[]{:S(2)}) %collective-permute-start.1) | collective-permute-done | bytes 1376288 | tf_op jit(solution)/shard_map/ppermute | solution.py:244
  63.1 0.1 collective-permute-start.12
  63.2 2.3 %collective-permute-done.10.rest_10_ = bf16[1536,256]{1,0:T(8,128)(2,1)S(1)} collective-permute-done((bf16[1536,256]{1,0:T(8,128)(2,1)S(1)}, bf16[1536,256]{1,0:T(8,128)(2,1)S(1)}, u32[]{:S(2)}, u32[]{:S(2)}) %collective-permute-start.10) | collective-permute-done | bytes 786464 | tf_op jit(solution)/shard_map/ppermute | solution.py:244
  65.5 5.1 %collective-permute-start.11 = (bf16[1536,256]{1,0:T(8,128)(2,1)S(1)}, bf16[1536,256]{1,0:T(8,128)(2,1)S(1)}, u32[]{:S(2)}, u32[]{:S(2)}) collective-permute-start(bf16[1536,256]{1,0:T(8,128)(2,1)S(1)} %collective-permute-done.10.rest_10_), channel_id=1, source_target_pairs={{0,8},{4,60},{8,16},{12,4},{16,24},{20,12},{24,32},{28,20},{32,40}... | collective-permute-start | bytes 2359304 | tf_op jit(solution)/shard_map/ppermute | solution.py:244
  70.7 0.5 collective-permute-start.4
  71.2 0.1 collective-permute-start.3
  71.3 9.4 %collective-permute-done.12.rest_6_ = bf16[448,1536]{1,0:T(8,128)(2,1)S(1)} collective-permute-done((bf16[448,1536]{1,0:T(8,128)(2,1)S(1)}, bf16[448,1536]{1,0:T(8,128)(2,1)S(1)}, u32[]{:S(2)}, u32[]{:S(2)}) %collective-permute-start.12) | collective-permute-done | bytes 1376288 | tf_op jit(solution)/shard_map/ppermute | solution.py:244
  80.7 13.9 %collective-permute-done.11.rest_11_ = bf16[1536,256]{1,0:T(8,128)(2,1)S(1)} collective-permute-done((bf16[1536,256]{1,0:T(8,128)(2,1)S(1)}, bf16[1536,256]{1,0:T(8,128)(2,1)S(1)}, u32[]{:S(2)}, u32[]{:S(2)}) %collective-permute-start.11) | collective-permute-done | bytes 786464 | tf_op jit(solution)/shard_map/ppermute | solution.py:244
  94.7 0.6 collective-permute-start.15
  95.3 0.1 fusion.4
  95.4 0.2 copy-done.1
  95.5 3.6 %collective-permute-start.14 = (bf16[768,256]{1,0:T(8,128)(2,1)S(1)}, bf16[768,256]{1,0:T(8,128)(2,1)S(1)}, u32[]{:S(2)}, u32[]{:S(2)}) collective-permute-start(bf16[768,256]{1,0:T(8,128)(2,1)S(1)} %get-tuple-element.24), channel_id=1, source_target_pairs={{0,8},{4,60},{8,16},{12,4},{16,24},{20,12},{24,32},{28,20},{32,40}... | collective-permute-start | bytes 1179656 | tf_op jit(solution)/shard_map/ppermute | solution.py:244
  99.2 1.1 copy-done.8
  100.3 1.1 copy-done.9
  101.4 10.9 %collective-permute-done.14.rest_12_ = bf16[768,256]{1,0:T(8,128)(2,1)S(1)} collective-permute-done((bf16[768,256]{1,0:T(8,128)(2,1)S(1)}, bf16[768,256]{1,0:T(8,128)(2,1)S(1)}, u32[]{:S(2)}, u32[]{:S(2)}) %collective-permute-start.14) | collective-permute-done | bytes 393248 | tf_op jit(solution)/shard_map/ppermute | solution.py:244
  112.4 0.7 copy-done.12
  113.0 0.2 copy-done.13
  113.2 0.2 copy-done.14
  113.4 12.5 %project.3 = bf16[1536,256]{1,0:T(8,128)(2,1)} custom-call(s32[1,64]{1,0:T(1,128)} %bitcast.38, bf16[448,1536]{1,0:T(8,128)(2,1)} %bitcast.19, bf16[448,1536]{1,0:T(8,128)(2,1)} %copy-done.7, bf16[448,1536]{1,0:T(8,128)(2,1)} %copy-done.4, bf16[448,1536]{1,0:T(8,128)(2,1)} %copy-done.9, bf16[448,1536]{1,0:T(8,128)(2,1)} %copy-done.5, ...), custom_call_target="tpu_custom_call" | custom-call | flops 2818572288 | bytes 14155776 | tf_op jit(solution)/shard_map/project/pallas_call | solution.py:165
  125.9 6.2 %all-to-all-start.1 = ((bf16[64,24,256]{2,1,0:T(8,128)(2,1)}), bf16[64,24,256]{2,1,0:T(8,128)(2,1)S(1)}, u32[]{:S(2)}, u32[]{:S(2)}) async-start(bf16[64,24,256]{2,1,0:T(8,128)(2,1)} %bitcast.24), calls=%async_computation.1 | async-start | bytes 1572864 | tf_op jit(solution)/shard_map/all_to_all | solution.py:310
  132.1 0.0 all-gather.2.cloned.1.call-done.rest_8_
  132.1 15.1 %project.2 = bf16[1536,512]{1,0:T(8,128)(2,1)} custom-call(s32[1,64]{1,0:T(1,128)} %bitcast.39, bf16[448,1536]{1,0:T(8,128)(2,1)} %bitcast.20, bf16[448,1536]{1,0:T(8,128)(2,1)} %copy-done.7, bf16[448,1536]{1,0:T(8,128)(2,1)} %copy-done.4, bf16[448,1536]{1,0:T(8,128)(2,1)} %copy-done.9, bf16[448,1536]{1,0:T(8,128)(2,1)} %copy-done.5, ...), custom_call_target="tpu_custom_call" | custom-call | flops 5637144576 | bytes 17301504 | tf_op jit(solution)/shard_map/project/pallas_call | solution.py:165
  147.3 7.8 %all-to-all-done.1 = bf16[64,24,256]{2,1,0:T(8,128)(2,1)S(1)} async-done(((bf16[64,24,256]{2,1,0:T(8,128)(2,1)}), bf16[64,24,256]{2,1,0:T(8,128)(2,1)S(1)}, u32[]{:S(2)}, u32[]{:S(2)}) %all-to-all-start.1) | async-done | bytes 786464 | tf_op jit(solution)/shard_map/all_to_all | solution.py:310
  155.1 6.3 %all-to-all-start = ((bf16[64,24,512]{2,1,0:T(8,128)(2,1)}), bf16[64,24,512]{2,1,0:T(8,128)(2,1)S(1)}, u32[]{:S(2)}, u32[]{:S(2)}) async-start(bf16[64,24,512]{2,1,0:T(8,128)(2,1)} %bitcast.28), calls=%async_computation | async-start | bytes 3145728 | tf_op jit(solution)/shard_map/all_to_all | solution.py:310
  161.4 0.6 dynamic_slice.3.live_ref
  162.0 1.0 fusion.3
  163.0 4.1 %attend.2.rest_0_ = bf16[128,256]{1,0:T(8,128)(2,1)} custom-call(s32[1]{0:T(128)} %dynamic_slice.3.live_ref, bf16[128,768]{1,0:T(8,128)(2,1)} %bitcast.31, bf16[768,256]{1,0:T(8,128)(2,1)} %bitcast.30, bf16[768,256]{1,0:T(8,128)(2,1)} %bitcast.29, bf16[128,768]{1,0:T(8,128)(2,1)} %bitcast.33, bf16[128,768]{1,0:T(8,128)(2,1)} %bitcast.35), custom_call_target="tpu_custom_call" | custom-call | tf_op jit(solution)/shard_map/attend/pallas_call | solution.py:226
  167.1 34.1 %all-to-all-done = bf16[64,24,512]{2,1,0:T(8,128)(2,1)S(1)} async-done(((bf16[64,24,512]{2,1,0:T(8,128)(2,1)}), bf16[64,24,512]{2,1,0:T(8,128)(2,1)S(1)}, u32[]{:S(2)}, u32[]{:S(2)}) %all-to-all-start) | async-done | bytes 1572896 | tf_op jit(solution)/shard_map/all_to_all | solution.py:310
  201.2 1.3 fusion.2
  202.5 6.0 %attend.3 = bf16[128,768]{1,0:T(8,128)(2,1)} custom-call(s32[1]{0:T(128)} %dynamic_slice.3.live_ref, bf16[128,768]{1,0:T(8,128)(2,1)} %bitcast.32, bf16[768,512]{1,0:T(8,128)(2,1)} %bitcast.27, bf16[768,512]{1,0:T(8,128)(2,1)} %bitcast.26, bf16[128,768]{1,0:T(8,128)(2,1)} %bitcast.34, bf16[128,768]{1,0:T(8,128)(2,1)} %bitcast.36, bf16[128,256]{1,0:T(8,128)(2,1)} %attend.2.rest_0_), custom_call_target="tpu_custom_call" | custom-call | tf_op jit(solution)/shard_map/attend/pallas_call | solution.py:226
  (61 shorter events, 0.3 us)
Async XLA Ops:
  6.5 125.6 %all-gather.2.cloned.1.call-start = ((), (), s32[]{:S(2)}) async-start(), calls=%async_computation.2 | async-start | bytes 6488064 | tf_op jit(solution)/shard_map/all_gather | solution.py:269
  6.5 3.4 %copy-start.18 = (s32[384]{0:T(512)S(1)}, s32[384]{0:T(512)}, u32[]{:S(2)}) copy-start(s32[384]{0:T(512)} %param.12) | copy-start | bytes 4612
  6.5 3.9 %copy-start.15 = (bf16[96,768]{1,0:T(8,128)(2,1)S(1)}, bf16[96,768]{1,0:T(8,128)(2,1)}, u32[]{:S(2)}) copy-start(bf16[96,768]{1,0:T(8,128)(2,1)} %param.15) | copy-start | bytes 442372
  6.5 3.9 %copy-start.16 = (bf16[96,768]{1,0:T(8,128)(2,1)S(1)}, bf16[96,768]{1,0:T(8,128)(2,1)}, u32[]{:S(2)}) copy-start(bf16[96,768]{1,0:T(8,128)(2,1)} %param.14) | copy-start | bytes 442372
  14.6 4.4 %collective-permute-start.5 = (bf16[192,768]{1,0:T(8,128)(2,1)S(1)}, bf16[192,768]{1,0:T(8,128)(2,1)S(1)}, u32[]{:S(2)}, u32[]{:S(2)}) collective-permute-start(bf16[192,768]{1,0:T(8,128)(2,1)S(1)} %pad_maximum_fusion.1), channel_id=1, source_target_pairs={{0,4},{4,0},{1,5},{5,1},{2,6},{6,2},{3,7},{7,3},{8,12},{12,8},{9,1... | collective-permute-start | bytes 884744 | tf_op jit(solution)/shard_map/ppermute | solution.py:248
  19.1 14.2 %copy-start = (bf16[2,224,1536]{2,1,0:T(8,128)(2,1)S(1)}, bf16[2,224,1536]{2,1,0:T(8,128)(2,1)}, u32[]{:S(2)}) copy-start(bf16[2,224,1536]{2,1,0:T(8,128)(2,1)} %live_rows.1) | copy-start | bytes 4128772
  19.9 4.9 %collective-permute-start.6 = (bf16[384,256]{1,0:T(8,128)(2,1)S(1)}, bf16[384,256]{1,0:T(8,128)(2,1)S(1)}, u32[]{:S(2)}, u32[]{:S(2)}) collective-permute-start(bf16[384,256]{1,0:T(8,128)(2,1)S(1)} %pad_maximum_fusion.3), channel_id=1, source_target_pairs={{0,64},{4,196},{64,128},{68,4},{128,192},{132,68},{192,0},{196,132... | collective-permute-start | bytes 589832 | tf_op jit(solution)/shard_map/ppermute | solution.py:244
  24.8 3.6 %collective-permute-start.7 = (bf16[192,256]{1,0:T(8,128)(2,1)S(1)}, bf16[192,256]{1,0:T(8,128)(2,1)S(1)}, u32[]{:S(2)}, u32[]{:S(2)}) collective-permute-start(bf16[192,256]{1,0:T(8,128)(2,1)S(1)} %get-tuple-element.31), channel_id=1, source_target_pairs={{0,64},{4,196},{64,128},{68,4},{128,192},{132,68},{192,0},{196,132... | collective-permute-start | bytes 294920 | tf_op jit(solution)/shard_map/ppermute | solution.py:244
  28.5 6.0 %collective-permute-start.8 = (bf16[576,256]{1,0:T(8,128)(2,1)S(1)}, bf16[576,256]{1,0:T(8,128)(2,1)S(1)}, u32[]{:S(2)}, u32[]{:S(2)}) collective-permute-start(bf16[576,256]{1,0:T(8,128)(2,1)S(1)} %pad_maximum_fusion.2), channel_id=1, source_target_pairs={{0,4},{4,0},{1,5},{5,1},{2,6},{6,2},{3,7},{7,3},{8,12},{12,8},{9,1... | collective-permute-start | bytes 884744 | tf_op jit(solution)/shard_map/ppermute | solution.py:248
  33.3 29.8 %collective-permute-start.1 = (bf16[448,1536]{1,0:T(8,128)(2,1)S(1)}, bf16[448,1536]{1,0:T(8,128)(2,1)S(1)}, u32[]{:S(2)}, u32[]{:S(2)}) collective-permute-start(bf16[448,1536]{1,0:T(8,128)(2,1)S(1)} %bitcast.21), channel_id=1, source_target_pairs={{0,1},{4,7},{1,2},{5,4},{2,3},{6,5},{3,0},{7,6},{8,9},{12,15},{9,1... | collective-permute-start | bytes 4128776 | tf_op jit(solution)/shard_map/ppermute | solution.py:244
  34.6 60.8 %copy-start.10 = (bf16[1536,256]{1,0:T(8,128)(2,1)}, bf16[1536,256]{1,0:T(8,128)(2,1)S(1)}, u32[]{:S(2)}) copy-start(bf16[1536,256]{1,0:T(8,128)(2,1)S(1)} %slice_dynamic-update-slice_fusion.rest_8_) | copy-start | bytes 2359300
  34.6 17.3 %collective-permute-start.9 = (bf16[1536,256]{1,0:T(8,128)(2,1)S(1)}, bf16[1536,256]{1,0:T(8,128)(2,1)S(1)}, u32[]{:S(2)}, u32[]{:S(2)}) collective-permute-start(bf16[1536,256]{1,0:T(8,128)(2,1)S(1)} %slice_dynamic-update-slice_fusion.rest_8_), channel_id=1, source_target_pairs={{0,8},{4,60},{8,16},{12,4},{16,24},{20,12},{24,32},{28,20},{32,40}... | collective-permute-start | bytes 2359304 | tf_op jit(solution)/shard_map/ppermute | solution.py:244
  39.8 31.4 %collective-permute-start.2 = (bf16[448,1536]{1,0:T(8,128)(2,1)S(1)}, bf16[448,1536]{1,0:T(8,128)(2,1)S(1)}, u32[]{:S(2)}, u32[]{:S(2)}) collective-permute-start(bf16[448,1536]{1,0:T(8,128)(2,1)S(1)} %bitcast.22), channel_id=1, source_target_pairs={{0,3},{4,5},{1,0},{5,6},{2,1},{6,7},{3,2},{7,4},{8,11},{12,13},{9,... | collective-permute-start | bytes 4128776 | tf_op jit(solution)/shard_map/ppermute | solution.py:244
  51.9 43.5 %copy-start.2 = (bf16[1536,256]{1,0:T(8,128)(2,1)}, bf16[1536,256]{1,0:T(8,128)(2,1)S(1)}, u32[]{:S(2)}) copy-start(bf16[1536,256]{1,0:T(8,128)(2,1)S(1)} %collective-permute-done.9.rest_9_) | copy-start | bytes 2359300
  51.9 13.7 %collective-permute-start.10 = (bf16[1536,256]{1,0:T(8,128)(2,1)S(1)}, bf16[1536,256]{1,0:T(8,128)(2,1)S(1)}, u32[]{:S(2)}, u32[]{:S(2)}) collective-permute-start(bf16[1536,256]{1,0:T(8,128)(2,1)S(1)} %collective-permute-done.9.rest_9_), channel_id=1, source_target_pairs={{0,8},{4,60},{8,16},{12,4},{16,24},{20,12},{24,32},{28,20},{32,40}... | collective-permute-start | bytes 2359304 | tf_op jit(solution)/shard_map/ppermute | solution.py:244
  63.1 49.2 %copy-start.4 = (bf16[448,1536]{1,0:T(8,128)(2,1)}, bf16[448,1536]{1,0:T(8,128)(2,1)S(1)}, u32[]{:S(2)}) copy-start(bf16[448,1536]{1,0:T(8,128)(2,1)S(1)} %collective-permute-done.1.rest_2_) | copy-start | bytes 4128772
  63.1 17.6 %collective-permute-start.12 = (bf16[448,1536]{1,0:T(8,128)(2,1)S(1)}, bf16[448,1536]{1,0:T(8,128)(2,1)S(1)}, u32[]{:S(2)}, u32[]{:S(2)}) collective-permute-start(bf16[448,1536]{1,0:T(8,128)(2,1)S(1)} %collective-permute-done.1.rest_2_), channel_id=1, source_target_pairs={{0,1},{4,7},{1,2},{5,4},{2,3},{6,5},{3,0},{7,6},{8,9},{12,15},{9,1... | collective-permute-start | bytes 4128776 | tf_op jit(solution)/shard_map/ppermute | solution.py:244
  65.5 29.8 %copy-start.3 = (bf16[1536,256]{1,0:T(8,128)(2,1)}, bf16[1536,256]{1,0:T(8,128)(2,1)S(1)}, u32[]{:S(2)}) copy-start(bf16[1536,256]{1,0:T(8,128)(2,1)S(1)} %collective-permute-done.10.rest_10_) | copy-start | bytes 2359300
  65.5 29.1 %collective-permute-start.11 = (bf16[1536,256]{1,0:T(8,128)(2,1)S(1)}, bf16[1536,256]{1,0:T(8,128)(2,1)S(1)}, u32[]{:S(2)}, u32[]{:S(2)}) collective-permute-start(bf16[1536,256]{1,0:T(8,128)(2,1)S(1)} %collective-permute-done.10.rest_10_), channel_id=1, source_target_pairs={{0,8},{4,60},{8,16},{12,4},{16,24},{20,12},{24,32},{28,20},{32,40}... | collective-permute-start | bytes 2359304 | tf_op jit(solution)/shard_map/ppermute | solution.py:244
  70.6 24.9 %collective-permute-start = (bf16[448,1536]{1,0:T(8,128)(2,1)S(1)}, bf16[448,1536]{1,0:T(8,128)(2,1)S(1)}, u32[]{:S(2)}, u32[]{:S(2)}) collective-permute-start(bf16[448,1536]{1,0:T(8,128)(2,1)S(1)} %bitcast.23), channel_id=1, source_target_pairs={{0,4},{4,0},{1,5},{5,1},{2,6},{6,2},{3,7},{7,3},{8,12},{12,8},{9,1... | collective-permute-start | bytes 4128776 | tf_op jit(solution)/shard_map/ppermute | solution.py:248
  70.7 28.5 %collective-permute-start.4 = (bf16[448,1536]{1,0:T(8,128)(2,1)S(1)}, bf16[448,1536]{1,0:T(8,128)(2,1)S(1)}, u32[]{:S(2)}, u32[]{:S(2)}) collective-permute-start(bf16[448,1536]{1,0:T(8,128)(2,1)S(1)} %collective-permute-done.1.rest_2_), channel_id=1, source_target_pairs={{0,4},{4,0},{1,5},{5,1},{2,6},{6,2},{3,7},{7,3},{8,12},{12,8},{9,1... | collective-permute-start | bytes 4128776 | tf_op jit(solution)/shard_map/ppermute | solution.py:248
  71.2 41.2 %copy-start.5 = (bf16[448,1536]{1,0:T(8,128)(2,1)}, bf16[448,1536]{1,0:T(8,128)(2,1)S(1)}, u32[]{:S(2)}) copy-start(bf16[448,1536]{1,0:T(8,128)(2,1)S(1)} %collective-permute-done.2.rest_4_) | copy-start | bytes 4128772
  71.2 28.0 %collective-permute-start.3 = (bf16[448,1536]{1,0:T(8,128)(2,1)S(1)}, bf16[448,1536]{1,0:T(8,128)(2,1)S(1)}, u32[]{:S(2)}, u32[]{:S(2)}) collective-permute-start(bf16[448,1536]{1,0:T(8,128)(2,1)S(1)} %collective-permute-done.2.rest_4_), channel_id=1, source_target_pairs={{0,4},{4,0},{1,5},{5,1},{2,6},{6,2},{3,7},{7,3},{8,12},{12,8},{9,1... | collective-permute-start | bytes 4128776 | tf_op jit(solution)/shard_map/ppermute | solution.py:248
  80.7 31.7 %copy-start.6 = (bf16[448,1536]{1,0:T(8,128)(2,1)}, bf16[448,1536]{1,0:T(8,128)(2,1)S(1)}, u32[]{:S(2)}) copy-start(bf16[448,1536]{1,0:T(8,128)(2,1)S(1)} %collective-permute-done.12.rest_6_) | copy-start | bytes 4128772
  94.6 0.9 copy-start.1
  94.6 17.7 %collective-permute-start.13 = (bf16[448,1536]{1,0:T(8,128)(2,1)S(1)}, bf16[448,1536]{1,0:T(8,128)(2,1)}, u32[]{:S(2)}, u32[]{:S(2)}) collective-permute-start(bf16[448,1536]{1,0:T(8,128)(2,1)S(1)} %collective-permute-done.12.rest_6_), channel_id=1, source_target_pairs={{0,4},{4,0},{1,5},{5,1},{2,6},{6,2},{3,7},{7,3},{8,12},{12,8},{9,1... | collective-permute-start | bytes 4128776 | tf_op jit(solution)/shard_map/ppermute | solution.py:248
  94.7 6.7 %collective-permute-start.15 = (bf16[768,256]{1,0:T(8,128)(2,1)S(1)}, bf16[768,256]{1,0:T(8,128)(2,1)S(1)}, u32[]{:S(2)}, u32[]{:S(2)}) collective-permute-start(bf16[768,256]{1,0:T(8,128)(2,1)S(1)} %slice.68), channel_id=1, source_target_pairs={{0,4},{4,0},{1,5},{5,1},{2,6},{6,2},{3,7},{7,3},{8,12},{12,8},{9,1... | collective-permute-start | bytes 1179656 | tf_op jit(solution)/shard_map/ppermute | solution.py:248
  95.5 16.8 %copy-start.7 = (bf16[448,1536]{1,0:T(8,128)(2,1)}, bf16[448,1536]{1,0:T(8,128)(2,1)S(1)}, u32[]{:S(2)}) copy-start(bf16[448,1536]{1,0:T(8,128)(2,1)S(1)} %collective-permute-done.rest_1_) | copy-start | bytes 4128772
  95.5 16.8 %collective-permute-start.14 = (bf16[768,256]{1,0:T(8,128)(2,1)S(1)}, bf16[768,256]{1,0:T(8,128)(2,1)S(1)}, u32[]{:S(2)}, u32[]{:S(2)}) collective-permute-start(bf16[768,256]{1,0:T(8,128)(2,1)S(1)} %get-tuple-element.24), channel_id=1, source_target_pairs={{0,8},{4,60},{8,16},{12,4},{16,24},{20,12},{24,32},{28,20},{32,40}... | collective-permute-start | bytes 1179656 | tf_op jit(solution)/shard_map/ppermute | solution.py:244
  99.2 1.1 copy-start.8
  99.2 13.1 %collective-permute-start.17 = (bf16[768,256]{1,0:T(8,128)(2,1)S(1)}, bf16[768,256]{1,0:T(8,128)(2,1)S(1)}, u32[]{:S(2)}, u32[]{:S(2)}) collective-permute-start(bf16[768,256]{1,0:T(8,128)(2,1)S(1)} %get-tuple-element.23), channel_id=1, source_target_pairs={{0,4},{4,0},{1,5},{5,1},{2,6},{6,2},{3,7},{7,3},{8,12},{12,8},{9,1... | collective-permute-start | bytes 1179656 | tf_op jit(solution)/shard_map/ppermute | solution.py:248
  100.3 1.1 copy-start.9
  100.3 12.0 %collective-permute-start.16 = (bf16[768,256]{1,0:T(8,128)(2,1)S(1)}, bf16[768,256]{1,0:T(8,128)(2,1)S(1)}, u32[]{:S(2)}, u32[]{:S(2)}) collective-permute-start(bf16[768,256]{1,0:T(8,128)(2,1)S(1)} %slice.69), channel_id=1, source_target_pairs={{0,4},{4,0},{1,5},{5,1},{2,6},{6,2},{3,7},{7,3},{8,12},{12,8},{9,1... | collective-permute-start | bytes 1179656 | tf_op jit(solution)/shard_map/ppermute | solution.py:248
  101.4 10.9 %copy-start.11 = (bf16[768,256]{1,0:T(8,128)(2,1)}, bf16[768,256]{1,0:T(8,128)(2,1)S(1)}, u32[]{:S(2)}) copy-start(bf16[768,256]{1,0:T(8,128)(2,1)S(1)} %collective-permute-done.15.rest_13_) | copy-start | bytes 1179652
  112.3 0.8 copy-start.12
  112.3 0.9 copy-start.13
  112.3 1.1 copy-start.14
  125.9 29.2 %all-to-all-start.1 = ((bf16[64,24,256]{2,1,0:T(8,128)(2,1)}), bf16[64,24,256]{2,1,0:T(8,128)(2,1)S(1)}, u32[]{:S(2)}, u32[]{:S(2)}) async-start(bf16[64,24,256]{2,1,0:T(8,128)(2,1)} %bitcast.24), calls=%async_computation.1 | async-start | bytes 1572864 | tf_op jit(solution)/shard_map/all_to_all | solution.py:310
  155.1 6.3 %copy-start.17 = (s32[64]{0:T(128)S(1)}, s32[64]{0:T(128)}, u32[]{:S(2)}) copy-start(s32[64]{0:T(128)} %param.13) | copy-start | bytes 772
  155.1 46.1 %all-to-all-start = ((bf16[64,24,512]{2,1,0:T(8,128)(2,1)}), bf16[64,24,512]{2,1,0:T(8,128)(2,1)S(1)}, u32[]{:S(2)}, u32[]{:S(2)}) async-start(bf16[64,24,512]{2,1,0:T(8,128)(2,1)} %bitcast.28), calls=%async_computation | async-start | bytes 3145728 | tf_op jit(solution)/shard_map/all_to_all | solution.py:310
Sparse Core Ops, SparseCore 0:
  20.0 94.4 all-gather.1

commit v6 on v5

--- a/solution.py
+++ b/solution.py
@@ -11,7 +11,7 @@
 HD = 64
 MAXB = 6
 USED = 224
-FIRST = 256
+FIRST = 384
 GRID = (4, 8, 2)
 PLANE = ("y", "z", "core")
 BF16 = jnp.bfloat16
@@ -59,11 +59,15 @@
     )(counts[None], table[None], jnp.transpose(pool, (1, 0, 2)))
 
 
-def piece_table(ny, nz):
+def piece_table(ny, nz, part):
     assert (ny, nz) == (4, 8)
     dys = (0, -1, 1, -2)
-    table = [(s, j, dy, -s) for s in range(5) for j, dy in enumerate(dys)]
-    return table + [(4 + s, j, -dy, s) for s in range(1, 4) for j, dy in enumerate(dys)]
+    dzs = (0, -1, -2, -3, 1, 2, 3, -4)
+    if part == 0:
+        table = [(s, j, dy, -s) for s in range(5) for j, dy in enumerate(dys)]
+        return table + [(4 + s, j, -dy, s) for s in range(1, 4) for j, dy in enumerate(dys)]
+    table = [(s, j, -s, dz) for s in range(3) for j, dz in enumerate(dzs)]
+    return table + [(3, j, 1, -dz) for j, dz in enumerate(dzs)]
 
 
 def project_kernel(dims, counts_ref, *rest):
@@ -78,21 +82,16 @@
     feats = w_ref.shape[0] // nh
 
     w_copies, x_copies = [], []
-    if len(pieces) == 1:
-        for k in range(nh):
-            part = pl.ds(k * feats, feats)
-            w_copies.append(pltpu.make_async_copy(pieces[0].at[part], w_ref.at[part], w_sem.at[k]))
-    else:
-        for k, (src, part, dy, dz) in enumerate(piece_table(ny, nz)):
-            chip = lax.rem(y + dy * sign + ny, ny) * nz + lax.rem(z + dz * sign + nz, nz)
-            at = pl.multiple_of(chip * shard, shard)
-            w_copies.append(
-                pltpu.make_async_copy(
-                    pieces[src].at[pl.ds(part * shard, shard)],
-                    w_ref.at[pl.ds(at, shard)],
-                    w_sem.at[k],
-                )
+    for k, (src, part, dy, dz) in enumerate(piece_table(ny, nz, 0 if len(pieces) == nz else 1)):
+        chip = lax.rem(y + dy * sign + ny, ny) * nz + lax.rem(z + dz * sign + nz, nz)
+        at = pl.multiple_of(chip * shard, shard)
+        w_copies.append(
+            pltpu.make_async_copy(
+                pieces[src].at[pl.ds(part * shard, shard)],
+                w_ref.at[pl.ds(at, shard)],
+                w_sem.at[k],
             )
+        )
     for k in range(2 * nh):
         who = core if k % 2 == 0 else 1 - core
         x_copies.append(
@@ -253,8 +252,10 @@
     return x[:half], x[half:]
 
 
+hold = lax.optimization_barrier
+
+
 def gather(key_weight, value_weight, rows_of):
-    hold = lax.optimization_barrier
     upper = lax.axis_index("core") == 0
     mine = jnp.where(upper, key_weight, value_weight)
     other = jnp.where(upper, value_weight, key_weight)
@@ -266,10 +267,10 @@
         return jnp.where(upper, jnp.concatenate([a, b]), jnp.concatenate([b, a]))
 
     chip_mine = chip(mine, near[:n])
-    second = lax.all_gather(chip_mine[:, FIRST:], ("y", "z"), axis=0, tiled=True)
-
+    chip_other = chip(other, near[n:])
     n = 2 * n
-    own = jnp.concatenate([chip_mine[:, :FIRST], chip(other, near[n // 2 :])[:, :FIRST]])
+    own = jnp.concatenate([chip_mine[:, :FIRST], chip_other[:, :FIRST]])
+    own_b = jnp.concatenate([chip_mine[:, FIRST:], chip_other[:, FIRST:]])
     behind = ring_step(rows, "head")
     ahead = ring_step(rows, "head", -1)
     y1 = ring_step(own, "y")
@@ -278,19 +279,32 @@
     group = jnp.concatenate(
         [own[:n], y1[:n], got[n : 2 * n], y2, own[n:], y1[n:], got[:n], got[2 * n :]]
     )
-    z1 = ring_step(group, "z")
-    z2 = ring_step(z1, "z")
-    z2, z1 = hold((z2, z1))
-    z3 = ring_step(z2, "z")
+    r1 = ring_step(own_b, "z")
+    r2 = ring_step(r1, "z")
+    m = group.shape[0]
+    z1 = ring_step(jnp.concatenate([group, r2]), "z")
+    r3 = z1[m:]
+    z2 = ring_step(z1[: m + n], "z")
+    z2, behind, ahead = hold((z2, behind, ahead))
+    r4 = z2[m:]
+    got = swap_cores(jnp.concatenate([r1, r2, r3, r4]))
+    ring = [own_b, r1, r2, r3]
+    line = jnp.concatenate(
+        [t[:n] for t in ring]
+        + [got[(2 * k + 1) * n : (2 * k + 2) * n] for k in range(3)]
+        + [r4]
+        + [t[n:] for t in ring]
+        + [got[2 * k * n : (2 * k + 1) * n] for k in range(3)]
+        + [got[6 * n :]]
+    )
+    z3 = ring_step(z2[:m], "z")
     opposite = ring_step(behind, "head")
-    across = [swap_cores(kinds(z1)[1])]
-    near_rows = [swap_cores(rows), swap_cores(ahead), swap_cores(behind)]
-    z3, z2, opposite = hold((z3, z2, opposite))
-    z4 = ring_step(kinds(z3)[0], "z")
-    across += [swap_cores(kinds(z2)[1]), swap_cores(kinds(z3)[1])]
-    near_rows.append(swap_cores(opposite))
+    l1 = ring_step(line, "y")
+    z4 = ring_step(z3[: m // 2], "z")
+    near_rows = [swap_cores(t) for t in (rows, ahead, behind, opposite)]
+    across = [swap_cores(t[m // 2 : m]) for t in (z1, z2, z3)]
     rows = [r for pair in zip((rows, behind, ahead, opposite), near_rows) for r in pair]
-    return rows, ([group, z1, z2, z3, z4] + across, [second])
+    return rows, [group, z1, z2, z3, z4] + across, (line, l1)
 
 
 def per_device(queries, new_keys, new_values, pool, block_table, block_counts, key_weight, value_weight):
@@ -299,20 +313,25 @@
         live = live_rows(block_counts, block_table, pool)
         return live.reshape(-1, live.shape[2])
 
-    rows, parts = gather(key_weight, value_weight, rows_of)
+    rows, first, (line, l1) = gather(key_weight, value_weight, rows_of)
     dims = (ny, nz, nh, 2 * key_weight.shape[0])
     convs = block_counts.shape[0]
     count = lax.dynamic_slice(block_counts, (lax.axis_index(PLANE),), (1,))
-    out = None
-    for pieces in parts:
-        sent = project(block_counts, rows, pieces, dims)
+
+    def move(sent):
         sent = sent.reshape(convs, -1, sent.shape[1])
         got = lax.all_to_all(sent, PLANE, split_axis=0, concat_axis=0, tiled=True)
         got = got.reshape(convs // 2, 2, got.shape[1], got.shape[2])
-        keys = got[:, 0].reshape(-1, got.shape[3])
-        values = got[:, 1].reshape(-1, got.shape[3])
-        out = attend(count, queries[0], keys, values, new_keys[0], new_values[0], out)
-    return out[None]
+        return got[:, 0].reshape(-1, got.shape[3]), got[:, 1].reshape(-1, got.shape[3])
+
+    sent = project(block_counts, rows, first, dims)
+    _, l1 = hold((sent, l1))
+    keys, values = move(sent)
+    l2 = ring_step(kinds(l1)[0], "y")
+    second = [line, l1, l2, swap_cores(kinds(l1)[1])]
+    out = attend(count, queries[0], keys, values, new_keys[0], new_values[0])
+    keys, values = move(project(block_counts, rows, second, dims))
+    return attend(count, queries[0], keys, values, new_keys[0], new_values[0], out)[None]
 
 
 def solution(mesh):

time: 216 us -> 241 us (1.12)
  starting transfers between devices: 43.1 us -> 64.1 us
  between operations: 13.7 us -> 0.36 us
  local copies, waits for them, and re-layouts: 11 us -> 23.1 us
  waiting for transfers between devices: 106 us -> 109 us
    all_to_all x2, waiting for transfers between devices: 41.9 us -> 24.6 us  [move(): got = lax.all_to_all(sent, PLANE, split_axis=0, concat_axis=0, tiled=True)]
    ppermute x9 -> x13, waiting for transfers between devices: 61.9 us -> 78.7 us  [ring_step(): return lax.ppermute(x, order, perm)]
    unnamed x44 -> x66, local copies, waits for them, and re-layouts: 6.76 us -> 17.4 us
    ppermute x9 -> x11, starting transfers between devices: 9.23 us -> 17 us  [swap_cores(): return lax.ppermute(x, 'core', [(0, 1), (1, 0)])]
    all_to_all x2, starting transfers between devices: 12.5 us -> 19.3 us  [move(): got = lax.all_to_all(sent, PLANE, split_axis=0, concat_axis=0, tiled=True)]
    ppermute x9 -> x13, starting transfers between devices: 21.3 us -> 27.7 us  [ring_step(): return lax.ppermute(x, order, perm)]
    ppermute x9 -> x11, waiting for transfers between devices: 1.69 us -> 5.9 us  [swap_cores(): return lax.ppermute(x, 'core', [(0, 1), (1, 0)])]
  transfers between devices with their start and end apart: 21 -> 26, of which waited for: 12 -> 15; matrix products, arithmetic and copies ran while one was open for 1% -> 5% of each run, Pallas kernels for 15% -> 14%
where the time goes in v6:
time: 241 us; the launch traced here: 240 us
  waiting for transfers between devices  109 us (45%)
  starting transfers between devices  64.1 us (27%)
  Pallas kernels  43.2 us (18%)
  local copies, waits for them, and re-layouts  23.1 us (10%)
    ppermute x13, waiting for transfers between devices, ring_step(): return lax.ppermute(x, order, perm)  78.7 us
    pallas_call x2, Pallas kernels, project(): pl.pallas_call(functools.partial(project_kernel, dims), out_shape=jax.Sha...  29.2 us
    ppermute x13, starting transfers between devices, ring_step(): return lax.ppermute(x, order, perm)  27.7 us
    all_to_all x2, waiting for transfers between devices, move(): got = lax.all_to_all(sent, PLANE, split_axis=0, concat_axis=0, tiled=True)  24.6 us
    all_to_all x2, starting transfers between devices, move(): got = lax.all_to_all(sent, PLANE, split_axis=0, concat_axis=0, tiled=True)  19.3 us
    unnamed x66, local copies, waits for them, and re-layouts  17.4 us
    ppermute x11, starting transfers between devices, swap_cores(): return lax.ppermute(x, 'core', [(0, 1), (1, 0)])  17 us
    pallas_call x2, Pallas kernels, attend(): pl.pallas_call(functools.partial(attend_kernel, first), out_shape=jax.Sha...  10 us
  transfers between devices with their start and end apart: 26, of which 15 were waited for; matrix products, arithmetic and copies ran while one was open for 5% of the time, Pallas kernels for 14%

profile of v6, /device:TPU:1, one launch (start us, length us, event | category | flops | bytes accessed | tf_op | source)
XLA Modules:
  0.0 240.4 jit_solution(10780569466522478987)
XLA Ops:
  0.0 1.2 broadcast_in_dim.12.table_ref
  1.2 3.4 %copy.12 = bf16[384,2,1536]{2,0,1:T(8,128)(2,1)} copy(bf16[384,2,1536]{2,1,0:T(2,128)(2,1)} %param.11) | data formatting | bytes 4718592 | tf_op args[3]
  4.7 4.0 %live_rows.1 = bf16[2,224,1536]{2,1,0:T(8,128)(2,1)} custom-call(s32[1,64]{1,0:T(1,128)} %bitcast.37, s32[1,384]{1,0:T(1,128)} %broadcast_in_dim.12.table_ref, bf16[2,384,1536]{2,1,0:T(8,128)(2,1)} %bitcast.22), custom_call_target="tpu_custom_call" | custom-call | tf_op jit(solution)/shard_map/live_rows/pallas_call | solution.py:52
  8.7 3.2 %collective-permute-start.1 = (bf16[192,768]{1,0:T(8,128)(2,1)S(1)}, bf16[192,768]{1,0:T(8,128)(2,1)S(1)}, u32[]{:S(2)}, u32[]{:S(2)}) collective-permute-start(bf16[192,768]{1,0:T(8,128)(2,1)S(1)} %pad_maximum_fusion.3), channel_id=1, source_target_pairs={{0,4},{4,0},{1,5},{5,1},{2,6},{6,2},{3,7},{7,3},{8,12},{12,8},{9,1... | collective-permute-start | bytes 884744 | tf_op jit(solution)/shard_map/ppermute | solution.py:247
  11.9 1.2 collective-permute-done.1
  13.4 0.7 constant_dynamic-update-slice_fusion.11
  14.1 1.1 collective-permute-start.2
  15.2 4.9 %collective-permute-done.2 = bf16[384,384]{1,0:T(8,128)(2,1)S(1)} collective-permute-done((bf16[384,384]{1,0:T(8,128)(2,1)S(1)}, bf16[384,384]{1,0:T(8,128)(2,1)S(1)}, u32[]{:S(2)}, u32[]{:S(2)}) %collective-permute-start.2) | collective-permute-done | bytes 294944 | tf_op jit(solution)/shard_map/ppermute | solution.py:243
  20.1 2.0 collective-permute-start.3
  22.1 2.1 collective-permute-done.3
  24.3 4.9 %collective-permute-start.4 = (bf16[576,384]{1,0:T(8,128)(2,1)S(1)}, bf16[576,384]{1,0:T(8,128)(2,1)S(1)}, u32[]{:S(2)}, u32[]{:S(2)}) collective-permute-start(bf16[576,384]{1,0:T(8,128)(2,1)S(1)} %pad_maximum_fusion.1), channel_id=1, source_target_pairs={{0,4},{4,0},{1,5},{5,1},{2,6},{6,2},{3,7},{7,3},{8,12},{12,8},{9,1... | collective-permute-start | bytes 1327112 | tf_op jit(solution)/shard_map/ppermute | solution.py:247
  29.1 1.4 collective-permute-done.4
  30.8 3.9 %collective-permute-start.5 = (bf16[384,384]{1,0:T(8,128)(2,1)S(1)}, bf16[384,384]{1,0:T(8,128)(2,1)S(1)}, u32[]{:S(2)}, u32[]{:S(2)}) collective-permute-start(bf16[384,384]{1,0:T(8,128)(2,1)S(1)} %pad_maximum_fusion.6), channel_id=1, source_target_pairs={{0,8},{4,60},{8,16},{12,4},{16,24},{20,12},{24,32},{28,20},{32,40}... | collective-permute-start | bytes 884744 | tf_op jit(solution)/shard_map/ppermute | solution.py:243
  34.7 3.6 %collective-permute-done.5 = bf16[384,384]{1,0:T(8,128)(2,1)S(1)} collective-permute-done((bf16[384,384]{1,0:T(8,128)(2,1)S(1)}, bf16[384,384]{1,0:T(8,128)(2,1)S(1)}, u32[]{:S(2)}, u32[]{:S(2)}) %collective-permute-start.5) | collective-permute-done | bytes 294944 | tf_op jit(solution)/shard_map/ppermute | solution.py:243
  38.4 3.1 %collective-permute-start.6 = (bf16[384,384]{1,0:T(8,128)(2,1)S(1)}, bf16[384,384]{1,0:T(8,128)(2,1)S(1)}, u32[]{:S(2)}, u32[]{:S(2)}) collective-permute-start(bf16[384,384]{1,0:T(8,128)(2,1)S(1)} %collective-permute-done.5), channel_id=1, source_target_pairs={{0,8},{4,60},{8,16},{12,4},{16,24},{20,12},{24,32},{28,20},{32,40}... | collective-permute-start | bytes 884744 | tf_op jit(solution)/shard_map/ppermute | solution.py:243
  41.6 3.6 %collective-permute-done.6 = bf16[384,384]{1,0:T(8,128)(2,1)S(1)} collective-permute-done((bf16[384,384]{1,0:T(8,128)(2,1)S(1)}, bf16[384,384]{1,0:T(8,128)(2,1)S(1)}, u32[]{:S(2)}, u32[]{:S(2)}) %collective-permute-start.6) | collective-permute-done | bytes 294944 | tf_op jit(solution)/shard_map/ppermute | solution.py:243
  45.2 3.2 %collective-permute-start.7 = (bf16[1920,384]{1,0:T(8,128)(2,1)S(1)}, bf16[1920,384]{1,0:T(8,128)(2,1)S(1)}, u32[]{:S(2)}, u32[]{:S(2)}) collective-permute-start(bf16[1920,384]{1,0:T(8,128)(2,1)S(1)} %constant_dynamic-update-slice_fusion), channel_id=1, source_target_pairs={{0,8},{4,60},{8,16},{12,4},{16,24},{20,12},{24,32},{28,20},{32,40}... | collective-permute-start | bytes 4423688 | tf_op jit(solution)/shard_map/ppermute | solution.py:243
  48.4 1.2 collective-permute-start.10
  49.6 1.5 collective-permute-start.9
  51.1 13.6 %collective-permute-done.7.rest_9_ = bf16[1920,384]{1,0:T(8,128)(2,1)S(1)} collective-permute-done((bf16[1920,384]{1,0:T(8,128)(2,1)S(1)}, bf16[1920,384]{1,0:T(8,128)(2,1)S(1)}, u32[]{:S(2)}, u32[]{:S(2)}) %collective-permute-start.7) | collective-permute-done | bytes 1474592 | tf_op jit(solution)/shard_map/ppermute | solution.py:243
  64.8 3.5 %collective-permute-start.8 = (bf16[1728,384]{1,0:T(8,128)(2,1)S(1)}, bf16[1728,384]{1,0:T(8,128)(2,1)S(1)}, u32[]{:S(2)}, u32[]{:S(2)}) collective-permute-start(bf16[1728,384]{1,0:T(8,128)(2,1)S(1)} %slice.166), channel_id=1, source_target_pairs={{0,8},{4,60},{8,16},{12,4},{16,24},{20,12},{24,32},{28,20},{32,40}... | collective-permute-start | bytes 3981320 | tf_op jit(solution)/shard_map/ppermute | solution.py:243
  68.4 10.3 %collective-permute-done.10.rest_4_ = bf16[448,1536]{1,0:T(8,128)(2,1)S(1)} collective-permute-done((bf16[448,1536]{1,0:T(8,128)(2,1)S(1)}, bf16[448,1536]{1,0:T(8,128)(2,1)S(1)}, u32[]{:S(2)}, u32[]{:S(2)}) %collective-permute-start.10) | collective-permute-done | bytes 1376288 | tf_op jit(solution)/shard_map/ppermute | solution.py:243
  78.7 2.3 collective-permute-done.9.rest_2_
  81.0 2.1 collective-permute-done.8.rest_10_
  83.2 4.9 %collective-permute-start.15 = (bf16[1344,384]{1,0:T(8,128)(2,1)S(1)}, bf16[1344,384]{1,0:T(8,128)(2,1)S(1)}, u32[]{:S(2)}, u32[]{:S(2)}) collective-permute-start(bf16[1344,384]{1,0:T(8,128)(2,1)S(1)} %pad_maximum_fusion), channel_id=1, source_target_pairs={{0,4},{4,0},{1,5},{5,1},{2,6},{6,2},{3,7},{7,3},{8,12},{12,8},{9,1... | collective-permute-start | bytes 3096584 | tf_op jit(solution)/shard_map/ppermute | solution.py:247
  88.9 0.7 slice_dynamic-update-slice_fusion.11
  91.4 2.5 %collective-permute-start.13 = (bf16[448,1536]{1,0:T(8,128)(2,1)S(1)}, bf16[448,1536]{1,0:T(8,128)(2,1)S(1)}, u32[]{:S(2)}, u32[]{:S(2)}) collective-permute-start(bf16[448,1536]{1,0:T(8,128)(2,1)S(1)} %collective-permute-done.9.rest_2_), channel_id=1, source_target_pairs={{0,1},{4,7},{1,2},{5,4},{2,3},{6,5},{3,0},{7,6},{8,9},{12,15},{9,1... | collective-permute-start | bytes 4128776 | tf_op jit(solution)/shard_map/ppermute | solution.py:243
  95.2 0.7 slice_dynamic-update-slice_fusion.7
  95.9 0.7 constant_dynamic-update-slice_fusion.6
  102.4 6.8 %collective-permute-done.13.rest_6_ = bf16[448,1536]{1,0:T(8,128)(2,1)S(1)} collective-permute-done((bf16[448,1536]{1,0:T(8,128)(2,1)S(1)}, bf16[448,1536]{1,0:T(8,128)(2,1)S(1)}, u32[]{:S(2)}, u32[]{:S(2)}) %collective-permute-start.13) | collective-permute-done | bytes 1376288 | tf_op jit(solution)/shard_map/ppermute | solution.py:243
  109.1 2.2 collective-permute-start.14
  111.7 3.3 %collective-permute-done.19.rest_14_ = bf16[768,384]{1,0:T(8,128)(2,1)S(1)} collective-permute-done((bf16[768,384]{1,0:T(8,128)(2,1)S(1)}, bf16[768,384]{1,0:T(8,128)(2,1)S(1)}, u32[]{:S(2)}, u32[]{:S(2)}) %collective-permute-start.19) | collective-permute-done | bytes 589856 | tf_op jit(solution)/shard_map/ppermute | solution.py:247
  115.3 2.5 %collective-permute-start.17 = (bf16[768,384]{1,0:T(8,128)(2,1)S(1)}, bf16[768,384]{1,0:T(8,128)(2,1)S(1)}, u32[]{:S(2)}, u32[]{:S(2)}) collective-permute-start(bf16[768,384]{1,0:T(8,128)(2,1)S(1)} %get-tuple-element.24), channel_id=1, source_target_pairs={{0,8},{4,60},{8,16},{12,4},{16,24},{20,12},{24,32},{28,20},{32,40}... | collective-permute-start | bytes 1769480 | tf_op jit(solution)/shard_map/ppermute | solution.py:243
  117.9 6.8 %collective-permute-done.17.rest_12_ = bf16[768,384]{1,0:T(8,128)(2,1)S(1)} collective-permute-done((bf16[768,384]{1,0:T(8,128)(2,1)S(1)}, bf16[768,384]{1,0:T(8,128)(2,1)S(1)}, u32[]{:S(2)}, u32[]{:S(2)}) %collective-permute-start.17) | collective-permute-done | bytes 589856 | tf_op jit(solution)/shard_map/ppermute | solution.py:243
  124.7 1.1 copy-done.10
  125.9 14.6 %project.2 = bf16[1536,384]{1,0:T(8,128)(2,1)} custom-call(s32[1,64]{1,0:T(1,128)} %bitcast.38, bf16[448,1536]{1,0:T(8,128)(2,1)} %bitcast.17, bf16[448,1536]{1,0:T(8,128)(2,1)} %copy-done.6, bf16[448,1536]{1,0:T(8,128)(2,1)} %copy-done.5, bf16[448,1536]{1,0:T(8,128)(2,1)} %copy-done.7, bf16[448,1536]{1,0:T(8,128)(2,1)} %copy-done.4, ...), custom_call_target="tpu_custom_call" | custom-call | flops 4227858432 | bytes 15728640 | tf_op jit(solution)/shard_map/project/pallas_call | solution.py:164
  140.5 8.5 %all-to-all-start.1 = ((bf16[64,24,384]{2,1,0:T(8,128)(2,1)}), bf16[64,24,384]{2,1,0:T(8,128)(2,1)S(1)}, u32[]{:S(2)}, u32[]{:S(2)}) async-start(bf16[64,24,384]{2,1,0:T(8,128)(2,1)} %bitcast.24), calls=%async_computation.1 | async-start | bytes 2359296 | tf_op jit(solution)/shard_map/all_to_all | solution.py:323
  149.3 1.2 copy-done.2
  151.0 2.7 %collective-permute-start.22 = (bf16[1536,384]{1,0:T(8,128)(2,1)S(1)}, bf16[1536,384]{1,0:T(8,128)(2,1)S(1)}, u32[]{:S(2)}, u32[]{:S(2)}) collective-permute-start(bf16[1536,384]{1,0:T(8,128)(2,1)S(1)} %get-tuple-element.18), channel_id=1, source_target_pairs={{0,64},{4,196},{64,128},{68,4},{128,192},{132,68},{192,0},{196,132... | collective-permute-start | bytes 3538952 | tf_op jit(solution)/shard_map/ppermute | solution.py:243
  153.7 22.6 %collective-permute-done.22.rest_10_ = bf16[1536,384]{1,0:T(8,128)(2,1)S(1)} collective-permute-done((bf16[1536,384]{1,0:T(8,128)(2,1)S(1)}, bf16[1536,384]{1,0:T(8,128)(2,1)S(1)}, u32[]{:S(2)}, u32[]{:S(2)}) %collective-permute-start.22) | collective-permute-done | bytes 1179680 | tf_op jit(solution)/shard_map/ppermute | solution.py:243
  176.4 1.0 copy-done.14
  177.4 14.6 %project.3 = bf16[1536,384]{1,0:T(8,128)(2,1)} custom-call(s32[1,64]{1,0:T(1,128)} %bitcast.39, bf16[448,1536]{1,0:T(8,128)(2,1)} %bitcast.18, bf16[448,1536]{1,0:T(8,128)(2,1)} %copy-done.6, bf16[448,1536]{1,0:T(8,128)(2,1)} %copy-done.5, bf16[448,1536]{1,0:T(8,128)(2,1)} %copy-done.7, bf16[448,1536]{1,0:T(8,128)(2,1)} %copy-done.4, ...), custom_call_target="tpu_custom_call" | custom-call | flops 4227858432 | bytes 15728640 | tf_op jit(solution)/shard_map/project/pallas_call | solution.py:164
  192.0 10.8 %all-to-all-start = ((bf16[64,24,384]{2,1,0:T(8,128)(2,1)}), bf16[64,24,384]{2,1,0:T(8,128)(2,1)S(1)}, u32[]{:S(2)}, u32[]{:S(2)}) async-start(bf16[64,24,384]{2,1,0:T(8,128)(2,1)} %bitcast.23), calls=%async_computation | async-start | bytes 2359296 | tf_op jit(solution)/shard_map/all_to_all | solution.py:323
  203.4 1.2 fusion.3
  204.6 5.0 %attend.2.rest_0_ = bf16[128,384]{1,0:T(8,128)(2,1)} custom-call(s32[1]{0:T(128)} %dynamic_slice.3.live_ref, bf16[128,768]{1,0:T(8,128)(2,1)} %bitcast.31, bf16[768,384]{1,0:T(8,128)(2,1)} %bitcast.30, bf16[768,384]{1,0:T(8,128)(2,1)} %bitcast.29, bf16[128,768]{1,0:T(8,128)(2,1)} %bitcast.33, bf16[128,768]{1,0:T(8,128)(2,1)} %bitcast.35), custom_call_target="tpu_custom_call" | custom-call | tf_op jit(solution)/shard_map/attend/pallas_call | solution.py:225
  209.5 24.6 %all-to-all-done = bf16[64,24,384]{2,1,0:T(8,128)(2,1)S(1)} async-done(((bf16[64,24,384]{2,1,0:T(8,128)(2,1)}), bf16[64,24,384]{2,1,0:T(8,128)(2,1)S(1)}, u32[]{:S(2)}, u32[]{:S(2)}) %all-to-all-start) | async-done | bytes 1179680 | tf_op jit(solution)/shard_map/all_to_all | solution.py:323
  234.2 1.2 fusion.4
  235.3 5.0 %attend.3 = bf16[128,768]{1,0:T(8,128)(2,1)} custom-call(s32[1]{0:T(128)} %dynamic_slice.3.live_ref, bf16[128,768]{1,0:T(8,128)(2,1)} %bitcast.32, bf16[768,384]{1,0:T(8,128)(2,1)} %bitcast.28, bf16[768,384]{1,0:T(8,128)(2,1)} %bitcast.27, bf16[128,768]{1,0:T(8,128)(2,1)} %bitcast.34, bf16[128,768]{1,0:T(8,128)(2,1)} %bitcast.36, bf16[128,384]{1,0:T(8,128)(2,1)} %attend.2.rest_0_), custom_call_target="tpu_custom_call" | custom-call | tf_op jit(solution)/shard_map/attend/pallas_call | solution.py:225
  (99 shorter events, 12.9 us)
Async XLA Ops:
  1.2 3.4 %copy-start.19 = (bf16[96,768]{1,0:T(8,128)(2,1)S(1)}, bf16[96,768]{1,0:T(8,128)(2,1)}, u32[]{:S(2)}) copy-start(bf16[96,768]{1,0:T(8,128)(2,1)} %param.15) | copy-start | bytes 442372
  1.2 3.4 %copy-start.20 = (bf16[96,768]{1,0:T(8,128)(2,1)S(1)}, bf16[96,768]{1,0:T(8,128)(2,1)}, u32[]{:S(2)}) copy-start(bf16[96,768]{1,0:T(8,128)(2,1)} %param.14) | copy-start | bytes 442372
  8.7 4.5 %collective-permute-start.1 = (bf16[192,768]{1,0:T(8,128)(2,1)S(1)}, bf16[192,768]{1,0:T(8,128)(2,1)S(1)}, u32[]{:S(2)}, u32[]{:S(2)}) collective-permute-start(bf16[192,768]{1,0:T(8,128)(2,1)S(1)} %pad_maximum_fusion.3), channel_id=1, source_target_pairs={{0,4},{4,0},{1,5},{5,1},{2,6},{6,2},{3,7},{7,3},{8,12},{12,8},{9,1... | collective-permute-start | bytes 884744 | tf_op jit(solution)/shard_map/ppermute | solution.py:247
  14.1 5.9 %collective-permute-start.2 = (bf16[384,384]{1,0:T(8,128)(2,1)S(1)}, bf16[384,384]{1,0:T(8,128)(2,1)S(1)}, u32[]{:S(2)}, u32[]{:S(2)}) collective-permute-start(bf16[384,384]{1,0:T(8,128)(2,1)S(1)} %pad_maximum_fusion.5), channel_id=1, source_target_pairs={{0,64},{4,196},{64,128},{68,4},{128,192},{132,68},{192,0},{196,132... | collective-permute-start | bytes 884744 | tf_op jit(solution)/shard_map/ppermute | solution.py:243
  20.1 4.1 %collective-permute-start.3 = (bf16[192,384]{1,0:T(8,128)(2,1)S(1)}, bf16[192,384]{1,0:T(8,128)(2,1)S(1)}, u32[]{:S(2)}, u32[]{:S(2)}) collective-permute-start(bf16[192,384]{1,0:T(8,128)(2,1)S(1)} %get-tuple-element.38), channel_id=1, source_target_pairs={{0,64},{4,196},{64,128},{68,4},{128,192},{132,68},{192,0},{196,132... | collective-permute-start | bytes 442376 | tf_op jit(solution)/shard_map/ppermute | solution.py:243
  24.3 6.3 %collective-permute-start.4 = (bf16[576,384]{1,0:T(8,128)(2,1)S(1)}, bf16[576,384]{1,0:T(8,128)(2,1)S(1)}, u32[]{:S(2)}, u32[]{:S(2)}) collective-permute-start(bf16[576,384]{1,0:T(8,128)(2,1)S(1)} %pad_maximum_fusion.1), channel_id=1, source_target_pairs={{0,4},{4,0},{1,5},{5,1},{2,6},{6,2},{3,7},{7,3},{8,12},{12,8},{9,1... | collective-permute-start | bytes 1327112 | tf_op jit(solution)/shard_map/ppermute | solution.py:247
  30.7 17.7 %copy-start = (bf16[2,224,1536]{2,1,0:T(8,128)(2,1)S(1)}, bf16[2,224,1536]{2,1,0:T(8,128)(2,1)}, u32[]{:S(2)}) copy-start(bf16[2,224,1536]{2,1,0:T(8,128)(2,1)} %live_rows.1) | copy-start | bytes 4128772
  30.8 7.6 %collective-permute-start.5 = (bf16[384,384]{1,0:T(8,128)(2,1)S(1)}, bf16[384,384]{1,0:T(8,128)(2,1)S(1)}, u32[]{:S(2)}, u32[]{:S(2)}) collective-permute-start(bf16[384,384]{1,0:T(8,128)(2,1)S(1)} %pad_maximum_fusion.6), channel_id=1, source_target_pairs={{0,8},{4,60},{8,16},{12,4},{16,24},{20,12},{24,32},{28,20},{32,40}... | collective-permute-start | bytes 884744 | tf_op jit(solution)/shard_map/ppermute | solution.py:243
  38.4 6.8 %collective-permute-start.6 = (bf16[384,384]{1,0:T(8,128)(2,1)S(1)}, bf16[384,384]{1,0:T(8,128)(2,1)S(1)}, u32[]{:S(2)}, u32[]{:S(2)}) collective-permute-start(bf16[384,384]{1,0:T(8,128)(2,1)S(1)} %collective-permute-done.5), channel_id=1, source_target_pairs={{0,8},{4,60},{8,16},{12,4},{16,24},{20,12},{24,32},{28,20},{32,40}... | collective-permute-start | bytes 884744 | tf_op jit(solution)/shard_map/ppermute | solution.py:243
  41.6 23.3 %copy-start.12 = (bf16[1536,384]{1,0:T(8,128)(2,1)}, bf16[1536,384]{1,0:T(8,128)(2,1)S(1)}, u32[]{:S(2)}) copy-start(bf16[1536,384]{1,0:T(8,128)(2,1)S(1)} %get-tuple-element.25.rest_8_) | copy-start | bytes 3538948
  45.2 19.5 %collective-permute-start.7 = (bf16[1920,384]{1,0:T(8,128)(2,1)S(1)}, bf16[1920,384]{1,0:T(8,128)(2,1)S(1)}, u32[]{:S(2)}, u32[]{:S(2)}) collective-permute-start(bf16[1920,384]{1,0:T(8,128)(2,1)S(1)} %constant_dynamic-update-slice_fusion), channel_id=1, source_target_pairs={{0,8},{4,60},{8,16},{12,4},{16,24},{20,12},{24,32},{28,20},{32,40}... | collective-permute-start | bytes 4423688 | tf_op jit(solution)/shard_map/ppermute | solution.py:243
  48.4 30.3 %collective-permute-start.10 = (bf16[448,1536]{1,0:T(8,128)(2,1)S(1)}, bf16[448,1536]{1,0:T(8,128)(2,1)S(1)}, u32[]{:S(2)}, u32[]{:S(2)}) collective-permute-start(bf16[448,1536]{1,0:T(8,128)(2,1)S(1)} %bitcast.19), channel_id=1, source_target_pairs={{0,3},{4,5},{1,0},{5,6},{2,1},{6,7},{3,2},{7,4},{8,11},{12,13},{9,... | collective-permute-start | bytes 4128776 | tf_op jit(solution)/shard_map/ppermute | solution.py:243
  49.6 31.4 %collective-permute-start.9 = (bf16[448,1536]{1,0:T(8,128)(2,1)S(1)}, bf16[448,1536]{1,0:T(8,128)(2,1)S(1)}, u32[]{:S(2)}, u32[]{:S(2)}) collective-permute-start(bf16[448,1536]{1,0:T(8,128)(2,1)S(1)} %bitcast.20), channel_id=1, source_target_pairs={{0,1},{4,7},{1,2},{5,4},{2,3},{6,5},{3,0},{7,6},{8,9},{12,15},{9,1... | collective-permute-start | bytes 4128776 | tf_op jit(solution)/shard_map/ppermute | solution.py:243
  64.7 33.9 %copy-start.1 = (bf16[1920,384]{1,0:T(8,128)(2,1)}, bf16[1920,384]{1,0:T(8,128)(2,1)S(1)}, u32[]{:S(2)}) copy-start(bf16[1920,384]{1,0:T(8,128)(2,1)S(1)} %collective-permute-done.7.rest_9_) | copy-start | bytes 4423684
  64.8 18.2 %collective-permute-start.8 = (bf16[1728,384]{1,0:T(8,128)(2,1)S(1)}, bf16[1728,384]{1,0:T(8,128)(2,1)S(1)}, u32[]{:S(2)}, u32[]{:S(2)}) collective-permute-start(bf16[1728,384]{1,0:T(8,128)(2,1)S(1)} %slice.166), channel_id=1, source_target_pairs={{0,8},{4,60},{8,16},{12,4},{16,24},{20,12},{24,32},{28,20},{32,40}... | collective-permute-start | bytes 3981320 | tf_op jit(solution)/shard_map/ppermute | solution.py:243
  78.7 12.5 %copy-start.4 = (bf16[448,1536]{1,0:T(8,128)(2,1)}, bf16[448,1536]{1,0:T(8,128)(2,1)S(1)}, u32[]{:S(2)}) copy-start(bf16[448,1536]{1,0:T(8,128)(2,1)S(1)} %collective-permute-done.10.rest_4_) | copy-start | bytes 4128772
  81.0 21.3 %copy-start.5 = (bf16[448,1536]{1,0:T(8,128)(2,1)}, bf16[448,1536]{1,0:T(8,128)(2,1)S(1)}, u32[]{:S(2)}) copy-start(bf16[448,1536]{1,0:T(8,128)(2,1)S(1)} %collective-permute-done.9.rest_2_) | copy-start | bytes 4128772
  83.1 28.3 %copy-start.3 = (bf16[1728,384]{1,0:T(8,128)(2,1)}, bf16[1728,384]{1,0:T(8,128)(2,1)S(1)}, u32[]{:S(2)}) copy-start(bf16[1728,384]{1,0:T(8,128)(2,1)S(1)} %collective-permute-done.8.rest_10_) | copy-start | bytes 3981316
  83.2 8.2 %collective-permute-start.15 = (bf16[1344,384]{1,0:T(8,128)(2,1)S(1)}, bf16[1344,384]{1,0:T(8,128)(2,1)S(1)}, u32[]{:S(2)}, u32[]{:S(2)}) collective-permute-start(bf16[1344,384]{1,0:T(8,128)(2,1)S(1)} %pad_maximum_fusion), channel_id=1, source_target_pairs={{0,4},{4,0},{1,5},{5,1},{2,6},{6,2},{3,7},{7,3},{8,12},{12,8},{9,1... | collective-permute-start | bytes 3096584 | tf_op jit(solution)/shard_map/ppermute | solution.py:247
  88.1 13.8 %collective-permute-start = (bf16[448,1536]{1,0:T(8,128)(2,1)S(1)}, bf16[448,1536]{1,0:T(8,128)(2,1)S(1)}, u32[]{:S(2)}, u32[]{:S(2)}) collective-permute-start(bf16[448,1536]{1,0:T(8,128)(2,1)S(1)} %bitcast.21), channel_id=1, source_target_pairs={{0,4},{4,0},{1,5},{5,1},{2,6},{6,2},{3,7},{7,3},{8,12},{12,8},{9,1... | collective-permute-start | bytes 4128776 | tf_op jit(solution)/shard_map/ppermute | solution.py:247
  89.6 12.6 %collective-permute-start.18 = (bf16[768,384]{1,0:T(8,128)(2,1)S(1)}, bf16[768,384]{1,0:T(8,128)(2,1)S(1)}, u32[]{:S(2)}, u32[]{:S(2)}) collective-permute-start(bf16[768,384]{1,0:T(8,128)(2,1)S(1)} %slice.182), channel_id=1, source_target_pairs={{0,4},{4,0},{1,5},{5,1},{2,6},{6,2},{3,7},{7,3},{8,12},{12,8},{9,1... | collective-permute-start | bytes 1769480 | tf_op jit(solution)/shard_map/ppermute | solution.py:247
  90.9 20.5 %collective-permute-start.16 = (bf16[1536,384]{1,0:T(8,128)(2,1)S(1)}, bf16[1536,384]{1,0:T(8,128)(2,1)S(1)}, u32[]{:S(2)}, u32[]{:S(2)}) collective-permute-start(bf16[1536,384]{1,0:T(8,128)(2,1)S(1)} %slice.144), channel_id=1, source_target_pairs={{0,8},{4,60},{8,16},{12,4},{16,24},{20,12},{24,32},{28,20},{32,40}... | collective-permute-start | bytes 3538952 | tf_op jit(solution)/shard_map/ppermute | solution.py:243
  91.2 24.1 %collective-permute-start.11 = (bf16[448,1536]{1,0:T(8,128)(2,1)S(1)}, bf16[448,1536]{1,0:T(8,128)(2,1)S(1)}, u32[]{:S(2)}, u32[]{:S(2)}) collective-permute-start(bf16[448,1536]{1,0:T(8,128)(2,1)S(1)} %collective-permute-done.10.rest_4_), channel_id=1, source_target_pairs={{0,4},{4,0},{1,5},{5,1},{2,6},{6,2},{3,7},{7,3},{8,12},{12,8},{9,1... | collective-permute-start | bytes 4128776 | tf_op jit(solution)/shard_map/ppermute | solution.py:247
  91.4 17.7 %collective-permute-start.13 = (bf16[448,1536]{1,0:T(8,128)(2,1)S(1)}, bf16[448,1536]{1,0:T(8,128)(2,1)S(1)}, u32[]{:S(2)}, u32[]{:S(2)}) collective-permute-start(bf16[448,1536]{1,0:T(8,128)(2,1)S(1)} %collective-permute-done.9.rest_2_), channel_id=1, source_target_pairs={{0,1},{4,7},{1,2},{5,4},{2,3},{6,5},{3,0},{7,6},{8,9},{12,15},{9,1... | collective-permute-start | bytes 4128776 | tf_op jit(solution)/shard_map/ppermute | solution.py:243
  102.0 9.7 %copy-start.6 = (bf16[448,1536]{1,0:T(8,128)(2,1)}, bf16[448,1536]{1,0:T(8,128)(2,1)S(1)}, u32[]{:S(2)}) copy-start(bf16[448,1536]{1,0:T(8,128)(2,1)S(1)} %collective-permute-done.rest_1_) | copy-start | bytes 4128772
  102.0 47.1 %collective-permute-start.21 = (bf16[3072,384]{1,0:T(8,128)(2,1)}, bf16[3072,384]{1,0:T(8,128)(2,1)S(1)}, u32[]{:S(2)}, u32[]{:S(2)}) collective-permute-start(bf16[3072,384]{1,0:T(8,128)(2,1)} %slice_dynamic-update-slice_fusion.rest_8_), channel_id=1, source_target_pairs={{0,64},{4,196},{64,128},{68,4},{128,192},{132,68},{192,0},{196,132... | collective-permute-start | bytes 7077896 | tf_op jit(solution)/shard_map/ppermute | solution.py:243
  102.3 9.4 %copy-start.15 = (bf16[768,384]{1,0:T(8,128)(2,1)}, bf16[768,384]{1,0:T(8,128)(2,1)S(1)}, u32[]{:S(2)}) copy-start(bf16[768,384]{1,0:T(8,128)(2,1)S(1)} %collective-permute-done.18.rest_13_) | copy-start | bytes 1769476
  102.3 15.6 %collective-permute-start.12 = (bf16[448,1536]{1,0:T(8,128)(2,1)S(1)}, bf16[448,1536]{1,0:T(8,128)(2,1)S(1)}, u32[]{:S(2)}, u32[]{:S(2)}) collective-permute-start(bf16[448,1536]{1,0:T(8,128)(2,1)S(1)} %collective-permute-done.9.rest_2_), channel_id=1, source_target_pairs={{0,4},{4,0},{1,5},{5,1},{2,6},{6,2},{3,7},{7,3},{8,12},{12,8},{9,1... | collective-permute-start | bytes 4128776 | tf_op jit(solution)/shard_map/ppermute | solution.py:247
  109.1 2.5 %copy-start.8 = (bf16[448,1536]{1,0:T(8,128)(2,1)}, bf16[448,1536]{1,0:T(8,128)(2,1)S(1)}, u32[]{:S(2)}) copy-start(bf16[448,1536]{1,0:T(8,128)(2,1)S(1)} %collective-permute-done.13.rest_6_) | copy-start | bytes 4128772
  109.1 15.5 %collective-permute-start.14 = (bf16[448,1536]{1,0:T(8,128)(2,1)S(1)}, bf16[448,1536]{1,0:T(8,128)(2,1)S(1)}, u32[]{:S(2)}, u32[]{:S(2)}) collective-permute-start(bf16[448,1536]{1,0:T(8,128)(2,1)S(1)} %collective-permute-done.13.rest_6_), channel_id=1, source_target_pairs={{0,4},{4,0},{1,5},{5,1},{2,6},{6,2},{3,7},{7,3},{8,12},{12,8},{9,1... | collective-permute-start | bytes 4128776 | tf_op jit(solution)/shard_map/ppermute | solution.py:247
  111.4 14.4 %copy-start.11 = (bf16[1536,384]{1,0:T(8,128)(2,1)}, bf16[1536,384]{1,0:T(8,128)(2,1)S(1)}, u32[]{:S(2)}) copy-start(bf16[1536,384]{1,0:T(8,128)(2,1)S(1)} %collective-permute-done.16.rest_11_) | copy-start | bytes 3538948
  111.4 3.5 %collective-permute-start.19 = (bf16[768,384]{1,0:T(8,128)(2,1)S(1)}, bf16[768,384]{1,0:T(8,128)(2,1)S(1)}, u32[]{:S(2)}, u32[]{:S(2)}) collective-permute-start(bf16[768,384]{1,0:T(8,128)(2,1)S(1)} %slice.147), channel_id=1, source_target_pairs={{0,4},{4,0},{1,5},{5,1},{2,6},{6,2},{3,7},{7,3},{8,12},{12,8},{9,1... | collective-permute-start | bytes 1769480 | tf_op jit(solution)/shard_map/ppermute | solution.py:247
  114.9 10.9 %copy-start.16 = (bf16[768,384]{1,0:T(8,128)(2,1)}, bf16[768,384]{1,0:T(8,128)(2,1)S(1)}, u32[]{:S(2)}) copy-start(bf16[768,384]{1,0:T(8,128)(2,1)S(1)} %collective-permute-done.19.rest_14_) | copy-start | bytes 1769476
  114.9 2.9 %collective-permute-start.20 = (bf16[768,384]{1,0:T(8,128)(2,1)S(1)}, bf16[768,384]{1,0:T(8,128)(2,1)S(1)}, u32[]{:S(2)}, u32[]{:S(2)}) collective-permute-start(bf16[768,384]{1,0:T(8,128)(2,1)S(1)} %get-tuple-element.23), channel_id=1, source_target_pairs={{0,4},{4,0},{1,5},{5,1},{2,6},{6,2},{3,7},{7,3},{8,12},{12,8},{9,1... | collective-permute-start | bytes 1769480 | tf_op jit(solution)/shard_map/ppermute | solution.py:247
  115.3 2.5 %copy-start.7 = (bf16[448,1536]{1,0:T(8,128)(2,1)}, bf16[448,1536]{1,0:T(8,128)(2,1)S(1)}, u32[]{:S(2)}) copy-start(bf16[448,1536]{1,0:T(8,128)(2,1)S(1)} %collective-permute-done.11.rest_3_) | copy-start | bytes 4128772
  115.3 9.3 %collective-permute-start.17 = (bf16[768,384]{1,0:T(8,128)(2,1)S(1)}, bf16[768,384]{1,0:T(8,128)(2,1)S(1)}, u32[]{:S(2)}, u32[]{:S(2)}) collective-permute-start(bf16[768,384]{1,0:T(8,128)(2,1)S(1)} %get-tuple-element.24), channel_id=1, source_target_pairs={{0,8},{4,60},{8,16},{12,4},{16,24},{20,12},{24,32},{28,20},{32,40}... | collective-permute-start | bytes 1769480 | tf_op jit(solution)/shard_map/ppermute | solution.py:243
  117.8 8.0 %copy-start.9 = (bf16[448,1536]{1,0:T(8,128)(2,1)}, bf16[448,1536]{1,0:T(8,128)(2,1)S(1)}, u32[]{:S(2)}) copy-start(bf16[448,1536]{1,0:T(8,128)(2,1)S(1)} %collective-permute-done.12.rest_5_) | copy-start | bytes 4128772
  117.9 8.0 %copy-start.17 = (bf16[768,384]{1,0:T(8,128)(2,1)}, bf16[768,384]{1,0:T(8,128)(2,1)S(1)}, u32[]{:S(2)}) copy-start(bf16[768,384]{1,0:T(8,128)(2,1)S(1)} %collective-permute-done.20.rest_15_) | copy-start | bytes 1769476
  124.7 1.3 copy-start.18
  124.7 1.1 copy-start.10
  140.5 51.5 %all-to-all-start.1 = ((bf16[64,24,384]{2,1,0:T(8,128)(2,1)}), bf16[64,24,384]{2,1,0:T(8,128)(2,1)S(1)}, u32[]{:S(2)}, u32[]{:S(2)}) async-start(bf16[64,24,384]{2,1,0:T(8,128)(2,1)} %bitcast.24), calls=%async_computation.1 | async-start | bytes 2359296 | tf_op jit(solution)/shard_map/all_to_all | solution.py:323
  149.0 1.5 copy-start.2
  150.5 3.2 %collective-permute-start.23 = (bf16[1536,384]{1,0:T(8,128)(2,1)S(1)}, bf16[1536,384]{1,0:T(8,128)(2,1)S(1)}, u32[]{:S(2)}, u32[]{:S(2)}) collective-permute-start(bf16[1536,384]{1,0:T(8,128)(2,1)S(1)} %get-tuple-element.17), channel_id=1, source_target_pairs={{0,4},{4,0},{1,5},{5,1},{2,6},{6,2},{3,7},{7,3},{8,12},{12,8},{9,1... | collective-permute-start | bytes 3538952 | tf_op jit(solution)/shard_map/ppermute | solution.py:247
  151.0 25.4 %collective-permute-start.22 = (bf16[1536,384]{1,0:T(8,128)(2,1)S(1)}, bf16[1536,384]{1,0:T(8,128)(2,1)S(1)}, u32[]{:S(2)}, u32[]{:S(2)}) collective-permute-start(bf16[1536,384]{1,0:T(8,128)(2,1)S(1)} %get-tuple-element.18), channel_id=1, source_target_pairs={{0,64},{4,196},{64,128},{68,4},{128,192},{132,68},{192,0},{196,132... | collective-permute-start | bytes 3538952 | tf_op jit(solution)/shard_map/ppermute | solution.py:243
  153.7 22.6 %copy-start.13 = (bf16[1536,384]{1,0:T(8,128)(2,1)}, bf16[1536,384]{1,0:T(8,128)(2,1)S(1)}, u32[]{:S(2)}) copy-start(bf16[1536,384]{1,0:T(8,128)(2,1)S(1)} %collective-permute-done.23.rest_11_) | copy-start | bytes 3538948
  176.3 1.0 copy-start.14
  192.0 10.8 %copy-start.21 = (s32[64]{0:T(128)S(1)}, s32[64]{0:T(128)}, u32[]{:S(2)}) copy-start(s32[64]{0:T(128)} %param.13) | copy-start | bytes 772
  192.0 42.2 %all-to-all-start = ((bf16[64,24,384]{2,1,0:T(8,128)(2,1)}), bf16[64,24,384]{2,1,0:T(8,128)(2,1)S(1)}, u32[]{:S(2)}, u32[]{:S(2)}) async-start(bf16[64,24,384]{2,1,0:T(8,128)(2,1)} %bitcast.23), calls=%async_computation | async-start | bytes 2359296 | tf_op jit(solution)/shard_map/all_to_all | solution.py:323

commit v7 on v3

--- a/solution.py
+++ b/solution.py
@@ -107,7 +107,7 @@
         x_copies.append(
             pltpu.make_async_copy(rows[k], x_ref.at[2 * (k // 2) + who], x_sem.at[k])
         )
-    for c in w_copies + x_copies:
+    for c in w_copies + x_copies[:2]:
         c.start()
 
     convs = counts_ref.shape[1]
@@ -142,6 +142,8 @@
     for s in range(nh):
         for c in x_copies[2 * s : 2 * s + 2]:
             c.wait()
+        for c in x_copies[2 * s + 2 : 2 * s + 4]:
+            c.start()
         quarter = lax.rem(head + quarters[s] * sign + nh, nh)
         at = pl.multiple_of(quarter * feats, feats)
 
@@ -191,46 +193,54 @@
     )(counts[None], *rows, *pieces)
 
 
-def attend_kernel(live_ref, q_ref, k_ref, v_ref, nk_ref, nv_ref, out_ref):
+def attend_kernel(first, live_ref, q_ref, k_ref, v_ref, nk_ref, nv_ref, *rest):
+    out_ref = rest[-1]
+    if first:
+        out_ref[:, :first] = rest[0][...]
     live = live_ref[0]
     hist = k_ref.shape[0]
     new = nk_ref.shape[0]
     scale = 1.0 / math.sqrt(HD)
     hist_ok = (iota((1, hist), 1) % MAXB) < live
-    new_ok = iota((new, new), 1) <= iota((new, new), 0)
-
-    @pl.loop(0, q_ref.shape[1] // (2 * HD))
+    token = iota((2 * new, new), 0)
+    token = jnp.where(token < new, token, token - new)
+    new_ok = iota((2 * new, new), 1) <= token
+
+    @pl.loop(0, k_ref.shape[1] // (2 * HD))
     def _(pair):
         lanes = pl.ds(pl.multiple_of(pair * 2 * HD, 2 * HD), 2 * HD)
-        q = q_ref[:, lanes] * jnp.asarray(scale, BF16)
+        all_lanes = pl.ds(pl.multiple_of(first + pair * 2 * HD, 2 * HD), 2 * HD)
+        q = q_ref[:, all_lanes] * jnp.asarray(scale, BF16)
         k, v = k_ref[:, lanes], v_ref[:, lanes]
-        nk, nv = nk_ref[:, lanes], nv_ref[:, lanes]
+        nk, nv = nk_ref[:, all_lanes], nv_ref[:, all_lanes]
         low = iota(q.shape, 1) < HD
-        outs = []
-        for mine in (low, jnp.logical_not(low)):
-            qh = jnp.where(mine, q, jnp.zeros_like(q))
-            sh = jnp.where(hist_ok, dot(qh, k, ((1,), (1,))), -jnp.inf)
-            sn = jnp.where(new_ok, dot(qh, nk, ((1,), (1,))), -jnp.inf)
-            top = jnp.maximum(
-                jnp.max(sh, axis=1, keepdims=True), jnp.max(sn, axis=1, keepdims=True)
-            )
-            eh, en = jnp.exp(sh - top), jnp.exp(sn - top)
-            total = jnp.sum(eh, axis=1, keepdims=True) + jnp.sum(en, axis=1, keepdims=True)
-            share = 1.0 / total
-            ph, pn = (eh * share).astype(BF16), (en * share).astype(BF16)
-            outs.append(dot(ph, v) + dot(pn, nv))
-        out_ref[:, lanes] = jnp.where(low, outs[0], outs[1]).astype(BF16)
-
-
-def attend(live, q, k, v, nk, nv):
+        none = jnp.zeros_like(q)
+        q2 = jnp.concatenate([jnp.where(low, q, none), jnp.where(low, none, q)], axis=0)
+        sh = jnp.where(hist_ok, dot(q2, k, ((1,), (1,))), -jnp.inf)
+        sn = jnp.where(new_ok, dot(q2, nk, ((1,), (1,))), -jnp.inf)
+        top = jnp.maximum(
+            jnp.max(sh, axis=1, keepdims=True), jnp.max(sn, axis=1, keepdims=True)
+        )
+        eh, en = jnp.exp(sh - top), jnp.exp(sn - top)
+        total = jnp.sum(eh, axis=1, keepdims=True) + jnp.sum(en, axis=1, keepdims=True)
+        share = 1.0 / total
+        ph, pn = (eh * share).astype(BF16), (en * share).astype(BF16)
+        out = dot(ph, v) + dot(pn, nv)
+        out_ref[:, all_lanes] = jnp.where(low, out[:new], out[new:]).astype(BF16)
+
+
+def attend(live, q, k, v, nk, nv, before=None):
+    first = 0 if before is None else before.shape[1]
+    more = () if before is None else (before,)
     return pl.pallas_call(
-        attend_kernel,
-        out_shape=jax.ShapeDtypeStruct(q.shape, BF16),
-        in_specs=[pl.BlockSpec(memory_space=pltpu.SMEM)] + [pl.BlockSpec(memory_space=pltpu.VMEM)] * 5,
+        functools.partial(attend_kernel, first),
+        out_shape=jax.ShapeDtypeStruct((q.shape[0], first + k.shape[1]), BF16),
+        in_specs=[pl.BlockSpec(memory_space=pltpu.SMEM)]
+        + [pl.BlockSpec(memory_space=pltpu.VMEM)] * (5 + len(more)),
         out_specs=pl.BlockSpec(memory_space=pltpu.VMEM),
         compiler_params=pltpu.CompilerParams(vmem_limit_bytes=VMEM_LIMIT),
         name="attend",
-    )(live, q, k, v, nk, nv)
+    )(live, q, k, v, nk, nv, *more)
 
 
 def ring_step(x, axis, way=1):

time: 216 us -> 213 us (0.986)
  Pallas kernels: 36 us -> 32.3 us
where the time goes in v7:
time: 213 us
  waiting for transfers between devices  103 us (48%)
  starting transfers between devices  65.9 us (31%)
  Pallas kernels  32.3 us (15%)
  local copies, waits for them, and re-layouts  9.58 us (4%)
    all_to_all x1, waiting for transfers between devices, per_device(): got = lax.all_to_all(sent, PLANE, split_axis=0, concat_axis=0, tiled=True)  56 us
    ppermute x15, waiting for transfers between devices, ring_step(): return lax.ppermute(x, order, perm)  45.3 us
    ppermute x15, starting transfers between devices, ring_step(): return lax.ppermute(x, order, perm)  34.5 us
    pallas_call x1, Pallas kernels, project(): pl.pallas_call(functools.partial(project_kernel, dims), out_shape=jax.Sha...  20.5 us
    ppermute x11, starting transfers between devices, swap_cores(): return lax.ppermute(x, 'core', [(0, 1), (1, 0)])  18.2 us
    all_to_all x1, starting transfers between devices, per_device(): got = lax.all_to_all(sent, PLANE, split_axis=0, concat_axis=0, tiled=True)  13.2 us
    pallas_call x1, Pallas kernels, attend(): pl.pallas_call(functools.partial(attend_kernel, first), out_shape=jax.Sha...  7.76 us
    unnamed x63, local copies, waits for them, and re-layouts  5.81 us
  transfers between devices with their start and end apart: 27, of which 11 were waited for; matrix products, arithmetic and copies ran while one was open for 3% of the time, Pallas kernels for 2%

profile of v7, /device:TPU:1, one launch (start us, length us, event | category | flops | bytes accessed | tf_op | source)
XLA Modules:
  0.0 212.5 jit_solution(14820598522398398279)
XLA Ops:
  0.0 1.0 broadcast_select_fusion.2
  1.0 3.3 %collective-permute-start.7 = (bf16[192,768]{1,0:T(8,128)(2,1)S(1)}, bf16[192,768]{1,0:T(8,128)(2,1)S(1)}, u32[]{:S(2)}, u32[]{:S(2)}) collective-permute-start(bf16[192,768]{1,0:T(8,128)(2,1)S(1)} %pad_maximum_fusion.3), channel_id=1, source_target_pairs={{0,4},{4,0},{1,5},{5,1},{2,6},{6,2},{3,7},{7,3},{8,12},{12,8},{9,1... | collective-permute-start | bytes 884744 | tf_op jit(solution)/shard_map/ppermute | solution.py:269
  4.4 1.2 broadcast_in_dim.11.table_ref
  5.6 3.3 %copy.12 = bf16[384,2,1536]{2,0,1:T(8,128)(2,1)} copy(bf16[384,2,1536]{2,1,0:T(2,128)(2,1)} %param.11) | data formatting | bytes 4718592 | tf_op args[3]
  8.9 4.1 %live_rows.1 = bf16[2,224,1536]{2,1,0:T(8,128)(2,1)} custom-call(s32[1,64]{1,0:T(1,128)} %bitcast.25, s32[1,384]{1,0:T(1,128)} %broadcast_in_dim.11.table_ref, bf16[2,384,1536]{2,1,0:T(8,128)(2,1)} %bitcast.14), custom_call_target="tpu_custom_call" | custom-call | tf_op jit(solution)/shard_map/live_rows/pallas_call | solution.py:51
  13.0 2.7 %collective-permute-start.1 = (bf16[448,1536]{1,0:T(8,128)(2,1)}, bf16[448,1536]{1,0:T(8,128)(2,1)S(1)}, u32[]{:S(2)}, u32[]{:S(2)}) collective-permute-start(bf16[448,1536]{1,0:T(8,128)(2,1)} %bitcast.19), channel_id=1, source_target_pairs={{0,1},{4,7},{1,2},{5,4},{2,3},{6,5},{3,0},{7,6},{8,9},{12,15},{9,1... | collective-permute-start | bytes 4128776 | tf_op jit(solution)/shard_map/ppermute | solution.py:253
  15.7 0.1 broadcast_select_fusion
  15.8 3.9 %collective-permute-start.18 = (bf16[192,768]{1,0:T(8,128)(2,1)S(1)}, bf16[192,768]{1,0:T(8,128)(2,1)S(1)}, u32[]{:S(2)}, u32[]{:S(2)}) collective-permute-start(bf16[192,768]{1,0:T(8,128)(2,1)S(1)} %get-tuple-element.11), channel_id=1, source_target_pairs={{0,8},{4,60},{8,16},{12,4},{16,24},{20,12},{24,32},{28,20},{32,40}... | collective-permute-start | bytes 884744 | tf_op jit(solution)/shard_map/ppermute | solution.py:253
  19.7 2.7 %collective-permute-start.8 = (bf16[192,768]{1,0:T(8,128)(2,1)S(1)}, bf16[192,768]{1,0:T(8,128)(2,1)S(1)}, u32[]{:S(2)}, u32[]{:S(2)}) collective-permute-start(bf16[192,768]{1,0:T(8,128)(2,1)S(1)} %get-tuple-element.12), channel_id=1, source_target_pairs={{0,64},{4,196},{64,128},{68,4},{128,192},{132,68},{192,0},{196,132... | collective-permute-start | bytes 884744 | tf_op jit(solution)/shard_map/ppermute | solution.py:253
  22.4 0.9 collective-permute-done.18
  23.4 3.4 %collective-permute-start.19 = (bf16[192,768]{1,0:T(8,128)(2,1)S(1)}, bf16[192,768]{1,0:T(8,128)(2,1)S(1)}, u32[]{:S(2)}, u32[]{:S(2)}) collective-permute-start(bf16[192,768]{1,0:T(8,128)(2,1)S(1)} %collective-permute-done.18), channel_id=1, source_target_pairs={{0,8},{4,60},{8,16},{12,4},{16,24},{20,12},{24,32},{28,20},{32,40}... | collective-permute-start | bytes 884744 | tf_op jit(solution)/shard_map/ppermute | solution.py:253
  26.8 2.8 %collective-permute-start.9 = (bf16[96,768]{1,0:T(8,128)(2,1)S(1)}, bf16[96,768]{1,0:T(8,128)(2,1)S(1)}, u32[]{:S(2)}, u32[]{:S(2)}) collective-permute-start(bf16[96,768]{1,0:T(8,128)(2,1)S(1)} %get-tuple-element.15), channel_id=1, source_target_pairs={{0,64},{4,196},{64,128},{68,4},{128,192},{132,68},{192,0},{196,132... | collective-permute-start | bytes 442376 | tf_op jit(solution)/shard_map/ppermute | solution.py:253
  29.6 0.8 collective-permute-done.19
  30.4 3.4 %collective-permute-start.20 = (bf16[192,768]{1,0:T(8,128)(2,1)S(1)}, bf16[192,768]{1,0:T(8,128)(2,1)S(1)}, u32[]{:S(2)}, u32[]{:S(2)}) collective-permute-start(bf16[192,768]{1,0:T(8,128)(2,1)S(1)} %collective-permute-done.19), channel_id=1, source_target_pairs={{0,8},{4,60},{8,16},{12,4},{16,24},{20,12},{24,32},{28,20},{32,40}... | collective-permute-start | bytes 884744 | tf_op jit(solution)/shard_map/ppermute | solution.py:253
  33.9 0.1 collective-permute-start.10
  34.0 3.5 %collective-permute-done.20 = bf16[192,768]{1,0:T(8,128)(2,1)S(1)} collective-permute-done((bf16[192,768]{1,0:T(8,128)(2,1)S(1)}, bf16[192,768]{1,0:T(8,128)(2,1)S(1)}, u32[]{:S(2)}, u32[]{:S(2)}) %collective-permute-start.20) | collective-permute-done | bytes 294944 | tf_op jit(solution)/shard_map/ppermute | solution.py:253
  37.5 3.5 %collective-permute-start.21 = (bf16[96,768]{1,0:T(8,128)(2,1)S(1)}, bf16[96,768]{1,0:T(8,128)(2,1)S(1)}, u32[]{:S(2)}, u32[]{:S(2)}) collective-permute-start(bf16[96,768]{1,0:T(8,128)(2,1)S(1)} %get-tuple-element.13), channel_id=1, source_target_pairs={{0,8},{4,60},{8,16},{12,4},{16,24},{20,12},{24,32},{28,20},{32,40}... | collective-permute-start | bytes 442376 | tf_op jit(solution)/shard_map/ppermute | solution.py:253
  41.0 2.1 collective-permute-done.21
  43.2 4.1 %collective-permute-start.22 = (bf16[672,768]{1,0:T(8,128)(2,1)S(1)}, bf16[672,768]{1,0:T(8,128)(2,1)S(1)}, u32[]{:S(2)}, u32[]{:S(2)}) collective-permute-start(bf16[672,768]{1,0:T(8,128)(2,1)S(1)} %pad_maximum_fusion), channel_id=1, source_target_pairs={{0,4},{4,0},{1,5},{5,1},{2,6},{6,2},{3,7},{7,3},{8,12},{12,8},{9,1... | collective-permute-start | bytes 3096584 | tf_op jit(solution)/shard_map/ppermute | solution.py:269
  47.5 3.0 %collective-permute-start.5 = (bf16[448,1536]{1,0:T(8,128)(2,1)S(1)}, bf16[448,1536]{1,0:T(8,128)(2,1)S(1)}, u32[]{:S(2)}, u32[]{:S(2)}) collective-permute-start(bf16[448,1536]{1,0:T(8,128)(2,1)S(1)} %collective-permute-done.1.rest_2_), channel_id=1, source_target_pairs={{0,1},{4,7},{1,2},{5,4},{2,3},{6,5},{3,0},{7,6},{8,9},{12,15},{9,1... | collective-permute-start | bytes 4128776 | tf_op jit(solution)/shard_map/ppermute | solution.py:253
  50.8 2.8 %collective-permute-start.23 = (bf16[1536,768]{1,0:T(8,128)(2,1)S(1)}, bf16[1536,768]{1,0:T(8,128)(2,1)S(1)}, u32[]{:S(2)}, u32[]{:S(2)}) collective-permute-start(bf16[1536,768]{1,0:T(8,128)(2,1)S(1)} %slice_dynamic-update-slice_fusion.rest_16_), channel_id=1, source_target_pairs={{0,64},{4,196},{64,128},{68,4},{128,192},{132,68},{192,0},{196,132... | collective-permute-start | bytes 7077896 | tf_op jit(solution)/shard_map/ppermute | solution.py:253
  53.6 9.2 %collective-permute-done.11.rest_9_ = bf16[768,768]{1,0:T(8,128)(2,1)S(1)} collective-permute-done((bf16[768,768]{1,0:T(8,128)(2,1)S(1)}, bf16[768,768]{1,0:T(8,128)(2,1)S(1)}, u32[]{:S(2)}, u32[]{:S(2)}) %collective-permute-start.11) | collective-permute-done | bytes 1179680 | tf_op jit(solution)/shard_map/ppermute | solution.py:253
  62.8 1.2 collective-permute-start.12
  64.0 1.0 collective-permute-start
  65.0 0.1 collective-permute-start.3
  65.1 0.7 collective-permute-done.5.rest_6_
  65.8 1.3 collective-permute-start.4
  67.1 11.0 %collective-permute-done.12.rest_10_ = bf16[768,768]{1,0:T(8,128)(2,1)S(1)} collective-permute-done((bf16[768,768]{1,0:T(8,128)(2,1)S(1)}, bf16[768,768]{1,0:T(8,128)(2,1)S(1)}, u32[]{:S(2)}, u32[]{:S(2)}) %collective-permute-start.12) | collective-permute-done | bytes 1179680 | tf_op jit(solution)/shard_map/ppermute | solution.py:253
  78.1 2.4 %collective-permute-start.13 = (bf16[768,768]{1,0:T(8,128)(2,1)S(1)}, bf16[768,768]{1,0:T(8,128)(2,1)S(1)}, u32[]{:S(2)}, u32[]{:S(2)}) collective-permute-start(bf16[768,768]{1,0:T(8,128)(2,1)S(1)} %collective-permute-done.12.rest_10_), channel_id=1, source_target_pairs={{0,8},{4,60},{8,16},{12,4},{16,24},{20,12},{24,32},{28,20},{32,40}... | collective-permute-start | bytes 3538952 | tf_op jit(solution)/shard_map/ppermute | solution.py:253
  80.7 1.8 collective-permute-start.6
  82.5 0.2 fusion.1
  82.7 0.6 collective-permute-start.15
  83.4 0.1 collective-permute-start.16
  83.5 0.6 collective-permute-start.25
  84.1 9.6 %collective-permute-done.13.rest_11_ = bf16[768,768]{1,0:T(8,128)(2,1)S(1)} collective-permute-done((bf16[768,768]{1,0:T(8,128)(2,1)S(1)}, bf16[768,768]{1,0:T(8,128)(2,1)S(1)}, u32[]{:S(2)}, u32[]{:S(2)}) %collective-permute-start.13) | collective-permute-done | bytes 1179680 | tf_op jit(solution)/shard_map/ppermute | solution.py:253
  93.7 2.5 %collective-permute-start.24 = (bf16[768,768]{1,0:T(8,128)(2,1)S(1)}, bf16[768,768]{1,0:T(8,128)(2,1)S(1)}, u32[]{:S(2)}, u32[]{:S(2)}) collective-permute-start(bf16[768,768]{1,0:T(8,128)(2,1)S(1)} %get-tuple-element.8), channel_id=1, source_target_pairs={{0,64},{4,196},{64,128},{68,4},{128,192},{132,68},{192,0},{196,132... | collective-permute-start | bytes 3538952 | tf_op jit(solution)/shard_map/ppermute | solution.py:253
  96.3 5.1 %collective-permute-start.17 = (bf16[384,768]{1,0:T(8,128)(2,1)S(1)}, bf16[384,768]{1,0:T(8,128)(2,1)S(1)}, u32[]{:S(2)}, u32[]{:S(2)}) collective-permute-start(bf16[384,768]{1,0:T(8,128)(2,1)S(1)} %get-tuple-element.9), channel_id=1, source_target_pairs={{0,4},{4,0},{1,5},{5,1},{2,6},{6,2},{3,7},{7,3},{8,12},{12,8},{9,1... | collective-permute-start | bytes 1769480 | tf_op jit(solution)/shard_map/ppermute | solution.py:269
  101.5 1.6 collective-permute-done.17.rest_15_
  103.1 7.4 %collective-permute-done.14.rest_12_ = bf16[384,768]{1,0:T(8,128)(2,1)S(1)} collective-permute-done((bf16[384,768]{1,0:T(8,128)(2,1)S(1)}, bf16[384,768]{1,0:T(8,128)(2,1)S(1)}, u32[]{:S(2)}, u32[]{:S(2)}) %collective-permute-start.14) | collective-permute-done | bytes 589856 | tf_op jit(solution)/shard_map/ppermute | solution.py:253
  110.6 0.7 copy-done.20
  111.3 0.5 copy-done.15
  111.8 1.0 copy-done.16
  112.8 20.5 %project.1 = bf16[1536,768]{1,0:T(8,128)(2,1)} custom-call(s32[1,64]{1,0:T(1,128)} %bitcast.26, bf16[448,1536]{1,0:T(8,128)(2,1)} %bitcast.20, bf16[448,1536]{1,0:T(8,128)(2,1)} %copy-done.11, bf16[448,1536]{1,0:T(8,128)(2,1)} %copy-done.9, bf16[448,1536]{1,0:T(8,128)(2,1)} %copy-done.12, bf16[448,1536]{1,0:T(8,128)(2,1)} %copy-done.8, ...), custom_call_target="tpu_custom_call" | custom-call | flops 8455716864 | bytes 20447232 | tf_op jit(solution)/shard_map/project/pallas_call | solution.py:174
  133.3 13.2 %all-to-all-start = ((bf16[64,24,768]{2,1,0:T(8,128)(2,1)}), bf16[64,24,768]{2,1,0:T(8,128)(2,1)S(1)}, u32[]{:S(2)}, u32[]{:S(2)}) async-start(bf16[64,24,768]{2,1,0:T(8,128)(2,1)} %bitcast.17), calls=%async_computation | async-start | bytes 4718592 | tf_op jit(solution)/shard_map/all_to_all | solution.py:334
  146.6 0.6 dynamic_slice.3.live_ref
  147.1 56.0 %all-to-all-done = bf16[64,24,768]{2,1,0:T(8,128)(2,1)S(1)} async-done(((bf16[64,24,768]{2,1,0:T(8,128)(2,1)}), bf16[64,24,768]{2,1,0:T(8,128)(2,1)S(1)}, u32[]{:S(2)}, u32[]{:S(2)}) %all-to-all-start) | async-done | bytes 2359328 | tf_op jit(solution)/shard_map/all_to_all | solution.py:334
  203.2 1.6 fusion
  204.7 7.8 %attend.1 = bf16[128,768]{1,0:T(8,128)(2,1)} custom-call(s32[1]{0:T(128)} %dynamic_slice.3.live_ref, bf16[128,768]{1,0:T(8,128)(2,1)} %bitcast.22, bf16[768,768]{1,0:T(8,128)(2,1)} %bitcast.16, bf16[768,768]{1,0:T(8,128)(2,1)} %bitcast.15, bf16[128,768]{1,0:T(8,128)(2,1)} %bitcast.23, bf16[128,768]{1,0:T(8,128)(2,1)} %bitcast.24), custom_call_target="tpu_custom_call" | custom-call | tf_op jit(solution)/shard_map/attend/pallas_call | solution.py:235
  (88 shorter events, 0.8 us)
Async XLA Ops:
  1.0 14.6 %collective-permute-start.7 = (bf16[192,768]{1,0:T(8,128)(2,1)S(1)}, bf16[192,768]{1,0:T(8,128)(2,1)S(1)}, u32[]{:S(2)}, u32[]{:S(2)}) collective-permute-start(bf16[192,768]{1,0:T(8,128)(2,1)S(1)} %pad_maximum_fusion.3), channel_id=1, source_target_pairs={{0,4},{4,0},{1,5},{5,1},{2,6},{6,2},{3,7},{7,3},{8,12},{12,8},{9,1... | collective-permute-start | bytes 884744 | tf_op jit(solution)/shard_map/ppermute | solution.py:269
  13.0 52.0 %collective-permute-start.2 = (bf16[448,1536]{1,0:T(8,128)(2,1)}, bf16[448,1536]{1,0:T(8,128)(2,1)S(1)}, u32[]{:S(2)}, u32[]{:S(2)}) collective-permute-start(bf16[448,1536]{1,0:T(8,128)(2,1)} %bitcast.18), channel_id=1, source_target_pairs={{0,3},{4,5},{1,0},{5,6},{2,1},{6,7},{3,2},{7,4},{8,11},{12,13},{9,... | collective-permute-start | bytes 4128776 | tf_op jit(solution)/shard_map/ppermute | solution.py:253
  13.0 34.5 %collective-permute-start.1 = (bf16[448,1536]{1,0:T(8,128)(2,1)}, bf16[448,1536]{1,0:T(8,128)(2,1)S(1)}, u32[]{:S(2)}, u32[]{:S(2)}) collective-permute-start(bf16[448,1536]{1,0:T(8,128)(2,1)} %bitcast.19), channel_id=1, source_target_pairs={{0,1},{4,7},{1,2},{5,4},{2,3},{6,5},{3,0},{7,6},{8,9},{12,15},{9,1... | collective-permute-start | bytes 4128776 | tf_op jit(solution)/shard_map/ppermute | solution.py:253
  15.8 7.6 %collective-permute-start.18 = (bf16[192,768]{1,0:T(8,128)(2,1)S(1)}, bf16[192,768]{1,0:T(8,128)(2,1)S(1)}, u32[]{:S(2)}, u32[]{:S(2)}) collective-permute-start(bf16[192,768]{1,0:T(8,128)(2,1)S(1)} %get-tuple-element.11), channel_id=1, source_target_pairs={{0,8},{4,60},{8,16},{12,4},{16,24},{20,12},{24,32},{28,20},{32,40}... | collective-permute-start | bytes 884744 | tf_op jit(solution)/shard_map/ppermute | solution.py:253
  19.7 7.1 %collective-permute-start.8 = (bf16[192,768]{1,0:T(8,128)(2,1)S(1)}, bf16[192,768]{1,0:T(8,128)(2,1)S(1)}, u32[]{:S(2)}, u32[]{:S(2)}) collective-permute-start(bf16[192,768]{1,0:T(8,128)(2,1)S(1)} %get-tuple-element.12), channel_id=1, source_target_pairs={{0,64},{4,196},{64,128},{68,4},{128,192},{132,68},{192,0},{196,132... | collective-permute-start | bytes 884744 | tf_op jit(solution)/shard_map/ppermute | solution.py:253
  23.4 7.1 %collective-permute-start.19 = (bf16[192,768]{1,0:T(8,128)(2,1)S(1)}, bf16[192,768]{1,0:T(8,128)(2,1)S(1)}, u32[]{:S(2)}, u32[]{:S(2)}) collective-permute-start(bf16[192,768]{1,0:T(8,128)(2,1)S(1)} %collective-permute-done.18), channel_id=1, source_target_pairs={{0,8},{4,60},{8,16},{12,4},{16,24},{20,12},{24,32},{28,20},{32,40}... | collective-permute-start | bytes 884744 | tf_op jit(solution)/shard_map/ppermute | solution.py:253
  26.8 7.1 %collective-permute-start.9 = (bf16[96,768]{1,0:T(8,128)(2,1)S(1)}, bf16[96,768]{1,0:T(8,128)(2,1)S(1)}, u32[]{:S(2)}, u32[]{:S(2)}) collective-permute-start(bf16[96,768]{1,0:T(8,128)(2,1)S(1)} %get-tuple-element.15), channel_id=1, source_target_pairs={{0,64},{4,196},{64,128},{68,4},{128,192},{132,68},{192,0},{196,132... | collective-permute-start | bytes 442376 | tf_op jit(solution)/shard_map/ppermute | solution.py:253
  30.4 7.1 %collective-permute-start.20 = (bf16[192,768]{1,0:T(8,128)(2,1)S(1)}, bf16[192,768]{1,0:T(8,128)(2,1)S(1)}, u32[]{:S(2)}, u32[]{:S(2)}) collective-permute-start(bf16[192,768]{1,0:T(8,128)(2,1)S(1)} %collective-permute-done.19), channel_id=1, source_target_pairs={{0,8},{4,60},{8,16},{12,4},{16,24},{20,12},{24,32},{28,20},{32,40}... | collective-permute-start | bytes 884744 | tf_op jit(solution)/shard_map/ppermute | solution.py:253
  33.9 7.1 %collective-permute-start.10 = (bf16[288,768]{1,0:T(8,128)(2,1)S(1)}, bf16[288,768]{1,0:T(8,128)(2,1)S(1)}, u32[]{:S(2)}, u32[]{:S(2)}) collective-permute-start(bf16[288,768]{1,0:T(8,128)(2,1)S(1)} %pad_maximum_fusion.1), channel_id=1, source_target_pairs={{0,4},{4,0},{1,5},{5,1},{2,6},{6,2},{3,7},{7,3},{8,12},{12,8},{9,1... | collective-permute-start | bytes 1327112 | tf_op jit(solution)/shard_map/ppermute | solution.py:269
  37.5 5.6 %collective-permute-start.21 = (bf16[96,768]{1,0:T(8,128)(2,1)S(1)}, bf16[96,768]{1,0:T(8,128)(2,1)S(1)}, u32[]{:S(2)}, u32[]{:S(2)}) collective-permute-start(bf16[96,768]{1,0:T(8,128)(2,1)S(1)} %get-tuple-element.13), channel_id=1, source_target_pairs={{0,8},{4,60},{8,16},{12,4},{16,24},{20,12},{24,32},{28,20},{32,40}... | collective-permute-start | bytes 442376 | tf_op jit(solution)/shard_map/ppermute | solution.py:253
  43.2 7.3 %collective-permute-start.22 = (bf16[672,768]{1,0:T(8,128)(2,1)S(1)}, bf16[672,768]{1,0:T(8,128)(2,1)S(1)}, u32[]{:S(2)}, u32[]{:S(2)}) collective-permute-start(bf16[672,768]{1,0:T(8,128)(2,1)S(1)} %pad_maximum_fusion), channel_id=1, source_target_pairs={{0,4},{4,0},{1,5},{5,1},{2,6},{6,2},{3,7},{7,3},{8,12},{12,8},{9,1... | collective-permute-start | bytes 3096584 | tf_op jit(solution)/shard_map/ppermute | solution.py:269
  47.3 16.7 %copy-start.1 = (bf16[2,224,1536]{2,1,0:T(8,128)(2,1)S(1)}, bf16[2,224,1536]{2,1,0:T(8,128)(2,1)}, u32[]{:S(2)}) copy-start(bf16[2,224,1536]{2,1,0:T(8,128)(2,1)} %live_rows.1) | copy-start | bytes 4128772
  47.4 33.3 %copy-start.5 = (bf16[768,768]{1,0:T(8,128)(2,1)}, bf16[768,768]{1,0:T(8,128)(2,1)S(1)}, u32[]{:S(2)}) copy-start(bf16[768,768]{1,0:T(8,128)(2,1)S(1)} %slice_dynamic-update-slice_fusion.14.rest_8_) | copy-start | bytes 3538948
  47.4 15.4 %collective-permute-start.11 = (bf16[768,768]{1,0:T(8,128)(2,1)S(1)}, bf16[768,768]{1,0:T(8,128)(2,1)S(1)}, u32[]{:S(2)}, u32[]{:S(2)}) collective-permute-start(bf16[768,768]{1,0:T(8,128)(2,1)S(1)} %slice_dynamic-update-slice_fusion.14.rest_8_), channel_id=1, source_target_pairs={{0,8},{4,60},{8,16},{12,4},{16,24},{20,12},{24,32},{28,20},{32,40}... | collective-permute-start | bytes 3538952 | tf_op jit(solution)/shard_map/ppermute | solution.py:253
  47.5 33.2 %copy-start.9 = (bf16[448,1536]{1,0:T(8,128)(2,1)}, bf16[448,1536]{1,0:T(8,128)(2,1)S(1)}, u32[]{:S(2)}) copy-start(bf16[448,1536]{1,0:T(8,128)(2,1)S(1)} %collective-permute-done.1.rest_2_) | copy-start | bytes 4128772
  47.5 18.3 %collective-permute-start.5 = (bf16[448,1536]{1,0:T(8,128)(2,1)S(1)}, bf16[448,1536]{1,0:T(8,128)(2,1)S(1)}, u32[]{:S(2)}, u32[]{:S(2)}) collective-permute-start(bf16[448,1536]{1,0:T(8,128)(2,1)S(1)} %collective-permute-done.1.rest_2_), channel_id=1, source_target_pairs={{0,1},{4,7},{1,2},{5,4},{2,3},{6,5},{3,0},{7,6},{8,9},{12,15},{9,1... | collective-permute-start | bytes 4128776 | tf_op jit(solution)/shard_map/ppermute | solution.py:253
  50.7 29.9 %copy-start.6 = (bf16[1536,768]{1,0:T(8,128)(2,1)}, bf16[1536,768]{1,0:T(8,128)(2,1)S(1)}, u32[]{:S(2)}) copy-start(bf16[1536,768]{1,0:T(8,128)(2,1)S(1)} %slice_dynamic-update-slice_fusion.rest_16_) | copy-start | bytes 7077892
  50.8 29.9 %collective-permute-start.23 = (bf16[1536,768]{1,0:T(8,128)(2,1)S(1)}, bf16[1536,768]{1,0:T(8,128)(2,1)S(1)}, u32[]{:S(2)}, u32[]{:S(2)}) collective-permute-start(bf16[1536,768]{1,0:T(8,128)(2,1)S(1)} %slice_dynamic-update-slice_fusion.rest_16_), channel_id=1, source_target_pairs={{0,64},{4,196},{64,128},{68,4},{128,192},{132,68},{192,0},{196,132... | collective-permute-start | bytes 7077896 | tf_op jit(solution)/shard_map/ppermute | solution.py:253
  62.8 19.9 %copy-start.3 = (bf16[768,768]{1,0:T(8,128)(2,1)}, bf16[768,768]{1,0:T(8,128)(2,1)S(1)}, u32[]{:S(2)}) copy-start(bf16[768,768]{1,0:T(8,128)(2,1)S(1)} %collective-permute-done.11.rest_9_) | copy-start | bytes 3538948
  62.8 15.3 %collective-permute-start.12 = (bf16[768,768]{1,0:T(8,128)(2,1)S(1)}, bf16[768,768]{1,0:T(8,128)(2,1)S(1)}, u32[]{:S(2)}, u32[]{:S(2)}) collective-permute-start(bf16[768,768]{1,0:T(8,128)(2,1)S(1)} %collective-permute-done.11.rest_9_), channel_id=1, source_target_pairs={{0,8},{4,60},{8,16},{12,4},{16,24},{20,12},{24,32},{28,20},{32,40}... | collective-permute-start | bytes 3538952 | tf_op jit(solution)/shard_map/ppermute | solution.py:253
  64.0 18.7 %collective-permute-start = (bf16[448,1536]{1,0:T(8,128)(2,1)S(1)}, bf16[448,1536]{1,0:T(8,128)(2,1)S(1)}, u32[]{:S(2)}, u32[]{:S(2)}) collective-permute-start(bf16[448,1536]{1,0:T(8,128)(2,1)S(1)} %bitcast.21), channel_id=1, source_target_pairs={{0,4},{4,0},{1,5},{5,1},{2,6},{6,2},{3,7},{7,3},{8,12},{12,8},{9,1... | collective-permute-start | bytes 4128776 | tf_op jit(solution)/shard_map/ppermute | solution.py:269
  65.0 17.7 %copy-start.8 = (bf16[448,1536]{1,0:T(8,128)(2,1)}, bf16[448,1536]{1,0:T(8,128)(2,1)S(1)}, u32[]{:S(2)}) copy-start(bf16[448,1536]{1,0:T(8,128)(2,1)S(1)} %collective-permute-done.2.rest_4_) | copy-start | bytes 4128772
  65.0 18.4 %collective-permute-start.3 = (bf16[448,1536]{1,0:T(8,128)(2,1)S(1)}, bf16[448,1536]{1,0:T(8,128)(2,1)S(1)}, u32[]{:S(2)}, u32[]{:S(2)}) collective-permute-start(bf16[448,1536]{1,0:T(8,128)(2,1)S(1)} %collective-permute-done.2.rest_4_), channel_id=1, source_target_pairs={{0,4},{4,0},{1,5},{5,1},{2,6},{6,2},{3,7},{7,3},{8,12},{12,8},{9,1... | collective-permute-start | bytes 4128776 | tf_op jit(solution)/shard_map/ppermute | solution.py:269
  65.8 44.8 %copy-start.10 = (bf16[448,1536]{1,0:T(8,128)(2,1)}, bf16[448,1536]{1,0:T(8,128)(2,1)S(1)}, u32[]{:S(2)}) copy-start(bf16[448,1536]{1,0:T(8,128)(2,1)S(1)} %collective-permute-done.5.rest_6_) | copy-start | bytes 4128772
  65.8 17.7 %collective-permute-start.4 = (bf16[448,1536]{1,0:T(8,128)(2,1)S(1)}, bf16[448,1536]{1,0:T(8,128)(2,1)S(1)}, u32[]{:S(2)}, u32[]{:S(2)}) collective-permute-start(bf16[448,1536]{1,0:T(8,128)(2,1)S(1)} %collective-permute-done.1.rest_2_), channel_id=1, source_target_pairs={{0,4},{4,0},{1,5},{5,1},{2,6},{6,2},{3,7},{7,3},{8,12},{12,8},{9,1... | collective-permute-start | bytes 4128776 | tf_op jit(solution)/shard_map/ppermute | solution.py:269
  78.1 4.6 %copy-start.4 = (bf16[768,768]{1,0:T(8,128)(2,1)}, bf16[768,768]{1,0:T(8,128)(2,1)S(1)}, u32[]{:S(2)}) copy-start(bf16[768,768]{1,0:T(8,128)(2,1)S(1)} %collective-permute-done.12.rest_10_) | copy-start | bytes 3538948
  78.1 15.6 %collective-permute-start.13 = (bf16[768,768]{1,0:T(8,128)(2,1)S(1)}, bf16[768,768]{1,0:T(8,128)(2,1)S(1)}, u32[]{:S(2)}, u32[]{:S(2)}) collective-permute-start(bf16[768,768]{1,0:T(8,128)(2,1)S(1)} %collective-permute-done.12.rest_10_), channel_id=1, source_target_pairs={{0,8},{4,60},{8,16},{12,4},{16,24},{20,12},{24,32},{28,20},{32,40}... | collective-permute-start | bytes 3538952 | tf_op jit(solution)/shard_map/ppermute | solution.py:253
  80.7 2.8 %copy-start = (bf16[1536,768]{1,0:T(8,128)(2,1)}, bf16[1536,768]{1,0:T(8,128)(2,1)S(1)}, u32[]{:S(2)}) copy-start(bf16[1536,768]{1,0:T(8,128)(2,1)S(1)} %collective-permute-done.23.rest_17_) | copy-start | bytes 7077892
  80.7 20.8 %collective-permute-start.6 = (bf16[448,1536]{1,0:T(8,128)(2,1)S(1)}, bf16[448,1536]{1,0:T(8,128)(2,1)S(1)}, u32[]{:S(2)}, u32[]{:S(2)}) collective-permute-start(bf16[448,1536]{1,0:T(8,128)(2,1)S(1)} %collective-permute-done.5.rest_6_), channel_id=1, source_target_pairs={{0,4},{4,0},{1,5},{5,1},{2,6},{6,2},{3,7},{7,3},{8,12},{12,8},{9,1... | collective-permute-start | bytes 4128776 | tf_op jit(solution)/shard_map/ppermute | solution.py:269
  82.7 27.8 %copy-start.11 = (bf16[448,1536]{1,0:T(8,128)(2,1)}, bf16[448,1536]{1,0:T(8,128)(2,1)S(1)}, u32[]{:S(2)}) copy-start(bf16[448,1536]{1,0:T(8,128)(2,1)S(1)} %collective-permute-done.rest_1_) | copy-start | bytes 4128772
  82.7 13.6 %collective-permute-start.15 = (bf16[384,768]{1,0:T(8,128)(2,1)S(1)}, bf16[384,768]{1,0:T(8,128)(2,1)S(1)}, u32[]{:S(2)}, u32[]{:S(2)}) collective-permute-start(bf16[384,768]{1,0:T(8,128)(2,1)S(1)} %slice.130), channel_id=1, source_target_pairs={{0,4},{4,0},{1,5},{5,1},{2,6},{6,2},{3,7},{7,3},{8,12},{12,8},{9,1... | collective-permute-start | bytes 1769480 | tf_op jit(solution)/shard_map/ppermute | solution.py:269
  83.4 27.2 %copy-start.12 = (bf16[448,1536]{1,0:T(8,128)(2,1)}, bf16[448,1536]{1,0:T(8,128)(2,1)S(1)}, u32[]{:S(2)}) copy-start(bf16[448,1536]{1,0:T(8,128)(2,1)S(1)} %collective-permute-done.3.rest_3_) | copy-start | bytes 4128772
  83.4 18.1 %collective-permute-start.16 = (bf16[384,768]{1,0:T(8,128)(2,1)S(1)}, bf16[384,768]{1,0:T(8,128)(2,1)S(1)}, u32[]{:S(2)}, u32[]{:S(2)}) collective-permute-start(bf16[384,768]{1,0:T(8,128)(2,1)S(1)} %slice.131), channel_id=1, source_target_pairs={{0,4},{4,0},{1,5},{5,1},{2,6},{6,2},{3,7},{7,3},{8,12},{12,8},{9,1... | collective-permute-start | bytes 1769480 | tf_op jit(solution)/shard_map/ppermute | solution.py:269
  83.5 27.1 %copy-start.13 = (bf16[448,1536]{1,0:T(8,128)(2,1)}, bf16[448,1536]{1,0:T(8,128)(2,1)S(1)}, u32[]{:S(2)}) copy-start(bf16[448,1536]{1,0:T(8,128)(2,1)S(1)} %collective-permute-done.4.rest_5_) | copy-start | bytes 4128772
  83.5 27.0 %collective-permute-start.25 = (bf16[768,768]{1,0:T(8,128)(2,1)S(1)}, bf16[768,768]{1,0:T(8,128)(2,1)S(1)}, u32[]{:S(2)}, u32[]{:S(2)}) collective-permute-start(bf16[768,768]{1,0:T(8,128)(2,1)S(1)} %get-tuple-element.7), channel_id=1, source_target_pairs={{0,4},{4,0},{1,5},{5,1},{2,6},{6,2},{3,7},{7,3},{8,12},{12,8},{9,1... | collective-permute-start | bytes 3538952 | tf_op jit(solution)/shard_map/ppermute | solution.py:269
  93.7 16.9 %copy-start.2 = (bf16[768,768]{1,0:T(8,128)(2,1)}, bf16[768,768]{1,0:T(8,128)(2,1)S(1)}, u32[]{:S(2)}) copy-start(bf16[768,768]{1,0:T(8,128)(2,1)S(1)} %collective-permute-done.13.rest_11_) | copy-start | bytes 3538948
  93.7 16.9 %collective-permute-start.24 = (bf16[768,768]{1,0:T(8,128)(2,1)S(1)}, bf16[768,768]{1,0:T(8,128)(2,1)S(1)}, u32[]{:S(2)}, u32[]{:S(2)}) collective-permute-start(bf16[768,768]{1,0:T(8,128)(2,1)S(1)} %get-tuple-element.8), channel_id=1, source_target_pairs={{0,64},{4,196},{64,128},{68,4},{128,192},{132,68},{192,0},{196,132... | collective-permute-start | bytes 3538952 | tf_op jit(solution)/shard_map/ppermute | solution.py:253
  96.3 14.3 %copy-start.17 = (bf16[384,768]{1,0:T(8,128)(2,1)}, bf16[384,768]{1,0:T(8,128)(2,1)S(1)}, u32[]{:S(2)}) copy-start(bf16[384,768]{1,0:T(8,128)(2,1)S(1)} %collective-permute-done.15.rest_13_) | copy-start | bytes 1769476
  96.3 6.8 %collective-permute-start.17 = (bf16[384,768]{1,0:T(8,128)(2,1)S(1)}, bf16[384,768]{1,0:T(8,128)(2,1)S(1)}, u32[]{:S(2)}, u32[]{:S(2)}) collective-permute-start(bf16[384,768]{1,0:T(8,128)(2,1)S(1)} %get-tuple-element.9), channel_id=1, source_target_pairs={{0,4},{4,0},{1,5},{5,1},{2,6},{6,2},{3,7},{7,3},{8,12},{12,8},{9,1... | collective-permute-start | bytes 1769480 | tf_op jit(solution)/shard_map/ppermute | solution.py:269
  101.5 9.1 %copy-start.18 = (bf16[384,768]{1,0:T(8,128)(2,1)}, bf16[384,768]{1,0:T(8,128)(2,1)S(1)}, u32[]{:S(2)}) copy-start(bf16[384,768]{1,0:T(8,128)(2,1)S(1)} %collective-permute-done.16.rest_14_) | copy-start | bytes 1769476
  101.5 9.0 %collective-permute-start.14 = (bf16[384,768]{1,0:T(8,128)(2,1)S(1)}, bf16[384,768]{1,0:T(8,128)(2,1)S(1)}, u32[]{:S(2)}, u32[]{:S(2)}) collective-permute-start(bf16[384,768]{1,0:T(8,128)(2,1)S(1)} %get-tuple-element.10), channel_id=1, source_target_pairs={{0,8},{4,60},{8,16},{12,4},{16,24},{20,12},{24,32},{28,20},{32,40}... | collective-permute-start | bytes 1769480 | tf_op jit(solution)/shard_map/ppermute | solution.py:253
  101.5 9.1 %copy-start.14 = (bf16[448,1536]{1,0:T(8,128)(2,1)}, bf16[448,1536]{1,0:T(8,128)(2,1)S(1)}, u32[]{:S(2)}) copy-start(bf16[448,1536]{1,0:T(8,128)(2,1)S(1)} %collective-permute-done.6.rest_7_) | copy-start | bytes 4128772
  103.1 7.5 %copy-start.19 = (bf16[384,768]{1,0:T(8,128)(2,1)}, bf16[384,768]{1,0:T(8,128)(2,1)S(1)}, u32[]{:S(2)}) copy-start(bf16[384,768]{1,0:T(8,128)(2,1)S(1)} %collective-permute-done.17.rest_15_) | copy-start | bytes 1769476
  110.5 0.8 copy-start.20
  110.6 1.2 copy-start.15
  111.8 1.0 copy-start.16
  133.3 13.2 %copy-start.7 = (s32[64]{0:T(128)S(1)}, s32[64]{0:T(128)}, u32[]{:S(2)}) copy-start(s32[64]{0:T(128)} %param.13) | copy-start | bytes 772
  133.3 69.8 %all-to-all-start = ((bf16[64,24,768]{2,1,0:T(8,128)(2,1)}), bf16[64,24,768]{2,1,0:T(8,128)(2,1)S(1)}, u32[]{:S(2)}, u32[]{:S(2)}) async-start(bf16[64,24,768]{2,1,0:T(8,128)(2,1)} %bitcast.17), calls=%async_computation | async-start | bytes 4718592 | tf_op jit(solution)/shard_map/all_to_all | solution.py:334

commit v8 on v7

--- a/solution.py
+++ b/solution.py
@@ -91,24 +91,45 @@
     cols = w_ref.shape[1]
     feats = w_ref.shape[0] // nh
 
-    w_copies, x_copies = [], []
-    for k, (src, part, dy, dz, owner) in enumerate(piece_table(ny, nz)):
-        chip = lax.rem(y + dy * sign + ny, ny) * nz + lax.rem(z + dz * sign + nz, nz)
-        at = pl.multiple_of((chip * 2 + owner) * shard, shard)
-        w_copies.append(
+    quarters = (0, -1, 1, -2)
+    table = piece_table(ny, nz)
+
+    def plane_of(s):
+        return lax.rem(y + quarters[s] * sign + ny, ny)
+
+    def copies(s, rows_from):
+        group = []
+        for k, (src, part, dy, dz, owner) in enumerate(table):
+            if (dy - quarters[s]) % ny:
+                continue
+            chip = plane_of(s) * nz + lax.rem(z + dz * sign + nz, nz)
+            at = pl.multiple_of((chip * 2 + owner) * shard, shard)
+            group.append(
+                pltpu.make_async_copy(
+                    pieces[src].at[pl.ds(part * shard, shard)],
+                    w_ref.at[pl.ds(at, shard)],
+                    w_sem.at[k],
+                )
+            )
+        both = [
             pltpu.make_async_copy(
-                pieces[src].at[pl.ds(part * shard, shard)],
-                w_ref.at[pl.ds(at, shard)],
-                w_sem.at[k],
+                rows[2 * rows_from + c], x_ref.at[2 * s + (core if c == 0 else 1 - core)], x_sem.at[2 * s + c]
             )
-        )
-    for k in range(2 * nh):
-        who = core if k % 2 == 0 else 1 - core
-        x_copies.append(
-            pltpu.make_async_copy(rows[k], x_ref.at[2 * (k // 2) + who], x_sem.at[k])
-        )
-    for c in w_copies + x_copies[:2]:
-        c.start()
+            for c in range(2)
+        ]
+        return group, both
+
+    def start(s):
+        for c in copies(s, 0)[0]:
+            c.start()
+        for k in range(nh):
+
+            @pl.when(lax.rem(head + quarters[k] * sign + nh, nh) == plane_of(s))
+            def _():
+                for c in copies(s, k)[1]:
+                    c.start()
+
+    start(0)
 
     convs = counts_ref.shape[1]
     each = out_ref.shape[0] // convs
@@ -135,17 +156,15 @@
         rows_of = pl.ds(pl.multiple_of(g * chunk, chunk), chunk)
         put_ref[rows_of] = (iota((chunk, total), 1) == source).astype(F32).astype(BF16)
 
-    for c in w_copies:
-        c.wait()
+    start(1)
     half = total // 2
-    quarters = (0, -1, 1, -2)
     for s in range(nh):
-        for c in x_copies[2 * s : 2 * s + 2]:
+        group, both = copies(s, 0)
+        for c in group + both:
             c.wait()
-        for c in x_copies[2 * s + 2 : 2 * s + 4]:
-            c.start()
-        quarter = lax.rem(head + quarters[s] * sign + nh, nh)
-        at = pl.multiple_of(quarter * feats, feats)
+        if s + 2 < nh:
+            start(s + 2)
+        at = pl.multiple_of(plane_of(s) * feats, feats)
 
         @pl.loop(0, 2)
         def _(cc):

time: 213 us -> 211 us (level)
  no operation moved by 1% of the time
where the time goes in v8:
time: 211 us; the launch traced here: 210 us
  waiting for transfers between devices  103 us (49%)
  starting transfers between devices  66 us (31%)
  Pallas kernels  30.2 us (14%)
  local copies, waits for them, and re-layouts  9.58 us (5%)
    all_to_all x1, waiting for transfers between devices, per_device(): got = lax.all_to_all(sent, PLANE, split_axis=0, concat_axis=0, tiled=True)  56 us
    ppermute x15, waiting for transfers between devices, ring_step(): return lax.ppermute(x, order, perm)  45.3 us
    ppermute x15, starting transfers between devices, ring_step(): return lax.ppermute(x, order, perm)  34.5 us
    pallas_call x1, Pallas kernels, project(): pl.pallas_call(functools.partial(project_kernel, dims), out_shape=jax.Sha...  18.4 us
    ppermute x11, starting transfers between devices, swap_cores(): return lax.ppermute(x, 'core', [(0, 1), (1, 0)])  18.2 us
    all_to_all x1, starting transfers between devices, per_device(): got = lax.all_to_all(sent, PLANE, split_axis=0, concat_axis=0, tiled=True)  13.3 us
    pallas_call x1, Pallas kernels, attend(): pl.pallas_call(functools.partial(attend_kernel, first), out_shape=jax.Sha...  7.76 us
    unnamed x63, local copies, waits for them, and re-layouts  5.81 us
  transfers between devices with their start and end apart: 27, of which 11 were waited for; matrix products, arithmetic and copies ran while one was open for 3% of the time, Pallas kernels for 2%

profile of v8, /device:TPU:1, one launch (start us, length us, event | category | flops | bytes accessed | tf_op | source)
XLA Modules:
  0.0 210.4 jit_solution(6278110535817756286)
XLA Ops:
  0.0 1.0 broadcast_select_fusion.2
  1.0 3.3 %collective-permute-start.7 = (bf16[192,768]{1,0:T(8,128)(2,1)S(1)}, bf16[192,768]{1,0:T(8,128)(2,1)S(1)}, u32[]{:S(2)}, u32[]{:S(2)}) collective-permute-start(bf16[192,768]{1,0:T(8,128)(2,1)S(1)} %pad_maximum_fusion.3), channel_id=1, source_target_pairs={{0,4},{4,0},{1,5},{5,1},{2,6},{6,2},{3,7},{7,3},{8,12},{12,8},{9,1... | collective-permute-start | bytes 884744 | tf_op jit(solution)/shard_map/ppermute | solution.py:288
  4.4 1.2 broadcast_in_dim.11.table_ref
  5.6 3.3 %copy.12 = bf16[384,2,1536]{2,0,1:T(8,128)(2,1)} copy(bf16[384,2,1536]{2,1,0:T(2,128)(2,1)} %param.11) | data formatting | bytes 4718592 | tf_op args[3]
  8.9 4.1 %live_rows.1 = bf16[2,224,1536]{2,1,0:T(8,128)(2,1)} custom-call(s32[1,64]{1,0:T(1,128)} %bitcast.25, s32[1,384]{1,0:T(1,128)} %broadcast_in_dim.11.table_ref, bf16[2,384,1536]{2,1,0:T(8,128)(2,1)} %bitcast.14), custom_call_target="tpu_custom_call" | custom-call | tf_op jit(solution)/shard_map/live_rows/pallas_call | solution.py:51
  13.0 2.7 %collective-permute-start.1 = (bf16[448,1536]{1,0:T(8,128)(2,1)}, bf16[448,1536]{1,0:T(8,128)(2,1)S(1)}, u32[]{:S(2)}, u32[]{:S(2)}) collective-permute-start(bf16[448,1536]{1,0:T(8,128)(2,1)} %bitcast.19), channel_id=1, source_target_pairs={{0,1},{4,7},{1,2},{5,4},{2,3},{6,5},{3,0},{7,6},{8,9},{12,15},{9,1... | collective-permute-start | bytes 4128776 | tf_op jit(solution)/shard_map/ppermute | solution.py:272
  15.7 0.1 broadcast_select_fusion
  15.8 3.9 %collective-permute-start.18 = (bf16[192,768]{1,0:T(8,128)(2,1)S(1)}, bf16[192,768]{1,0:T(8,128)(2,1)S(1)}, u32[]{:S(2)}, u32[]{:S(2)}) collective-permute-start(bf16[192,768]{1,0:T(8,128)(2,1)S(1)} %get-tuple-element.11), channel_id=1, source_target_pairs={{0,8},{4,60},{8,16},{12,4},{16,24},{20,12},{24,32},{28,20},{32,40}... | collective-permute-start | bytes 884744 | tf_op jit(solution)/shard_map/ppermute | solution.py:272
  19.7 2.7 %collective-permute-start.8 = (bf16[192,768]{1,0:T(8,128)(2,1)S(1)}, bf16[192,768]{1,0:T(8,128)(2,1)S(1)}, u32[]{:S(2)}, u32[]{:S(2)}) collective-permute-start(bf16[192,768]{1,0:T(8,128)(2,1)S(1)} %get-tuple-element.12), channel_id=1, source_target_pairs={{0,64},{4,196},{64,128},{68,4},{128,192},{132,68},{192,0},{196,132... | collective-permute-start | bytes 884744 | tf_op jit(solution)/shard_map/ppermute | solution.py:272
  22.4 0.9 collective-permute-done.18
  23.4 3.4 %collective-permute-start.19 = (bf16[192,768]{1,0:T(8,128)(2,1)S(1)}, bf16[192,768]{1,0:T(8,128)(2,1)S(1)}, u32[]{:S(2)}, u32[]{:S(2)}) collective-permute-start(bf16[192,768]{1,0:T(8,128)(2,1)S(1)} %collective-permute-done.18), channel_id=1, source_target_pairs={{0,8},{4,60},{8,16},{12,4},{16,24},{20,12},{24,32},{28,20},{32,40}... | collective-permute-start | bytes 884744 | tf_op jit(solution)/shard_map/ppermute | solution.py:272
  26.8 2.8 %collective-permute-start.9 = (bf16[96,768]{1,0:T(8,128)(2,1)S(1)}, bf16[96,768]{1,0:T(8,128)(2,1)S(1)}, u32[]{:S(2)}, u32[]{:S(2)}) collective-permute-start(bf16[96,768]{1,0:T(8,128)(2,1)S(1)} %get-tuple-element.15), channel_id=1, source_target_pairs={{0,64},{4,196},{64,128},{68,4},{128,192},{132,68},{192,0},{196,132... | collective-permute-start | bytes 442376 | tf_op jit(solution)/shard_map/ppermute | solution.py:272
  29.6 0.8 collective-permute-done.19
  30.4 3.4 %collective-permute-start.20 = (bf16[192,768]{1,0:T(8,128)(2,1)S(1)}, bf16[192,768]{1,0:T(8,128)(2,1)S(1)}, u32[]{:S(2)}, u32[]{:S(2)}) collective-permute-start(bf16[192,768]{1,0:T(8,128)(2,1)S(1)} %collective-permute-done.19), channel_id=1, source_target_pairs={{0,8},{4,60},{8,16},{12,4},{16,24},{20,12},{24,32},{28,20},{32,40}... | collective-permute-start | bytes 884744 | tf_op jit(solution)/shard_map/ppermute | solution.py:272
  33.9 0.1 collective-permute-start.10
  34.0 3.5 %collective-permute-done.20 = bf16[192,768]{1,0:T(8,128)(2,1)S(1)} collective-permute-done((bf16[192,768]{1,0:T(8,128)(2,1)S(1)}, bf16[192,768]{1,0:T(8,128)(2,1)S(1)}, u32[]{:S(2)}, u32[]{:S(2)}) %collective-permute-start.20) | collective-permute-done | bytes 294944 | tf_op jit(solution)/shard_map/ppermute | solution.py:272
  37.5 3.5 %collective-permute-start.21 = (bf16[96,768]{1,0:T(8,128)(2,1)S(1)}, bf16[96,768]{1,0:T(8,128)(2,1)S(1)}, u32[]{:S(2)}, u32[]{:S(2)}) collective-permute-start(bf16[96,768]{1,0:T(8,128)(2,1)S(1)} %get-tuple-element.13), channel_id=1, source_target_pairs={{0,8},{4,60},{8,16},{12,4},{16,24},{20,12},{24,32},{28,20},{32,40}... | collective-permute-start | bytes 442376 | tf_op jit(solution)/shard_map/ppermute | solution.py:272
  41.0 2.1 collective-permute-done.21
  43.2 4.1 %collective-permute-start.22 = (bf16[672,768]{1,0:T(8,128)(2,1)S(1)}, bf16[672,768]{1,0:T(8,128)(2,1)S(1)}, u32[]{:S(2)}, u32[]{:S(2)}) collective-permute-start(bf16[672,768]{1,0:T(8,128)(2,1)S(1)} %pad_maximum_fusion), channel_id=1, source_target_pairs={{0,4},{4,0},{1,5},{5,1},{2,6},{6,2},{3,7},{7,3},{8,12},{12,8},{9,1... | collective-permute-start | bytes 3096584 | tf_op jit(solution)/shard_map/ppermute | solution.py:288
  47.5 3.0 %collective-permute-start.5 = (bf16[448,1536]{1,0:T(8,128)(2,1)S(1)}, bf16[448,1536]{1,0:T(8,128)(2,1)S(1)}, u32[]{:S(2)}, u32[]{:S(2)}) collective-permute-start(bf16[448,1536]{1,0:T(8,128)(2,1)S(1)} %collective-permute-done.1.rest_2_), channel_id=1, source_target_pairs={{0,1},{4,7},{1,2},{5,4},{2,3},{6,5},{3,0},{7,6},{8,9},{12,15},{9,1... | collective-permute-start | bytes 4128776 | tf_op jit(solution)/shard_map/ppermute | solution.py:272
  50.8 2.8 %collective-permute-start.23 = (bf16[1536,768]{1,0:T(8,128)(2,1)S(1)}, bf16[1536,768]{1,0:T(8,128)(2,1)S(1)}, u32[]{:S(2)}, u32[]{:S(2)}) collective-permute-start(bf16[1536,768]{1,0:T(8,128)(2,1)S(1)} %slice_dynamic-update-slice_fusion.rest_16_), channel_id=1, source_target_pairs={{0,64},{4,196},{64,128},{68,4},{128,192},{132,68},{192,0},{196,132... | collective-permute-start | bytes 7077896 | tf_op jit(solution)/shard_map/ppermute | solution.py:272
  53.6 9.2 %collective-permute-done.11.rest_9_ = bf16[768,768]{1,0:T(8,128)(2,1)S(1)} collective-permute-done((bf16[768,768]{1,0:T(8,128)(2,1)S(1)}, bf16[768,768]{1,0:T(8,128)(2,1)S(1)}, u32[]{:S(2)}, u32[]{:S(2)}) %collective-permute-start.11) | collective-permute-done | bytes 1179680 | tf_op jit(solution)/shard_map/ppermute | solution.py:272
  62.8 1.2 collective-permute-start.12
  64.0 1.0 collective-permute-start
  65.0 0.1 collective-permute-start.3
  65.1 0.7 collective-permute-done.5.rest_6_
  65.8 1.3 collective-permute-start.4
  67.1 11.0 %collective-permute-done.12.rest_10_ = bf16[768,768]{1,0:T(8,128)(2,1)S(1)} collective-permute-done((bf16[768,768]{1,0:T(8,128)(2,1)S(1)}, bf16[768,768]{1,0:T(8,128)(2,1)S(1)}, u32[]{:S(2)}, u32[]{:S(2)}) %collective-permute-start.12) | collective-permute-done | bytes 1179680 | tf_op jit(solution)/shard_map/ppermute | solution.py:272
  78.1 2.4 %collective-permute-start.13 = (bf16[768,768]{1,0:T(8,128)(2,1)S(1)}, bf16[768,768]{1,0:T(8,128)(2,1)S(1)}, u32[]{:S(2)}, u32[]{:S(2)}) collective-permute-start(bf16[768,768]{1,0:T(8,128)(2,1)S(1)} %collective-permute-done.12.rest_10_), channel_id=1, source_target_pairs={{0,8},{4,60},{8,16},{12,4},{16,24},{20,12},{24,32},{28,20},{32,40}... | collective-permute-start | bytes 3538952 | tf_op jit(solution)/shard_map/ppermute | solution.py:272
  80.7 1.8 collective-permute-start.6
  82.5 0.2 fusion.1
  82.7 0.6 collective-permute-start.15
  83.4 0.1 collective-permute-start.16
  83.5 0.6 collective-permute-start.25
  84.1 9.6 %collective-permute-done.13.rest_11_ = bf16[768,768]{1,0:T(8,128)(2,1)S(1)} collective-permute-done((bf16[768,768]{1,0:T(8,128)(2,1)S(1)}, bf16[768,768]{1,0:T(8,128)(2,1)S(1)}, u32[]{:S(2)}, u32[]{:S(2)}) %collective-permute-start.13) | collective-permute-done | bytes 1179680 | tf_op jit(solution)/shard_map/ppermute | solution.py:272
  93.7 2.5 %collective-permute-start.24 = (bf16[768,768]{1,0:T(8,128)(2,1)S(1)}, bf16[768,768]{1,0:T(8,128)(2,1)S(1)}, u32[]{:S(2)}, u32[]{:S(2)}) collective-permute-start(bf16[768,768]{1,0:T(8,128)(2,1)S(1)} %get-tuple-element.8), channel_id=1, source_target_pairs={{0,64},{4,196},{64,128},{68,4},{128,192},{132,68},{192,0},{196,132... | collective-permute-start | bytes 3538952 | tf_op jit(solution)/shard_map/ppermute | solution.py:272
  96.3 5.1 %collective-permute-start.17 = (bf16[384,768]{1,0:T(8,128)(2,1)S(1)}, bf16[384,768]{1,0:T(8,128)(2,1)S(1)}, u32[]{:S(2)}, u32[]{:S(2)}) collective-permute-start(bf16[384,768]{1,0:T(8,128)(2,1)S(1)} %get-tuple-element.9), channel_id=1, source_target_pairs={{0,4},{4,0},{1,5},{5,1},{2,6},{6,2},{3,7},{7,3},{8,12},{12,8},{9,1... | collective-permute-start | bytes 1769480 | tf_op jit(solution)/shard_map/ppermute | solution.py:288
  101.5 1.6 collective-permute-done.17.rest_15_
  103.1 7.4 %collective-permute-done.14.rest_12_ = bf16[384,768]{1,0:T(8,128)(2,1)S(1)} collective-permute-done((bf16[384,768]{1,0:T(8,128)(2,1)S(1)}, bf16[384,768]{1,0:T(8,128)(2,1)S(1)}, u32[]{:S(2)}, u32[]{:S(2)}) %collective-permute-start.14) | collective-permute-done | bytes 589856 | tf_op jit(solution)/shard_map/ppermute | solution.py:272
  110.6 0.7 copy-done.20
  111.3 0.5 copy-done.15
  111.8 1.0 copy-done.16
  112.8 18.4 %project.1 = bf16[1536,768]{1,0:T(8,128)(2,1)} custom-call(s32[1,64]{1,0:T(1,128)} %bitcast.26, bf16[448,1536]{1,0:T(8,128)(2,1)} %bitcast.20, bf16[448,1536]{1,0:T(8,128)(2,1)} %copy-done.11, bf16[448,1536]{1,0:T(8,128)(2,1)} %copy-done.9, bf16[448,1536]{1,0:T(8,128)(2,1)} %copy-done.12, bf16[448,1536]{1,0:T(8,128)(2,1)} %copy-done.8, ...), custom_call_target="tpu_custom_call" | custom-call | flops 8455716864 | bytes 20447232 | tf_op jit(solution)/shard_map/project/pallas_call | solution.py:193
  131.2 13.3 %all-to-all-start = ((bf16[64,24,768]{2,1,0:T(8,128)(2,1)}), bf16[64,24,768]{2,1,0:T(8,128)(2,1)S(1)}, u32[]{:S(2)}, u32[]{:S(2)}) async-start(bf16[64,24,768]{2,1,0:T(8,128)(2,1)} %bitcast.17), calls=%async_computation | async-start | bytes 4718592 | tf_op jit(solution)/shard_map/all_to_all | solution.py:353
  144.5 0.6 dynamic_slice.3.live_ref
  145.1 56.0 %all-to-all-done = bf16[64,24,768]{2,1,0:T(8,128)(2,1)S(1)} async-done(((bf16[64,24,768]{2,1,0:T(8,128)(2,1)}), bf16[64,24,768]{2,1,0:T(8,128)(2,1)S(1)}, u32[]{:S(2)}, u32[]{:S(2)}) %all-to-all-start) | async-done | bytes 2359328 | tf_op jit(solution)/shard_map/all_to_all | solution.py:353
  201.1 1.6 fusion
  202.7 7.8 %attend.1 = bf16[128,768]{1,0:T(8,128)(2,1)} custom-call(s32[1]{0:T(128)} %dynamic_slice.3.live_ref, bf16[128,768]{1,0:T(8,128)(2,1)} %bitcast.22, bf16[768,768]{1,0:T(8,128)(2,1)} %bitcast.16, bf16[768,768]{1,0:T(8,128)(2,1)} %bitcast.15, bf16[128,768]{1,0:T(8,128)(2,1)} %bitcast.23, bf16[128,768]{1,0:T(8,128)(2,1)} %bitcast.24), custom_call_target="tpu_custom_call" | custom-call | tf_op jit(solution)/shard_map/attend/pallas_call | solution.py:254
  (88 shorter events, 0.8 us)
Async XLA Ops:
  1.0 14.6 %collective-permute-start.7 = (bf16[192,768]{1,0:T(8,128)(2,1)S(1)}, bf16[192,768]{1,0:T(8,128)(2,1)S(1)}, u32[]{:S(2)}, u32[]{:S(2)}) collective-permute-start(bf16[192,768]{1,0:T(8,128)(2,1)S(1)} %pad_maximum_fusion.3), channel_id=1, source_target_pairs={{0,4},{4,0},{1,5},{5,1},{2,6},{6,2},{3,7},{7,3},{8,12},{12,8},{9,1... | collective-permute-start | bytes 884744 | tf_op jit(solution)/shard_map/ppermute | solution.py:288
  13.0 52.0 %collective-permute-start.2 = (bf16[448,1536]{1,0:T(8,128)(2,1)}, bf16[448,1536]{1,0:T(8,128)(2,1)S(1)}, u32[]{:S(2)}, u32[]{:S(2)}) collective-permute-start(bf16[448,1536]{1,0:T(8,128)(2,1)} %bitcast.18), channel_id=1, source_target_pairs={{0,3},{4,5},{1,0},{5,6},{2,1},{6,7},{3,2},{7,4},{8,11},{12,13},{9,... | collective-permute-start | bytes 4128776 | tf_op jit(solution)/shard_map/ppermute | solution.py:272
  13.0 34.5 %collective-permute-start.1 = (bf16[448,1536]{1,0:T(8,128)(2,1)}, bf16[448,1536]{1,0:T(8,128)(2,1)S(1)}, u32[]{:S(2)}, u32[]{:S(2)}) collective-permute-start(bf16[448,1536]{1,0:T(8,128)(2,1)} %bitcast.19), channel_id=1, source_target_pairs={{0,1},{4,7},{1,2},{5,4},{2,3},{6,5},{3,0},{7,6},{8,9},{12,15},{9,1... | collective-permute-start | bytes 4128776 | tf_op jit(solution)/shard_map/ppermute | solution.py:272
  15.8 7.6 %collective-permute-start.18 = (bf16[192,768]{1,0:T(8,128)(2,1)S(1)}, bf16[192,768]{1,0:T(8,128)(2,1)S(1)}, u32[]{:S(2)}, u32[]{:S(2)}) collective-permute-start(bf16[192,768]{1,0:T(8,128)(2,1)S(1)} %get-tuple-element.11), channel_id=1, source_target_pairs={{0,8},{4,60},{8,16},{12,4},{16,24},{20,12},{24,32},{28,20},{32,40}... | collective-permute-start | bytes 884744 | tf_op jit(solution)/shard_map/ppermute | solution.py:272
  19.7 7.1 %collective-permute-start.8 = (bf16[192,768]{1,0:T(8,128)(2,1)S(1)}, bf16[192,768]{1,0:T(8,128)(2,1)S(1)}, u32[]{:S(2)}, u32[]{:S(2)}) collective-permute-start(bf16[192,768]{1,0:T(8,128)(2,1)S(1)} %get-tuple-element.12), channel_id=1, source_target_pairs={{0,64},{4,196},{64,128},{68,4},{128,192},{132,68},{192,0},{196,132... | collective-permute-start | bytes 884744 | tf_op jit(solution)/shard_map/ppermute | solution.py:272
  23.4 7.1 %collective-permute-start.19 = (bf16[192,768]{1,0:T(8,128)(2,1)S(1)}, bf16[192,768]{1,0:T(8,128)(2,1)S(1)}, u32[]{:S(2)}, u32[]{:S(2)}) collective-permute-start(bf16[192,768]{1,0:T(8,128)(2,1)S(1)} %collective-permute-done.18), channel_id=1, source_target_pairs={{0,8},{4,60},{8,16},{12,4},{16,24},{20,12},{24,32},{28,20},{32,40}... | collective-permute-start | bytes 884744 | tf_op jit(solution)/shard_map/ppermute | solution.py:272
  26.8 7.1 %collective-permute-start.9 = (bf16[96,768]{1,0:T(8,128)(2,1)S(1)}, bf16[96,768]{1,0:T(8,128)(2,1)S(1)}, u32[]{:S(2)}, u32[]{:S(2)}) collective-permute-start(bf16[96,768]{1,0:T(8,128)(2,1)S(1)} %get-tuple-element.15), channel_id=1, source_target_pairs={{0,64},{4,196},{64,128},{68,4},{128,192},{132,68},{192,0},{196,132... | collective-permute-start | bytes 442376 | tf_op jit(solution)/shard_map/ppermute | solution.py:272
  30.4 7.1 %collective-permute-start.20 = (bf16[192,768]{1,0:T(8,128)(2,1)S(1)}, bf16[192,768]{1,0:T(8,128)(2,1)S(1)}, u32[]{:S(2)}, u32[]{:S(2)}) collective-permute-start(bf16[192,768]{1,0:T(8,128)(2,1)S(1)} %collective-permute-done.19), channel_id=1, source_target_pairs={{0,8},{4,60},{8,16},{12,4},{16,24},{20,12},{24,32},{28,20},{32,40}... | collective-permute-start | bytes 884744 | tf_op jit(solution)/shard_map/ppermute | solution.py:272
  33.9 7.1 %collective-permute-start.10 = (bf16[288,768]{1,0:T(8,128)(2,1)S(1)}, bf16[288,768]{1,0:T(8,128)(2,1)S(1)}, u32[]{:S(2)}, u32[]{:S(2)}) collective-permute-start(bf16[288,768]{1,0:T(8,128)(2,1)S(1)} %pad_maximum_fusion.1), channel_id=1, source_target_pairs={{0,4},{4,0},{1,5},{5,1},{2,6},{6,2},{3,7},{7,3},{8,12},{12,8},{9,1... | collective-permute-start | bytes 1327112 | tf_op jit(solution)/shard_map/ppermute | solution.py:288
  37.5 5.6 %collective-permute-start.21 = (bf16[96,768]{1,0:T(8,128)(2,1)S(1)}, bf16[96,768]{1,0:T(8,128)(2,1)S(1)}, u32[]{:S(2)}, u32[]{:S(2)}) collective-permute-start(bf16[96,768]{1,0:T(8,128)(2,1)S(1)} %get-tuple-element.13), channel_id=1, source_target_pairs={{0,8},{4,60},{8,16},{12,4},{16,24},{20,12},{24,32},{28,20},{32,40}... | collective-permute-start | bytes 442376 | tf_op jit(solution)/shard_map/ppermute | solution.py:272
  43.2 7.3 %collective-permute-start.22 = (bf16[672,768]{1,0:T(8,128)(2,1)S(1)}, bf16[672,768]{1,0:T(8,128)(2,1)S(1)}, u32[]{:S(2)}, u32[]{:S(2)}) collective-permute-start(bf16[672,768]{1,0:T(8,128)(2,1)S(1)} %pad_maximum_fusion), channel_id=1, source_target_pairs={{0,4},{4,0},{1,5},{5,1},{2,6},{6,2},{3,7},{7,3},{8,12},{12,8},{9,1... | collective-permute-start | bytes 3096584 | tf_op jit(solution)/shard_map/ppermute | solution.py:288
  47.3 16.7 %copy-start.1 = (bf16[2,224,1536]{2,1,0:T(8,128)(2,1)S(1)}, bf16[2,224,1536]{2,1,0:T(8,128)(2,1)}, u32[]{:S(2)}) copy-start(bf16[2,224,1536]{2,1,0:T(8,128)(2,1)} %live_rows.1) | copy-start | bytes 4128772
  47.4 33.3 %copy-start.5 = (bf16[768,768]{1,0:T(8,128)(2,1)}, bf16[768,768]{1,0:T(8,128)(2,1)S(1)}, u32[]{:S(2)}) copy-start(bf16[768,768]{1,0:T(8,128)(2,1)S(1)} %slice_dynamic-update-slice_fusion.14.rest_8_) | copy-start | bytes 3538948
  47.4 15.4 %collective-permute-start.11 = (bf16[768,768]{1,0:T(8,128)(2,1)S(1)}, bf16[768,768]{1,0:T(8,128)(2,1)S(1)}, u32[]{:S(2)}, u32[]{:S(2)}) collective-permute-start(bf16[768,768]{1,0:T(8,128)(2,1)S(1)} %slice_dynamic-update-slice_fusion.14.rest_8_), channel_id=1, source_target_pairs={{0,8},{4,60},{8,16},{12,4},{16,24},{20,12},{24,32},{28,20},{32,40}... | collective-permute-start | bytes 3538952 | tf_op jit(solution)/shard_map/ppermute | solution.py:272
  47.5 33.2 %copy-start.9 = (bf16[448,1536]{1,0:T(8,128)(2,1)}, bf16[448,1536]{1,0:T(8,128)(2,1)S(1)}, u32[]{:S(2)}) copy-start(bf16[448,1536]{1,0:T(8,128)(2,1)S(1)} %collective-permute-done.1.rest_2_) | copy-start | bytes 4128772
  47.5 18.3 %collective-permute-start.5 = (bf16[448,1536]{1,0:T(8,128)(2,1)S(1)}, bf16[448,1536]{1,0:T(8,128)(2,1)S(1)}, u32[]{:S(2)}, u32[]{:S(2)}) collective-permute-start(bf16[448,1536]{1,0:T(8,128)(2,1)S(1)} %collective-permute-done.1.rest_2_), channel_id=1, source_target_pairs={{0,1},{4,7},{1,2},{5,4},{2,3},{6,5},{3,0},{7,6},{8,9},{12,15},{9,1... | collective-permute-start | bytes 4128776 | tf_op jit(solution)/shard_map/ppermute | solution.py:272
  50.7 29.9 %copy-start.6 = (bf16[1536,768]{1,0:T(8,128)(2,1)}, bf16[1536,768]{1,0:T(8,128)(2,1)S(1)}, u32[]{:S(2)}) copy-start(bf16[1536,768]{1,0:T(8,128)(2,1)S(1)} %slice_dynamic-update-slice_fusion.rest_16_) | copy-start | bytes 7077892
  50.8 29.9 %collective-permute-start.23 = (bf16[1536,768]{1,0:T(8,128)(2,1)S(1)}, bf16[1536,768]{1,0:T(8,128)(2,1)S(1)}, u32[]{:S(2)}, u32[]{:S(2)}) collective-permute-start(bf16[1536,768]{1,0:T(8,128)(2,1)S(1)} %slice_dynamic-update-slice_fusion.rest_16_), channel_id=1, source_target_pairs={{0,64},{4,196},{64,128},{68,4},{128,192},{132,68},{192,0},{196,132... | collective-permute-start | bytes 7077896 | tf_op jit(solution)/shard_map/ppermute | solution.py:272
  62.8 19.9 %copy-start.3 = (bf16[768,768]{1,0:T(8,128)(2,1)}, bf16[768,768]{1,0:T(8,128)(2,1)S(1)}, u32[]{:S(2)}) copy-start(bf16[768,768]{1,0:T(8,128)(2,1)S(1)} %collective-permute-done.11.rest_9_) | copy-start | bytes 3538948
  62.8 15.3 %collective-permute-start.12 = (bf16[768,768]{1,0:T(8,128)(2,1)S(1)}, bf16[768,768]{1,0:T(8,128)(2,1)S(1)}, u32[]{:S(2)}, u32[]{:S(2)}) collective-permute-start(bf16[768,768]{1,0:T(8,128)(2,1)S(1)} %collective-permute-done.11.rest_9_), channel_id=1, source_target_pairs={{0,8},{4,60},{8,16},{12,4},{16,24},{20,12},{24,32},{28,20},{32,40}... | collective-permute-start | bytes 3538952 | tf_op jit(solution)/shard_map/ppermute | solution.py:272
  64.0 18.7 %collective-permute-start = (bf16[448,1536]{1,0:T(8,128)(2,1)S(1)}, bf16[448,1536]{1,0:T(8,128)(2,1)S(1)}, u32[]{:S(2)}, u32[]{:S(2)}) collective-permute-start(bf16[448,1536]{1,0:T(8,128)(2,1)S(1)} %bitcast.21), channel_id=1, source_target_pairs={{0,4},{4,0},{1,5},{5,1},{2,6},{6,2},{3,7},{7,3},{8,12},{12,8},{9,1... | collective-permute-start | bytes 4128776 | tf_op jit(solution)/shard_map/ppermute | solution.py:288
  65.0 17.7 %copy-start.8 = (bf16[448,1536]{1,0:T(8,128)(2,1)}, bf16[448,1536]{1,0:T(8,128)(2,1)S(1)}, u32[]{:S(2)}) copy-start(bf16[448,1536]{1,0:T(8,128)(2,1)S(1)} %collective-permute-done.2.rest_4_) | copy-start | bytes 4128772
  65.0 18.4 %collective-permute-start.3 = (bf16[448,1536]{1,0:T(8,128)(2,1)S(1)}, bf16[448,1536]{1,0:T(8,128)(2,1)S(1)}, u32[]{:S(2)}, u32[]{:S(2)}) collective-permute-start(bf16[448,1536]{1,0:T(8,128)(2,1)S(1)} %collective-permute-done.2.rest_4_), channel_id=1, source_target_pairs={{0,4},{4,0},{1,5},{5,1},{2,6},{6,2},{3,7},{7,3},{8,12},{12,8},{9,1... | collective-permute-start | bytes 4128776 | tf_op jit(solution)/shard_map/ppermute | solution.py:288
  65.8 44.8 %copy-start.10 = (bf16[448,1536]{1,0:T(8,128)(2,1)}, bf16[448,1536]{1,0:T(8,128)(2,1)S(1)}, u32[]{:S(2)}) copy-start(bf16[448,1536]{1,0:T(8,128)(2,1)S(1)} %collective-permute-done.5.rest_6_) | copy-start | bytes 4128772
  65.8 17.7 %collective-permute-start.4 = (bf16[448,1536]{1,0:T(8,128)(2,1)S(1)}, bf16[448,1536]{1,0:T(8,128)(2,1)S(1)}, u32[]{:S(2)}, u32[]{:S(2)}) collective-permute-start(bf16[448,1536]{1,0:T(8,128)(2,1)S(1)} %collective-permute-done.1.rest_2_), channel_id=1, source_target_pairs={{0,4},{4,0},{1,5},{5,1},{2,6},{6,2},{3,7},{7,3},{8,12},{12,8},{9,1... | collective-permute-start | bytes 4128776 | tf_op jit(solution)/shard_map/ppermute | solution.py:288
  78.1 4.6 %copy-start.4 = (bf16[768,768]{1,0:T(8,128)(2,1)}, bf16[768,768]{1,0:T(8,128)(2,1)S(1)}, u32[]{:S(2)}) copy-start(bf16[768,768]{1,0:T(8,128)(2,1)S(1)} %collective-permute-done.12.rest_10_) | copy-start | bytes 3538948
  78.1 15.6 %collective-permute-start.13 = (bf16[768,768]{1,0:T(8,128)(2,1)S(1)}, bf16[768,768]{1,0:T(8,128)(2,1)S(1)}, u32[]{:S(2)}, u32[]{:S(2)}) collective-permute-start(bf16[768,768]{1,0:T(8,128)(2,1)S(1)} %collective-permute-done.12.rest_10_), channel_id=1, source_target_pairs={{0,8},{4,60},{8,16},{12,4},{16,24},{20,12},{24,32},{28,20},{32,40}... | collective-permute-start | bytes 3538952 | tf_op jit(solution)/shard_map/ppermute | solution.py:272
  80.7 2.8 %copy-start = (bf16[1536,768]{1,0:T(8,128)(2,1)}, bf16[1536,768]{1,0:T(8,128)(2,1)S(1)}, u32[]{:S(2)}) copy-start(bf16[1536,768]{1,0:T(8,128)(2,1)S(1)} %collective-permute-done.23.rest_17_) | copy-start | bytes 7077892
  80.7 20.8 %collective-permute-start.6 = (bf16[448,1536]{1,0:T(8,128)(2,1)S(1)}, bf16[448,1536]{1,0:T(8,128)(2,1)S(1)}, u32[]{:S(2)}, u32[]{:S(2)}) collective-permute-start(bf16[448,1536]{1,0:T(8,128)(2,1)S(1)} %collective-permute-done.5.rest_6_), channel_id=1, source_target_pairs={{0,4},{4,0},{1,5},{5,1},{2,6},{6,2},{3,7},{7,3},{8,12},{12,8},{9,1... | collective-permute-start | bytes 4128776 | tf_op jit(solution)/shard_map/ppermute | solution.py:288
  82.7 27.8 %copy-start.11 = (bf16[448,1536]{1,0:T(8,128)(2,1)}, bf16[448,1536]{1,0:T(8,128)(2,1)S(1)}, u32[]{:S(2)}) copy-start(bf16[448,1536]{1,0:T(8,128)(2,1)S(1)} %collective-permute-done.rest_1_) | copy-start | bytes 4128772
  82.7 13.6 %collective-permute-start.15 = (bf16[384,768]{1,0:T(8,128)(2,1)S(1)}, bf16[384,768]{1,0:T(8,128)(2,1)S(1)}, u32[]{:S(2)}, u32[]{:S(2)}) collective-permute-start(bf16[384,768]{1,0:T(8,128)(2,1)S(1)} %slice.130), channel_id=1, source_target_pairs={{0,4},{4,0},{1,5},{5,1},{2,6},{6,2},{3,7},{7,3},{8,12},{12,8},{9,1... | collective-permute-start | bytes 1769480 | tf_op jit(solution)/shard_map/ppermute | solution.py:288
  83.4 27.2 %copy-start.12 = (bf16[448,1536]{1,0:T(8,128)(2,1)}, bf16[448,1536]{1,0:T(8,128)(2,1)S(1)}, u32[]{:S(2)}) copy-start(bf16[448,1536]{1,0:T(8,128)(2,1)S(1)} %collective-permute-done.3.rest_3_) | copy-start | bytes 4128772
  83.4 18.1 %collective-permute-start.16 = (bf16[384,768]{1,0:T(8,128)(2,1)S(1)}, bf16[384,768]{1,0:T(8,128)(2,1)S(1)}, u32[]{:S(2)}, u32[]{:S(2)}) collective-permute-start(bf16[384,768]{1,0:T(8,128)(2,1)S(1)} %slice.131), channel_id=1, source_target_pairs={{0,4},{4,0},{1,5},{5,1},{2,6},{6,2},{3,7},{7,3},{8,12},{12,8},{9,1... | collective-permute-start | bytes 1769480 | tf_op jit(solution)/shard_map/ppermute | solution.py:288
  83.5 27.1 %copy-start.13 = (bf16[448,1536]{1,0:T(8,128)(2,1)}, bf16[448,1536]{1,0:T(8,128)(2,1)S(1)}, u32[]{:S(2)}) copy-start(bf16[448,1536]{1,0:T(8,128)(2,1)S(1)} %collective-permute-done.4.rest_5_) | copy-start | bytes 4128772
  83.5 27.0 %collective-permute-start.25 = (bf16[768,768]{1,0:T(8,128)(2,1)S(1)}, bf16[768,768]{1,0:T(8,128)(2,1)S(1)}, u32[]{:S(2)}, u32[]{:S(2)}) collective-permute-start(bf16[768,768]{1,0:T(8,128)(2,1)S(1)} %get-tuple-element.7), channel_id=1, source_target_pairs={{0,4},{4,0},{1,5},{5,1},{2,6},{6,2},{3,7},{7,3},{8,12},{12,8},{9,1... | collective-permute-start | bytes 3538952 | tf_op jit(solution)/shard_map/ppermute | solution.py:288
  93.7 16.9 %copy-start.2 = (bf16[768,768]{1,0:T(8,128)(2,1)}, bf16[768,768]{1,0:T(8,128)(2,1)S(1)}, u32[]{:S(2)}) copy-start(bf16[768,768]{1,0:T(8,128)(2,1)S(1)} %collective-permute-done.13.rest_11_) | copy-start | bytes 3538948
  93.7 16.9 %collective-permute-start.24 = (bf16[768,768]{1,0:T(8,128)(2,1)S(1)}, bf16[768,768]{1,0:T(8,128)(2,1)S(1)}, u32[]{:S(2)}, u32[]{:S(2)}) collective-permute-start(bf16[768,768]{1,0:T(8,128)(2,1)S(1)} %get-tuple-element.8), channel_id=1, source_target_pairs={{0,64},{4,196},{64,128},{68,4},{128,192},{132,68},{192,0},{196,132... | collective-permute-start | bytes 3538952 | tf_op jit(solution)/shard_map/ppermute | solution.py:272
  96.3 14.3 %copy-start.17 = (bf16[384,768]{1,0:T(8,128)(2,1)}, bf16[384,768]{1,0:T(8,128)(2,1)S(1)}, u32[]{:S(2)}) copy-start(bf16[384,768]{1,0:T(8,128)(2,1)S(1)} %collective-permute-done.15.rest_13_) | copy-start | bytes 1769476
  96.3 6.8 %collective-permute-start.17 = (bf16[384,768]{1,0:T(8,128)(2,1)S(1)}, bf16[384,768]{1,0:T(8,128)(2,1)S(1)}, u32[]{:S(2)}, u32[]{:S(2)}) collective-permute-start(bf16[384,768]{1,0:T(8,128)(2,1)S(1)} %get-tuple-element.9), channel_id=1, source_target_pairs={{0,4},{4,0},{1,5},{5,1},{2,6},{6,2},{3,7},{7,3},{8,12},{12,8},{9,1... | collective-permute-start | bytes 1769480 | tf_op jit(solution)/shard_map/ppermute | solution.py:288
  101.5 9.1 %copy-start.18 = (bf16[384,768]{1,0:T(8,128)(2,1)}, bf16[384,768]{1,0:T(8,128)(2,1)S(1)}, u32[]{:S(2)}) copy-start(bf16[384,768]{1,0:T(8,128)(2,1)S(1)} %collective-permute-done.16.rest_14_) | copy-start | bytes 1769476
  101.5 9.0 %collective-permute-start.14 = (bf16[384,768]{1,0:T(8,128)(2,1)S(1)}, bf16[384,768]{1,0:T(8,128)(2,1)S(1)}, u32[]{:S(2)}, u32[]{:S(2)}) collective-permute-start(bf16[384,768]{1,0:T(8,128)(2,1)S(1)} %get-tuple-element.10), channel_id=1, source_target_pairs={{0,8},{4,60},{8,16},{12,4},{16,24},{20,12},{24,32},{28,20},{32,40}... | collective-permute-start | bytes 1769480 | tf_op jit(solution)/shard_map/ppermute | solution.py:272
  101.5 9.1 %copy-start.14 = (bf16[448,1536]{1,0:T(8,128)(2,1)}, bf16[448,1536]{1,0:T(8,128)(2,1)S(1)}, u32[]{:S(2)}) copy-start(bf16[448,1536]{1,0:T(8,128)(2,1)S(1)} %collective-permute-done.6.rest_7_) | copy-start | bytes 4128772
  103.1 7.5 %copy-start.19 = (bf16[384,768]{1,0:T(8,128)(2,1)}, bf16[384,768]{1,0:T(8,128)(2,1)S(1)}, u32[]{:S(2)}) copy-start(bf16[384,768]{1,0:T(8,128)(2,1)S(1)} %collective-permute-done.17.rest_15_) | copy-start | bytes 1769476
  110.5 0.8 copy-start.20
  110.6 1.2 copy-start.15
  111.8 1.0 copy-start.16
  131.2 13.3 %copy-start.7 = (s32[64]{0:T(128)S(1)}, s32[64]{0:T(128)}, u32[]{:S(2)}) copy-start(s32[64]{0:T(128)} %param.13) | copy-start | bytes 772
  131.2 69.9 %all-to-all-start = ((bf16[64,24,768]{2,1,0:T(8,128)(2,1)}), bf16[64,24,768]{2,1,0:T(8,128)(2,1)S(1)}, u32[]{:S(2)}, u32[]{:S(2)}) async-start(bf16[64,24,768]{2,1,0:T(8,128)(2,1)} %bitcast.17), calls=%async_computation | async-start | bytes 4718592 | tf_op jit(solution)/shard_map/all_to_all | solution.py:353

commit v9 on v8

--- a/solution.py
+++ b/solution.py
@@ -225,7 +225,7 @@
     token = jnp.where(token < new, token, token - new)
     new_ok = iota((2 * new, new), 1) <= token
 
-    @pl.loop(0, k_ref.shape[1] // (2 * HD))
+    @pl.loop(0, k_ref.shape[1] // (2 * HD), unroll=2)
     def _(pair):
         lanes = pl.ds(pl.multiple_of(pair * 2 * HD, 2 * HD), 2 * HD)
         all_lanes = pl.ds(pl.multiple_of(first + pair * 2 * HD, 2 * HD), 2 * HD)

time: 211 us -> 210 us (level)
  no operation moved by 1% of the time
where the time goes in v9:
time: 210 us
  waiting for transfers between devices  103 us (49%)
  starting transfers between devices  66 us (31%)
  Pallas kernels  29.7 us (14%)
  local copies, waits for them, and re-layouts  9.58 us (5%)
    all_to_all x1, waiting for transfers between devices, per_device(): got = lax.all_to_all(sent, PLANE, split_axis=0, concat_axis=0, tiled=True)  56 us
    ppermute x15, waiting for transfers between devices, ring_step(): return lax.ppermute(x, order, perm)  45.3 us
    ppermute x15, starting transfers between devices, ring_step(): return lax.ppermute(x, order, perm)  34.5 us
    pallas_call x1, Pallas kernels, project(): pl.pallas_call(functools.partial(project_kernel, dims), out_shape=jax.Sha...  18.4 us
    ppermute x11, starting transfers between devices, swap_cores(): return lax.ppermute(x, 'core', [(0, 1), (1, 0)])  18.2 us
    all_to_all x1, starting transfers between devices, per_device(): got = lax.all_to_all(sent, PLANE, split_axis=0, concat_axis=0, tiled=True)  13.3 us
    pallas_call x1, Pallas kernels, attend(): pl.pallas_call(functools.partial(attend_kernel, first), out_shape=jax.Sha...  7.23 us
    unnamed x63, local copies, waits for them, and re-layouts  5.81 us
  transfers between devices with their start and end apart: 27, of which 11 were waited for; matrix products, arithmetic and copies ran while one was open for 3% of the time, Pallas kernels for 2%

profile of v9, /device:TPU:1, one launch (start us, length us, event | category | flops | bytes accessed | tf_op | source)
XLA Modules:
  0.0 209.9 jit_solution(7753217298072614577)
XLA Ops:
  0.0 1.0 broadcast_select_fusion.2
  1.0 3.3 %collective-permute-start.7 = (bf16[192,768]{1,0:T(8,128)(2,1)S(1)}, bf16[192,768]{1,0:T(8,128)(2,1)S(1)}, u32[]{:S(2)}, u32[]{:S(2)}) collective-permute-start(bf16[192,768]{1,0:T(8,128)(2,1)S(1)} %pad_maximum_fusion.3), channel_id=1, source_target_pairs={{0,4},{4,0},{1,5},{5,1},{2,6},{6,2},{3,7},{7,3},{8,12},{12,8},{9,1... | collective-permute-start | bytes 884744 | tf_op jit(solution)/shard_map/ppermute | solution.py:288
  4.4 1.2 broadcast_in_dim.11.table_ref
  5.6 3.3 %copy.12 = bf16[384,2,1536]{2,0,1:T(8,128)(2,1)} copy(bf16[384,2,1536]{2,1,0:T(2,128)(2,1)} %param.11) | data formatting | bytes 4718592 | tf_op args[3]
  8.9 4.1 %live_rows.1 = bf16[2,224,1536]{2,1,0:T(8,128)(2,1)} custom-call(s32[1,64]{1,0:T(1,128)} %bitcast.25, s32[1,384]{1,0:T(1,128)} %broadcast_in_dim.11.table_ref, bf16[2,384,1536]{2,1,0:T(8,128)(2,1)} %bitcast.14), custom_call_target="tpu_custom_call" | custom-call | tf_op jit(solution)/shard_map/live_rows/pallas_call | solution.py:51
  13.0 2.7 %collective-permute-start.1 = (bf16[448,1536]{1,0:T(8,128)(2,1)}, bf16[448,1536]{1,0:T(8,128)(2,1)S(1)}, u32[]{:S(2)}, u32[]{:S(2)}) collective-permute-start(bf16[448,1536]{1,0:T(8,128)(2,1)} %bitcast.19), channel_id=1, source_target_pairs={{0,1},{4,7},{1,2},{5,4},{2,3},{6,5},{3,0},{7,6},{8,9},{12,15},{9,1... | collective-permute-start | bytes 4128776 | tf_op jit(solution)/shard_map/ppermute | solution.py:272
  15.7 0.1 broadcast_select_fusion
  15.8 3.9 %collective-permute-start.18 = (bf16[192,768]{1,0:T(8,128)(2,1)S(1)}, bf16[192,768]{1,0:T(8,128)(2,1)S(1)}, u32[]{:S(2)}, u32[]{:S(2)}) collective-permute-start(bf16[192,768]{1,0:T(8,128)(2,1)S(1)} %get-tuple-element.11), channel_id=1, source_target_pairs={{0,8},{4,60},{8,16},{12,4},{16,24},{20,12},{24,32},{28,20},{32,40}... | collective-permute-start | bytes 884744 | tf_op jit(solution)/shard_map/ppermute | solution.py:272
  19.7 2.7 %collective-permute-start.8 = (bf16[192,768]{1,0:T(8,128)(2,1)S(1)}, bf16[192,768]{1,0:T(8,128)(2,1)S(1)}, u32[]{:S(2)}, u32[]{:S(2)}) collective-permute-start(bf16[192,768]{1,0:T(8,128)(2,1)S(1)} %get-tuple-element.12), channel_id=1, source_target_pairs={{0,64},{4,196},{64,128},{68,4},{128,192},{132,68},{192,0},{196,132... | collective-permute-start | bytes 884744 | tf_op jit(solution)/shard_map/ppermute | solution.py:272
  22.4 0.9 collective-permute-done.18
  23.4 3.4 %collective-permute-start.19 = (bf16[192,768]{1,0:T(8,128)(2,1)S(1)}, bf16[192,768]{1,0:T(8,128)(2,1)S(1)}, u32[]{:S(2)}, u32[]{:S(2)}) collective-permute-start(bf16[192,768]{1,0:T(8,128)(2,1)S(1)} %collective-permute-done.18), channel_id=1, source_target_pairs={{0,8},{4,60},{8,16},{12,4},{16,24},{20,12},{24,32},{28,20},{32,40}... | collective-permute-start | bytes 884744 | tf_op jit(solution)/shard_map/ppermute | solution.py:272
  26.8 2.8 %collective-permute-start.9 = (bf16[96,768]{1,0:T(8,128)(2,1)S(1)}, bf16[96,768]{1,0:T(8,128)(2,1)S(1)}, u32[]{:S(2)}, u32[]{:S(2)}) collective-permute-start(bf16[96,768]{1,0:T(8,128)(2,1)S(1)} %get-tuple-element.15), channel_id=1, source_target_pairs={{0,64},{4,196},{64,128},{68,4},{128,192},{132,68},{192,0},{196,132... | collective-permute-start | bytes 442376 | tf_op jit(solution)/shard_map/ppermute | solution.py:272
  29.6 0.8 collective-permute-done.19
  30.4 3.4 %collective-permute-start.20 = (bf16[192,768]{1,0:T(8,128)(2,1)S(1)}, bf16[192,768]{1,0:T(8,128)(2,1)S(1)}, u32[]{:S(2)}, u32[]{:S(2)}) collective-permute-start(bf16[192,768]{1,0:T(8,128)(2,1)S(1)} %collective-permute-done.19), channel_id=1, source_target_pairs={{0,8},{4,60},{8,16},{12,4},{16,24},{20,12},{24,32},{28,20},{32,40}... | collective-permute-start | bytes 884744 | tf_op jit(solution)/shard_map/ppermute | solution.py:272
  33.9 0.1 collective-permute-start.10
  34.0 3.5 %collective-permute-done.20 = bf16[192,768]{1,0:T(8,128)(2,1)S(1)} collective-permute-done((bf16[192,768]{1,0:T(8,128)(2,1)S(1)}, bf16[192,768]{1,0:T(8,128)(2,1)S(1)}, u32[]{:S(2)}, u32[]{:S(2)}) %collective-permute-start.20) | collective-permute-done | bytes 294944 | tf_op jit(solution)/shard_map/ppermute | solution.py:272
  37.5 3.5 %collective-permute-start.21 = (bf16[96,768]{1,0:T(8,128)(2,1)S(1)}, bf16[96,768]{1,0:T(8,128)(2,1)S(1)}, u32[]{:S(2)}, u32[]{:S(2)}) collective-permute-start(bf16[96,768]{1,0:T(8,128)(2,1)S(1)} %get-tuple-element.13), channel_id=1, source_target_pairs={{0,8},{4,60},{8,16},{12,4},{16,24},{20,12},{24,32},{28,20},{32,40}... | collective-permute-start | bytes 442376 | tf_op jit(solution)/shard_map/ppermute | solution.py:272
  41.0 2.1 collective-permute-done.21
  43.2 4.1 %collective-permute-start.22 = (bf16[672,768]{1,0:T(8,128)(2,1)S(1)}, bf16[672,768]{1,0:T(8,128)(2,1)S(1)}, u32[]{:S(2)}, u32[]{:S(2)}) collective-permute-start(bf16[672,768]{1,0:T(8,128)(2,1)S(1)} %pad_maximum_fusion), channel_id=1, source_target_pairs={{0,4},{4,0},{1,5},{5,1},{2,6},{6,2},{3,7},{7,3},{8,12},{12,8},{9,1... | collective-permute-start | bytes 3096584 | tf_op jit(solution)/shard_map/ppermute | solution.py:288
  47.5 3.0 %collective-permute-start.5 = (bf16[448,1536]{1,0:T(8,128)(2,1)S(1)}, bf16[448,1536]{1,0:T(8,128)(2,1)S(1)}, u32[]{:S(2)}, u32[]{:S(2)}) collective-permute-start(bf16[448,1536]{1,0:T(8,128)(2,1)S(1)} %collective-permute-done.1.rest_2_), channel_id=1, source_target_pairs={{0,1},{4,7},{1,2},{5,4},{2,3},{6,5},{3,0},{7,6},{8,9},{12,15},{9,1... | collective-permute-start | bytes 4128776 | tf_op jit(solution)/shard_map/ppermute | solution.py:272
  50.8 2.8 %collective-permute-start.23 = (bf16[1536,768]{1,0:T(8,128)(2,1)S(1)}, bf16[1536,768]{1,0:T(8,128)(2,1)S(1)}, u32[]{:S(2)}, u32[]{:S(2)}) collective-permute-start(bf16[1536,768]{1,0:T(8,128)(2,1)S(1)} %slice_dynamic-update-slice_fusion.rest_16_), channel_id=1, source_target_pairs={{0,64},{4,196},{64,128},{68,4},{128,192},{132,68},{192,0},{196,132... | collective-permute-start | bytes 7077896 | tf_op jit(solution)/shard_map/ppermute | solution.py:272
  53.6 9.2 %collective-permute-done.11.rest_9_ = bf16[768,768]{1,0:T(8,128)(2,1)S(1)} collective-permute-done((bf16[768,768]{1,0:T(8,128)(2,1)S(1)}, bf16[768,768]{1,0:T(8,128)(2,1)S(1)}, u32[]{:S(2)}, u32[]{:S(2)}) %collective-permute-start.11) | collective-permute-done | bytes 1179680 | tf_op jit(solution)/shard_map/ppermute | solution.py:272
  62.8 1.2 collective-permute-start.12
  64.0 1.0 collective-permute-start
  65.0 0.1 collective-permute-start.3
  65.1 0.7 collective-permute-done.5.rest_6_
  65.8 1.3 collective-permute-start.4
  67.1 11.0 %collective-permute-done.12.rest_10_ = bf16[768,768]{1,0:T(8,128)(2,1)S(1)} collective-permute-done((bf16[768,768]{1,0:T(8,128)(2,1)S(1)}, bf16[768,768]{1,0:T(8,128)(2,1)S(1)}, u32[]{:S(2)}, u32[]{:S(2)}) %collective-permute-start.12) | collective-permute-done | bytes 1179680 | tf_op jit(solution)/shard_map/ppermute | solution.py:272
  78.1 2.4 %collective-permute-start.13 = (bf16[768,768]{1,0:T(8,128)(2,1)S(1)}, bf16[768,768]{1,0:T(8,128)(2,1)S(1)}, u32[]{:S(2)}, u32[]{:S(2)}) collective-permute-start(bf16[768,768]{1,0:T(8,128)(2,1)S(1)} %collective-permute-done.12.rest_10_), channel_id=1, source_target_pairs={{0,8},{4,60},{8,16},{12,4},{16,24},{20,12},{24,32},{28,20},{32,40}... | collective-permute-start | bytes 3538952 | tf_op jit(solution)/shard_map/ppermute | solution.py:272
  80.7 1.8 collective-permute-start.6
  82.5 0.2 fusion.1
  82.7 0.6 collective-permute-start.15
  83.4 0.1 collective-permute-start.16
  83.5 0.6 collective-permute-start.25
  84.1 9.6 %collective-permute-done.13.rest_11_ = bf16[768,768]{1,0:T(8,128)(2,1)S(1)} collective-permute-done((bf16[768,768]{1,0:T(8,128)(2,1)S(1)}, bf16[768,768]{1,0:T(8,128)(2,1)S(1)}, u32[]{:S(2)}, u32[]{:S(2)}) %collective-permute-start.13) | collective-permute-done | bytes 1179680 | tf_op jit(solution)/shard_map/ppermute | solution.py:272
  93.7 2.5 %collective-permute-start.24 = (bf16[768,768]{1,0:T(8,128)(2,1)S(1)}, bf16[768,768]{1,0:T(8,128)(2,1)S(1)}, u32[]{:S(2)}, u32[]{:S(2)}) collective-permute-start(bf16[768,768]{1,0:T(8,128)(2,1)S(1)} %get-tuple-element.8), channel_id=1, source_target_pairs={{0,64},{4,196},{64,128},{68,4},{128,192},{132,68},{192,0},{196,132... | collective-permute-start | bytes 3538952 | tf_op jit(solution)/shard_map/ppermute | solution.py:272
  96.3 5.1 %collective-permute-start.17 = (bf16[384,768]{1,0:T(8,128)(2,1)S(1)}, bf16[384,768]{1,0:T(8,128)(2,1)S(1)}, u32[]{:S(2)}, u32[]{:S(2)}) collective-permute-start(bf16[384,768]{1,0:T(8,128)(2,1)S(1)} %get-tuple-element.9), channel_id=1, source_target_pairs={{0,4},{4,0},{1,5},{5,1},{2,6},{6,2},{3,7},{7,3},{8,12},{12,8},{9,1... | collective-permute-start | bytes 1769480 | tf_op jit(solution)/shard_map/ppermute | solution.py:288
  101.5 1.6 collective-permute-done.17.rest_15_
  103.1 7.4 %collective-permute-done.14.rest_12_ = bf16[384,768]{1,0:T(8,128)(2,1)S(1)} collective-permute-done((bf16[384,768]{1,0:T(8,128)(2,1)S(1)}, bf16[384,768]{1,0:T(8,128)(2,1)S(1)}, u32[]{:S(2)}, u32[]{:S(2)}) %collective-permute-start.14) | collective-permute-done | bytes 589856 | tf_op jit(solution)/shard_map/ppermute | solution.py:272
  110.6 0.7 copy-done.20
  111.3 0.5 copy-done.15
  111.8 1.0 copy-done.16
  112.8 18.4 %project.1 = bf16[1536,768]{1,0:T(8,128)(2,1)} custom-call(s32[1,64]{1,0:T(1,128)} %bitcast.26, bf16[448,1536]{1,0:T(8,128)(2,1)} %bitcast.20, bf16[448,1536]{1,0:T(8,128)(2,1)} %copy-done.11, bf16[448,1536]{1,0:T(8,128)(2,1)} %copy-done.9, bf16[448,1536]{1,0:T(8,128)(2,1)} %copy-done.12, bf16[448,1536]{1,0:T(8,128)(2,1)} %copy-done.8, ...), custom_call_target="tpu_custom_call" | custom-call | flops 8455716864 | bytes 20447232 | tf_op jit(solution)/shard_map/project/pallas_call | solution.py:193
  131.2 13.3 %all-to-all-start = ((bf16[64,24,768]{2,1,0:T(8,128)(2,1)}), bf16[64,24,768]{2,1,0:T(8,128)(2,1)S(1)}, u32[]{:S(2)}, u32[]{:S(2)}) async-start(bf16[64,24,768]{2,1,0:T(8,128)(2,1)} %bitcast.17), calls=%async_computation | async-start | bytes 4718592 | tf_op jit(solution)/shard_map/all_to_all | solution.py:353
  144.5 0.6 dynamic_slice.3.live_ref
  145.1 56.0 %all-to-all-done = bf16[64,24,768]{2,1,0:T(8,128)(2,1)S(1)} async-done(((bf16[64,24,768]{2,1,0:T(8,128)(2,1)}), bf16[64,24,768]{2,1,0:T(8,128)(2,1)S(1)}, u32[]{:S(2)}, u32[]{:S(2)}) %all-to-all-start) | async-done | bytes 2359328 | tf_op jit(solution)/shard_map/all_to_all | solution.py:353
  201.1 1.6 fusion
  202.7 7.2 %attend.1 = bf16[128,768]{1,0:T(8,128)(2,1)} custom-call(s32[1]{0:T(128)} %dynamic_slice.3.live_ref, bf16[128,768]{1,0:T(8,128)(2,1)} %bitcast.22, bf16[768,768]{1,0:T(8,128)(2,1)} %bitcast.16, bf16[768,768]{1,0:T(8,128)(2,1)} %bitcast.15, bf16[128,768]{1,0:T(8,128)(2,1)} %bitcast.23, bf16[128,768]{1,0:T(8,128)(2,1)} %bitcast.24), custom_call_target="tpu_custom_call" | custom-call | tf_op jit(solution)/shard_map/attend/pallas_call | solution.py:254
  (88 shorter events, 0.8 us)
Async XLA Ops:
  1.0 14.6 %collective-permute-start.7 = (bf16[192,768]{1,0:T(8,128)(2,1)S(1)}, bf16[192,768]{1,0:T(8,128)(2,1)S(1)}, u32[]{:S(2)}, u32[]{:S(2)}) collective-permute-start(bf16[192,768]{1,0:T(8,128)(2,1)S(1)} %pad_maximum_fusion.3), channel_id=1, source_target_pairs={{0,4},{4,0},{1,5},{5,1},{2,6},{6,2},{3,7},{7,3},{8,12},{12,8},{9,1... | collective-permute-start | bytes 884744 | tf_op jit(solution)/shard_map/ppermute | solution.py:288
  13.0 52.0 %collective-permute-start.2 = (bf16[448,1536]{1,0:T(8,128)(2,1)}, bf16[448,1536]{1,0:T(8,128)(2,1)S(1)}, u32[]{:S(2)}, u32[]{:S(2)}) collective-permute-start(bf16[448,1536]{1,0:T(8,128)(2,1)} %bitcast.18), channel_id=1, source_target_pairs={{0,3},{4,5},{1,0},{5,6},{2,1},{6,7},{3,2},{7,4},{8,11},{12,13},{9,... | collective-permute-start | bytes 4128776 | tf_op jit(solution)/shard_map/ppermute | solution.py:272
  13.0 34.5 %collective-permute-start.1 = (bf16[448,1536]{1,0:T(8,128)(2,1)}, bf16[448,1536]{1,0:T(8,128)(2,1)S(1)}, u32[]{:S(2)}, u32[]{:S(2)}) collective-permute-start(bf16[448,1536]{1,0:T(8,128)(2,1)} %bitcast.19), channel_id=1, source_target_pairs={{0,1},{4,7},{1,2},{5,4},{2,3},{6,5},{3,0},{7,6},{8,9},{12,15},{9,1... | collective-permute-start | bytes 4128776 | tf_op jit(solution)/shard_map/ppermute | solution.py:272
  15.8 7.6 %collective-permute-start.18 = (bf16[192,768]{1,0:T(8,128)(2,1)S(1)}, bf16[192,768]{1,0:T(8,128)(2,1)S(1)}, u32[]{:S(2)}, u32[]{:S(2)}) collective-permute-start(bf16[192,768]{1,0:T(8,128)(2,1)S(1)} %get-tuple-element.11), channel_id=1, source_target_pairs={{0,8},{4,60},{8,16},{12,4},{16,24},{20,12},{24,32},{28,20},{32,40}... | collective-permute-start | bytes 884744 | tf_op jit(solution)/shard_map/ppermute | solution.py:272
  19.7 7.1 %collective-permute-start.8 = (bf16[192,768]{1,0:T(8,128)(2,1)S(1)}, bf16[192,768]{1,0:T(8,128)(2,1)S(1)}, u32[]{:S(2)}, u32[]{:S(2)}) collective-permute-start(bf16[192,768]{1,0:T(8,128)(2,1)S(1)} %get-tuple-element.12), channel_id=1, source_target_pairs={{0,64},{4,196},{64,128},{68,4},{128,192},{132,68},{192,0},{196,132... | collective-permute-start | bytes 884744 | tf_op jit(solution)/shard_map/ppermute | solution.py:272
  23.4 7.1 %collective-permute-start.19 = (bf16[192,768]{1,0:T(8,128)(2,1)S(1)}, bf16[192,768]{1,0:T(8,128)(2,1)S(1)}, u32[]{:S(2)}, u32[]{:S(2)}) collective-permute-start(bf16[192,768]{1,0:T(8,128)(2,1)S(1)} %collective-permute-done.18), channel_id=1, source_target_pairs={{0,8},{4,60},{8,16},{12,4},{16,24},{20,12},{24,32},{28,20},{32,40}... | collective-permute-start | bytes 884744 | tf_op jit(solution)/shard_map/ppermute | solution.py:272
  26.8 7.1 %collective-permute-start.9 = (bf16[96,768]{1,0:T(8,128)(2,1)S(1)}, bf16[96,768]{1,0:T(8,128)(2,1)S(1)}, u32[]{:S(2)}, u32[]{:S(2)}) collective-permute-start(bf16[96,768]{1,0:T(8,128)(2,1)S(1)} %get-tuple-element.15), channel_id=1, source_target_pairs={{0,64},{4,196},{64,128},{68,4},{128,192},{132,68},{192,0},{196,132... | collective-permute-start | bytes 442376 | tf_op jit(solution)/shard_map/ppermute | solution.py:272
  30.4 7.1 %collective-permute-start.20 = (bf16[192,768]{1,0:T(8,128)(2,1)S(1)}, bf16[192,768]{1,0:T(8,128)(2,1)S(1)}, u32[]{:S(2)}, u32[]{:S(2)}) collective-permute-start(bf16[192,768]{1,0:T(8,128)(2,1)S(1)} %collective-permute-done.19), channel_id=1, source_target_pairs={{0,8},{4,60},{8,16},{12,4},{16,24},{20,12},{24,32},{28,20},{32,40}... | collective-permute-start | bytes 884744 | tf_op jit(solution)/shard_map/ppermute | solution.py:272
  33.9 7.1 %collective-permute-start.10 = (bf16[288,768]{1,0:T(8,128)(2,1)S(1)}, bf16[288,768]{1,0:T(8,128)(2,1)S(1)}, u32[]{:S(2)}, u32[]{:S(2)}) collective-permute-start(bf16[288,768]{1,0:T(8,128)(2,1)S(1)} %pad_maximum_fusion.1), channel_id=1, source_target_pairs={{0,4},{4,0},{1,5},{5,1},{2,6},{6,2},{3,7},{7,3},{8,12},{12,8},{9,1... | collective-permute-start | bytes 1327112 | tf_op jit(solution)/shard_map/ppermute | solution.py:288
  37.5 5.6 %collective-permute-start.21 = (bf16[96,768]{1,0:T(8,128)(2,1)S(1)}, bf16[96,768]{1,0:T(8,128)(2,1)S(1)}, u32[]{:S(2)}, u32[]{:S(2)}) collective-permute-start(bf16[96,768]{1,0:T(8,128)(2,1)S(1)} %get-tuple-element.13), channel_id=1, source_target_pairs={{0,8},{4,60},{8,16},{12,4},{16,24},{20,12},{24,32},{28,20},{32,40}... | collective-permute-start | bytes 442376 | tf_op jit(solution)/shard_map/ppermute | solution.py:272
  43.2 7.3 %collective-permute-start.22 = (bf16[672,768]{1,0:T(8,128)(2,1)S(1)}, bf16[672,768]{1,0:T(8,128)(2,1)S(1)}, u32[]{:S(2)}, u32[]{:S(2)}) collective-permute-start(bf16[672,768]{1,0:T(8,128)(2,1)S(1)} %pad_maximum_fusion), channel_id=1, source_target_pairs={{0,4},{4,0},{1,5},{5,1},{2,6},{6,2},{3,7},{7,3},{8,12},{12,8},{9,1... | collective-permute-start | bytes 3096584 | tf_op jit(solution)/shard_map/ppermute | solution.py:288
  47.3 16.7 %copy-start.1 = (bf16[2,224,1536]{2,1,0:T(8,128)(2,1)S(1)}, bf16[2,224,1536]{2,1,0:T(8,128)(2,1)}, u32[]{:S(2)}) copy-start(bf16[2,224,1536]{2,1,0:T(8,128)(2,1)} %live_rows.1) | copy-start | bytes 4128772
  47.4 33.3 %copy-start.5 = (bf16[768,768]{1,0:T(8,128)(2,1)}, bf16[768,768]{1,0:T(8,128)(2,1)S(1)}, u32[]{:S(2)}) copy-start(bf16[768,768]{1,0:T(8,128)(2,1)S(1)} %slice_dynamic-update-slice_fusion.14.rest_8_) | copy-start | bytes 3538948
  47.4 15.4 %collective-permute-start.11 = (bf16[768,768]{1,0:T(8,128)(2,1)S(1)}, bf16[768,768]{1,0:T(8,128)(2,1)S(1)}, u32[]{:S(2)}, u32[]{:S(2)}) collective-permute-start(bf16[768,768]{1,0:T(8,128)(2,1)S(1)} %slice_dynamic-update-slice_fusion.14.rest_8_), channel_id=1, source_target_pairs={{0,8},{4,60},{8,16},{12,4},{16,24},{20,12},{24,32},{28,20},{32,40}... | collective-permute-start | bytes 3538952 | tf_op jit(solution)/shard_map/ppermute | solution.py:272
  47.5 33.2 %copy-start.9 = (bf16[448,1536]{1,0:T(8,128)(2,1)}, bf16[448,1536]{1,0:T(8,128)(2,1)S(1)}, u32[]{:S(2)}) copy-start(bf16[448,1536]{1,0:T(8,128)(2,1)S(1)} %collective-permute-done.1.rest_2_) | copy-start | bytes 4128772
  47.5 18.3 %collective-permute-start.5 = (bf16[448,1536]{1,0:T(8,128)(2,1)S(1)}, bf16[448,1536]{1,0:T(8,128)(2,1)S(1)}, u32[]{:S(2)}, u32[]{:S(2)}) collective-permute-start(bf16[448,1536]{1,0:T(8,128)(2,1)S(1)} %collective-permute-done.1.rest_2_), channel_id=1, source_target_pairs={{0,1},{4,7},{1,2},{5,4},{2,3},{6,5},{3,0},{7,6},{8,9},{12,15},{9,1... | collective-permute-start | bytes 4128776 | tf_op jit(solution)/shard_map/ppermute | solution.py:272
  50.7 29.9 %copy-start.6 = (bf16[1536,768]{1,0:T(8,128)(2,1)}, bf16[1536,768]{1,0:T(8,128)(2,1)S(1)}, u32[]{:S(2)}) copy-start(bf16[1536,768]{1,0:T(8,128)(2,1)S(1)} %slice_dynamic-update-slice_fusion.rest_16_) | copy-start | bytes 7077892
  50.8 29.9 %collective-permute-start.23 = (bf16[1536,768]{1,0:T(8,128)(2,1)S(1)}, bf16[1536,768]{1,0:T(8,128)(2,1)S(1)}, u32[]{:S(2)}, u32[]{:S(2)}) collective-permute-start(bf16[1536,768]{1,0:T(8,128)(2,1)S(1)} %slice_dynamic-update-slice_fusion.rest_16_), channel_id=1, source_target_pairs={{0,64},{4,196},{64,128},{68,4},{128,192},{132,68},{192,0},{196,132... | collective-permute-start | bytes 7077896 | tf_op jit(solution)/shard_map/ppermute | solution.py:272
  62.8 19.9 %copy-start.3 = (bf16[768,768]{1,0:T(8,128)(2,1)}, bf16[768,768]{1,0:T(8,128)(2,1)S(1)}, u32[]{:S(2)}) copy-start(bf16[768,768]{1,0:T(8,128)(2,1)S(1)} %collective-permute-done.11.rest_9_) | copy-start | bytes 3538948
  62.8 15.3 %collective-permute-start.12 = (bf16[768,768]{1,0:T(8,128)(2,1)S(1)}, bf16[768,768]{1,0:T(8,128)(2,1)S(1)}, u32[]{:S(2)}, u32[]{:S(2)}) collective-permute-start(bf16[768,768]{1,0:T(8,128)(2,1)S(1)} %collective-permute-done.11.rest_9_), channel_id=1, source_target_pairs={{0,8},{4,60},{8,16},{12,4},{16,24},{20,12},{24,32},{28,20},{32,40}... | collective-permute-start | bytes 3538952 | tf_op jit(solution)/shard_map/ppermute | solution.py:272
  64.0 18.7 %collective-permute-start = (bf16[448,1536]{1,0:T(8,128)(2,1)S(1)}, bf16[448,1536]{1,0:T(8,128)(2,1)S(1)}, u32[]{:S(2)}, u32[]{:S(2)}) collective-permute-start(bf16[448,1536]{1,0:T(8,128)(2,1)S(1)} %bitcast.21), channel_id=1, source_target_pairs={{0,4},{4,0},{1,5},{5,1},{2,6},{6,2},{3,7},{7,3},{8,12},{12,8},{9,1... | collective-permute-start | bytes 4128776 | tf_op jit(solution)/shard_map/ppermute | solution.py:288
  65.0 17.7 %copy-start.8 = (bf16[448,1536]{1,0:T(8,128)(2,1)}, bf16[448,1536]{1,0:T(8,128)(2,1)S(1)}, u32[]{:S(2)}) copy-start(bf16[448,1536]{1,0:T(8,128)(2,1)S(1)} %collective-permute-done.2.rest_4_) | copy-start | bytes 4128772
  65.0 18.4 %collective-permute-start.3 = (bf16[448,1536]{1,0:T(8,128)(2,1)S(1)}, bf16[448,1536]{1,0:T(8,128)(2,1)S(1)}, u32[]{:S(2)}, u32[]{:S(2)}) collective-permute-start(bf16[448,1536]{1,0:T(8,128)(2,1)S(1)} %collective-permute-done.2.rest_4_), channel_id=1, source_target_pairs={{0,4},{4,0},{1,5},{5,1},{2,6},{6,2},{3,7},{7,3},{8,12},{12,8},{9,1... | collective-permute-start | bytes 4128776 | tf_op jit(solution)/shard_map/ppermute | solution.py:288
  65.8 44.8 %copy-start.10 = (bf16[448,1536]{1,0:T(8,128)(2,1)}, bf16[448,1536]{1,0:T(8,128)(2,1)S(1)}, u32[]{:S(2)}) copy-start(bf16[448,1536]{1,0:T(8,128)(2,1)S(1)} %collective-permute-done.5.rest_6_) | copy-start | bytes 4128772
  65.8 17.7 %collective-permute-start.4 = (bf16[448,1536]{1,0:T(8,128)(2,1)S(1)}, bf16[448,1536]{1,0:T(8,128)(2,1)S(1)}, u32[]{:S(2)}, u32[]{:S(2)}) collective-permute-start(bf16[448,1536]{1,0:T(8,128)(2,1)S(1)} %collective-permute-done.1.rest_2_), channel_id=1, source_target_pairs={{0,4},{4,0},{1,5},{5,1},{2,6},{6,2},{3,7},{7,3},{8,12},{12,8},{9,1... | collective-permute-start | bytes 4128776 | tf_op jit(solution)/shard_map/ppermute | solution.py:288
  78.1 4.6 %copy-start.4 = (bf16[768,768]{1,0:T(8,128)(2,1)}, bf16[768,768]{1,0:T(8,128)(2,1)S(1)}, u32[]{:S(2)}) copy-start(bf16[768,768]{1,0:T(8,128)(2,1)S(1)} %collective-permute-done.12.rest_10_) | copy-start | bytes 3538948
  78.1 15.6 %collective-permute-start.13 = (bf16[768,768]{1,0:T(8,128)(2,1)S(1)}, bf16[768,768]{1,0:T(8,128)(2,1)S(1)}, u32[]{:S(2)}, u32[]{:S(2)}) collective-permute-start(bf16[768,768]{1,0:T(8,128)(2,1)S(1)} %collective-permute-done.12.rest_10_), channel_id=1, source_target_pairs={{0,8},{4,60},{8,16},{12,4},{16,24},{20,12},{24,32},{28,20},{32,40}... | collective-permute-start | bytes 3538952 | tf_op jit(solution)/shard_map/ppermute | solution.py:272
  80.7 2.8 %copy-start = (bf16[1536,768]{1,0:T(8,128)(2,1)}, bf16[1536,768]{1,0:T(8,128)(2,1)S(1)}, u32[]{:S(2)}) copy-start(bf16[1536,768]{1,0:T(8,128)(2,1)S(1)} %collective-permute-done.23.rest_17_) | copy-start | bytes 7077892
  80.7 20.8 %collective-permute-start.6 = (bf16[448,1536]{1,0:T(8,128)(2,1)S(1)}, bf16[448,1536]{1,0:T(8,128)(2,1)S(1)}, u32[]{:S(2)}, u32[]{:S(2)}) collective-permute-start(bf16[448,1536]{1,0:T(8,128)(2,1)S(1)} %collective-permute-done.5.rest_6_), channel_id=1, source_target_pairs={{0,4},{4,0},{1,5},{5,1},{2,6},{6,2},{3,7},{7,3},{8,12},{12,8},{9,1... | collective-permute-start | bytes 4128776 | tf_op jit(solution)/shard_map/ppermute | solution.py:288
  82.7 27.8 %copy-start.11 = (bf16[448,1536]{1,0:T(8,128)(2,1)}, bf16[448,1536]{1,0:T(8,128)(2,1)S(1)}, u32[]{:S(2)}) copy-start(bf16[448,1536]{1,0:T(8,128)(2,1)S(1)} %collective-permute-done.rest_1_) | copy-start | bytes 4128772
  82.7 13.6 %collective-permute-start.15 = (bf16[384,768]{1,0:T(8,128)(2,1)S(1)}, bf16[384,768]{1,0:T(8,128)(2,1)S(1)}, u32[]{:S(2)}, u32[]{:S(2)}) collective-permute-start(bf16[384,768]{1,0:T(8,128)(2,1)S(1)} %slice.130), channel_id=1, source_target_pairs={{0,4},{4,0},{1,5},{5,1},{2,6},{6,2},{3,7},{7,3},{8,12},{12,8},{9,1... | collective-permute-start | bytes 1769480 | tf_op jit(solution)/shard_map/ppermute | solution.py:288
  83.4 27.2 %copy-start.12 = (bf16[448,1536]{1,0:T(8,128)(2,1)}, bf16[448,1536]{1,0:T(8,128)(2,1)S(1)}, u32[]{:S(2)}) copy-start(bf16[448,1536]{1,0:T(8,128)(2,1)S(1)} %collective-permute-done.3.rest_3_) | copy-start | bytes 4128772
  83.4 18.1 %collective-permute-start.16 = (bf16[384,768]{1,0:T(8,128)(2,1)S(1)}, bf16[384,768]{1,0:T(8,128)(2,1)S(1)}, u32[]{:S(2)}, u32[]{:S(2)}) collective-permute-start(bf16[384,768]{1,0:T(8,128)(2,1)S(1)} %slice.131), channel_id=1, source_target_pairs={{0,4},{4,0},{1,5},{5,1},{2,6},{6,2},{3,7},{7,3},{8,12},{12,8},{9,1... | collective-permute-start | bytes 1769480 | tf_op jit(solution)/shard_map/ppermute | solution.py:288
  83.5 27.1 %copy-start.13 = (bf16[448,1536]{1,0:T(8,128)(2,1)}, bf16[448,1536]{1,0:T(8,128)(2,1)S(1)}, u32[]{:S(2)}) copy-start(bf16[448,1536]{1,0:T(8,128)(2,1)S(1)} %collective-permute-done.4.rest_5_) | copy-start | bytes 4128772
  83.5 27.0 %collective-permute-start.25 = (bf16[768,768]{1,0:T(8,128)(2,1)S(1)}, bf16[768,768]{1,0:T(8,128)(2,1)S(1)}, u32[]{:S(2)}, u32[]{:S(2)}) collective-permute-start(bf16[768,768]{1,0:T(8,128)(2,1)S(1)} %get-tuple-element.7), channel_id=1, source_target_pairs={{0,4},{4,0},{1,5},{5,1},{2,6},{6,2},{3,7},{7,3},{8,12},{12,8},{9,1... | collective-permute-start | bytes 3538952 | tf_op jit(solution)/shard_map/ppermute | solution.py:288
  93.7 16.9 %copy-start.2 = (bf16[768,768]{1,0:T(8,128)(2,1)}, bf16[768,768]{1,0:T(8,128)(2,1)S(1)}, u32[]{:S(2)}) copy-start(bf16[768,768]{1,0:T(8,128)(2,1)S(1)} %collective-permute-done.13.rest_11_) | copy-start | bytes 3538948
  93.7 16.9 %collective-permute-start.24 = (bf16[768,768]{1,0:T(8,128)(2,1)S(1)}, bf16[768,768]{1,0:T(8,128)(2,1)S(1)}, u32[]{:S(2)}, u32[]{:S(2)}) collective-permute-start(bf16[768,768]{1,0:T(8,128)(2,1)S(1)} %get-tuple-element.8), channel_id=1, source_target_pairs={{0,64},{4,196},{64,128},{68,4},{128,192},{132,68},{192,0},{196,132... | collective-permute-start | bytes 3538952 | tf_op jit(solution)/shard_map/ppermute | solution.py:272
  96.3 14.3 %copy-start.17 = (bf16[384,768]{1,0:T(8,128)(2,1)}, bf16[384,768]{1,0:T(8,128)(2,1)S(1)}, u32[]{:S(2)}) copy-start(bf16[384,768]{1,0:T(8,128)(2,1)S(1)} %collective-permute-done.15.rest_13_) | copy-start | bytes 1769476
  96.3 6.8 %collective-permute-start.17 = (bf16[384,768]{1,0:T(8,128)(2,1)S(1)}, bf16[384,768]{1,0:T(8,128)(2,1)S(1)}, u32[]{:S(2)}, u32[]{:S(2)}) collective-permute-start(bf16[384,768]{1,0:T(8,128)(2,1)S(1)} %get-tuple-element.9), channel_id=1, source_target_pairs={{0,4},{4,0},{1,5},{5,1},{2,6},{6,2},{3,7},{7,3},{8,12},{12,8},{9,1... | collective-permute-start | bytes 1769480 | tf_op jit(solution)/shard_map/ppermute | solution.py:288
  101.5 9.1 %copy-start.18 = (bf16[384,768]{1,0:T(8,128)(2,1)}, bf16[384,768]{1,0:T(8,128)(2,1)S(1)}, u32[]{:S(2)}) copy-start(bf16[384,768]{1,0:T(8,128)(2,1)S(1)} %collective-permute-done.16.rest_14_) | copy-start | bytes 1769476
  101.5 9.0 %collective-permute-start.14 = (bf16[384,768]{1,0:T(8,128)(2,1)S(1)}, bf16[384,768]{1,0:T(8,128)(2,1)S(1)}, u32[]{:S(2)}, u32[]{:S(2)}) collective-permute-start(bf16[384,768]{1,0:T(8,128)(2,1)S(1)} %get-tuple-element.10), channel_id=1, source_target_pairs={{0,8},{4,60},{8,16},{12,4},{16,24},{20,12},{24,32},{28,20},{32,40}... | collective-permute-start | bytes 1769480 | tf_op jit(solution)/shard_map/ppermute | solution.py:272
  101.5 9.1 %copy-start.14 = (bf16[448,1536]{1,0:T(8,128)(2,1)}, bf16[448,1536]{1,0:T(8,128)(2,1)S(1)}, u32[]{:S(2)}) copy-start(bf16[448,1536]{1,0:T(8,128)(2,1)S(1)} %collective-permute-done.6.rest_7_) | copy-start | bytes 4128772
  103.1 7.5 %copy-start.19 = (bf16[384,768]{1,0:T(8,128)(2,1)}, bf16[384,768]{1,0:T(8,128)(2,1)S(1)}, u32[]{:S(2)}) copy-start(bf16[384,768]{1,0:T(8,128)(2,1)S(1)} %collective-permute-done.17.rest_15_) | copy-start | bytes 1769476
  110.5 0.8 copy-start.20
  110.6 1.2 copy-start.15
  111.8 1.0 copy-start.16
  131.2 13.3 %copy-start.7 = (s32[64]{0:T(128)S(1)}, s32[64]{0:T(128)}, u32[]{:S(2)}) copy-start(s32[64]{0:T(128)} %param.13) | copy-start | bytes 772
  131.2 69.9 %all-to-all-start = ((bf16[64,24,768]{2,1,0:T(8,128)(2,1)}), bf16[64,24,768]{2,1,0:T(8,128)(2,1)S(1)}, u32[]{:S(2)}, u32[]{:S(2)}) async-start(bf16[64,24,768]{2,1,0:T(8,128)(2,1)} %bitcast.17), calls=%async_computation | async-start | bytes 4718592 | tf_op jit(solution)/shard_map/all_to_all | solution.py:353
